TPU v7x, 32 devices: a whole 2x2x4 slice. The times are simulated.
32 devices in a mesh: seq: 8 (over z, core), tensor: 4 (over y, x).
Axes of the slice: x: 2, y: 2, z: 4, core: 2. Of those that a mesh axis runs over, the one named last changes fastest.
Arguments:
- queries: bfloat16 [2048, 1024], P('seq', 'tensor'), may hold values from -6 to 6
- keys: bfloat16 [2048, 1024], P('seq', 'tensor'), may hold values from -6 to 6
- values: bfloat16 [2048, 1024], P('seq', 'tensor'), may hold values from -6 to 6
- log_decay: float32 [8, 2048], P('tensor', 'seq'), may hold values from -1.6 to 0, as said below
- norm_gain: float32 [1024], P('tensor'), may hold values from 0.1 to 1.9
- out_weight: bfloat16 [1024, 6144], P('tensor'), may hold values from -0.25 to 0.25
- out_grad: bfloat16 [2048, 6144], P('seq', 'tensor'), may hold values from -6 to 6
Outputs:
- layer_out: bfloat16 [2048, 6144], P('seq', 'tensor')
- query_grad: bfloat16 [2048, 1024], P('seq', 'tensor')
- key_grad: bfloat16 [2048, 1024], P('seq', 'tensor')
- value_grad: bfloat16 [2048, 1024], P('seq', 'tensor')
Inputs may be any that keep to these rules, and one draw needn't show every extreme that they name: `log_decay`: strictly negative.
All inputs are finite; a program needn't handle non-finite values.
Results may differ from a plain program's by a relative error of at most 0.015.
Values may be sent and summed in bfloat16 or wider, within the bound.
No kernel may reach another device: no remote copies, remote signals or barrier semaphores. Data moves between devices by JAX's collectives and lax.ppermute only.
A program may use at most 64 MiB of HBM per device.

v0:
```python
import jax
import jax.numpy as jnp
from jax import lax
from jax.sharding import PartitionSpec as P

EXACT = lax.Precision.HIGHEST
EPSILON = 1e-05


def from_behind(value, axis, steps):
    count = lax.axis_size(axis)
    initial, last = (max(0, -steps), min(count, count - steps))
    return lax.ppermute(value, axis, [(source, source + steps) for source in range(initial, last)])


def hop_states(total, fresh, later):
    shrink = jnp.exp(total)[:, None, None]
    offset = -1 if later else 1

    def advance(number, held):
        return from_behind((shrink * held + fresh).astype(jnp.bfloat16), "seq", offset).astype(
            jnp.float32
        )

    return lax.fori_loop(0, lax.axis_size("seq") - 1, advance, jnp.zeros_like(fresh))


def on_device(queries, keys, values, log_decay, norm_gain, out_weight, out_grad):
    length = queries.shape[0]
    heads = log_decay.shape[0]
    size = queries.shape[1] // heads

    def spread(rows):
        return rows.astype(jnp.float32).reshape(length, heads, size)

    query_rows = spread(queries)
    key_rows = spread(keys)
    value_rows = spread(values)
    running = jnp.cumsum(log_decay, axis=1)
    total = running[:, -1]
    lower = jnp.arange(length)[:, None] >= jnp.arange(length)[None, :]
    weight = jnp.exp(jnp.where(lower, running[:, :, None] - running[:, None, :], -1e30))
    grow = jnp.exp(running).T[:, :, None]
    fade = jnp.exp(total[None, :] - running.T)[:, :, None]
    scores = jnp.einsum("the,she->hts", query_rows, key_rows, precision=EXACT) * weight
    fresh = jnp.einsum("she,shf->hef", key_rows * fade, value_rows, precision=EXACT)

    def carry(states, later):
        return hop_states(total, states, later)

    state_in = carry(fresh, False)
    inner = jnp.einsum("hts,shf->thf", scores, value_rows, precision=EXACT)
    mixed = inner + jnp.einsum("the,hef->thf", query_rows * grow, state_in, precision=EXACT)
    scale = lax.rsqrt(jnp.mean(mixed * mixed, axis=-1, keepdims=True) + EPSILON)
    gain = norm_gain.reshape(heads, size)
    normed = (mixed * scale * gain).reshape(length, heads * size).astype(jnp.bfloat16)
    partial_value = jnp.dot(normed, out_weight, preferred_element_type=jnp.float32)
    layer_out = lax.psum_scatter(
        partial_value.astype(jnp.bfloat16), "tensor", scatter_dimension=1, tiled=True
    )
    grad_normed = lax.dot_general(
        lax.all_gather(out_grad, "tensor", axis=1, tiled=True),
        out_weight,
        (((1,), (1,)), ((), ())),
        preferred_element_type=jnp.float32,
    ).reshape(length, heads, size)
    lifted = gain * grad_normed
    grad_mixed = scale * lifted - mixed * scale**3 * jnp.mean(
        mixed * lifted, axis=-1, keepdims=True
    )
    upward = jnp.einsum("the,thf->hef", query_rows * grow, grad_mixed, precision=EXACT)
    state_back = carry(upward, True)
    grad_scores = jnp.einsum("thf,shf->hts", grad_mixed, value_rows, precision=EXACT) * weight
    grad_query = jnp.einsum(
        "hts,she->the", grad_scores, key_rows, precision=EXACT
    ) + grow * jnp.einsum("thf,hef->the", grad_mixed, state_in, precision=EXACT)
    grad_key = jnp.einsum(
        "hts,the->she", grad_scores, query_rows, precision=EXACT
    ) + fade * jnp.einsum("shf,hef->she", value_rows, state_back, precision=EXACT)
    grad_value = jnp.einsum(
        "hts,thf->shf", scores, grad_mixed, precision=EXACT
    ) + fade * jnp.einsum("she,hef->shf", key_rows, state_back, precision=EXACT)
    return (
        layer_out,
        grad_query.reshape(length, heads * size).astype(jnp.bfloat16),
        grad_key.reshape(length, heads * size).astype(jnp.bfloat16),
        grad_value.reshape(length, heads * size).astype(jnp.bfloat16),
    )


def solution(mesh):
    in_specs = (
        P("seq", "tensor"),
        P("seq", "tensor"),
        P("seq", "tensor"),
        P("tensor", "seq"),
        P("tensor"),
        P("tensor", None),
        P("seq", "tensor"),
    )
    out_specs = (P("seq", "tensor"), P("seq", "tensor"), P("seq", "tensor"), P("seq", "tensor"))
    return jax.shard_map(
        on_device, mesh=mesh, in_specs=in_specs, out_specs=out_specs, check_vma=False
    )
```

profile of v0, /device:TPU:0, one launch (start us, length us, event | category | flops | bytes accessed | tf_op | source)
XLA Modules:
  0.0 189.6 jit_solution(1812499405629348486)
XLA Ops:
  16.0 2.0 %convolution_bitcast_fusion.5 = f32[256,2,128]{0,2,1:T(8,128)} fusion(f32[2,256,256]{2,1,0:T(8,128)S(1)} %convolution_multiply_fusion, bf16[256,256]{1,0:T(8,128)(2,1)} %param.13), kind=kOutput, calls=%fused_computation.19 | convolution fusion | flops 201326592 | bytes 917504 | tf_op jit(solution)/shard_map/hts,shf->thf/dot_general | solution.py:52
  18.0 38.5 %all-gather.2.cloned.1.call-done = bf16[256,6144]{1,0:T(8,128)(2,1)} async-done(((bf16[256,1536]{1,0:T(8,128)(2,1)}), bf16[256,6144]{1,0:T(8,128)(2,1)}) %all-gather.2.cloned.1.call-update) | async-done | bytes 3145744 | tf_op jit(solution)/shard_map/all_gather | solution.py:62
  56.6 3.6 %fusion.29 = f32[256,256]{0,1:T(8,128)} fusion(bf16[256,6144]{1,0:T(8,128)(2,1)} %all-gather.2.cloned.1.call-done, bf16[256,6144]{1,0:T(8,128)(2,1)S(1)} %copy-done), kind=kOutput, calls=%fused_computation.58 | convolution fusion | flops 805306368 | bytes 6553600 | tf_op jit(solution)/shard_map/dot_general | solution.py:61
  60.2 36.4 %while.22 = (s32[]{:T(128)}, f32[2,128,128]{2,1,0:T(8,128)S(1)}, f32[2,1,1]{0,2,1:T(1,128)S(1)}, f32[2,128,128]{2,1,0:T(8,128)S(1)}, s32[]{:T(128)}, /*index=5*/s32[]{:T(128)}) while((s32[]{:T(128)}, f32[2,128,128]{2,1,0:T(8,128)S(1)}, f32[2,1,1]{0,2,1:T(1,128)S(1)}, f32[2,128,128]{2,1,0:T(8,128)S(1)}, s32[]{:T(128)}, ...), condition=%wide.region_3.4_spmd.clone, body=%wide.region_2.3_spmd.clone.sunk | while | flops 163843 | bytes 786559 | solution.py:25
  60.3 1.7 collective-permute-start
  63.0 4.1 %collective-permute-start = (bf16[2,128,128]{2,1,0:T(8,128)(2,1)S(1)}, bf16[2,128,128]{2,1,0:T(8,128)(2,1)S(1)}, u32[]{:S(2)}, u32[]{:S(2)}) collective-permute-start(bf16[2,128,128]{2,1,0:T(8,128)(2,1)S(1)} %fusion.57), channel_id=1, source_target_pairs={{0,4},{4,8},{8,12},{12,16},{16,20},{20,24},{24,28},{1,5},{5,9},{9,... | collective-permute-start | bytes 196616 | tf_op jit(solution)/shard_map/while/body/eval_jaxpr/ppermute | solution.py:13
  68.1 4.7 %collective-permute-start = (bf16[2,128,128]{2,1,0:T(8,128)(2,1)S(1)}, bf16[2,128,128]{2,1,0:T(8,128)(2,1)S(1)}, u32[]{:S(2)}, u32[]{:S(2)}) collective-permute-start(bf16[2,128,128]{2,1,0:T(8,128)(2,1)S(1)} %fusion.57), channel_id=1, source_target_pairs={{0,4},{4,8},{8,12},{12,16},{16,20},{20,24},{24,28},{1,5},{5,9},{9,... | collective-permute-start | bytes 196616 | tf_op jit(solution)/shard_map/while/body/eval_jaxpr/ppermute | solution.py:13
  73.8 4.7 %collective-permute-start = (bf16[2,128,128]{2,1,0:T(8,128)(2,1)S(1)}, bf16[2,128,128]{2,1,0:T(8,128)(2,1)S(1)}, u32[]{:S(2)}, u32[]{:S(2)}) collective-permute-start(bf16[2,128,128]{2,1,0:T(8,128)(2,1)S(1)} %fusion.57), channel_id=1, source_target_pairs={{0,4},{4,8},{8,12},{12,16},{16,20},{20,24},{24,28},{1,5},{5,9},{9,... | collective-permute-start | bytes 196616 | tf_op jit(solution)/shard_map/while/body/eval_jaxpr/ppermute | solution.py:13
  79.5 4.7 %collective-permute-start = (bf16[2,128,128]{2,1,0:T(8,128)(2,1)S(1)}, bf16[2,128,128]{2,1,0:T(8,128)(2,1)S(1)}, u32[]{:S(2)}, u32[]{:S(2)}) collective-permute-start(bf16[2,128,128]{2,1,0:T(8,128)(2,1)S(1)} %fusion.57), channel_id=1, source_target_pairs={{0,4},{4,8},{8,12},{12,16},{16,20},{20,24},{24,28},{1,5},{5,9},{9,... | collective-permute-start | bytes 196616 | tf_op jit(solution)/shard_map/while/body/eval_jaxpr/ppermute | solution.py:13
  85.2 4.7 %collective-permute-start = (bf16[2,128,128]{2,1,0:T(8,128)(2,1)S(1)}, bf16[2,128,128]{2,1,0:T(8,128)(2,1)S(1)}, u32[]{:S(2)}, u32[]{:S(2)}) collective-permute-start(bf16[2,128,128]{2,1,0:T(8,128)(2,1)S(1)} %fusion.57), channel_id=1, source_target_pairs={{0,4},{4,8},{8,12},{12,16},{16,20},{20,24},{24,28},{1,5},{5,9},{9,... | collective-permute-start | bytes 196616 | tf_op jit(solution)/shard_map/while/body/eval_jaxpr/ppermute | solution.py:13
  91.0 4.7 %collective-permute-start = (bf16[2,128,128]{2,1,0:T(8,128)(2,1)S(1)}, bf16[2,128,128]{2,1,0:T(8,128)(2,1)S(1)}, u32[]{:S(2)}, u32[]{:S(2)}) collective-permute-start(bf16[2,128,128]{2,1,0:T(8,128)(2,1)S(1)} %fusion.57), channel_id=1, source_target_pairs={{0,4},{4,8},{8,12},{12,16},{16,20},{20,24},{24,28},{1,5},{5,9},{9,... | collective-permute-start | bytes 196616 | tf_op jit(solution)/shard_map/while/body/eval_jaxpr/ppermute | solution.py:13
  99.2 2.7 %convolution_convert_fusion = bf16[256,6144]{1,0:T(8,128)(2,1)} fusion(bf16[256,256]{0,1:T(8,128)(2,1)S(1)} %bitcast.121, bf16[256,6144]{1,0:T(8,128)(2,1)S(1)} %copy-done), kind=kOutput, calls=%fused_computation.6 | convolution fusion | flops 806879232 | bytes 6422528 | tf_op jit(solution)/shard_map/dot_general | solution.py:57
  101.9 2.0 %fusion.14 = f32[2,128,128]{2,1,0:T(8,128)} fusion(f32[256,2,128]{0,2,1:T(8,128)S(1)} %get-tuple-element.106, bf16[256,2,128]{0,2,1:T(8,128)(2,1)} %bitcast.117, f32[256,2]{0,1:T(2,128)S(1)} %get-tuple-element.110), kind=kOutput, calls=%fused_computation.33 | convolution fusion | flops 100794368 | bytes 526336 | tf_op jit(solution)/shard_map/the,thf->hef/dot_general | solution.py:71
  103.9 64.7 %while.23 = (s32[]{:T(128)}, f32[2,128,128]{2,1,0:T(8,128)}, f32[2,1,1]{0,2,1:T(1,128)S(1)}, f32[2,128,128]{2,1,0:T(8,128)}, s32[]{:T(128)}, /*index=5*/s32[]{:T(128)}) while((s32[]{:T(128)}, f32[2,128,128]{2,1,0:T(8,128)}, f32[2,1,1]{0,2,1:T(1,128)S(1)}, f32[2,128,128]{2,1,0:T(8,128)}, s32[]{:T(128)}, /*index=5*/s32[]{:T(128)}) %tuple.61), condition=%wide.region_8.9_spmd.clone, body=%wide.region_7.8_spmd.clone.sunk | while | flops 163843 | bytes 786559 | solution.py:25
  106.8 4.5 %collective-permute-done.1 = bf16[2,128,128]{2,1,0:T(8,128)(2,1)} collective-permute-done((bf16[2,128,128]{2,1,0:T(8,128)(2,1)}, bf16[2,128,128]{2,1,0:T(8,128)(2,1)}, u32[]{:S(2)}, u32[]{:S(2)}) %collective-permute-start.1) | collective-permute-done | bytes 65568 | tf_op jit(solution)/shard_map/while/body/eval_jaxpr/ppermute | solution.py:13
  112.8 1.7 fusion.58
  115.8 5.5 %collective-permute-done.1 = bf16[2,128,128]{2,1,0:T(8,128)(2,1)} collective-permute-done((bf16[2,128,128]{2,1,0:T(8,128)(2,1)}, bf16[2,128,128]{2,1,0:T(8,128)(2,1)}, u32[]{:S(2)}, u32[]{:S(2)}) %collective-permute-start.1) | collective-permute-done | bytes 65568 | tf_op jit(solution)/shard_map/while/body/eval_jaxpr/ppermute | solution.py:13
  125.8 4.9 %collective-permute-done.1 = bf16[2,128,128]{2,1,0:T(8,128)(2,1)} collective-permute-done((bf16[2,128,128]{2,1,0:T(8,128)(2,1)}, bf16[2,128,128]{2,1,0:T(8,128)(2,1)}, u32[]{:S(2)}, u32[]{:S(2)}) %collective-permute-start.1) | collective-permute-done | bytes 65568 | tf_op jit(solution)/shard_map/while/body/eval_jaxpr/ppermute | solution.py:13
  132.1 1.7 fusion.58
  135.1 4.6 %collective-permute-done.1 = bf16[2,128,128]{2,1,0:T(8,128)(2,1)} collective-permute-done((bf16[2,128,128]{2,1,0:T(8,128)(2,1)}, bf16[2,128,128]{2,1,0:T(8,128)(2,1)}, u32[]{:S(2)}, u32[]{:S(2)}) %collective-permute-start.1) | collective-permute-done | bytes 65568 | tf_op jit(solution)/shard_map/while/body/eval_jaxpr/ppermute | solution.py:13
  144.1 4.9 %collective-permute-done.1 = bf16[2,128,128]{2,1,0:T(8,128)(2,1)} collective-permute-done((bf16[2,128,128]{2,1,0:T(8,128)(2,1)}, bf16[2,128,128]{2,1,0:T(8,128)(2,1)}, u32[]{:S(2)}, u32[]{:S(2)}) %collective-permute-start.1) | collective-permute-done | bytes 65568 | tf_op jit(solution)/shard_map/while/body/eval_jaxpr/ppermute | solution.py:13
  153.5 4.6 %collective-permute-done.1 = bf16[2,128,128]{2,1,0:T(8,128)(2,1)} collective-permute-done((bf16[2,128,128]{2,1,0:T(8,128)(2,1)}, bf16[2,128,128]{2,1,0:T(8,128)(2,1)}, u32[]{:S(2)}, u32[]{:S(2)}) %collective-permute-start.1) | collective-permute-done | bytes 65568 | tf_op jit(solution)/shard_map/while/body/eval_jaxpr/ppermute | solution.py:13
  162.6 4.6 %collective-permute-done.1 = bf16[2,128,128]{2,1,0:T(8,128)(2,1)} collective-permute-done((bf16[2,128,128]{2,1,0:T(8,128)(2,1)}, bf16[2,128,128]{2,1,0:T(8,128)(2,1)}, u32[]{:S(2)}, u32[]{:S(2)}) %collective-permute-start.1) | collective-permute-done | bytes 65568 | tf_op jit(solution)/shard_map/while/body/eval_jaxpr/ppermute | solution.py:13
  169.9 2.1 %fusion.13 = bf16[256,2,128]{0,2,1:T(8,128)(2,1)} fusion(f32[256,2,128]{0,2,1:T(8,128)S(1)} %fusion.9, f32[256,2,128]{0,2,1:T(8,128)S(1)} %get-tuple-element.106, f32[2,256,256]{2,1,0:T(8,128)} %copy-done.2), kind=kOutput, calls=%fused_computation.26 | convolution fusion | flops 201457664 | bytes 1179648 | tf_op jit(solution)/shard_map/hts,thf->shf/dot_general | solution.py:80
  (84 shorter events, 57.8 us)
Async XLA Ops:
  7.2 49.4 %copy-start = (bf16[256,6144]{1,0:T(8,128)(2,1)S(1)}, bf16[256,6144]{1,0:T(8,128)(2,1)}, u32[]{:S(2)}) copy-start(bf16[256,6144]{1,0:T(8,128)(2,1)} %param.16) | copy-start | bytes 9437188
  7.2 49.4 %all-gather.2.cloned.1.call-start = ((), (), s32[]{:S(2)}) async-start(), calls=%async_computation.2 | async-start | bytes 3932160 | tf_op jit(solution)/shard_map/all_gather | solution.py:62
  7.9 174.8 %reduce-scatter.2.cloned.1.call-start = ((), (), s32[]{:S(2)}) async-start(), calls=%async_computation.1 | async-start | bytes 3932160 | tf_op jit(solution)/shard_map/reduce_scatter | solution.py:58
  12.7 47.5 %copy-start.3 = (bf16[256,256]{0,1:T(8,128)(2,1)}, bf16[256,256]{0,1:T(8,128)(2,1)S(1)}, u32[]{:S(2)}) copy-start(bf16[256,256]{0,1:T(8,128)(2,1)S(1)} %copy.31) | copy-start | bytes 393220
  12.7 1.3 copy-start.4
  15.2 0.8 copy-start.2
  60.3 2.6 %collective-permute-start = (bf16[2,128,128]{2,1,0:T(8,128)(2,1)S(1)}, bf16[2,128,128]{2,1,0:T(8,128)(2,1)S(1)}, u32[]{:S(2)}, u32[]{:S(2)}) collective-permute-start(bf16[2,128,128]{2,1,0:T(8,128)(2,1)S(1)} %fusion.57), channel_id=1, source_target_pairs={{0,4},{4,8},{8,12},{12,16},{16,20},{20,24},{24,28},{1,5},{5,9},{9,... | collective-permute-start | bytes 196616 | tf_op jit(solution)/shard_map/while/body/eval_jaxpr/ppermute | solution.py:13
  63.0 5.0 %collective-permute-start = (bf16[2,128,128]{2,1,0:T(8,128)(2,1)S(1)}, bf16[2,128,128]{2,1,0:T(8,128)(2,1)S(1)}, u32[]{:S(2)}, u32[]{:S(2)}) collective-permute-start(bf16[2,128,128]{2,1,0:T(8,128)(2,1)S(1)} %fusion.57), channel_id=1, source_target_pairs={{0,4},{4,8},{8,12},{12,16},{16,20},{20,24},{24,28},{1,5},{5,9},{9,... | collective-permute-start | bytes 196616 | tf_op jit(solution)/shard_map/while/body/eval_jaxpr/ppermute | solution.py:13
  68.1 5.6 %collective-permute-start = (bf16[2,128,128]{2,1,0:T(8,128)(2,1)S(1)}, bf16[2,128,128]{2,1,0:T(8,128)(2,1)S(1)}, u32[]{:S(2)}, u32[]{:S(2)}) collective-permute-start(bf16[2,128,128]{2,1,0:T(8,128)(2,1)S(1)} %fusion.57), channel_id=1, source_target_pairs={{0,4},{4,8},{8,12},{12,16},{16,20},{20,24},{24,28},{1,5},{5,9},{9,... | collective-permute-start | bytes 196616 | tf_op jit(solution)/shard_map/while/body/eval_jaxpr/ppermute | solution.py:13
  73.8 5.6 %collective-permute-start = (bf16[2,128,128]{2,1,0:T(8,128)(2,1)S(1)}, bf16[2,128,128]{2,1,0:T(8,128)(2,1)S(1)}, u32[]{:S(2)}, u32[]{:S(2)}) collective-permute-start(bf16[2,128,128]{2,1,0:T(8,128)(2,1)S(1)} %fusion.57), channel_id=1, source_target_pairs={{0,4},{4,8},{8,12},{12,16},{16,20},{20,24},{24,28},{1,5},{5,9},{9,... | collective-permute-start | bytes 196616 | tf_op jit(solution)/shard_map/while/body/eval_jaxpr/ppermute | solution.py:13
  79.5 5.6 %collective-permute-start = (bf16[2,128,128]{2,1,0:T(8,128)(2,1)S(1)}, bf16[2,128,128]{2,1,0:T(8,128)(2,1)S(1)}, u32[]{:S(2)}, u32[]{:S(2)}) collective-permute-start(bf16[2,128,128]{2,1,0:T(8,128)(2,1)S(1)} %fusion.57), channel_id=1, source_target_pairs={{0,4},{4,8},{8,12},{12,16},{16,20},{20,24},{24,28},{1,5},{5,9},{9,... | collective-permute-start | bytes 196616 | tf_op jit(solution)/shard_map/while/body/eval_jaxpr/ppermute | solution.py:13
  85.2 5.6 %collective-permute-start = (bf16[2,128,128]{2,1,0:T(8,128)(2,1)S(1)}, bf16[2,128,128]{2,1,0:T(8,128)(2,1)S(1)}, u32[]{:S(2)}, u32[]{:S(2)}) collective-permute-start(bf16[2,128,128]{2,1,0:T(8,128)(2,1)S(1)} %fusion.57), channel_id=1, source_target_pairs={{0,4},{4,8},{8,12},{12,16},{16,20},{20,24},{24,28},{1,5},{5,9},{9,... | collective-permute-start | bytes 196616 | tf_op jit(solution)/shard_map/while/body/eval_jaxpr/ppermute | solution.py:13
  91.0 5.6 %collective-permute-start = (bf16[2,128,128]{2,1,0:T(8,128)(2,1)S(1)}, bf16[2,128,128]{2,1,0:T(8,128)(2,1)S(1)}, u32[]{:S(2)}, u32[]{:S(2)}) collective-permute-start(bf16[2,128,128]{2,1,0:T(8,128)(2,1)S(1)} %fusion.57), channel_id=1, source_target_pairs={{0,4},{4,8},{8,12},{12,16},{16,20},{20,24},{24,28},{1,5},{5,9},{9,... | collective-permute-start | bytes 196616 | tf_op jit(solution)/shard_map/while/body/eval_jaxpr/ppermute | solution.py:13
  105.5 5.8 %collective-permute-start.1 = (bf16[2,128,128]{2,1,0:T(8,128)(2,1)}, bf16[2,128,128]{2,1,0:T(8,128)(2,1)}, u32[]{:S(2)}, u32[]{:S(2)}) collective-permute-start(bf16[2,128,128]{2,1,0:T(8,128)(2,1)} %fusion.58), channel_id=1, source_target_pairs={{4,0},{8,4},{12,8},{16,12},{20,16},{24,20},{28,24},{5,1},{9,5},{13... | collective-permute-start | bytes 196616 | tf_op jit(solution)/shard_map/while/body/eval_jaxpr/ppermute | solution.py:13
  114.5 6.8 %collective-permute-start.1 = (bf16[2,128,128]{2,1,0:T(8,128)(2,1)}, bf16[2,128,128]{2,1,0:T(8,128)(2,1)}, u32[]{:S(2)}, u32[]{:S(2)}) collective-permute-start(bf16[2,128,128]{2,1,0:T(8,128)(2,1)} %fusion.58), channel_id=1, source_target_pairs={{4,0},{8,4},{12,8},{16,12},{20,16},{24,20},{28,24},{5,1},{9,5},{13... | collective-permute-start | bytes 196616 | tf_op jit(solution)/shard_map/while/body/eval_jaxpr/ppermute | solution.py:13
  124.5 6.2 %collective-permute-start.1 = (bf16[2,128,128]{2,1,0:T(8,128)(2,1)}, bf16[2,128,128]{2,1,0:T(8,128)(2,1)}, u32[]{:S(2)}, u32[]{:S(2)}) collective-permute-start(bf16[2,128,128]{2,1,0:T(8,128)(2,1)} %fusion.58), channel_id=1, source_target_pairs={{4,0},{8,4},{12,8},{16,12},{20,16},{24,20},{28,24},{5,1},{9,5},{13... | collective-permute-start | bytes 196616 | tf_op jit(solution)/shard_map/while/body/eval_jaxpr/ppermute | solution.py:13
  133.8 5.9 %collective-permute-start.1 = (bf16[2,128,128]{2,1,0:T(8,128)(2,1)}, bf16[2,128,128]{2,1,0:T(8,128)(2,1)}, u32[]{:S(2)}, u32[]{:S(2)}) collective-permute-start(bf16[2,128,128]{2,1,0:T(8,128)(2,1)} %fusion.58), channel_id=1, source_target_pairs={{4,0},{8,4},{12,8},{16,12},{20,16},{24,20},{28,24},{5,1},{9,5},{13... | collective-permute-start | bytes 196616 | tf_op jit(solution)/shard_map/while/body/eval_jaxpr/ppermute | solution.py:13
  142.9 6.2 %collective-permute-start.1 = (bf16[2,128,128]{2,1,0:T(8,128)(2,1)}, bf16[2,128,128]{2,1,0:T(8,128)(2,1)}, u32[]{:S(2)}, u32[]{:S(2)}) collective-permute-start(bf16[2,128,128]{2,1,0:T(8,128)(2,1)} %fusion.58), channel_id=1, source_target_pairs={{4,0},{8,4},{12,8},{16,12},{20,16},{24,20},{28,24},{5,1},{9,5},{13... | collective-permute-start | bytes 196616 | tf_op jit(solution)/shard_map/while/body/eval_jaxpr/ppermute | solution.py:13
  152.2 5.9 %collective-permute-start.1 = (bf16[2,128,128]{2,1,0:T(8,128)(2,1)}, bf16[2,128,128]{2,1,0:T(8,128)(2,1)}, u32[]{:S(2)}, u32[]{:S(2)}) collective-permute-start(bf16[2,128,128]{2,1,0:T(8,128)(2,1)} %fusion.58), channel_id=1, source_target_pairs={{4,0},{8,4},{12,8},{16,12},{20,16},{24,20},{28,24},{5,1},{9,5},{13... | collective-permute-start | bytes 196616 | tf_op jit(solution)/shard_map/while/body/eval_jaxpr/ppermute | solution.py:13
  161.3 5.9 %collective-permute-start.1 = (bf16[2,128,128]{2,1,0:T(8,128)(2,1)}, bf16[2,128,128]{2,1,0:T(8,128)(2,1)}, u32[]{:S(2)}, u32[]{:S(2)}) collective-permute-start(bf16[2,128,128]{2,1,0:T(8,128)(2,1)} %fusion.58), channel_id=1, source_target_pairs={{4,0},{8,4},{12,8},{16,12},{20,16},{24,20},{28,24},{5,1},{9,5},{13... | collective-permute-start | bytes 196616 | tf_op jit(solution)/shard_map/while/body/eval_jaxpr/ppermute | solution.py:13
  175.1 2.5 %copy-start.1 = (f32[2,256,256]{2,1,0:T(8,128)}, f32[2,256,256]{2,1,0:T(8,128)S(1)}, u32[]{:S(2)}) copy-start(f32[2,256,256]{2,1,0:T(8,128)S(1)} %convolution_multiply_fusion.1) | copy-start | bytes 1572868
Sparse Core Ops, SparseCore 0:
  9.9 46.6 all-gather.1
  102.0 47.4 reduce-scatter.1
where the time goes:
time: 193 us; the launch traced here: 190 us
  waiting for transfers between devices  79 us (41%)
  starting transfers between devices  38.4 us (20%)
  other arithmetic  24.8 us (13%)
  matrix products  24.2 us (13%)
  between operations  14.2 us (7%)
  local copies, waits for them, and re-layouts  8.74 us (5%)
    ppermute x14, waiting for transfers between devices, from_behind(): lax.ppermute(value, axis, [(source, source + steps) for source in range(i...  39.8 us
    all_gather x1, waiting for transfers between devices, on_device(): lax.all_gather(out_grad, 'tensor', axis=1, tiled=True)  38.5 us
    ppermute x14, starting transfers between devices, from_behind(): lax.ppermute(value, axis, [(source, source + steps) for source in range(i...  38.3 us
    convert_element_type x14, other arithmetic, advance(): (shrink * held + fresh).astype(jnp.bfloat16)  12.3 us
    convert_element_type x14, other arithmetic, advance(): from_behind((shrink * held + fresh).astype(jnp.bfloat16), 'seq', offset)  10.5 us
    unnamed x17, local copies, waits for them, and re-layouts  7.66 us
  transfers between devices with their start and end apart: 16, of which 15 were waited for; matrix products, arithmetic and copies ran while one was open for 25% of the time, Pallas kernels for 0%

commit v1 on v0

v1 whole, which is shorter than its diff:
```python
import functools

import jax
import jax.numpy as jnp
from jax import lax
from jax.experimental import pallas as pl
from jax.experimental.pallas import tpu as pltpu
from jax.sharding import PartitionSpec as P

EXACT = lax.Precision.HIGHEST
EPSILON = 1e-05
F32 = jnp.float32
BF16 = jnp.bfloat16
TAIL = 16

NN = (((1,), (0,)), ((), ()))
NT = (((1,), (1,)), ((), ()))
TN = (((0,), (0,)), ((), ()))


def dot(a, b, dims):
    return lax.dot_general(a, b, dims, preferred_element_type=F32)


def split(x):
    high = x.astype(BF16)
    return high, (x - high.astype(F32)).astype(BF16)


def dot_fb(a, b, dims):
    high, low = split(a)
    return dot(high, b, dims) + dot(low, b, dims)


def dot_bf(a, b, dims):
    high, low = split(b)
    return dot(a, high, dims) + dot(a, low, dims)


def dot_ff(a, b, dims):
    ah, al = split(a)
    bh, bl = split(b)
    return dot(ah, bh, dims) + (dot(ah, bl, dims) + dot(al, bh, dims))


def triangle(length):
    rows = lax.broadcasted_iota(jnp.int32, (length, length), 0)
    cols = lax.broadcasted_iota(jnp.int32, (length, length), 1)
    return rows >= cols


def running_columns(decay, lower):
    return lax.dot_general(lower.astype(F32), decay, NT, precision=EXACT, preferred_element_type=F32)


def running_rows(decay, lower):
    return lax.dot_general(decay, lower.astype(F32), NT, precision=EXACT, preferred_element_type=F32)


def put_totals(ref, base, totals):
    rows = []
    for total in totals:
        first = total.astype(BF16).astype(F32)
        second = (total - first).astype(BF16).astype(F32)
        rows += [first, second, total - first - second]
    at = lax.broadcasted_iota(jnp.int32, (TAIL, 128), 0)
    tail = jnp.zeros((TAIL, 128), F32)
    for number, row in enumerate(rows):
        tail = jnp.where(at == number, row, tail)
    ref[base : base + TAIL, :] = tail.astype(BF16)


def get_totals(ref, base, heads):
    tail = ref[base : base + TAIL, :].astype(F32)
    return [
        tail[3 * h : 3 * h + 1] + tail[3 * h + 1 : 3 * h + 2] + tail[3 * h + 2 : 3 * h + 3]
        for h in range(heads)
    ]


def head(ref, h):
    return ref[:, h * 128 : (h + 1) * 128]


def total_row(columns, h):
    length = columns.shape[0]
    return jnp.broadcast_to(columns[length - 1 : length, h : h + 1], (1, 128))


def fresh_kernel(k_ref, v_ref, decay_ref, message_ref):
    heads, length = decay_ref.shape
    lower = triangle(length)
    columns = running_columns(decay_ref[...], lower)
    totals = []
    for h in range(heads):
        total = total_row(columns, h)
        totals.append(total)
        fade = jnp.exp(total - columns[:, h : h + 1])
        state = dot_bf(head(k_ref, h), fade * head(v_ref, h).astype(F32), TN)
        message_ref[h * 128 : (h + 1) * 128, :] = state.astype(BF16)
    put_totals(message_ref, heads * 128, totals)


def join_kernel(heads, later, core, own_ref, other_ref, message_ref):
    base = heads * 128
    own_totals = get_totals(own_ref, base, heads)
    other_totals = get_totals(other_ref, base, heads)
    first = core == 0
    for h in range(heads):
        rows = slice(h * 128, (h + 1) * 128)
        own = own_ref[rows, :].astype(F32)
        other = other_ref[rows, :].astype(F32)
        if later:
            decays_own = jnp.logical_not(first)
        else:
            decays_own = first
        shrink = jnp.exp(jnp.where(decays_own, other_totals[h], own_totals[h]))
        joined = jnp.where(decays_own, shrink * own + other, own + shrink * other)
        message_ref[rows, :] = joined.astype(BF16)
    put_totals(message_ref, base, [own_totals[h] + other_totals[h] for h in range(heads)])


def gather_state(heads, partner_ref, chip_refs, inside):
    base = heads * 128
    states = []
    partner_totals = get_totals(partner_ref, base, heads)
    chip_totals = [get_totals(ref, base, heads) for ref in chip_refs]
    for h in range(heads):
        rows = slice(h * 128, (h + 1) * 128)
        summed = jnp.zeros((128, 128), F32)
        passed = jnp.zeros((1, 128), F32)
        for number, ref in enumerate(chip_refs):
            summed = summed + jnp.exp(passed) * ref[rows, :].astype(F32)
            passed = passed + chip_totals[number][h]
        within = partner_ref[rows, :].astype(F32) + jnp.exp(partner_totals[h]) * summed
        states.append(jnp.where(inside, within, summed))
    return states


def inner_kernel(q_ref, k_ref, v_ref, decay_ref, inner_ref):
    heads, length = decay_ref.shape
    lower = triangle(length)
    columns = running_columns(decay_ref[...], lower)
    across = running_rows(decay_ref[...], lower)
    for h in range(heads):
        weight = jnp.exp(jnp.where(lower, columns[:, h : h + 1] - across[h : h + 1, :], -1e30))
        scores = dot(head(q_ref, h), head(k_ref, h), NT) * weight
        inner_ref[:, h * 128 : (h + 1) * 128] = dot_fb(scores, head(v_ref, h), NN)


def mixed_kernel(heads, chips, where_ref, q_ref, decay_ref, inner_ref, gain_ref, partner_ref, *refs):
    chip_refs = refs[:chips]
    mixed_ref, normed_ref, state_ref = refs[chips:]
    length = decay_ref.shape[1]
    inside = where_ref[0] == 1
    states = gather_state(heads, partner_ref, chip_refs, inside)
    lower = triangle(length)
    columns = running_columns(decay_ref[...], lower)
    for h in range(heads):
        lanes = slice(h * 128, (h + 1) * 128)
        grow = jnp.exp(columns[:, h : h + 1])
        mixed = inner_ref[:, lanes] + grow * dot_bf(head(q_ref, h), states[h], NN)
        scale = lax.rsqrt(jnp.mean(mixed * mixed, axis=-1, keepdims=True) + EPSILON)
        mixed_ref[:, lanes] = mixed
        normed_ref[:, lanes] = (mixed * scale * gain_ref[:, lanes]).astype(BF16)
        state_ref[lanes, :] = states[h]


def own_partial_kernel(grad_ref, weight_ref, out_ref):
    out_ref[...] = dot(grad_ref[...], weight_ref[...], NT)


def partial_kernel(where_ref, grad_ref, mine_ref, theirs_ref, out_ref):
    core = where_ref[0]
    half = mine_ref.shape[0]
    grad = grad_ref[...]
    out_ref[:, pl.ds(pl.multiple_of(core * half, half), half)] = dot(grad, mine_ref[...], NT).astype(BF16)
    out_ref[:, pl.ds(pl.multiple_of((1 - core) * half, half), half)] = dot(grad, theirs_ref[...], NT).astype(BF16)


def grad_mixed_kernel(heads, parts, q_ref, decay_ref, gain_ref, mixed_ref, own_ref, *refs):
    part_refs = refs[:parts]
    grad_ref, message_ref = refs[parts:]
    length = decay_ref.shape[1]
    lower = triangle(length)
    columns = running_columns(decay_ref[...], lower)
    totals = []
    for h in range(heads):
        lanes = slice(h * 128, (h + 1) * 128)
        normed = own_ref[:, lanes]
        for ref in part_refs:
            normed = normed + ref[:, lanes].astype(F32)
        lifted = normed * gain_ref[:, lanes]
        mixed = mixed_ref[:, lanes]
        scale = lax.rsqrt(jnp.mean(mixed * mixed, axis=-1, keepdims=True) + EPSILON)
        unit = mixed * scale
        grad = scale * (lifted - unit * jnp.mean(unit * lifted, axis=-1, keepdims=True))
        grad_ref[:, lanes] = grad
        upward = dot_bf(head(q_ref, h), jnp.exp(columns[:, h : h + 1]) * grad, TN)
        message_ref[lanes, :] = upward.astype(BF16)
        totals.append(total_row(columns, h))
    put_totals(message_ref, heads * 128, totals)


def inner_grad_kernel(q_ref, k_ref, v_ref, decay_ref, grad_ref, state_ref, dq_ref, dk_ref, dv_ref):
    heads, length = decay_ref.shape
    lower = triangle(length)
    columns = running_columns(decay_ref[...], lower)
    across = running_rows(decay_ref[...], lower)
    for h in range(heads):
        lanes = slice(h * 128, (h + 1) * 128)
        q, k, v, grad = head(q_ref, h), head(k_ref, h), head(v_ref, h), grad_ref[:, lanes]
        weight = jnp.exp(jnp.where(lower, columns[:, h : h + 1] - across[h : h + 1, :], -1e30))
        scores = dot(q, k, NT) * weight
        grad_scores = dot_fb(grad, v, NT) * weight
        carried = jnp.exp(columns[:, h : h + 1]) * dot_ff(grad, state_ref[lanes, :], NT)
        dq_ref[:, lanes] = (dot_fb(grad_scores, k, NN) + carried).astype(BF16)
        dk_ref[:, lanes] = dot_fb(grad_scores, q, TN)
        dv_ref[:, lanes] = dot_ff(scores, grad, TN)


def outer_grad_kernel(heads, chips, where_ref, k_ref, v_ref, decay_ref, dk_in, dv_in, partner_ref, *refs):
    chip_refs = refs[:chips]
    dk_ref, dv_ref = refs[chips:]
    length = decay_ref.shape[1]
    inside = where_ref[0] == 0
    states = gather_state(heads, partner_ref, chip_refs, inside)
    lower = triangle(length)
    columns = running_columns(decay_ref[...], lower)
    for h in range(heads):
        lanes = slice(h * 128, (h + 1) * 128)
        fade = jnp.exp(total_row(columns, h) - columns[:, h : h + 1])
        dk_ref[:, lanes] = (dk_in[:, lanes] + fade * dot_bf(head(v_ref, h), states[h], NT)).astype(BF16)
        dv_ref[:, lanes] = (dv_in[:, lanes] + fade * dot_bf(head(k_ref, h), states[h], NN)).astype(BF16)


def layer_kernel(others, where_ref, normed_ref, weight_ref, *refs):
    normed_refs = refs[:others]
    mine_refs = refs[others : 2 * others]
    theirs_refs = refs[2 * others : 3 * others]
    out_ref = refs[3 * others]
    core = where_ref[0]
    half = weight_ref.shape[0] // 2
    mine = pl.ds(pl.multiple_of(core * half, half), half)
    theirs = pl.ds(pl.multiple_of((1 - core) * half, half), half)
    width = weight_ref.shape[1]
    step = 384
    for begin in range(0, width, step):
        lanes = slice(begin, begin + step)
        total = dot(normed_ref[...], weight_ref[:, lanes], NN)
        for k in range(others):
            total = total + dot(normed_refs[k][:, mine], mine_refs[k][:, lanes], NN)
            total = total + dot(normed_refs[k][:, theirs], theirs_refs[k][:, lanes], NN)
        out_ref[:, lanes] = total.astype(BF16)


SMEM = pl.BlockSpec(memory_space=pltpu.SMEM)
VMEM = pl.BlockSpec(memory_space=pltpu.VMEM)


def call(kernel, name, outs, args, flops, scalars=0):
    moved = sum(a.size * a.dtype.itemsize for a in args) + sum(o.size * o.dtype.itemsize for o in outs)
    return pl.pallas_call(
        kernel,
        name=name,
        out_shape=outs,
        in_specs=[SMEM] * scalars + [VMEM] * (len(args) - scalars),
        out_specs=[VMEM] * len(outs),
        compiler_params=pltpu.CompilerParams(vmem_limit_bytes=40 * 2**20),
        cost_estimate=pl.CostEstimate(flops=int(flops), bytes_accessed=moved, transcendentals=0),
    )(*args)


def on_device(queries, keys, values, log_decay, norm_gain, out_weight, out_grad):
    length, columns = queries.shape
    heads = log_decay.shape[0]
    seq = lax.axis_size("seq")
    tensor = lax.axis_size("tensor")
    chips = seq // 2
    model = out_weight.shape[1]
    width = model // tensor
    half = columns // 2
    place = lax.axis_index("tensor")
    core = lax.rem(lax.axis_index("seq"), 2)
    where = core.astype(jnp.int32).reshape(1)
    gain = norm_gain.reshape(1, columns)

    def swap_tensor(value, k):
        return lax.ppermute(value, "tensor", [(i, i ^ k) for i in range(tensor)])

    def swap_core(value):
        return lax.ppermute(value, "seq", [(i, i ^ 1) for i in range(seq)])

    def to_chip(value, k):
        return lax.ppermute(
            value, "seq", [(i, i + 2 * k) for i in range(seq) if 0 <= i + 2 * k < seq]
        )

    def shape(rows, cols, dtype):
        return jax.ShapeDtypeStruct((rows, cols), dtype)

    others = range(1, tensor)
    message = shape(columns + TAIL, 128, BF16)

    mine = [
        swap_tensor(
            lax.dynamic_slice(out_weight, (core * half, (place ^ k) * width), (half, width)), k
        )
        for k in others
    ]
    (fresh,) = call(fresh_kernel, "fresh_state", [message], [keys, values, log_decay], 40e6)
    fresh_other = swap_core(fresh)

    def joined(own, other, later):
        def kernel(where_ref, own_ref, other_ref, message_ref):
            join_kernel(heads, later, where_ref[0], own_ref, other_ref, message_ref)

        (out,) = call(kernel, "join_states", [message], [where, own, other], 1e6, 1)
        return out

    chip_state = joined(fresh, fresh_other, False)
    arrived = [to_chip(chip_state, k) for k in range(1, chips)]
    (inner,) = call(
        inner_kernel, "inner", [shape(length, columns, F32)], [queries, keys, values, log_decay], 80e6
    )
    mixed, normed, state_in = call(
        functools.partial(mixed_kernel, heads, chips - 1),
        "mixed",
        [shape(length, columns, F32), shape(length, columns, BF16), shape(columns, 128, F32)],
        [where, queries, log_decay, inner, gain, fresh_other, *arrived],
        40e6,
        1,
    )
    weight_own = lax.dynamic_slice(out_weight, (0, place * width), (columns, width))
    (own_partial,) = call(
        own_partial_kernel, "own_partial", [shape(length, columns, F32)], [out_grad, weight_own], 2 * length * columns * width
    )
    theirs = [swap_core(piece) for piece in mine]
    partials = []
    for k in others:
        (partial,) = call(
            partial_kernel,
            "partial",
            [shape(length, columns, BF16)],
            [where, out_grad, mine[k - 1], theirs[k - 1]],
            2 * length * columns * width,
            1,
        )
        partials.append(swap_tensor(partial, k))
    normed_others = [swap_tensor(normed, k) for k in others]
    grad_mixed, upward = call(
        functools.partial(grad_mixed_kernel, heads, tensor - 1),
        "grad_mixed",
        [shape(length, columns, F32), message],
        [queries, log_decay, gain, mixed, own_partial, *partials],
        40e6,
    )
    upward_other = swap_core(upward)
    chip_upward = joined(upward, upward_other, True)
    returned = [to_chip(chip_upward, -k) for k in range(1, chips)]
    query_grad, dk_inner, dv_inner = call(
        inner_grad_kernel,
        "inner_grad",
        [shape(length, columns, BF16), shape(length, columns, F32), shape(length, columns, F32)],
        [queries, keys, values, log_decay, grad_mixed, state_in],
        400e6,
    )
    (layer_out,) = call(
        functools.partial(layer_kernel, tensor - 1),
        "layer",
        [shape(length, width, BF16)],
        [where, normed, weight_own, *normed_others, *mine, *theirs],
        2 * length * columns * tensor * width,
        1,
    )
    key_grad, value_grad = call(
        functools.partial(outer_grad_kernel, heads, chips - 1),
        "outer_grad",
        [shape(length, columns, BF16), shape(length, columns, BF16)],
        [where, keys, values, log_decay, dk_inner, dv_inner, upward_other, *returned],
        80e6,
        1,
    )
    return layer_out, query_grad, key_grad, value_grad


def solution(mesh):
    in_specs = (
        P("seq", "tensor"),
        P("seq", "tensor"),
        P("seq", "tensor"),
        P("tensor", "seq"),
        P("tensor"),
        P("tensor", None),
        P("seq", "tensor"),
    )
    out_specs = (P("seq", "tensor"), P("seq", "tensor"), P("seq", "tensor"), P("seq", "tensor"))
    return jax.shard_map(
        on_device, mesh=mesh, in_specs=in_specs, out_specs=out_specs, check_vma=False
    )
```

time: 193 us -> 79.4 us (0.41); the launches traced: 190 us -> 78.9 us
  waiting for transfers between devices: 79 us -> 29.2 us
  other arithmetic: 24.8 us -> 0 us
  matrix products: 24.2 us -> 0 us
  Pallas kernels: 0 us -> 14.6 us
  between operations: 14.2 us -> 0.91 us
  starting transfers between devices: 38.4 us -> 26.7 us
    all_gather x1 -> x0, waiting for transfers between devices: 38.5 us -> none  [on_device(): lax.all_gather(out_grad, 'tensor', axis=1, tiled=True)]
    dot_general x14 -> x0, matrix products: 24.2 us -> none  [the longest x1 3.6 us: on_device(): lax.dot_general(lax.all_gather(out_grad, 'tensor', axis=1, tiled=True), o...]
    convert_element_type x28 -> x0, other arithmetic: 22.8 us -> none  [the longest x14 12.3 us: advance(): (shrink * held + fresh).astype(jnp.bfloat16)]
    pallas_call x0 -> x13, Pallas kernels: none -> 14.6 us  [call(): pl.pallas_call(kernel, name=name, out_shape=outs, in_specs=[SMEM] * scala...]
    ppermute x14 -> x20, starting transfers between devices: 38.3 us -> 26.7 us  [the longest x6 14.4 us: to_chip(): lax.ppermute(value, 'seq', [(i, i + 2 * k) for i in range(seq) if 0 <= i...]
    ppermute x14 -> x20, waiting for transfers between devices: 39.8 us -> 29.2 us  [the longest x9 22.8 us: swap_tensor(): return lax.ppermute(value, 'tensor', [(i, i ^ k) for i in range(tensor)])]
    unnamed x17 -> x26, local copies, waits for them, and re-layouts: 7.66 us -> 4.92 us
    dynamic_slice x0 -> x2, local copies, waits for them, and re-layouts: none -> 2.59 us  [the longest x1 1.41 us: on_device(): lax.dynamic_slice(out_weight, (core * half, (place ^ k) * width), (half,...]
  transfers between devices with their start and end apart: 16 -> 20, of which waited for: 15 -> 7; matrix products, arithmetic and copies ran while one was open for 25% -> 2% of each run, Pallas kernels for 0% -> 17%
where the time goes in v1:
time: 79.4 us; the launch traced here: 78.9 us
  waiting for transfers between devices  29.2 us (37%)
  starting transfers between devices  26.7 us (34%)
  Pallas kernels  14.6 us (18%)
  local copies, waits for them, and re-layouts  7.51 us (9%)
  between operations  0.91 us (1%)
    ppermute x9, waiting for transfers between devices, swap_tensor(): return lax.ppermute(value, 'tensor', [(i, i ^ k) for i in range(tensor)])  22.8 us
    pallas_call x13, Pallas kernels, call(): pl.pallas_call(kernel, name=name, out_shape=outs, in_specs=[SMEM] * scala...  14.6 us
    ppermute x6, starting transfers between devices, to_chip(): lax.ppermute(value, 'seq', [(i, i + 2 * k) for i in range(seq) if 0 <= i...  14.4 us
    ppermute x9, starting transfers between devices, swap_tensor(): return lax.ppermute(value, 'tensor', [(i, i ^ k) for i in range(tensor)])  11.7 us
    unnamed x26, local copies, waits for them, and re-layouts  4.92 us
    ppermute x6, waiting for transfers between devices, to_chip(): lax.ppermute(value, 'seq', [(i, i + 2 * k) for i in range(seq) if 0 <= i...  3.89 us
    ppermute x5, waiting for transfers between devices, swap_core(): return lax.ppermute(value, 'seq', [(i, i ^ 1) for i in range(seq)])  2.5 us
  transfers between devices with their start and end apart: 20, of which 7 were waited for; matrix products, arithmetic and copies ran while one was open for 2% of the time, Pallas kernels for 17%

profile of v1, /device:TPU:0, one launch (start us, length us, event | category | flops | bytes accessed | tf_op | source)
XLA Modules:
  0.0 78.9 jit_solution(8483762939929293271)
XLA Ops:
  0.7 1.4 %fusion = (bf16[128,1536]{1,0:T(8,128)(2,1)S(1)}, bf16[128,1536]{1,0:T(8,128)(2,1)S(1)}, bf16[128,1536]{1,0:T(8,128)(2,1)S(1)}) fusion(bf16[256,6144]{1,0:T(8,128)(2,1)} %param.12, s32[]{:T(128)S(6)} %select_n.18, s32[]{:T(128)S(6)} %select_n.21, s32[]{:T(128)S(6)} %select_n.19, s32[]{:T(128)S(6)} %select_n.20), kind=kLoop, calls=%fused_computation.1 | loop fusion | bytes 2359312 | tf_op jit(solution)/shard_map/dynamic_slice | solution.py:307
  2.1 3.0 %collective-permute-start.7 = (bf16[128,1536]{1,0:T(8,128)(2,1)S(1)}, bf16[128,1536]{1,0:T(8,128)(2,1)S(1)}, u32[]{:S(2)}, u32[]{:S(2)}) collective-permute-start(bf16[128,1536]{1,0:T(8,128)(2,1)S(1)} %get-tuple-element.25), channel_id=1, source_target_pairs={{0,1},{1,0},{2,3},{3,2},{4,5},{5,4},{6,7},{7,6},{8,9},{9,8},{10,11... | collective-permute-start | bytes 1179656 | tf_op jit(solution)/shard_map/ppermute | solution.py:289
  5.1 1.5 %collective-permute-start.8 = (bf16[128,1536]{1,0:T(8,128)(2,1)S(1)}, bf16[128,1536]{1,0:T(8,128)(2,1)S(1)}, u32[]{:S(2)}, u32[]{:S(2)}) collective-permute-start(bf16[128,1536]{1,0:T(8,128)(2,1)S(1)} %get-tuple-element.26), channel_id=1, source_target_pairs={{0,2},{1,3},{2,0},{3,1},{4,6},{5,7},{6,4},{7,5},{8,10},{9,11},{10,... | collective-permute-start | bytes 1179656 | tf_op jit(solution)/shard_map/ppermute | solution.py:289
  6.7 8.4 %collective-permute-done.7.refs_3_.mine_ref = bf16[128,1536]{1,0:T(8,128)(2,1)S(1)} collective-permute-done((bf16[128,1536]{1,0:T(8,128)(2,1)S(1)}, bf16[128,1536]{1,0:T(8,128)(2,1)S(1)}, u32[]{:S(2)}, u32[]{:S(2)}) %collective-permute-start.7) | collective-permute-done | bytes 393248 | tf_op jit(solution)/shard_map/ppermute | solution.py:289
  15.1 9.1 %collective-permute-done.8.refs_4_.mine_ref = bf16[128,1536]{1,0:T(8,128)(2,1)S(1)} collective-permute-done((bf16[128,1536]{1,0:T(8,128)(2,1)S(1)}, bf16[128,1536]{1,0:T(8,128)(2,1)S(1)}, u32[]{:S(2)}, u32[]{:S(2)}) %collective-permute-start.8) | collective-permute-done | bytes 393248 | tf_op jit(solution)/shard_map/ppermute | solution.py:289
  28.0 1.2 %collective-permute-done.other_ref.partner_ref = bf16[272,128]{1,0:T(8,128)(2,1)S(1)} collective-permute-done((bf16[272,128]{1,0:T(8,128)(2,1)S(1)}, bf16[272,128]{1,0:T(8,128)(2,1)S(1)}, u32[]{:S(2)}, u32[]{:S(2)}) %collective-permute-start) | collective-permute-done | bytes 69664 | tf_op jit(solution)/shard_map/ppermute | solution.py:292
  29.9 3.5 %collective-permute-start.1 = (bf16[272,128]{1,0:T(8,128)(2,1)}, bf16[272,128]{1,0:T(8,128)(2,1)S(1)}, u32[]{:S(2)}, u32[]{:S(2)}) collective-permute-start(bf16[272,128]{1,0:T(8,128)(2,1)} %join_states.2), channel_id=1, source_target_pairs={{0,8},{4,12},{8,16},{12,20},{16,24},{20,28},{1,9},{5,13},{9,17},{1... | collective-permute-start | bytes 208904 | tf_op jit(solution)/shard_map/ppermute | solution.py:295
  33.4 1.2 %partial.3 = bf16[256,256]{1,0:T(8,128)(2,1)} custom-call(s32[1]{0:T(128)} %bitcast.where_ref, bf16[256,1536]{1,0:T(8,128)(2,1)S(1)} %copy-done, bf16[128,1536]{1,0:T(8,128)(2,1)S(1)} %collective-permute-done.7.refs_3_.mine_ref, bf16[128,1536]{1,0:T(8,128)(2,1)S(1)} %collective-permute-done.10.refs_6_.theirs_ref), custom_call_target="tpu_custom_call" | custom-call | flops 201326592 | bytes 1703940 | tf_op jit(solution)/shard_map/partial/pallas_call | solution.py:263
  35.5 5.1 %collective-permute-start.2 = (bf16[272,128]{1,0:T(8,128)(2,1)}, bf16[272,128]{1,0:T(8,128)(2,1)}, u32[]{:S(2)}, u32[]{:S(2)}) collective-permute-start(bf16[272,128]{1,0:T(8,128)(2,1)} %join_states.2), channel_id=1, source_target_pairs={{0,16},{4,20},{8,24},{12,28},{1,17},{5,21},{9,25},{13,29},{2,18},{... | collective-permute-start | bytes 208904 | tf_op jit(solution)/shard_map/ppermute | solution.py:295
  41.3 1.9 %collective-permute-start.3 = (bf16[272,128]{1,0:T(8,128)(2,1)}, bf16[272,128]{1,0:T(8,128)(2,1)}, u32[]{:S(2)}, u32[]{:S(2)}) collective-permute-start(bf16[272,128]{1,0:T(8,128)(2,1)} %join_states.2), channel_id=1, source_target_pairs={{0,24},{4,28},{1,25},{5,29},{2,26},{6,30},{3,27},{7,31}} | collective-permute-start | bytes 208904 | tf_op jit(solution)/shard_map/ppermute | solution.py:295
  46.6 1.5 %mixed.1 = (f32[256,256]{1,0:T(8,128)S(1)}, bf16[256,256]{1,0:T(8,128)(2,1)S(1)}, f32[256,128]{1,0:T(8,128)S(1)}) custom-call(s32[1]{0:T(128)} %bitcast.where_ref, bf16[256,256]{1,0:T(8,128)(2,1)S(1)} %copy-done.1, f32[2,256]{1,0:T(2,128)S(1)} %copy-done.11, f32[256,256]{1,0:T(8,128)S(1)} %inner.1.inner_ref, f32[1,256]{1,0:T(1,128)S(1)} %bitcast.2, ...), custom_call_target="tpu_custom_call" | custom-call | flops 40000000 | bytes 1199108 | tf_op jit(solution)/shard_map/mixed/pallas_call | solution.py:263
  49.3 1.5 %collective-permute-start.5 = (bf16[256,256]{1,0:T(8,128)(2,1)S(1)}, bf16[256,256]{1,0:T(8,128)(2,1)S(1)}, u32[]{:S(2)}, u32[]{:S(2)}) collective-permute-start(bf16[256,256]{1,0:T(8,128)(2,1)S(1)} %get-tuple-element.14.normed_ref), channel_id=1, source_target_pairs={{0,2},{1,3},{2,0},{3,1},{4,6},{5,7},{6,4},{7,5},{8,10},{9,11},{10,... | collective-permute-start | bytes 393224 | tf_op jit(solution)/shard_map/ppermute | solution.py:289
  52.3 1.5 %collective-permute-start.14 = (bf16[256,256]{1,0:T(8,128)(2,1)S(1)}, bf16[256,256]{1,0:T(8,128)(2,1)S(1)}, u32[]{:S(2)}, u32[]{:S(2)}) collective-permute-start(bf16[256,256]{1,0:T(8,128)(2,1)S(1)} %partial.4), channel_id=1, source_target_pairs={{0,2},{1,3},{2,0},{3,1},{4,6},{5,7},{6,4},{7,5},{8,10},{9,11},{10,... | collective-permute-start | bytes 393224 | tf_op jit(solution)/shard_map/ppermute | solution.py:289
  54.3 1.3 %collective-permute-start.15 = (bf16[256,256]{1,0:T(8,128)(2,1)S(1)}, bf16[256,256]{1,0:T(8,128)(2,1)S(1)}, u32[]{:S(2)}, u32[]{:S(2)}) collective-permute-start(bf16[256,256]{1,0:T(8,128)(2,1)S(1)} %partial.5), channel_id=1, source_target_pairs={{0,3},{1,2},{2,1},{3,0},{4,7},{5,6},{6,5},{7,4},{8,11},{9,10},{10,... | collective-permute-start | bytes 393224 | tf_op jit(solution)/shard_map/ppermute | solution.py:289
  57.2 5.3 %collective-permute-done.14.refs_1_ = bf16[256,256]{1,0:T(8,128)(2,1)S(1)} collective-permute-done((bf16[256,256]{1,0:T(8,128)(2,1)S(1)}, bf16[256,256]{1,0:T(8,128)(2,1)S(1)}, u32[]{:S(2)}, u32[]{:S(2)}) %collective-permute-start.14) | collective-permute-done | bytes 131104 | tf_op jit(solution)/shard_map/ppermute | solution.py:289
  62.5 1.7 %grad_mixed.1 = (f32[256,256]{1,0:T(8,128)S(1)}, bf16[272,128]{1,0:T(8,128)(2,1)S(1)}) custom-call(bf16[256,256]{1,0:T(8,128)(2,1)S(1)} %copy-done.1, f32[2,256]{1,0:T(2,128)S(1)} %copy-done.11, f32[1,256]{1,0:T(1,128)S(1)} %bitcast.3, f32[256,256]{1,0:T(8,128)S(1)} %get-tuple-element.15.mixed_ref, f32[256,256]{1,0:T(8,128)S(1)} %own_partial.1.own_ref, ...), custom_call_target="tpu_custom_call" | custom-call | flops 40000000 | bytes 1383424 | tf_op jit(solution)/shard_map/grad_mixed/pallas_call | solution.py:263
  64.3 1.2 %collective-permute-done.16.other_ref.partner_ref = bf16[272,128]{1,0:T(8,128)(2,1)S(1)} collective-permute-done((bf16[272,128]{1,0:T(8,128)(2,1)S(1)}, bf16[272,128]{1,0:T(8,128)(2,1)S(1)}, u32[]{:S(2)}, u32[]{:S(2)}) %collective-permute-start.16) | collective-permute-done | bytes 69664 | tf_op jit(solution)/shard_map/ppermute | solution.py:292
  65.6 1.3 %collective-permute-start.17 = (bf16[272,128]{1,0:T(8,128)(2,1)S(1)}, bf16[272,128]{1,0:T(8,128)(2,1)S(1)}, u32[]{:S(2)}, u32[]{:S(2)}) collective-permute-start(bf16[272,128]{1,0:T(8,128)(2,1)S(1)} %join_states.3), channel_id=1, source_target_pairs={{8,0},{12,4},{16,8},{20,12},{24,16},{28,20},{9,1},{13,5},{17,9},{2... | collective-permute-start | bytes 208904 | tf_op jit(solution)/shard_map/ppermute | solution.py:295
  66.9 1.3 %collective-permute-start.18 = (bf16[272,128]{1,0:T(8,128)(2,1)S(1)}, bf16[272,128]{1,0:T(8,128)(2,1)S(1)}, u32[]{:S(2)}, u32[]{:S(2)}) collective-permute-start(bf16[272,128]{1,0:T(8,128)(2,1)S(1)} %join_states.3), channel_id=1, source_target_pairs={{16,0},{20,4},{24,8},{28,12},{17,1},{21,5},{25,9},{29,13},{18,2},{... | collective-permute-start | bytes 208904 | tf_op jit(solution)/shard_map/ppermute | solution.py:295
  68.2 1.3 %collective-permute-start.19 = (bf16[272,128]{1,0:T(8,128)(2,1)S(1)}, bf16[272,128]{1,0:T(8,128)(2,1)S(1)}, u32[]{:S(2)}, u32[]{:S(2)}) collective-permute-start(bf16[272,128]{1,0:T(8,128)(2,1)S(1)} %join_states.3), channel_id=1, source_target_pairs={{24,0},{28,4},{25,1},{29,5},{26,2},{30,6},{27,3},{31,7}} | collective-permute-start | bytes 208904 | tf_op jit(solution)/shard_map/ppermute | solution.py:295
  69.5 2.5 %layer.1 = bf16[256,1536]{1,0:T(8,128)(2,1)} custom-call(s32[1]{0:T(128)} %bitcast.where_ref, bf16[256,256]{1,0:T(8,128)(2,1)S(1)} %get-tuple-element.14.normed_ref, bf16[256,1536]{1,0:T(8,128)(2,1)S(1)} %constant_dynamic-slice_fusion.weight_ref, bf16[256,256]{1,0:T(8,128)(2,1)S(1)} %collective-permute-done.4.refs_0_, ...), custom_call_target="tpu_custom_call" | custom-call | flops 805306368 | bytes 4456452 | tf_op jit(solution)/shard_map/layer/pallas_call | solution.py:263
  72.1 2.2 %inner_grad.1 = (bf16[256,256]{1,0:T(8,128)(2,1)}, f32[256,256]{1,0:T(8,128)S(1)}, f32[256,256]{1,0:T(8,128)S(1)}) custom-call(bf16[256,256]{1,0:T(8,128)(2,1)S(1)} %copy-done.1, bf16[256,256]{1,0:T(8,128)(2,1)S(1)} %copy-done.3, bf16[256,256]{1,0:T(8,128)(2,1)S(1)} %copy-done.5, f32[2,256]{1,0:T(2,128)S(1)} %copy-done.11, ...), custom_call_target="tpu_custom_call" | custom-call | flops 400000000 | bytes 1443840 | tf_op jit(solution)/shard_map/inner_grad/pallas_call | solution.py:263
  74.3 3.3 %collective-permute-done.19.refs_2_ = bf16[272,128]{1,0:T(8,128)(2,1)S(1)} collective-permute-done((bf16[272,128]{1,0:T(8,128)(2,1)S(1)}, bf16[272,128]{1,0:T(8,128)(2,1)S(1)}, u32[]{:S(2)}, u32[]{:S(2)}) %collective-permute-start.19) | collective-permute-done | bytes 69664 | tf_op jit(solution)/shard_map/ppermute | solution.py:295
  77.6 1.3 %outer_grad.1 = (bf16[256,256]{1,0:T(8,128)(2,1)}, bf16[256,256]{1,0:T(8,128)(2,1)}) custom-call(s32[1]{0:T(128)} %bitcast.where_ref, bf16[256,256]{1,0:T(8,128)(2,1)S(1)} %copy-done.3, bf16[256,256]{1,0:T(8,128)(2,1)S(1)} %copy-done.5, f32[2,256]{1,0:T(2,128)S(1)} %copy-done.11, f32[256,256]{1,0:T(8,128)S(1)} %get-tuple-element.19.dk_in, ...), custom_call_target="tpu_custom_call" | custom-call | flops 80000000 | bytes 1329156 | tf_op jit(solution)/shard_map/outer_grad/pallas_call | solution.py:263
  (57 shorter events, 14.4 us)
Async XLA Ops:
  0.6 42.6 %copy-start.11 = (f32[2,256]{1,0:T(2,128)S(1)}, f32[2,256]{1,0:T(2,128)}, u32[]{:S(2)}) copy-start(f32[2,256]{1,0:T(2,128)} %decay_ref.11) | copy-start | bytes 6148
  0.6 42.6 %copy-start.3 = (bf16[256,256]{1,0:T(8,128)(2,1)S(1)}, bf16[256,256]{1,0:T(8,128)(2,1)}, u32[]{:S(2)}) copy-start(bf16[256,256]{1,0:T(8,128)(2,1)} %k_ref.7) | copy-start | bytes 393220
  0.7 42.6 %copy-start.5 = (bf16[256,256]{1,0:T(8,128)(2,1)S(1)}, bf16[256,256]{1,0:T(8,128)(2,1)}, u32[]{:S(2)}) copy-start(bf16[256,256]{1,0:T(8,128)(2,1)} %v_ref.7) | copy-start | bytes 393220
  0.7 44.1 %copy-start.12 = (f32[256]{0:T(256)S(1)}, f32[256]{0:T(256)}, u32[]{:S(2)}) copy-start(f32[256]{0:T(256)} %param.11) | copy-start | bytes 3076
  2.1 12.9 %collective-permute-start.7 = (bf16[128,1536]{1,0:T(8,128)(2,1)S(1)}, bf16[128,1536]{1,0:T(8,128)(2,1)S(1)}, u32[]{:S(2)}, u32[]{:S(2)}) collective-permute-start(bf16[128,1536]{1,0:T(8,128)(2,1)S(1)} %get-tuple-element.25), channel_id=1, source_target_pairs={{0,1},{1,0},{2,3},{3,2},{4,5},{5,4},{6,7},{7,6},{8,9},{9,8},{10,11... | collective-permute-start | bytes 1179656 | tf_op jit(solution)/shard_map/ppermute | solution.py:289
  5.1 19.0 %collective-permute-start.8 = (bf16[128,1536]{1,0:T(8,128)(2,1)S(1)}, bf16[128,1536]{1,0:T(8,128)(2,1)S(1)}, u32[]{:S(2)}, u32[]{:S(2)}) collective-permute-start(bf16[128,1536]{1,0:T(8,128)(2,1)S(1)} %get-tuple-element.26), channel_id=1, source_target_pairs={{0,2},{1,3},{2,0},{3,1},{4,6},{5,7},{6,4},{7,5},{8,10},{9,11},{10,... | collective-permute-start | bytes 1179656 | tf_op jit(solution)/shard_map/ppermute | solution.py:289
  6.7 17.5 %collective-permute-start.9 = (bf16[128,1536]{1,0:T(8,128)(2,1)S(1)}, bf16[128,1536]{1,0:T(8,128)(2,1)S(1)}, u32[]{:S(2)}, u32[]{:S(2)}) collective-permute-start(bf16[128,1536]{1,0:T(8,128)(2,1)S(1)} %get-tuple-element.24), channel_id=1, source_target_pairs={{0,3},{1,2},{2,1},{3,0},{4,7},{5,6},{6,5},{7,4},{8,11},{9,10},{10,... | collective-permute-start | bytes 1179656 | tf_op jit(solution)/shard_map/ppermute | solution.py:289
  15.1 18.3 %collective-permute-start.10 = (bf16[128,1536]{1,0:T(8,128)(2,1)S(1)}, bf16[128,1536]{1,0:T(8,128)(2,1)S(1)}, u32[]{:S(2)}, u32[]{:S(2)}) collective-permute-start(bf16[128,1536]{1,0:T(8,128)(2,1)S(1)} %collective-permute-done.7.refs_3_.mine_ref), channel_id=1, source_target_pairs={{0,4},{4,0},{8,12},{12,8},{16,20},{20,16},{24,28},{28,24},{1,5},{5... | collective-permute-start | bytes 1179656 | tf_op jit(solution)/shard_map/ppermute | solution.py:292
  24.1 26.7 %collective-permute-start.11 = (bf16[128,1536]{1,0:T(8,128)(2,1)S(1)}, bf16[128,1536]{1,0:T(8,128)(2,1)S(1)}, u32[]{:S(2)}, u32[]{:S(2)}) collective-permute-start(bf16[128,1536]{1,0:T(8,128)(2,1)S(1)} %collective-permute-done.8.refs_4_.mine_ref), channel_id=1, source_target_pairs={{0,4},{4,0},{8,12},{12,8},{16,20},{20,16},{24,28},{28,24},{1,5},{5... | collective-permute-start | bytes 1179656 | tf_op jit(solution)/shard_map/ppermute | solution.py:292
  24.1 28.1 %collective-permute-start.12 = (bf16[128,1536]{1,0:T(8,128)(2,1)S(1)}, bf16[128,1536]{1,0:T(8,128)(2,1)S(1)}, u32[]{:S(2)}, u32[]{:S(2)}) collective-permute-start(bf16[128,1536]{1,0:T(8,128)(2,1)S(1)} %collective-permute-done.9.refs_5_.mine_ref), channel_id=1, source_target_pairs={{0,4},{4,0},{8,12},{12,8},{16,20},{20,16},{24,28},{28,24},{1,5},{5... | collective-permute-start | bytes 1179656 | tf_op jit(solution)/shard_map/ppermute | solution.py:292
  27.9 1.3 %collective-permute-start = (bf16[272,128]{1,0:T(8,128)(2,1)S(1)}, bf16[272,128]{1,0:T(8,128)(2,1)S(1)}, u32[]{:S(2)}, u32[]{:S(2)}) collective-permute-start(bf16[272,128]{1,0:T(8,128)(2,1)S(1)} %fresh_state.1.own_ref), channel_id=1, source_target_pairs={{0,4},{4,0},{8,12},{12,8},{16,20},{20,16},{24,28},{28,24},{1,5},{5... | collective-permute-start | bytes 208904 | tf_op jit(solution)/shard_map/ppermute | solution.py:292
  29.9 10.7 %collective-permute-start.1 = (bf16[272,128]{1,0:T(8,128)(2,1)}, bf16[272,128]{1,0:T(8,128)(2,1)S(1)}, u32[]{:S(2)}, u32[]{:S(2)}) collective-permute-start(bf16[272,128]{1,0:T(8,128)(2,1)} %join_states.2), channel_id=1, source_target_pairs={{0,8},{4,12},{8,16},{12,20},{16,24},{20,28},{1,9},{5,13},{9,17},{1... | collective-permute-start | bytes 208904 | tf_op jit(solution)/shard_map/ppermute | solution.py:295
  34.7 19.7 %collective-permute-start.13 = (bf16[256,256]{1,0:T(8,128)(2,1)}, bf16[256,256]{1,0:T(8,128)(2,1)}, u32[]{:S(2)}, u32[]{:S(2)}) collective-permute-start(bf16[256,256]{1,0:T(8,128)(2,1)} %partial.3), channel_id=1, source_target_pairs={{0,1},{1,0},{2,3},{3,2},{4,5},{5,4},{6,7},{7,6},{8,9},{9,8},{10,11... | collective-permute-start | bytes 393224 | tf_op jit(solution)/shard_map/ppermute | solution.py:289
  35.5 8.6 %collective-permute-start.2 = (bf16[272,128]{1,0:T(8,128)(2,1)}, bf16[272,128]{1,0:T(8,128)(2,1)}, u32[]{:S(2)}, u32[]{:S(2)}) collective-permute-start(bf16[272,128]{1,0:T(8,128)(2,1)} %join_states.2), channel_id=1, source_target_pairs={{0,16},{4,20},{8,24},{12,28},{1,17},{5,21},{9,25},{13,29},{2,18},{... | collective-permute-start | bytes 208904 | tf_op jit(solution)/shard_map/ppermute | solution.py:295
  41.3 3.5 %collective-permute-start.3 = (bf16[272,128]{1,0:T(8,128)(2,1)}, bf16[272,128]{1,0:T(8,128)(2,1)}, u32[]{:S(2)}, u32[]{:S(2)}) collective-permute-start(bf16[272,128]{1,0:T(8,128)(2,1)} %join_states.2), channel_id=1, source_target_pairs={{0,24},{4,28},{1,25},{5,29},{2,26},{6,30},{3,27},{7,31}} | collective-permute-start | bytes 208904 | tf_op jit(solution)/shard_map/ppermute | solution.py:295
  48.1 20.1 %collective-permute-start.4 = (bf16[256,256]{1,0:T(8,128)(2,1)S(1)}, bf16[256,256]{1,0:T(8,128)(2,1)S(1)}, u32[]{:S(2)}, u32[]{:S(2)}) collective-permute-start(bf16[256,256]{1,0:T(8,128)(2,1)S(1)} %get-tuple-element.14.normed_ref), channel_id=1, source_target_pairs={{0,1},{1,0},{2,3},{3,2},{4,5},{5,4},{6,7},{7,6},{8,9},{9,8},{10,11... | collective-permute-start | bytes 393224 | tf_op jit(solution)/shard_map/ppermute | solution.py:289
  49.3 20.2 %collective-permute-start.5 = (bf16[256,256]{1,0:T(8,128)(2,1)S(1)}, bf16[256,256]{1,0:T(8,128)(2,1)S(1)}, u32[]{:S(2)}, u32[]{:S(2)}) collective-permute-start(bf16[256,256]{1,0:T(8,128)(2,1)S(1)} %get-tuple-element.14.normed_ref), channel_id=1, source_target_pairs={{0,2},{1,3},{2,0},{3,1},{4,6},{5,7},{6,4},{7,5},{8,10},{9,11},{10,... | collective-permute-start | bytes 393224 | tf_op jit(solution)/shard_map/ppermute | solution.py:289
  50.9 18.7 %collective-permute-start.6 = (bf16[256,256]{1,0:T(8,128)(2,1)S(1)}, bf16[256,256]{1,0:T(8,128)(2,1)S(1)}, u32[]{:S(2)}, u32[]{:S(2)}) collective-permute-start(bf16[256,256]{1,0:T(8,128)(2,1)S(1)} %get-tuple-element.14.normed_ref), channel_id=1, source_target_pairs={{0,3},{1,2},{2,1},{3,0},{4,7},{5,6},{6,5},{7,4},{8,11},{9,10},{10,... | collective-permute-start | bytes 393224 | tf_op jit(solution)/shard_map/ppermute | solution.py:289
  52.3 10.2 %collective-permute-start.14 = (bf16[256,256]{1,0:T(8,128)(2,1)S(1)}, bf16[256,256]{1,0:T(8,128)(2,1)S(1)}, u32[]{:S(2)}, u32[]{:S(2)}) collective-permute-start(bf16[256,256]{1,0:T(8,128)(2,1)S(1)} %partial.4), channel_id=1, source_target_pairs={{0,2},{1,3},{2,0},{3,1},{4,6},{5,7},{6,4},{7,5},{8,10},{9,11},{10,... | collective-permute-start | bytes 393224 | tf_op jit(solution)/shard_map/ppermute | solution.py:289
  54.3 8.2 %collective-permute-start.15 = (bf16[256,256]{1,0:T(8,128)(2,1)S(1)}, bf16[256,256]{1,0:T(8,128)(2,1)S(1)}, u32[]{:S(2)}, u32[]{:S(2)}) collective-permute-start(bf16[256,256]{1,0:T(8,128)(2,1)S(1)} %partial.5), channel_id=1, source_target_pairs={{0,3},{1,2},{2,1},{3,0},{4,7},{5,6},{6,5},{7,4},{8,11},{9,10},{10,... | collective-permute-start | bytes 393224 | tf_op jit(solution)/shard_map/ppermute | solution.py:289
  64.2 1.3 %collective-permute-start.16 = (bf16[272,128]{1,0:T(8,128)(2,1)S(1)}, bf16[272,128]{1,0:T(8,128)(2,1)S(1)}, u32[]{:S(2)}, u32[]{:S(2)}) collective-permute-start(bf16[272,128]{1,0:T(8,128)(2,1)S(1)} %get-tuple-element.21.own_ref), channel_id=1, source_target_pairs={{0,4},{4,0},{8,12},{12,8},{16,20},{20,16},{24,28},{28,24},{1,5},{5... | collective-permute-start | bytes 208904 | tf_op jit(solution)/shard_map/ppermute | solution.py:292
  65.6 8.7 %collective-permute-start.17 = (bf16[272,128]{1,0:T(8,128)(2,1)S(1)}, bf16[272,128]{1,0:T(8,128)(2,1)S(1)}, u32[]{:S(2)}, u32[]{:S(2)}) collective-permute-start(bf16[272,128]{1,0:T(8,128)(2,1)S(1)} %join_states.3), channel_id=1, source_target_pairs={{8,0},{12,4},{16,8},{20,12},{24,16},{28,20},{9,1},{13,5},{17,9},{2... | collective-permute-start | bytes 208904 | tf_op jit(solution)/shard_map/ppermute | solution.py:295
  66.9 7.4 %collective-permute-start.18 = (bf16[272,128]{1,0:T(8,128)(2,1)S(1)}, bf16[272,128]{1,0:T(8,128)(2,1)S(1)}, u32[]{:S(2)}, u32[]{:S(2)}) collective-permute-start(bf16[272,128]{1,0:T(8,128)(2,1)S(1)} %join_states.3), channel_id=1, source_target_pairs={{16,0},{20,4},{24,8},{28,12},{17,1},{21,5},{25,9},{29,13},{18,2},{... | collective-permute-start | bytes 208904 | tf_op jit(solution)/shard_map/ppermute | solution.py:295
  68.2 9.4 %collective-permute-start.19 = (bf16[272,128]{1,0:T(8,128)(2,1)S(1)}, bf16[272,128]{1,0:T(8,128)(2,1)S(1)}, u32[]{:S(2)}, u32[]{:S(2)}) collective-permute-start(bf16[272,128]{1,0:T(8,128)(2,1)S(1)} %join_states.3), channel_id=1, source_target_pairs={{24,0},{28,4},{25,1},{29,5},{26,2},{30,6},{27,3},{31,7}} | collective-permute-start | bytes 208904 | tf_op jit(solution)/shard_map/ppermute | solution.py:295
  (9 other events, 84.4 us)

commit v2 on v0

v2 whole, which is shorter than its diff:
```python
import functools

import jax
import jax.numpy as jnp
from jax import lax
from jax.experimental import pallas as pl
from jax.experimental.pallas import tpu as pltpu
from jax.sharding import PartitionSpec as P

EXACT = lax.Precision.HIGHEST
EPSILON = 1e-05
F32 = jnp.float32
BF16 = jnp.bfloat16
TAIL = 16
HD = 128

NN = (((1,), (0,)), ((), ()))
NT = (((1,), (1,)), ((), ()))
TN = (((0,), (0,)), ((), ()))


def dot(a, b, dims):
    return lax.dot_general(a, b, dims, preferred_element_type=F32)


def split(x):
    high = x.astype(BF16)
    return high, (x - high.astype(F32)).astype(BF16)


def dot_fb(a, b, dims):
    high, low = split(a)
    return dot(high, b, dims) + dot(low, b, dims)


def dot_bf(a, b, dims):
    high, low = split(b)
    return dot(a, high, dims) + dot(a, low, dims)


def dot_ff(a, b, dims):
    ah, al = split(a)
    bh, bl = split(b)
    return dot(ah, bh, dims) + (dot(ah, bl, dims) + dot(al, bh, dims))


def triangle(length):
    rows = lax.broadcasted_iota(jnp.int32, (length, length), 0)
    cols = lax.broadcasted_iota(jnp.int32, (length, length), 1)
    return rows >= cols


def running_columns(decay, lower):
    return lax.dot_general(lower.astype(F32), decay, NT, precision=EXACT, preferred_element_type=F32)


def running_rows(decay, lower):
    return lax.dot_general(decay, lower.astype(F32), NT, precision=EXACT, preferred_element_type=F32)


def put_total(ref, base, total):
    first = total.astype(BF16).astype(F32)
    second = (total - first).astype(BF16).astype(F32)
    third = total - first - second
    at = lax.broadcasted_iota(jnp.int32, (TAIL, 128), 0)
    tail = jnp.where(at == 0, first, jnp.where(at == 1, second, jnp.where(at == 2, third, 0.0)))
    ref[base : base + TAIL, :] = tail.astype(BF16)


def get_total(ref, base):
    tail = ref[base : base + TAIL, :].astype(F32)
    return tail[0:1] + tail[1:2] + tail[2:3]


def total_of(columns, block):
    length = columns.shape[0]
    return jnp.broadcast_to(columns[length - 1 : length, block : block + 1], (1, HD))


def chip_sum(chip, ref, later):
    chips = ref.shape[0]
    summed = jnp.zeros((HD, HD), F32)
    for number in reversed(range(chips)) if later else range(chips):
        block = ref.at[number]
        joined = jnp.exp(get_total(block, HD)) * summed + block[0:HD, :].astype(F32)
        summed = jnp.where(number > chip if later else number < chip, joined, summed)
    return summed


def put_message(ref, state, total):
    state = state.astype(BF16)
    for number in range(ref.shape[0]):
        block = ref.at[number]
        block[0:HD, :] = state
        put_total(block, HD, total)


def lanes_of(number):
    return pl.ds(pl.multiple_of(number * HD, HD), HD)


def fresh_kernel(
    where_ref, q_ref, k_ref, v_ref, q_got, k_got, v_got, decay_ref, decay_got_ref, q_out, k_out, v_out, col_ref, row_ref, first_ref, message_ref
):
    core = where_ref[0]
    length = q_ref.shape[0]
    for out, ref, got in ((q_out, q_ref, q_got), (k_out, k_ref, k_got), (v_out, v_ref, v_got)):
        out[core] = ref[:, lanes_of(core)]
        out[1 - core] = got[:, lanes_of(core)]
    mine = jnp.where(core == 0, decay_ref[0:1, :], decay_ref[1:2, :])
    theirs = jnp.where(core == 0, decay_got_ref[0:1, :], decay_got_ref[1:2, :])
    block = lax.broadcasted_iota(jnp.int32, (2, length), 0)
    decay = jnp.where(block == core, mine, theirs)
    lower = triangle(length)
    columns = running_columns(decay, lower)
    col_ref[...] = columns
    row_ref[...] = running_rows(decay, lower)
    states = []
    for b in range(2):
        fade = jnp.exp(columns[length - 1 : length, b : b + 1] - columns[:, b : b + 1])
        states.append(dot_bf(k_out[b], fade * v_out[b].astype(F32), TN))
    totals = [total_of(columns, b) for b in range(2)]
    first_ref[...] = states[0]
    put_message(message_ref, jnp.exp(totals[1]) * states[0] + states[1], totals[0] + totals[1])


def weights(columns, across, lower, b):
    return jnp.exp(jnp.where(lower, columns[:, b : b + 1] - across[b : b + 1, :], -1e30))


def inner_kernel(q_ref, k_ref, v_ref, col_ref, row_ref, first_ref, inner_ref):
    columns, across = col_ref[...], row_ref[...]
    lower = triangle(columns.shape[0])
    for b in range(2):
        scores = dot(q_ref[b], k_ref[b], NT) * weights(columns, across, lower, b)
        inner = dot_fb(scores, v_ref[b], NN)
        if b == 1:
            inner = inner + jnp.exp(columns[:, 1:2]) * dot_bf(q_ref[b], first_ref[...], NN)
        inner_ref[b] = inner


def scale_of(mixed):
    return lax.rsqrt(jnp.mean(mixed * mixed, axis=-1, keepdims=True) + EPSILON)


def mixed_kernel(where_ref, q_ref, col_ref, inner_ref, gain_ref, first_ref, chips_ref, mixed_ref, keep_ref, send_ref, state_ref):
    core = where_ref[0]
    columns = col_ref[...]
    gain = gain_ref[:, lanes_of(core)]
    state = chip_sum(where_ref[1], chips_ref, False)
    high, low = split(state)
    shrink = jnp.exp(total_of(columns, 0))
    state_ref[0] = state
    state_ref[1] = shrink * state + first_ref[...]
    normed = []
    for b in range(2):
        grow = jnp.exp(columns[:, b : b + 1])
        if b == 1:
            grow = grow * shrink
        mixed = inner_ref[b] + grow * (dot(q_ref[b], high, NN) + dot(q_ref[b], low, NN))
        mixed_ref[b] = mixed
        normed.append((mixed * scale_of(mixed) * gain))
    keep_ref[...] = jnp.where(core == 0, normed[0], normed[1]).astype(BF16)
    send_ref[...] = jnp.where(core == 0, normed[1], normed[0]).astype(BF16)


def order_kernel(where_ref, keep_ref, got_ref, *out_refs):
    core = where_ref[0]
    for number, ref in enumerate(out_refs):
        part = slice(number * HD, (number + 1) * HD)
        ref[:, lanes_of(core)] = keep_ref[:, part]
        ref[:, lanes_of(1 - core)] = got_ref[:, part]


def own_partial_kernel(where_ref, grad_ref, got_ref, weight_ref, out_ref):
    core = where_ref[0]
    weight = weight_ref[pl.ds(pl.multiple_of(core * HD, HD), HD), :]
    out_ref[core] = dot(grad_ref[...], weight, NT)
    out_ref[1 - core] = dot(got_ref[...], weight, NT)


def partial_kernel(where_ref, grad_ref, got_ref, weight_ref, out_ref):
    core = where_ref[0]
    weight = weight_ref[...]
    out_ref[core] = dot(grad_ref[...], weight, NT).astype(BF16)
    out_ref[1 - core] = dot(got_ref[...], weight, NT).astype(BF16)


def grad_mixed_kernel(where_ref, q_ref, col_ref, gain_ref, mixed_ref, own_ref, *refs):
    part_refs, (grad_ref, second_ref, message_ref) = refs[:-3], refs[-3:]
    columns = col_ref[...]
    gain = gain_ref[:, lanes_of(where_ref[0])]
    ups = []
    for b in range(2):
        normed = own_ref[b]
        for ref in part_refs:
            normed = normed + ref[b].astype(F32)
        lifted = normed * gain
        mixed = mixed_ref[b]
        scale = scale_of(mixed)
        unit = mixed * scale
        grad = scale * (lifted - unit * jnp.mean(unit * lifted, axis=-1, keepdims=True))
        grad_ref[b] = grad
        ups.append(dot_bf(q_ref[b], jnp.exp(columns[:, b : b + 1]) * grad, TN))
    second_ref[...] = ups[1]
    totals = [total_of(columns, b) for b in range(2)]
    put_message(message_ref, ups[0] + jnp.exp(totals[0]) * ups[1], totals[0] + totals[1])


def inner_grad_kernel(
    where_ref, q_ref, k_ref, v_ref, col_ref, row_ref, grad_ref, state_ref, second_ref, keep_ref, send_ref, dk_ref, dv_ref
):
    core = where_ref[0]
    columns, across = col_ref[...], row_ref[...]
    length = columns.shape[0]
    lower = triangle(length)
    queries = []
    for b in range(2):
        q, k, v, grad = q_ref[b], k_ref[b], v_ref[b], grad_ref[b]
        weight = weights(columns, across, lower, b)
        scores = dot(q, k, NT) * weight
        grad_scores = dot_fb(grad, v, NT) * weight
        carried = jnp.exp(columns[:, b : b + 1]) * dot_ff(grad, state_ref[b], NT)
        queries.append(dot_fb(grad_scores, k, NN) + carried)
        dk = dot_fb(grad_scores, q, TN)
        dv = dot_ff(scores, grad, TN)
        if b == 0:
            fade = jnp.exp(columns[length - 1 : length, 0:1] - columns[:, 0:1])
            dk = dk + fade * dot_bf(v, second_ref[...], NT)
            dv = dv + fade * dot_bf(k, second_ref[...], NN)
        dk_ref[b] = dk
        dv_ref[b] = dv
    keep_ref[...] = jnp.where(core == 0, queries[0], queries[1]).astype(BF16)
    send_ref[...] = jnp.where(core == 0, queries[1], queries[0]).astype(BF16)


def outer_grad_kernel(where_ref, k_ref, v_ref, col_ref, dk_ref, dv_ref, chips_ref, keep_ref, send_ref):
    core = where_ref[0]
    columns = col_ref[...]
    length = columns.shape[0]
    high, low = split(chip_sum(where_ref[1], chips_ref, True))
    keys, values = [], []
    for b in range(2):
        fade = jnp.exp(columns[length - 1 : length, b : b + 1] - columns[:, b : b + 1])
        if b == 0:
            fade = fade * jnp.exp(total_of(columns, 1))
        keys.append(dk_ref[b] + fade * (dot(v_ref[b], high, NT) + dot(v_ref[b], low, NT)))
        values.append(dv_ref[b] + fade * (dot(k_ref[b], high, NN) + dot(k_ref[b], low, NN)))
    for number, pair in enumerate((keys, values)):
        part = slice(number * HD, (number + 1) * HD)
        keep_ref[:, part] = jnp.where(core == 0, pair[0], pair[1]).astype(BF16)
        send_ref[:, part] = jnp.where(core == 0, pair[1], pair[0]).astype(BF16)


def layer_kernel(others, where_ref, normed_ref, weight_ref, *refs):
    normed_refs = refs[:others]
    mine_refs = refs[others : 2 * others]
    theirs_refs = refs[2 * others : 3 * others]
    out_ref = refs[3 * others]
    core = where_ref[0]
    width = weight_ref.shape[1]
    step = 384 if width % 384 == 0 else 128
    for begin in range(0, width, step):
        lanes = slice(begin, begin + step)
        total = dot(normed_ref[...], weight_ref[:, lanes], NN)
        for k in range(others):
            total = total + dot(normed_refs[k][:, lanes_of(core)], mine_refs[k][:, lanes], NN)
            total = total + dot(normed_refs[k][:, lanes_of(1 - core)], theirs_refs[k][:, lanes], NN)
        out_ref[:, lanes] = total.astype(BF16)


SMEM = pl.BlockSpec(memory_space=pltpu.SMEM)
VMEM = pl.BlockSpec(memory_space=pltpu.VMEM)


def call(kernel, name, outs, args):
    return pl.pallas_call(
        kernel,
        name=name,
        out_shape=outs,
        in_specs=[SMEM] + [VMEM] * (len(args) - 1),
        out_specs=[VMEM] * len(outs),
        compiler_params=pltpu.CompilerParams(vmem_limit_bytes=40 * 2**20),
        cost_estimate=pl.CostEstimate(flops=1, bytes_accessed=1, transcendentals=0),
    )(*args)


def without_where(kernel):
    return lambda where_ref, *refs: kernel(*refs)


def after(values, *earlier):
    tied = lax.optimization_barrier((tuple(values), earlier))
    return list(tied[0])


def on_device(queries, keys, values, log_decay, norm_gain, out_weight, out_grad):
    length, columns = queries.shape
    seq = lax.axis_size("seq")
    tensor = lax.axis_size("tensor")
    chips = seq // 2
    model = out_weight.shape[1]
    width = model // tensor
    place = lax.axis_index("tensor")
    core = lax.rem(lax.axis_index("seq"), 2)
    where = jnp.stack([core, lax.axis_index("seq") // 2]).astype(jnp.int32)
    gain = norm_gain.reshape(1, columns)

    def swap_tensor(value, k):
        return lax.ppermute(value, "tensor", [(i, i ^ k) for i in range(tensor)])

    def swap_core(value):
        return lax.ppermute(value, "seq", [(i, i ^ 1) for i in range(seq)])

    def swap_chips(value):
        groups = [[i for i in range(seq) if i % 2 == side] for side in range(2)]
        return lax.all_to_all(value, "seq", 0, 0, axis_index_groups=groups)

    def shape(dtype, *dims):
        return jax.ShapeDtypeStruct(dims, dtype)

    others = range(1, tensor)
    message = shape(BF16, chips, HD + TAIL, HD)
    pair16 = shape(BF16, 2, length, HD)
    pair32 = shape(F32, 2, length, HD)
    one16 = shape(BF16, length, HD)
    both16 = shape(BF16, length, columns)

    slices = [
        lax.dynamic_slice(out_weight, (core * HD, (place ^ step) * width), (HD, width))
        for step in others
    ]
    mine = [swap_tensor(piece, step) for piece, step in zip(slices, others)]
    got = [swap_core(rows) for rows in (queries, keys, values)]
    decay_got = swap_core(log_decay)
    (out_grad,) = after([out_grad], *slices)
    grad_got = swap_core(out_grad)
    q, k, v, col, row, first, fresh = call(
        fresh_kernel,
        "fresh",
        [pair16, pair16, pair16, shape(F32, length, 2), shape(F32, 2, length), shape(F32, HD, HD), message],
        [where, queries, keys, values, *got, log_decay, decay_got],
    )
    arrived = swap_chips(fresh)
    (inner,) = call(without_where(inner_kernel), "inner", [pair32], [where, q, k, v, col, row, first])
    weight_own = lax.dynamic_slice(out_weight, (0, place * width), (columns, width))
    (own_partial,) = call(own_partial_kernel, "own_partial", [pair32], [where, out_grad, grad_got, weight_own])
    (arrived,) = after([arrived], inner, own_partial)
    mixed, normed_keep, normed_send, states = call(
        mixed_kernel,
        "mixed",
        [pair32, one16, one16, shape(F32, 2, HD, HD)],
        [where, q, col, inner, gain, first, arrived],
    )
    normed_got = swap_core(normed_send)
    (normed,) = call(order_kernel, "order", [both16], [where, normed_keep, normed_got])
    partials, theirs = [], []
    for number, piece in enumerate(mine):
        (piece,) = after([piece], mixed if number else arrived, *partials, *theirs[: max(number - 1, 0)])
        theirs.append(swap_core(piece))
        (partial,) = call(partial_kernel, "partial", [pair16], [where, out_grad, grad_got, piece])
        partials.append(partial)
    sent = [swap_tensor(partial, step) for partial, step in zip(partials, others)]
    sent = after(sent, *theirs)
    grad_mixed, second, upward = call(
        grad_mixed_kernel,
        "grad_mixed",
        [pair32, shape(F32, HD, HD), message],
        [where, q, col, gain, mixed, own_partial, *sent],
    )
    returned = swap_chips(upward)
    (normed,) = after([normed], grad_mixed)
    normed_others = [swap_tensor(normed, step) for step in others]
    dq_keep, dq_send, dk_inner, dv_inner = call(
        inner_grad_kernel,
        "inner_grad",
        [one16, one16, pair32, pair32],
        [where, q, k, v, col, row, grad_mixed, states, second],
    )
    dq_got = swap_core(dq_send)
    (layer_out,) = call(
        functools.partial(layer_kernel, tensor - 1),
        "layer",
        [shape(BF16, length, width)],
        [where, normed, weight_own, *normed_others, *mine, *theirs],
    )
    (query_grad,) = call(order_kernel, "order", [both16], [where, dq_keep, dq_got])
    keep, send = call(
        outer_grad_kernel,
        "outer_grad",
        [both16, both16],
        [where, k, v, col, dk_inner, dv_inner, returned],
    )
    got = swap_core(send)
    key_grad, value_grad = call(order_kernel, "order", [both16, both16], [where, keep, got])
    return layer_out, query_grad, key_grad, value_grad


def solution(mesh):
    in_specs = (
        P("seq", "tensor"),
        P("seq", "tensor"),
        P("seq", "tensor"),
        P("tensor", "seq"),
        P("tensor"),
        P("tensor", None),
        P("seq", "tensor"),
    )
    out_specs = (P("seq", "tensor"), P("seq", "tensor"), P("seq", "tensor"), P("seq", "tensor"))
    return jax.shard_map(
        on_device, mesh=mesh, in_specs=in_specs, out_specs=out_specs, check_vma=False
    )
```

time: 193 us -> 86 us (0.45); the launches traced: 190 us -> 84.9 us
  waiting for transfers between devices: 79 us -> 7.73 us
  other arithmetic: 24.8 us -> 0.07 us
  matrix products: 24.2 us -> 0 us
  local copies, waits for them, and re-layouts: 8.74 us -> 31.3 us
  Pallas kernels: 0 us -> 20.1 us
  starting transfers between devices: 38.4 us -> 24.8 us
  between operations: 14.2 us -> 0.98 us
    all_gather x1 -> x0, waiting for transfers between devices: 38.5 us -> none  [on_device(): lax.all_gather(out_grad, 'tensor', axis=1, tiled=True)]
    ppermute x14 -> x20, waiting for transfers between devices: 39.8 us -> 7.72 us  [the longest x9 4.57 us: swap_tensor(): return lax.ppermute(value, 'tensor', [(i, i ^ k) for i in range(tensor)])]
    dot_general x14 -> x0, matrix products: 24.2 us -> none  [the longest x1 3.6 us: on_device(): lax.dot_general(lax.all_gather(out_grad, 'tensor', axis=1, tiled=True), o...]
    ppermute x14 -> x20, starting transfers between devices: 38.3 us -> 14.7 us  [the longest x9 12.1 us: swap_tensor(): return lax.ppermute(value, 'tensor', [(i, i ^ k) for i in range(tensor)])]
    convert_element_type x28 -> x0, other arithmetic: 22.8 us -> none  [the longest x14 12.3 us: advance(): (shrink * held + fresh).astype(jnp.bfloat16)]
    pallas_call x0 -> x14, Pallas kernels: none -> 20.1 us  [call(): pl.pallas_call(kernel, name=name, out_shape=outs, in_specs=[SMEM] + [VMEM...]
    unnamed x17 -> x90, local copies, waits for them, and re-layouts: 7.66 us -> 27.7 us
    all_to_all x0 -> x2, starting transfers between devices: none -> 10.1 us  [swap_chips(): return lax.all_to_all(value, 'seq', 0, 0, axis_index_groups=groups)]
  transfers between devices with their start and end apart: 16 -> 22, of which waited for: 15 -> 7; matrix products, arithmetic and copies ran while one was open for 25% -> 1% of each run, Pallas kernels for 0% -> 21%
where the time goes in v2:
time: 86 us; the launch traced here: 84.9 us
  local copies, waits for them, and re-layouts  31.3 us (36%)
  starting transfers between devices  24.8 us (29%)
  Pallas kernels  20.1 us (23%)
  waiting for transfers between devices  7.73 us (9%)
  between operations  0.98 us (1%)
    unnamed x90, local copies, waits for them, and re-layouts  27.7 us
    pallas_call x14, Pallas kernels, call(): pl.pallas_call(kernel, name=name, out_shape=outs, in_specs=[SMEM] + [VMEM...  20.1 us
    ppermute x9, starting transfers between devices, swap_tensor(): return lax.ppermute(value, 'tensor', [(i, i ^ k) for i in range(tensor)])  12.1 us
    all_to_all x2, starting transfers between devices, swap_chips(): return lax.all_to_all(value, 'seq', 0, 0, axis_index_groups=groups)  10.1 us
    ppermute x9, waiting for transfers between devices, swap_tensor(): return lax.ppermute(value, 'tensor', [(i, i ^ k) for i in range(tensor)])  4.57 us
    ppermute x11, waiting for transfers between devices, swap_core(): return lax.ppermute(value, 'seq', [(i, i ^ 1) for i in range(seq)])  3.16 us
    ppermute x11, starting transfers between devices, swap_core(): return lax.ppermute(value, 'seq', [(i, i ^ 1) for i in range(seq)])  2.63 us
    dynamic_slice x1, local copies, waits for them, and re-layouts, on_device(): lax.dynamic_slice(out_weight, (core * HD, (place ^ step) * width), (HD, w...  2.38 us
  transfers between devices with their start and end apart: 22, of which 7 were waited for; matrix products, arithmetic and copies ran while one was open for 1% of the time, Pallas kernels for 21%

profile of v2, /device:TPU:0, one launch (start us, length us, event | category | flops | bytes accessed | tf_op | source)
XLA Modules:
  0.0 84.9 jit_solution(13389775225927785177)
XLA Ops:
  0.7 2.4 %fusion = (bf16[128,1536]{1,0:T(8,128)(2,1)}, bf16[128,1536]{1,0:T(8,128)(2,1)}, bf16[128,1536]{1,0:T(8,128)(2,1)}) fusion(bf16[256,6144]{1,0:T(8,128)(2,1)} %param.12, s32[]{:T(128)S(6)} %select_n.23, s32[]{:T(128)S(6)} %select_n.26, s32[]{:T(128)S(6)} %select_n.25, s32[]{:T(128)S(6)} %select_n.24), kind=kLoop, calls=%fused_computation.2 | loop fusion | bytes 2359312 | tf_op jit(solution)/shard_map/dynamic_slice | solution.py:330
  3.5 2.5 %collective-permute-start.6 = (bf16[128,1536]{1,0:T(8,128)(2,1)}, bf16[128,1536]{1,0:T(8,128)(2,1)S(1)}, u32[]{:S(2)}, u32[]{:S(2)}) collective-permute-start(bf16[128,1536]{1,0:T(8,128)(2,1)} %get-tuple-element.68), channel_id=1, source_target_pairs={{0,1},{1,0},{2,3},{3,2},{4,5},{5,4},{6,7},{7,6},{8,9},{9,8},{10,11... | collective-permute-start | bytes 1179656 | tf_op jit(solution)/shard_map/ppermute | solution.py:310
  8.4 1.5 %collective-permute-start.8 = (bf16[128,1536]{1,0:T(8,128)(2,1)}, bf16[128,1536]{1,0:T(8,128)(2,1)S(1)}, u32[]{:S(2)}, u32[]{:S(2)}) collective-permute-start(bf16[128,1536]{1,0:T(8,128)(2,1)} %get-tuple-element.67), channel_id=1, source_target_pairs={{0,2},{1,3},{2,0},{3,1},{4,6},{5,7},{6,4},{7,5},{8,10},{9,11},{10,... | collective-permute-start | bytes 1179656 | tf_op jit(solution)/shard_map/ppermute | solution.py:310
  18.3 2.1 %fresh.1 = (bf16[2,256,128]{2,1,0:T(8,128)(2,1)S(1)}, bf16[2,256,128]{2,1,0:T(8,128)(2,1)S(1)}, bf16[2,256,128]{2,1,0:T(8,128)(2,1)S(1)}, f32[256,2]{1,0:T(8,128...) custom-call(s32[2]{0:T(128)S(1)} %pad_add_fusion.where_ref, ...), custom_call_target="tpu_custom_call" | custom-call | flops 1 | bytes 1 | tf_op jit(solution)/shard_map/fresh/pallas_call | solution.py:277
  21.7 4.9 %all-to-all-start = ((bf16[4,144,128]{2,1,0:T(8,128)(2,1)}), bf16[4,144,128]{2,1,0:T(8,128)(2,1)}, u32[]{:S(2)}, u32[]{:S(2)}) async-start(bf16[4,144,128]{2,1,0:T(8,128)(2,1)} %get-tuple-element.41), calls=%async_computation | async-start | bytes 294912 | tf_op jit(solution)/shard_map/all_to_all | solution.py:317
  26.5 1.2 %constant_dynamic-slice_fusion.weight_ref = bf16[256,1536]{1,0:T(8,128)(2,1)S(1)} fusion(bf16[256,6144]{1,0:T(8,128)(2,1)} %param.12, s32[]{:T(128)S(6)} %select_n.27), kind=kLoop, calls=%fused_computation.1 | loop fusion | bytes 1572868 | tf_op jit(solution)/shard_map/dynamic_slice | solution.py:346
  31.2 1.1 %own_partial.1.own_ref = f32[2,256,128]{2,1,0:T(8,128)S(1)} custom-call(s32[2]{0:T(128)S(1)} %pad_add_fusion.where_ref, bf16[256,1536]{1,0:T(8,128)(2,1)S(1)} %copy-done, bf16[256,1536]{1,0:T(8,128)(2,1)S(1)} %collective-permute-done.4.got_ref, bf16[256,1536]{1,0:T(8,128)(2,1)S(1)} %constant_dynamic-slice_fusion.weight_ref), custom_call_target="tpu_custom_call" | custom-call | flops 1 | bytes 1 | tf_op jit(solution)/shard_map/own_partial/pallas_call | solution.py:277
  34.9 1.3 %mixed.1 = (f32[2,256,128]{2,1,0:T(8,128)S(1)}, bf16[256,128]{1,0:T(8,128)(2,1)S(1)}, bf16[256,128]{1,0:T(8,128)(2,1)S(1)}, f32[2,128,128]{2,1,0:T(8,128)S(1)}) custom-call(s32[2]{0:T(128)S(1)} %pad_add_fusion.where_ref, bf16[2,256,128]{2,1,0:T(8,128)(2,1)S(1)} %get-tuple-element.35.refs_0_.q_ref, f32[256,2]{1,0:T(8,128)S(1)} %get-tuple-element.36.refs_3_.col_ref, ...), custom_call_target="tpu_custom_call" | custom-call | flops 1 | bytes 1 | tf_op jit(solution)/shard_map/mixed/pallas_call | solution.py:277
  36.8 1.1 %partial.3 = bf16[2,256,128]{2,1,0:T(8,128)(2,1)S(1)} custom-call(s32[2]{0:T(128)S(1)} %pad_add_fusion.where_ref, bf16[256,1536]{1,0:T(8,128)(2,1)S(1)} %copy-done, bf16[256,1536]{1,0:T(8,128)(2,1)S(1)} %collective-permute-done.4.got_ref, bf16[128,1536]{1,0:T(8,128)(2,1)S(1)} %collective-permute-done.6.weight_ref.refs_3_), custom_call_target="tpu_custom_call" | custom-call | flops 1 | bytes 1 | tf_op jit(solution)/shard_map/partial/pallas_call | solution.py:277
  38.5 1.1 %partial.4 = bf16[2,256,128]{2,1,0:T(8,128)(2,1)S(1)} custom-call(s32[2]{0:T(128)S(1)} %pad_add_fusion.where_ref, bf16[256,1536]{1,0:T(8,128)(2,1)S(1)} %copy-done, bf16[256,1536]{1,0:T(8,128)(2,1)S(1)} %collective-permute-done.4.got_ref, bf16[128,1536]{1,0:T(8,128)(2,1)S(1)} %collective-permute-done.8.weight_ref.refs_4_), custom_call_target="tpu_custom_call" | custom-call | flops 1 | bytes 1 | tf_op jit(solution)/shard_map/partial/pallas_call | solution.py:277
  39.7 1.6 %collective-permute-start.9 = (bf16[2,256,128]{2,1,0:T(8,128)(2,1)S(1)}, bf16[2,256,128]{2,1,0:T(8,128)(2,1)S(1)}, u32[]{:S(2)}, u32[]{:S(2)}) collective-permute-start(bf16[2,256,128]{2,1,0:T(8,128)(2,1)S(1)} %partial.4), channel_id=1, source_target_pairs={{0,2},{1,3},{2,0},{3,1},{4,6},{5,7},{6,4},{7,5},{8,10},{9,11},{10,... | collective-permute-start | bytes 393224 | tf_op jit(solution)/shard_map/ppermute | solution.py:310
  41.3 1.1 %collective-permute-start.7 = (bf16[2,256,128]{2,1,0:T(8,128)(2,1)S(1)}, bf16[2,256,128]{2,1,0:T(8,128)(2,1)S(1)}, u32[]{:S(2)}, u32[]{:S(2)}) collective-permute-start(bf16[2,256,128]{2,1,0:T(8,128)(2,1)S(1)} %partial.3), channel_id=1, source_target_pairs={{0,1},{1,0},{2,3},{3,2},{4,5},{5,4},{6,7},{7,6},{8,9},{9,8},{10,11... | collective-permute-start | bytes 393224 | tf_op jit(solution)/shard_map/ppermute | solution.py:310
  42.4 1.6 %partial.5 = bf16[2,256,128]{2,1,0:T(8,128)(2,1)S(1)} custom-call(s32[2]{0:T(128)S(1)} %pad_add_fusion.where_ref, bf16[256,1536]{1,0:T(8,128)(2,1)S(1)} %copy-done, bf16[256,1536]{1,0:T(8,128)(2,1)S(1)} %collective-permute-done.4.got_ref, bf16[128,1536]{1,0:T(8,128)(2,1)} %collective-permute-done.10.weight_ref.refs_5_), custom_call_target="tpu_custom_call" | custom-call | flops 1 | bytes 1 | tf_op jit(solution)/shard_map/partial/pallas_call | solution.py:277
  45.7 1.6 %collective-permute-done.7.refs_0_ = bf16[2,256,128]{2,1,0:T(8,128)(2,1)S(1)} collective-permute-done((bf16[2,256,128]{2,1,0:T(8,128)(2,1)S(1)}, bf16[2,256,128]{2,1,0:T(8,128)(2,1)S(1)}, u32[]{:S(2)}, u32[]{:S(2)}) %collective-permute-start.7) | collective-permute-done | bytes 131104 | tf_op jit(solution)/shard_map/ppermute | solution.py:310
  48.0 2.2 %collective-permute-done.12.refs_2_ = bf16[2,256,128]{2,1,0:T(8,128)(2,1)S(1)} collective-permute-done((bf16[2,256,128]{2,1,0:T(8,128)(2,1)S(1)}, bf16[2,256,128]{2,1,0:T(8,128)(2,1)S(1)}, u32[]{:S(2)}, u32[]{:S(2)}) %collective-permute-start.12) | collective-permute-done | bytes 131104 | tf_op jit(solution)/shard_map/ppermute | solution.py:310
  50.3 1.2 %grad_mixed.1 = (f32[2,256,128]{2,1,0:T(8,128)S(1)}, f32[128,128]{1,0:T(8,128)S(1)}, bf16[4,144,128]{2,1,0:T(8,128)(2,1)S(1)}) custom-call(s32[2]{0:T(128)S(1)} %pad_add_fusion.where_ref, bf16[2,256,128]{2,1,0:T(8,128)(2,1)S(1)} %get-tuple-element.35.refs_0_.q_ref, f32[256,2]{1,0:T(8,128)S(1)} %get-tuple-element.36.refs_3_.col_ref, f32[1,256]{1,0:T(1,128)S(1)} %bitcast.4, ...), custom_call_target="tpu_custom_call" | custom-call | flops 1 | bytes 1 | tf_op jit(solution)/shard_map/grad_mixed/pallas_call | solution.py:277
  53.4 5.2 %all-to-all-start.1 = ((bf16[4,144,128]{2,1,0:T(8,128)(2,1)}), bf16[4,144,128]{2,1,0:T(8,128)(2,1)S(1)}, u32[]{:S(2)}, u32[]{:S(2)}) async-start(bf16[4,144,128]{2,1,0:T(8,128)(2,1)} %copy-done.24), calls=%async_computation.1 | async-start | bytes 294912 | tf_op jit(solution)/shard_map/all_to_all | solution.py:317
  58.6 1.5 %collective-permute-done.5.got_ref = bf16[256,128]{1,0:T(8,128)(2,1)S(1)} collective-permute-done((bf16[256,128]{1,0:T(8,128)(2,1)}, bf16[256,128]{1,0:T(8,128)(2,1)S(1)}, u32[]{:S(2)}, u32[]{:S(2)}) %collective-permute-start.5) | collective-permute-done | bytes 65568 | tf_op jit(solution)/shard_map/ppermute | solution.py:313
  62.5 1.1 %collective-permute-start.16 = (bf16[256,256]{1,0:T(8,128)(2,1)S(1)}, bf16[256,256]{1,0:T(8,128)(2,1)}, u32[]{:S(2)}, u32[]{:S(2)}) collective-permute-start(bf16[256,256]{1,0:T(8,128)(2,1)S(1)} %order.3.normed_ref), channel_id=1, source_target_pairs={{0,2},{1,3},{2,0},{3,1},{4,6},{5,7},{6,4},{7,5},{8,10},{9,11},{10,... | collective-permute-start | bytes 393224 | tf_op jit(solution)/shard_map/ppermute | solution.py:310
  63.6 1.5 %collective-permute-start.17 = (bf16[256,256]{1,0:T(8,128)(2,1)S(1)}, bf16[256,256]{1,0:T(8,128)(2,1)}, u32[]{:S(2)}, u32[]{:S(2)}) collective-permute-start(bf16[256,256]{1,0:T(8,128)(2,1)S(1)} %order.3.normed_ref), channel_id=1, source_target_pairs={{0,3},{1,2},{2,1},{3,0},{4,7},{5,6},{6,5},{7,4},{8,11},{9,10},{10,... | collective-permute-start | bytes 393224 | tf_op jit(solution)/shard_map/ppermute | solution.py:310
  68.7 1.9 %inner_grad.1 = (bf16[256,128]{1,0:T(8,128)(2,1)S(1)}, bf16[256,128]{1,0:T(8,128)(2,1)S(1)}, f32[2,256,128]{2,1,0:T(8,128)S(1)}, f32[2,256,128]{2,1,0:T(8,128)S(1)}) custom-call(s32[2]{0:T(128)S(1)} %pad_add_fusion.where_ref, bf16[2,256,128]{2,1,0:T(8,128)(2,1)S(1)} %get-tuple-element.35.refs_0_.q_ref, ...), custom_call_target="tpu_custom_call" | custom-call | flops 1 | bytes 1 | tf_op jit(solution)/shard_map/inner_grad/pallas_call | solution.py:277
  78.6 1.2 %order.4 = bf16[256,256]{1,0:T(8,128)(2,1)} custom-call(s32[2]{0:T(128)S(1)} %pad_add_fusion.where_ref, bf16[256,128]{1,0:T(8,128)(2,1)S(1)} %copy-done.41, bf16[256,128]{1,0:T(8,128)(2,1)S(1)} %collective-permute-done.18.got_ref), custom_call_target="tpu_custom_call" | custom-call | flops 1 | bytes 1 | tf_op jit(solution)/shard_map/order/pallas_call | solution.py:277
  79.9 3.7 %layer.1 = bf16[256,1536]{1,0:T(8,128)(2,1)} custom-call(s32[2]{0:T(128)S(1)} %pad_add_fusion.where_ref, bf16[256,256]{1,0:T(8,128)(2,1)S(1)} %order.3.normed_ref, bf16[256,1536]{1,0:T(8,128)(2,1)S(1)} %constant_dynamic-slice_fusion.weight_ref, bf16[256,256]{1,0:T(8,128)(2,1)} %collective-permute-done.15.refs_0_, ...), custom_call_target="tpu_custom_call" | custom-call | flops 1 | bytes 1 | tf_op jit(solution)/shard_map/layer/pallas_call | solution.py:277
  83.7 1.3 %order.5 = (bf16[256,256]{1,0:T(8,128)(2,1)}, bf16[256,256]{1,0:T(8,128)(2,1)}) custom-call(s32[2]{0:T(128)S(1)} %pad_add_fusion.where_ref, bf16[256,256]{1,0:T(8,128)(2,1)S(1)} %get-tuple-element.62.keep_ref, bf16[256,256]{1,0:T(8,128)(2,1)S(1)} %collective-permute-done.19.got_ref), custom_call_target="tpu_custom_call" | custom-call | flops 1 | bytes 1 | tf_op jit(solution)/shard_map/order/pallas_call | solution.py:277
  (127 shorter events, 38.2 us)
Async XLA Ops:
  0.6 30.6 %copy-start = (bf16[256,1536]{1,0:T(8,128)(2,1)S(1)}, bf16[256,1536]{1,0:T(8,128)(2,1)}, u32[]{:S(2)}) copy-start(bf16[256,1536]{1,0:T(8,128)(2,1)} %grad_ref.3) | copy-start | bytes 2359300
  3.1 30.0 %copy-start.42 = (f32[256]{0:T(256)S(1)}, f32[256]{0:T(256)}, u32[]{:S(2)}) copy-start(f32[256]{0:T(256)} %param.11) | copy-start | bytes 3076
  3.1 28.2 %collective-permute-start.4 = (bf16[256,1536]{1,0:T(8,128)(2,1)}, bf16[256,1536]{1,0:T(8,128)(2,1)S(1)}, u32[]{:S(2)}, u32[]{:S(2)}) collective-permute-start(bf16[256,1536]{1,0:T(8,128)(2,1)} %grad_ref.3), channel_id=1, source_target_pairs={{0,4},{4,0},{8,12},{12,8},{16,20},{20,16},{24,28},{28,24},{1,5},{5... | collective-permute-start | bytes 2359304 | tf_op jit(solution)/shard_map/ppermute | solution.py:313
  3.5 29.6 %collective-permute-start.6 = (bf16[128,1536]{1,0:T(8,128)(2,1)}, bf16[128,1536]{1,0:T(8,128)(2,1)S(1)}, u32[]{:S(2)}, u32[]{:S(2)}) collective-permute-start(bf16[128,1536]{1,0:T(8,128)(2,1)} %get-tuple-element.68), channel_id=1, source_target_pairs={{0,1},{1,0},{2,3},{3,2},{4,5},{5,4},{6,7},{7,6},{8,9},{9,8},{10,11... | collective-permute-start | bytes 1179656 | tf_op jit(solution)/shard_map/ppermute | solution.py:310
  6.0 1.4 %collective-permute-start.3 = (f32[2,256]{1,0:T(2,128)}, f32[2,256]{1,0:T(2,128)S(1)}, u32[]{:S(2)}, u32[]{:S(2)}) collective-permute-start(f32[2,256]{1,0:T(2,128)} %decay_ref.1), channel_id=1, source_target_pairs={{0,4},{4,0},{8,12},{12,8},{16,20},{20,16},{24,28},{28,24},{1,5},{5... | collective-permute-start | bytes 6152 | tf_op jit(solution)/shard_map/ppermute | solution.py:313
  6.2 1.6 %collective-permute-start = (bf16[256,256]{1,0:T(8,128)(2,1)}, bf16[256,256]{1,0:T(8,128)(2,1)S(1)}, u32[]{:S(2)}, u32[]{:S(2)}) collective-permute-start(bf16[256,256]{1,0:T(8,128)(2,1)} %q_ref.1), channel_id=1, source_target_pairs={{0,4},{4,0},{8,12},{12,8},{16,20},{20,16},{24,28},{28,24},{1,5},{5... | collective-permute-start | bytes 393224 | tf_op jit(solution)/shard_map/ppermute | solution.py:313
  6.5 3.5 %collective-permute-start.1 = (bf16[256,256]{1,0:T(8,128)(2,1)}, bf16[256,256]{1,0:T(8,128)(2,1)S(1)}, u32[]{:S(2)}, u32[]{:S(2)}) collective-permute-start(bf16[256,256]{1,0:T(8,128)(2,1)} %k_ref.1), channel_id=1, source_target_pairs={{0,4},{4,0},{8,12},{12,8},{16,20},{20,16},{24,28},{28,24},{1,5},{5... | collective-permute-start | bytes 393224 | tf_op jit(solution)/shard_map/ppermute | solution.py:313
  7.4 4.1 %collective-permute-start.2 = (bf16[256,256]{1,0:T(8,128)(2,1)}, bf16[256,256]{1,0:T(8,128)(2,1)S(1)}, u32[]{:S(2)}, u32[]{:S(2)}) collective-permute-start(bf16[256,256]{1,0:T(8,128)(2,1)} %v_ref.1), channel_id=1, source_target_pairs={{0,4},{4,0},{8,12},{12,8},{16,20},{20,16},{24,28},{28,24},{1,5},{5... | collective-permute-start | bytes 393224 | tf_op jit(solution)/shard_map/ppermute | solution.py:313
  8.4 29.5 %collective-permute-start.8 = (bf16[128,1536]{1,0:T(8,128)(2,1)}, bf16[128,1536]{1,0:T(8,128)(2,1)S(1)}, u32[]{:S(2)}, u32[]{:S(2)}) collective-permute-start(bf16[128,1536]{1,0:T(8,128)(2,1)} %get-tuple-element.67), channel_id=1, source_target_pairs={{0,2},{1,3},{2,0},{3,1},{4,6},{5,7},{6,4},{7,5},{8,10},{9,11},{10,... | collective-permute-start | bytes 1179656 | tf_op jit(solution)/shard_map/ppermute | solution.py:310
  10.6 29.0 %collective-permute-start.10 = (bf16[128,1536]{1,0:T(8,128)(2,1)}, bf16[128,1536]{1,0:T(8,128)(2,1)}, u32[]{:S(2)}, u32[]{:S(2)}) collective-permute-start(bf16[128,1536]{1,0:T(8,128)(2,1)} %get-tuple-element.66), channel_id=1, source_target_pairs={{0,3},{1,2},{2,1},{3,0},{4,7},{5,6},{6,5},{7,4},{8,11},{9,10},{10,... | collective-permute-start | bytes 1179656 | tf_op jit(solution)/shard_map/ppermute | solution.py:310
  21.7 11.4 %all-to-all-start = ((bf16[4,144,128]{2,1,0:T(8,128)(2,1)}), bf16[4,144,128]{2,1,0:T(8,128)(2,1)}, u32[]{:S(2)}, u32[]{:S(2)}) async-start(bf16[4,144,128]{2,1,0:T(8,128)(2,1)} %get-tuple-element.41), calls=%async_computation | async-start | bytes 294912 | tf_op jit(solution)/shard_map/all_to_all | solution.py:317
  33.1 6.6 %collective-permute-start.11 = (bf16[128,1536]{1,0:T(8,128)(2,1)S(1)}, bf16[128,1536]{1,0:T(8,128)(2,1)S(1)}, u32[]{:S(2)}, u32[]{:S(2)}) collective-permute-start(bf16[128,1536]{1,0:T(8,128)(2,1)S(1)} %collective-permute-done.6.weight_ref.refs_3_), channel_id=1, source_target_pairs={{0,4},{4,0},{8,12},{12,8},{16,20},{20,16},{24,28},{28,24},{1,5},{5... | collective-permute-start | bytes 1179656 | tf_op jit(solution)/shard_map/ppermute | solution.py:313
  37.9 9.3 %collective-permute-start.13 = (bf16[128,1536]{1,0:T(8,128)(2,1)S(1)}, bf16[128,1536]{1,0:T(8,128)(2,1)S(1)}, u32[]{:S(2)}, u32[]{:S(2)}) collective-permute-start(bf16[128,1536]{1,0:T(8,128)(2,1)S(1)} %collective-permute-done.8.weight_ref.refs_4_), channel_id=1, source_target_pairs={{0,4},{4,0},{8,12},{12,8},{16,20},{20,16},{24,28},{28,24},{1,5},{5... | collective-permute-start | bytes 1179656 | tf_op jit(solution)/shard_map/ppermute | solution.py:313
  39.7 10.6 %collective-permute-start.14 = (bf16[128,1536]{1,0:T(8,128)(2,1)}, bf16[128,1536]{1,0:T(8,128)(2,1)S(1)}, u32[]{:S(2)}, u32[]{:S(2)}) collective-permute-start(bf16[128,1536]{1,0:T(8,128)(2,1)} %collective-permute-done.10.weight_ref.refs_5_), channel_id=1, source_target_pairs={{0,4},{4,0},{8,12},{12,8},{16,20},{20,16},{24,28},{28,24},{1,5},{5... | collective-permute-start | bytes 1179656 | tf_op jit(solution)/shard_map/ppermute | solution.py:313
  39.7 5.9 %collective-permute-start.9 = (bf16[2,256,128]{2,1,0:T(8,128)(2,1)S(1)}, bf16[2,256,128]{2,1,0:T(8,128)(2,1)S(1)}, u32[]{:S(2)}, u32[]{:S(2)}) collective-permute-start(bf16[2,256,128]{2,1,0:T(8,128)(2,1)S(1)} %partial.4), channel_id=1, source_target_pairs={{0,2},{1,3},{2,0},{3,1},{4,6},{5,7},{6,4},{7,5},{8,10},{9,11},{10,... | collective-permute-start | bytes 393224 | tf_op jit(solution)/shard_map/ppermute | solution.py:310
  41.3 5.9 %collective-permute-start.7 = (bf16[2,256,128]{2,1,0:T(8,128)(2,1)S(1)}, bf16[2,256,128]{2,1,0:T(8,128)(2,1)S(1)}, u32[]{:S(2)}, u32[]{:S(2)}) collective-permute-start(bf16[2,256,128]{2,1,0:T(8,128)(2,1)S(1)} %partial.3), channel_id=1, source_target_pairs={{0,1},{1,0},{2,3},{3,2},{4,5},{5,4},{6,7},{7,6},{8,9},{9,8},{10,11... | collective-permute-start | bytes 393224 | tf_op jit(solution)/shard_map/ppermute | solution.py:310
  44.0 6.3 %collective-permute-start.12 = (bf16[2,256,128]{2,1,0:T(8,128)(2,1)S(1)}, bf16[2,256,128]{2,1,0:T(8,128)(2,1)S(1)}, u32[]{:S(2)}, u32[]{:S(2)}) collective-permute-start(bf16[2,256,128]{2,1,0:T(8,128)(2,1)S(1)} %partial.5), channel_id=1, source_target_pairs={{0,3},{1,2},{2,1},{3,0},{4,7},{5,6},{6,5},{7,4},{8,11},{9,10},{10,... | collective-permute-start | bytes 393224 | tf_op jit(solution)/shard_map/ppermute | solution.py:310
  53.4 19.2 %all-to-all-start.1 = ((bf16[4,144,128]{2,1,0:T(8,128)(2,1)}), bf16[4,144,128]{2,1,0:T(8,128)(2,1)S(1)}, u32[]{:S(2)}, u32[]{:S(2)}) async-start(bf16[4,144,128]{2,1,0:T(8,128)(2,1)} %copy-done.24), calls=%async_computation.1 | async-start | bytes 294912 | tf_op jit(solution)/shard_map/all_to_all | solution.py:317
  58.6 1.5 %collective-permute-start.5 = (bf16[256,128]{1,0:T(8,128)(2,1)}, bf16[256,128]{1,0:T(8,128)(2,1)S(1)}, u32[]{:S(2)}, u32[]{:S(2)}) collective-permute-start(bf16[256,128]{1,0:T(8,128)(2,1)} %copy-done.44), channel_id=1, source_target_pairs={{0,4},{4,0},{8,12},{12,8},{16,20},{20,16},{24,28},{28,24},{1,5},{5... | collective-permute-start | bytes 196616 | tf_op jit(solution)/shard_map/ppermute | solution.py:313
  61.5 18.4 %collective-permute-start.15 = (bf16[256,256]{1,0:T(8,128)(2,1)S(1)}, bf16[256,256]{1,0:T(8,128)(2,1)}, u32[]{:S(2)}, u32[]{:S(2)}) collective-permute-start(bf16[256,256]{1,0:T(8,128)(2,1)S(1)} %order.3.normed_ref), channel_id=1, source_target_pairs={{0,1},{1,0},{2,3},{3,2},{4,5},{5,4},{6,7},{7,6},{8,9},{9,8},{10,11... | collective-permute-start | bytes 393224 | tf_op jit(solution)/shard_map/ppermute | solution.py:310
  62.5 17.4 %collective-permute-start.16 = (bf16[256,256]{1,0:T(8,128)(2,1)S(1)}, bf16[256,256]{1,0:T(8,128)(2,1)}, u32[]{:S(2)}, u32[]{:S(2)}) collective-permute-start(bf16[256,256]{1,0:T(8,128)(2,1)S(1)} %order.3.normed_ref), channel_id=1, source_target_pairs={{0,2},{1,3},{2,0},{3,1},{4,6},{5,7},{6,4},{7,5},{8,10},{9,11},{10,... | collective-permute-start | bytes 393224 | tf_op jit(solution)/shard_map/ppermute | solution.py:310
  63.6 16.3 %collective-permute-start.17 = (bf16[256,256]{1,0:T(8,128)(2,1)S(1)}, bf16[256,256]{1,0:T(8,128)(2,1)}, u32[]{:S(2)}, u32[]{:S(2)}) collective-permute-start(bf16[256,256]{1,0:T(8,128)(2,1)S(1)} %order.3.normed_ref), channel_id=1, source_target_pairs={{0,3},{1,2},{2,1},{3,0},{4,7},{5,6},{6,5},{7,4},{8,11},{9,10},{10,... | collective-permute-start | bytes 393224 | tf_op jit(solution)/shard_map/ppermute | solution.py:310
  76.3 7.4 %collective-permute-start.19 = (bf16[256,256]{1,0:T(8,128)(2,1)S(1)}, bf16[256,256]{1,0:T(8,128)(2,1)S(1)}, u32[]{:S(2)}, u32[]{:S(2)}) collective-permute-start(bf16[256,256]{1,0:T(8,128)(2,1)S(1)} %get-tuple-element.63), channel_id=1, source_target_pairs={{0,4},{4,0},{8,12},{12,8},{16,20},{20,16},{24,28},{28,24},{1,5},{5... | collective-permute-start | bytes 393224 | tf_op jit(solution)/shard_map/ppermute | solution.py:313
  76.4 1.4 %collective-permute-start.18 = (bf16[256,128]{1,0:T(8,128)(2,1)S(1)}, bf16[256,128]{1,0:T(8,128)(2,1)S(1)}, u32[]{:S(2)}, u32[]{:S(2)}) collective-permute-start(bf16[256,128]{1,0:T(8,128)(2,1)S(1)} %get-tuple-element.58), channel_id=1, source_target_pairs={{0,4},{4,0},{8,12},{12,8},{16,20},{20,16},{24,28},{28,24},{1,5},{5... | collective-permute-start | bytes 196616 | tf_op jit(solution)/shard_map/ppermute | solution.py:313
  (43 other events, 138.0 us)

commit v3 on v2

--- a/solution.py
+++ b/solution.py
@@ -77,22 +77,31 @@
     return jnp.broadcast_to(columns[length - 1 : length, block : block + 1], (1, HD))
 
 
-def chip_sum(chip, ref, later):
-    chips = ref.shape[0]
+def chip_sum(refs):
     summed = jnp.zeros((HD, HD), F32)
-    for number in reversed(range(chips)) if later else range(chips):
-        block = ref.at[number]
-        joined = jnp.exp(get_total(block, HD)) * summed + block[0:HD, :].astype(F32)
-        summed = jnp.where(number > chip if later else number < chip, joined, summed)
+    passed = jnp.zeros((1, HD), F32)
+    for ref in refs:
+        summed = summed + jnp.exp(passed) * ref[0:HD, :].astype(F32)
+        passed = passed + get_total(ref, HD)
     return summed
 
 
 def put_message(ref, state, total):
-    state = state.astype(BF16)
-    for number in range(ref.shape[0]):
-        block = ref.at[number]
-        block[0:HD, :] = state
-        put_total(block, HD, total)
+    ref[0:HD, :] = state.astype(BF16)
+    put_total(ref, HD, total)
+
+
+def join_kernel(own_ref, got_ref, out_ref):
+    total = get_total(own_ref, HD)
+    state = own_ref[0:HD, :].astype(F32) + jnp.exp(total) * got_ref[0:HD, :].astype(F32)
+    put_message(out_ref, state, total + get_total(got_ref, HD))
+
+
+def stitch_kernel(where_ref, mine_ref, theirs_ref, out_ref):
+    side = where_ref[1]
+    rows = mine_ref.shape[0]
+    out_ref[pl.ds(pl.multiple_of(side * rows, rows), rows), :] = mine_ref[...]
+    out_ref[pl.ds(pl.multiple_of((1 - side) * rows, rows), rows), :] = theirs_ref[...]
 
 
 def lanes_of(number):
@@ -143,11 +152,12 @@
     return lax.rsqrt(jnp.mean(mixed * mixed, axis=-1, keepdims=True) + EPSILON)
 
 
-def mixed_kernel(where_ref, q_ref, col_ref, inner_ref, gain_ref, first_ref, chips_ref, mixed_ref, keep_ref, send_ref, state_ref):
+def mixed_kernel(where_ref, q_ref, col_ref, inner_ref, gain_ref, first_ref, *refs):
+    chip_refs, (mixed_ref, keep_ref, send_ref, state_ref) = refs[:-4], refs[-4:]
     core = where_ref[0]
     columns = col_ref[...]
     gain = gain_ref[:, lanes_of(core)]
-    state = chip_sum(where_ref[1], chips_ref, False)
+    state = chip_sum(chip_refs)
     high, low = split(state)
     shrink = jnp.exp(total_of(columns, 0))
     state_ref[0] = state
@@ -172,18 +182,15 @@
         ref[:, lanes_of(1 - core)] = got_ref[:, part]
 
 
-def own_partial_kernel(where_ref, grad_ref, got_ref, weight_ref, out_ref):
-    core = where_ref[0]
-    weight = weight_ref[pl.ds(pl.multiple_of(core * HD, HD), HD), :]
-    out_ref[core] = dot(grad_ref[...], weight, NT)
-    out_ref[1 - core] = dot(got_ref[...], weight, NT)
-
-
-def partial_kernel(where_ref, grad_ref, got_ref, weight_ref, out_ref):
-    core = where_ref[0]
-    weight = weight_ref[...]
-    out_ref[core] = dot(grad_ref[...], weight, NT).astype(BF16)
-    out_ref[1 - core] = dot(got_ref[...], weight, NT).astype(BF16)
+def partial_kernel(where_ref, grad_ref, got_ref, *refs):
+    core = where_ref[0]
+    first_ref, second_ref, first_out, second_out = refs
+    first = first_ref[pl.ds(pl.multiple_of(core * HD, HD), HD), :] if first_ref.shape[0] > HD else first_ref[...]
+    weight = jnp.concatenate([first, second_ref[...]], axis=0)
+    for block, ref in ((core, grad_ref), (1 - core, got_ref)):
+        product = dot(ref[...], weight, NT)
+        first_out[block] = product[:, :HD].astype(first_out.dtype)
+        second_out[block] = product[:, HD:].astype(second_out.dtype)
 
 
 def grad_mixed_kernel(where_ref, q_ref, col_ref, gain_ref, mixed_ref, own_ref, *refs):
@@ -234,11 +241,12 @@
     send_ref[...] = jnp.where(core == 0, queries[1], queries[0]).astype(BF16)
 
 
-def outer_grad_kernel(where_ref, k_ref, v_ref, col_ref, dk_ref, dv_ref, chips_ref, keep_ref, send_ref):
+def outer_grad_kernel(where_ref, k_ref, v_ref, col_ref, dk_ref, dv_ref, *refs):
+    chip_refs, (keep_ref, send_ref) = refs[:-2], refs[-2:]
     core = where_ref[0]
     columns = col_ref[...]
     length = columns.shape[0]
-    high, low = split(chip_sum(where_ref[1], chips_ref, True))
+    high, low = split(chip_sum(chip_refs))
     keys, values = [], []
     for b in range(2):
         fade = jnp.exp(columns[length - 1 : length, b : b + 1] - columns[:, b : b + 1])
@@ -280,7 +288,7 @@
         out_shape=outs,
         in_specs=[SMEM] + [VMEM] * (len(args) - 1),
         out_specs=[VMEM] * len(outs),
-        compiler_params=pltpu.CompilerParams(vmem_limit_bytes=40 * 2**20),
+        compiler_params=pltpu.CompilerParams(vmem_limit_bytes=16 * 2**20),
         cost_estimate=pl.CostEstimate(flops=1, bytes_accessed=1, transcendentals=0),
     )(*args)
 
@@ -303,7 +311,8 @@
     width = model // tensor
     place = lax.axis_index("tensor")
     core = lax.rem(lax.axis_index("seq"), 2)
-    where = jnp.stack([core, lax.axis_index("seq") // 2]).astype(jnp.int32)
+    side = lax.rem(lax.axis_index("seq") // 2, 2)
+    where = jnp.stack([core, side]).astype(jnp.int32)
     gain = norm_gain.reshape(1, columns)
 
     def swap_tensor(value, k):
@@ -312,55 +321,90 @@
     def swap_core(value):
         return lax.ppermute(value, "seq", [(i, i ^ 1) for i in range(seq)])
 
-    def swap_chips(value):
-        groups = [[i for i in range(seq) if i % 2 == side] for side in range(2)]
-        return lax.all_to_all(value, "seq", 0, 0, axis_index_groups=groups)
+    def swap_side(value):
+        return lax.ppermute(value, "seq", [(i, i ^ 2) for i in range(seq)])
+
+    def to_chip(value, step):
+        return lax.ppermute(
+            value, "seq", [(i, i + 2 * step) for i in range(seq) if 0 <= i + 2 * step < seq]
+        )
+
+    def carry(own, sign):
+        messages = []
+        step = 1
+        while step < chips:
+            messages.append(to_chip(own, sign * step))
+            step *= 2
+            if step < chips:
+                (own,) = call(without_where(join_kernel), "join", [message], [where, own, messages[-1]])
+        return messages
 
     def shape(dtype, *dims):
         return jax.ShapeDtypeStruct(dims, dtype)
 
     others = range(1, tensor)
-    message = shape(BF16, chips, HD + TAIL, HD)
+    message = shape(BF16, HD + TAIL, HD)
     pair16 = shape(BF16, 2, length, HD)
     pair32 = shape(F32, 2, length, HD)
     one16 = shape(BF16, length, HD)
     both16 = shape(BF16, length, columns)
 
-    slices = [
-        lax.dynamic_slice(out_weight, (core * HD, (place ^ step) * width), (HD, width))
-        for step in others
-    ]
-    mine = [swap_tensor(piece, step) for piece, step in zip(slices, others)]
+    far = [step for step in others if step & (step - 1)]
+    near = [step for step in others if not step & (step - 1)]
+    order = far + near
+
+    def fetch(step, source):
+        rows = HD // 2 if step in far else HD
+        begin = core * HD + side * rows if step in far else core * HD
+        piece = lax.dynamic_slice(source, (begin, (place ^ step) * width), (rows, width))
+        return piece, swap_tensor(piece, step)
+
+    slices, arriving = [], []
+    for step in order:
+        (source,) = after([out_weight], *slices[-1:])
+        piece, coming = fetch(step, source)
+        slices.append(piece)
+        arriving.append(coming)
     got = [swap_core(rows) for rows in (queries, keys, values)]
     decay_got = swap_core(log_decay)
     (out_grad,) = after([out_grad], *slices)
     grad_got = swap_core(out_grad)
+    got = after(got, grad_got)
     q, k, v, col, row, first, fresh = call(
         fresh_kernel,
         "fresh",
         [pair16, pair16, pair16, shape(F32, length, 2), shape(F32, 2, length), shape(F32, HD, HD), message],
         [where, queries, keys, values, *got, log_decay, decay_got],
     )
-    arrived = swap_chips(fresh)
+    arrived = [to_chip(fresh, step) for step in range(1, chips)]
     (inner,) = call(without_where(inner_kernel), "inner", [pair32], [where, q, k, v, col, row, first])
     weight_own = lax.dynamic_slice(out_weight, (0, place * width), (columns, width))
-    (own_partial,) = call(own_partial_kernel, "own_partial", [pair32], [where, out_grad, grad_got, weight_own])
-    (arrived,) = after([arrived], inner, own_partial)
+    mine = []
+    for step, piece in zip(order, arriving):
+        if step in far:
+            (piece,) = call(stitch_kernel, "stitch", [shape(BF16, HD, width)], [where, piece, swap_side(piece)])
+        mine.append(piece)
     mixed, normed_keep, normed_send, states = call(
         mixed_kernel,
         "mixed",
         [pair32, one16, one16, shape(F32, 2, HD, HD)],
-        [where, q, col, inner, gain, first, arrived],
+        [where, q, col, inner, gain, first, *arrived],
     )
     normed_got = swap_core(normed_send)
     (normed,) = call(order_kernel, "order", [both16], [where, normed_keep, normed_got])
+    pieces = [weight_own, *mine]
     partials, theirs = [], []
-    for number, piece in enumerate(mine):
-        (piece,) = after([piece], mixed if number else arrived, *partials, *theirs[: max(number - 1, 0)])
-        theirs.append(swap_core(piece))
-        (partial,) = call(partial_kernel, "partial", [pair16], [where, out_grad, grad_got, piece])
-        partials.append(partial)
-    sent = [swap_tensor(partial, step) for partial, step in zip(partials, others)]
+    for number in range(0, tensor, 2):
+        pair = after(pieces[number : number + 2], mixed if number else arrived[-1], *partials)
+        theirs += [swap_core(piece) for piece in (pair if number else pair[1:])]
+        partials += call(
+            partial_kernel,
+            "partial",
+            [pair16 if number else pair32, pair16],
+            [where, out_grad, grad_got, *pair],
+        )
+    own_partial, *partials = partials
+    sent = [swap_tensor(partial, step) for partial, step in zip(partials, order)]
     sent = after(sent, *theirs)
     grad_mixed, second, upward = call(
         grad_mixed_kernel,
@@ -368,9 +412,9 @@
         [pair32, shape(F32, HD, HD), message],
         [where, q, col, gain, mixed, own_partial, *sent],
     )
-    returned = swap_chips(upward)
-    (normed,) = after([normed], grad_mixed)
-    normed_others = [swap_tensor(normed, step) for step in others]
+    returned = carry(upward, -1)
+    (normed,) = after([normed], *partials)
+    normed_others = [swap_tensor(normed, step) for step in order]
     dq_keep, dq_send, dk_inner, dv_inner = call(
         inner_grad_kernel,
         "inner_grad",
@@ -389,7 +433,7 @@
         outer_grad_kernel,
         "outer_grad",
         [both16, both16],
-        [where, k, v, col, dk_inner, dv_inner, returned],
+        [where, k, v, col, dk_inner, dv_inner, *returned],
     )
     got = swap_core(send)
     key_grad, value_grad = call(order_kernel, "order", [both16, both16], [where, keep, got])

time: 86 us -> 74.7 us (0.87)
  local copies, waits for them, and re-layouts: 31.3 us -> 8.41 us
  waiting for transfers between devices: 7.73 us -> 21.4 us
  Pallas kernels: 20.1 us -> 16.9 us
  starting transfers between devices: 24.8 us -> 26.6 us
    unnamed x90 -> x12, local copies, waits for them, and re-layouts: 27.7 us -> 3.41 us
    ppermute x0 -> x6, starting transfers between devices: none -> 12.5 us  [the longest x5 10.7 us: to_chip(): lax.ppermute(value, 'seq', [(i, i + 2 * step) for i in range(seq) if 0 <=...]
    ppermute x9, waiting for transfers between devices: 4.57 us -> 15.6 us  [swap_tensor(): return lax.ppermute(value, 'tensor', [(i, i ^ k) for i in range(tensor)])]
    all_to_all x2 -> x0, starting transfers between devices: 10.1 us -> none  [swap_chips(): return lax.all_to_all(value, 'seq', 0, 0, axis_index_groups=groups)]
    ppermute x0 -> x6, waiting for transfers between devices: none -> 4.49 us  [the longest x5 4.48 us: to_chip(): lax.ppermute(value, 'seq', [(i, i + 2 * step) for i in range(seq) if 0 <=...]
    pallas_call x14, Pallas kernels: 20.1 us -> 16.9 us  [call(): pl.pallas_call(kernel, name=name, out_shape=outs, in_specs=[SMEM] + [VMEM...]
    ppermute x11, waiting for transfers between devices: 3.16 us -> 1.31 us  [swap_core(): return lax.ppermute(value, 'seq', [(i, i ^ 1) for i in range(seq)])]
    dynamic_slice x1 -> x3, local copies, waits for them, and re-layouts: 2.38 us -> 3.81 us  [fetch(): lax.dynamic_slice(source, (begin, (place ^ step) * width), (rows, width))]
  transfers between devices with their start and end apart: 22 -> 26, of which waited for: 7 -> 6; matrix products, arithmetic and copies ran while one was open for 1% -> 2% of each run, Pallas kernels for 21% -> 19%
where the time goes in v3:
time: 74.7 us; the launch traced here: 74.3 us
  starting transfers between devices  26.6 us (36%)
  waiting for transfers between devices  21.4 us (29%)
  Pallas kernels  16.9 us (23%)
  local copies, waits for them, and re-layouts  8.41 us (11%)
  between operations  0.97 us (1%)
    pallas_call x14, Pallas kernels, call(): pl.pallas_call(kernel, name=name, out_shape=outs, in_specs=[SMEM] + [VMEM...  16.9 us
    ppermute x9, waiting for transfers between devices, swap_tensor(): return lax.ppermute(value, 'tensor', [(i, i ^ k) for i in range(tensor)])  15.6 us
    ppermute x9, starting transfers between devices, swap_tensor(): return lax.ppermute(value, 'tensor', [(i, i ^ k) for i in range(tensor)])  11.6 us
    ppermute x5, starting transfers between devices, to_chip(): lax.ppermute(value, 'seq', [(i, i + 2 * step) for i in range(seq) if 0 <=...  10.7 us
    ppermute x5, waiting for transfers between devices, to_chip(): lax.ppermute(value, 'seq', [(i, i + 2 * step) for i in range(seq) if 0 <=...  4.48 us
    dynamic_slice x3, local copies, waits for them, and re-layouts, fetch(): lax.dynamic_slice(source, (begin, (place ^ step) * width), (rows, width))  3.81 us
    unnamed x12, local copies, waits for them, and re-layouts  3.41 us
    ppermute x11, starting transfers between devices, swap_core(): return lax.ppermute(value, 'seq', [(i, i ^ 1) for i in range(seq)])  2.48 us
  transfers between devices with their start and end apart: 26, of which 6 were waited for; matrix products, arithmetic and copies ran while one was open for 2% of the time, Pallas kernels for 19%

profile of v3, /device:TPU:0, one launch (start us, length us, event | category | flops | bytes accessed | tf_op | source)
XLA Modules:
  0.0 74.3 jit_solution(5259554158066377994)
XLA Ops:
  2.8 1.8 %dynamic_slice.14 = bf16[128,1536]{1,0:T(8,128)(2,1)} dynamic-slice(bf16[256,6144]{1,0:T(8,128)(2,1)} %param.12, s32[]{:T(128)S(6)} %select_n.27, s32[]{:T(128)S(6)} %select_n.29), dynamic_slice_sizes={128,1536} | dynamic-slice | bytes 786436 | tf_op jit(solution)/shard_map/dynamic_slice | solution.py:359
  5.0 3.4 %collective-permute-start.9 = (bf16[64,1536]{1,0:T(8,128)(2,1)S(1)}, bf16[64,1536]{1,0:T(8,128)(2,1)S(1)}, u32[]{:S(2)}, u32[]{:S(2)}) collective-permute-start(bf16[64,1536]{1,0:T(8,128)(2,1)S(1)} %dynamic_slice.12), channel_id=1, source_target_pairs={{0,3},{1,2},{2,1},{3,0},{4,7},{5,6},{6,5},{7,4},{8,11},{9,10},{10,... | collective-permute-start | bytes 589832 | tf_op jit(solution)/shard_map/ppermute | solution.py:319
  9.2 4.8 %collective-permute-done.9.mine_ref = bf16[64,1536]{1,0:T(8,128)(2,1)S(1)} collective-permute-done((bf16[64,1536]{1,0:T(8,128)(2,1)S(1)}, bf16[64,1536]{1,0:T(8,128)(2,1)S(1)}, u32[]{:S(2)}, u32[]{:S(2)}) %collective-permute-start.9) | collective-permute-done | bytes 196640 | tf_op jit(solution)/shard_map/ppermute | solution.py:319
  14.0 1.8 %collective-permute-start.10 = (bf16[64,1536]{1,0:T(8,128)(2,1)S(1)}, bf16[64,1536]{1,0:T(8,128)(2,1)S(1)}, u32[]{:S(2)}, u32[]{:S(2)}) collective-permute-start(bf16[64,1536]{1,0:T(8,128)(2,1)S(1)} %collective-permute-done.9.mine_ref), channel_id=1, source_target_pairs={{0,8},{4,12},{8,0},{12,4},{16,24},{20,28},{24,16},{28,20},{1,9},{5... | collective-permute-start | bytes 589832 | tf_op jit(solution)/shard_map/ppermute | solution.py:325
  15.8 1.5 %collective-permute-start.12 = (bf16[128,1536]{1,0:T(8,128)(2,1)}, bf16[128,1536]{1,0:T(8,128)(2,1)S(1)}, u32[]{:S(2)}, u32[]{:S(2)}) collective-permute-start(bf16[128,1536]{1,0:T(8,128)(2,1)} %dynamic_slice.14), channel_id=1, source_target_pairs={{0,2},{1,3},{2,0},{3,1},{4,6},{5,7},{6,4},{7,5},{8,10},{9,11},{10,... | collective-permute-start | bytes 1179656 | tf_op jit(solution)/shard_map/ppermute | solution.py:319
  17.3 1.5 %collective-permute-start.11 = (bf16[128,1536]{1,0:T(8,128)(2,1)S(1)}, bf16[128,1536]{1,0:T(8,128)(2,1)S(1)}, u32[]{:S(2)}, u32[]{:S(2)}) collective-permute-start(bf16[128,1536]{1,0:T(8,128)(2,1)S(1)} %dynamic_slice.13), channel_id=1, source_target_pairs={{0,1},{1,0},{2,3},{3,2},{4,5},{5,4},{6,7},{7,6},{8,9},{9,8},{10,11... | collective-permute-start | bytes 1179656 | tf_op jit(solution)/shard_map/ppermute | solution.py:319
  18.9 1.3 %collective-permute-done.4.decay_got_ref = f32[2,256]{1,0:T(2,128)S(1)} collective-permute-done((f32[2,256]{1,0:T(2,128)}, f32[2,256]{1,0:T(2,128)S(1)}, u32[]{:S(2)}, u32[]{:S(2)}) %collective-permute-start.4) | collective-permute-done | bytes 2080 | tf_op jit(solution)/shard_map/ppermute | solution.py:322
  23.6 1.4 %fresh.1 = (bf16[2,256,128]{2,1,0:T(8,128)(2,1)S(1)}, bf16[2,256,128]{2,1,0:T(8,128)(2,1)S(1)}, bf16[2,256,128]{2,1,0:T(8,128)(2,1)S(1)}, f32[256,2]{1,0:T(8,128...) custom-call(s32[2]{0:T(128)S(1)} %pad_add_fusion.where_ref, ...), custom_call_target="tpu_custom_call" | custom-call | flops 1 | bytes 1 | tf_op jit(solution)/shard_map/fresh/pallas_call | solution.py:285
  25.0 4.4 %collective-permute-start.7 = (bf16[144,128]{1,0:T(8,128)(2,1)S(1)}, bf16[144,128]{1,0:T(8,128)(2,1)S(1)}, u32[]{:S(2)}, u32[]{:S(2)}) collective-permute-start(bf16[144,128]{1,0:T(8,128)(2,1)S(1)} %get-tuple-element.56), channel_id=1, source_target_pairs={{0,24},{4,28},{1,25},{5,29},{2,26},{6,30},{3,27},{7,31}} | collective-permute-start | bytes 110600 | tf_op jit(solution)/shard_map/ppermute | solution.py:328
  29.4 1.3 %collective-permute-start.5 = (bf16[144,128]{1,0:T(8,128)(2,1)S(1)}, bf16[144,128]{1,0:T(8,128)(2,1)S(1)}, u32[]{:S(2)}, u32[]{:S(2)}) collective-permute-start(bf16[144,128]{1,0:T(8,128)(2,1)S(1)} %get-tuple-element.56), channel_id=1, source_target_pairs={{0,8},{4,12},{8,16},{12,20},{16,24},{20,28},{1,9},{5,13},{9,17},{1... | collective-permute-start | bytes 110600 | tf_op jit(solution)/shard_map/ppermute | solution.py:328
  30.7 2.5 %collective-permute-start.6 = (bf16[144,128]{1,0:T(8,128)(2,1)S(1)}, bf16[144,128]{1,0:T(8,128)(2,1)S(1)}, u32[]{:S(2)}, u32[]{:S(2)}) collective-permute-start(bf16[144,128]{1,0:T(8,128)(2,1)S(1)} %get-tuple-element.56), channel_id=1, source_target_pairs={{0,16},{4,20},{8,24},{12,28},{1,17},{5,21},{9,25},{13,29},{2,18},{... | collective-permute-start | bytes 110600 | tf_op jit(solution)/shard_map/ppermute | solution.py:328
  33.2 1.2 %constant_dynamic-slice_fusion.refs_0_.weight_ref = bf16[256,1536]{1,0:T(8,128)(2,1)S(1)} fusion(bf16[256,6144]{1,0:T(8,128)(2,1)} %param.12, s32[]{:T(128)S(6)} %select_n.30), kind=kLoop, calls=%fused_computation.1 | loop fusion | bytes 1572868 | tf_op jit(solution)/shard_map/dynamic_slice | solution.py:381
  36.1 1.2 %partial.2 = (f32[2,256,128]{2,1,0:T(8,128)S(1)}, bf16[2,256,128]{2,1,0:T(8,128)(2,1)S(1)}) custom-call(s32[2]{0:T(128)S(1)} %pad_add_fusion.where_ref, bf16[256,1536]{1,0:T(8,128)(2,1)S(1)} %copy-done, bf16[256,1536]{1,0:T(8,128)(2,1)S(1)} %collective-permute-done.3.got_ref, bf16[256,1536]{1,0:T(8,128)(2,1)S(1)} %constant_dynamic-slice_fusion.refs_0_.weight_ref, ...), custom_call_target="tpu_custom_call" | custom-call | flops 1 | bytes 1 | tf_op jit(solution)/shard_map/partial/pallas_call | solution.py:285
  41.1 4.8 %collective-permute-done.20.refs_1_ = bf16[2,256,128]{2,1,0:T(8,128)(2,1)S(1)} collective-permute-done((bf16[2,256,128]{2,1,0:T(8,128)(2,1)S(1)}, bf16[2,256,128]{2,1,0:T(8,128)(2,1)S(1)}, u32[]{:S(2)}, u32[]{:S(2)}) %collective-permute-start.20) | collective-permute-done | bytes 131104 | tf_op jit(solution)/shard_map/ppermute | solution.py:319
  46.4 5.5 %collective-permute-done.19.refs_0_ = bf16[2,256,128]{2,1,0:T(8,128)(2,1)S(1)} collective-permute-done((bf16[2,256,128]{2,1,0:T(8,128)(2,1)S(1)}, bf16[2,256,128]{2,1,0:T(8,128)(2,1)S(1)}, u32[]{:S(2)}, u32[]{:S(2)}) %collective-permute-start.19) | collective-permute-done | bytes 131104 | tf_op jit(solution)/shard_map/ppermute | solution.py:319
  53.1 1.3 %collective-permute-start.23 = (bf16[144,128]{1,0:T(8,128)(2,1)S(1)}, bf16[144,128]{1,0:T(8,128)(2,1)S(1)}, u32[]{:S(2)}, u32[]{:S(2)}) collective-permute-start(bf16[144,128]{1,0:T(8,128)(2,1)S(1)} %get-tuple-element.79.refs_0_), channel_id=1, source_target_pairs={{8,0},{12,4},{16,8},{20,12},{24,16},{28,20},{9,1},{13,5},{17,9},{2... | collective-permute-start | bytes 110600 | tf_op jit(solution)/shard_map/ppermute | solution.py:328
  54.5 4.5 %collective-permute-done.23.refs_1_.refs_0_ = bf16[144,128]{1,0:T(8,128)(2,1)S(1)} collective-permute-done((bf16[144,128]{1,0:T(8,128)(2,1)S(1)}, bf16[144,128]{1,0:T(8,128)(2,1)S(1)}, u32[]{:S(2)}, u32[]{:S(2)}) %collective-permute-start.23) | collective-permute-done | bytes 36896 | tf_op jit(solution)/shard_map/ppermute | solution.py:328
  59.5 1.3 %collective-permute-start.24 = (bf16[144,128]{1,0:T(8,128)(2,1)S(1)}, bf16[144,128]{1,0:T(8,128)(2,1)S(1)}, u32[]{:S(2)}, u32[]{:S(2)}) collective-permute-start(bf16[144,128]{1,0:T(8,128)(2,1)S(1)} %join.1), channel_id=1, source_target_pairs={{16,0},{20,4},{24,8},{28,12},{17,1},{21,5},{25,9},{29,13},{18,2},{... | collective-permute-start | bytes 110600 | tf_op jit(solution)/shard_map/ppermute | solution.py:328
  61.9 1.5 %collective-permute-start.14 = (bf16[256,256]{1,0:T(8,128)(2,1)S(1)}, bf16[256,256]{1,0:T(8,128)(2,1)S(1)}, u32[]{:S(2)}, u32[]{:S(2)}) collective-permute-start(bf16[256,256]{1,0:T(8,128)(2,1)S(1)} %order.3.normed_ref), channel_id=1, source_target_pairs={{0,1},{1,0},{2,3},{3,2},{4,5},{5,4},{6,7},{7,6},{8,9},{9,8},{10,11... | collective-permute-start | bytes 393224 | tf_op jit(solution)/shard_map/ppermute | solution.py:319
  63.4 1.5 %collective-permute-start.15 = (bf16[256,256]{1,0:T(8,128)(2,1)S(1)}, bf16[256,256]{1,0:T(8,128)(2,1)S(1)}, u32[]{:S(2)}, u32[]{:S(2)}) collective-permute-start(bf16[256,256]{1,0:T(8,128)(2,1)S(1)} %order.3.normed_ref), channel_id=1, source_target_pairs={{0,2},{1,3},{2,0},{3,1},{4,6},{5,7},{6,4},{7,5},{8,10},{9,11},{10,... | collective-permute-start | bytes 393224 | tf_op jit(solution)/shard_map/ppermute | solution.py:319
  64.9 1.9 %inner_grad.1 = (bf16[256,128]{1,0:T(8,128)(2,1)S(1)}, bf16[256,128]{1,0:T(8,128)(2,1)S(1)}, f32[2,256,128]{2,1,0:T(8,128)S(1)}, f32[2,256,128]{2,1,0:T(8,128)S(1)}) custom-call(s32[2]{0:T(128)S(1)} %pad_add_fusion.where_ref, bf16[2,256,128]{2,1,0:T(8,128)(2,1)S(1)} %get-tuple-element.50.refs_0_.q_ref, ...), custom_call_target="tpu_custom_call" | custom-call | flops 1 | bytes 1 | tf_op jit(solution)/shard_map/inner_grad/pallas_call | solution.py:285
  68.7 3.1 %layer.1 = bf16[256,1536]{1,0:T(8,128)(2,1)} custom-call(s32[2]{0:T(128)S(1)} %pad_add_fusion.where_ref, bf16[256,256]{1,0:T(8,128)(2,1)S(1)} %order.3.normed_ref, bf16[256,1536]{1,0:T(8,128)(2,1)S(1)} %constant_dynamic-slice_fusion.refs_0_.weight_ref, bf16[256,256]{1,0:T(8,128)(2,1)S(1)} %collective-permute-done.13.refs_0_, ...), custom_call_target="tpu_custom_call" | custom-call | flops 1 | bytes 1 | tf_op jit(solution)/shard_map/layer/pallas_call | solution.py:285
  71.8 1.2 %order.4 = bf16[256,256]{1,0:T(8,128)(2,1)} custom-call(s32[2]{0:T(128)S(1)} %pad_add_fusion.where_ref, bf16[256,128]{1,0:T(8,128)(2,1)S(1)} %get-tuple-element.75.keep_ref, bf16[256,128]{1,0:T(8,128)(2,1)S(1)} %collective-permute-done.22.got_ref), custom_call_target="tpu_custom_call" | custom-call | flops 1 | bytes 1 | tf_op jit(solution)/shard_map/order/pallas_call | solution.py:285
  73.0 1.3 %order.5 = (bf16[256,256]{1,0:T(8,128)(2,1)}, bf16[256,256]{1,0:T(8,128)(2,1)}) custom-call(s32[2]{0:T(128)S(1)} %pad_add_fusion.where_ref, bf16[256,256]{1,0:T(8,128)(2,1)S(1)} %get-tuple-element.80.keep_ref, bf16[256,256]{1,0:T(8,128)(2,1)S(1)} %collective-permute-done.25.got_ref), custom_call_target="tpu_custom_call" | custom-call | flops 1 | bytes 1 | tf_op jit(solution)/shard_map/order/pallas_call | solution.py:285
  (59 shorter events, 17.5 us)
Async XLA Ops:
  4.5 14.3 %collective-permute-start.3 = (bf16[256,1536]{1,0:T(8,128)(2,1)}, bf16[256,1536]{1,0:T(8,128)(2,1)S(1)}, u32[]{:S(2)}, u32[]{:S(2)}) collective-permute-start(bf16[256,1536]{1,0:T(8,128)(2,1)} %grad_ref.1), channel_id=1, source_target_pairs={{0,4},{4,0},{8,12},{12,8},{16,20},{20,16},{24,28},{28,24},{1,5},{5... | collective-permute-start | bytes 2359304 | tf_op jit(solution)/shard_map/ppermute | solution.py:322
  5.0 9.0 %collective-permute-start.9 = (bf16[64,1536]{1,0:T(8,128)(2,1)S(1)}, bf16[64,1536]{1,0:T(8,128)(2,1)S(1)}, u32[]{:S(2)}, u32[]{:S(2)}) collective-permute-start(bf16[64,1536]{1,0:T(8,128)(2,1)S(1)} %dynamic_slice.12), channel_id=1, source_target_pairs={{0,3},{1,2},{2,1},{3,0},{4,7},{5,6},{6,5},{7,4},{8,11},{9,10},{10,... | collective-permute-start | bytes 589832 | tf_op jit(solution)/shard_map/ppermute | solution.py:319
  8.4 7.3 %collective-permute-start = (bf16[256,256]{1,0:T(8,128)(2,1)}, bf16[256,256]{1,0:T(8,128)(2,1)S(1)}, u32[]{:S(2)}, u32[]{:S(2)}) collective-permute-start(bf16[256,256]{1,0:T(8,128)(2,1)} %q_ref.1), channel_id=1, source_target_pairs={{0,4},{4,0},{8,12},{12,8},{16,20},{20,16},{24,28},{28,24},{1,5},{5... | collective-permute-start | bytes 393224 | tf_op jit(solution)/shard_map/ppermute | solution.py:322
  8.7 8.6 %collective-permute-start.1 = (bf16[256,256]{1,0:T(8,128)(2,1)}, bf16[256,256]{1,0:T(8,128)(2,1)S(1)}, u32[]{:S(2)}, u32[]{:S(2)}) collective-permute-start(bf16[256,256]{1,0:T(8,128)(2,1)} %k_ref.1), channel_id=1, source_target_pairs={{0,4},{4,0},{8,12},{12,8},{16,20},{20,16},{24,28},{28,24},{1,5},{5... | collective-permute-start | bytes 393224 | tf_op jit(solution)/shard_map/ppermute | solution.py:322
  8.9 9.9 %collective-permute-start.2 = (bf16[256,256]{1,0:T(8,128)(2,1)}, bf16[256,256]{1,0:T(8,128)(2,1)S(1)}, u32[]{:S(2)}, u32[]{:S(2)}) collective-permute-start(bf16[256,256]{1,0:T(8,128)(2,1)} %v_ref.1), channel_id=1, source_target_pairs={{0,4},{4,0},{8,12},{12,8},{16,20},{20,16},{24,28},{28,24},{1,5},{5... | collective-permute-start | bytes 393224 | tf_op jit(solution)/shard_map/ppermute | solution.py:322
  14.0 16.7 %collective-permute-start.10 = (bf16[64,1536]{1,0:T(8,128)(2,1)S(1)}, bf16[64,1536]{1,0:T(8,128)(2,1)S(1)}, u32[]{:S(2)}, u32[]{:S(2)}) collective-permute-start(bf16[64,1536]{1,0:T(8,128)(2,1)S(1)} %collective-permute-done.9.mine_ref), channel_id=1, source_target_pairs={{0,8},{4,12},{8,0},{12,4},{16,24},{20,28},{24,16},{28,20},{1,9},{5... | collective-permute-start | bytes 589832 | tf_op jit(solution)/shard_map/ppermute | solution.py:325
  15.8 22.4 %collective-permute-start.12 = (bf16[128,1536]{1,0:T(8,128)(2,1)}, bf16[128,1536]{1,0:T(8,128)(2,1)S(1)}, u32[]{:S(2)}, u32[]{:S(2)}) collective-permute-start(bf16[128,1536]{1,0:T(8,128)(2,1)} %dynamic_slice.14), channel_id=1, source_target_pairs={{0,2},{1,3},{2,0},{3,1},{4,6},{5,7},{6,4},{7,5},{8,10},{9,11},{10,... | collective-permute-start | bytes 1179656 | tf_op jit(solution)/shard_map/ppermute | solution.py:319
  17.3 20.9 %collective-permute-start.11 = (bf16[128,1536]{1,0:T(8,128)(2,1)S(1)}, bf16[128,1536]{1,0:T(8,128)(2,1)S(1)}, u32[]{:S(2)}, u32[]{:S(2)}) collective-permute-start(bf16[128,1536]{1,0:T(8,128)(2,1)S(1)} %dynamic_slice.13), channel_id=1, source_target_pairs={{0,1},{1,0},{2,3},{3,2},{4,5},{5,4},{6,7},{7,6},{8,9},{9,8},{10,11... | collective-permute-start | bytes 1179656 | tf_op jit(solution)/shard_map/ppermute | solution.py:319
  25.0 11.0 %collective-permute-start.7 = (bf16[144,128]{1,0:T(8,128)(2,1)S(1)}, bf16[144,128]{1,0:T(8,128)(2,1)S(1)}, u32[]{:S(2)}, u32[]{:S(2)}) collective-permute-start(bf16[144,128]{1,0:T(8,128)(2,1)S(1)} %get-tuple-element.56), channel_id=1, source_target_pairs={{0,24},{4,28},{1,25},{5,29},{2,26},{6,30},{3,27},{7,31}} | collective-permute-start | bytes 110600 | tf_op jit(solution)/shard_map/ppermute | solution.py:328
  29.4 7.8 %collective-permute-start.5 = (bf16[144,128]{1,0:T(8,128)(2,1)S(1)}, bf16[144,128]{1,0:T(8,128)(2,1)S(1)}, u32[]{:S(2)}, u32[]{:S(2)}) collective-permute-start(bf16[144,128]{1,0:T(8,128)(2,1)S(1)} %get-tuple-element.56), channel_id=1, source_target_pairs={{0,8},{4,12},{8,16},{12,20},{16,24},{20,28},{1,9},{5,13},{9,17},{1... | collective-permute-start | bytes 110600 | tf_op jit(solution)/shard_map/ppermute | solution.py:328
  30.7 6.5 %collective-permute-start.6 = (bf16[144,128]{1,0:T(8,128)(2,1)S(1)}, bf16[144,128]{1,0:T(8,128)(2,1)S(1)}, u32[]{:S(2)}, u32[]{:S(2)}) collective-permute-start(bf16[144,128]{1,0:T(8,128)(2,1)S(1)} %get-tuple-element.56), channel_id=1, source_target_pairs={{0,16},{4,20},{8,24},{12,28},{1,17},{5,21},{9,25},{13,29},{2,18},{... | collective-permute-start | bytes 110600 | tf_op jit(solution)/shard_map/ppermute | solution.py:328
  38.2 13.7 %collective-permute-start.17 = (bf16[128,1536]{1,0:T(8,128)(2,1)S(1)}, bf16[128,1536]{1,0:T(8,128)(2,1)S(1)}, u32[]{:S(2)}, u32[]{:S(2)}) collective-permute-start(bf16[128,1536]{1,0:T(8,128)(2,1)S(1)} %collective-permute-done.11.refs_0_.refs_4_), channel_id=1, source_target_pairs={{0,4},{4,0},{8,12},{12,8},{16,20},{20,16},{24,28},{28,24},{1,5},{5... | collective-permute-start | bytes 1179656 | tf_op jit(solution)/shard_map/ppermute | solution.py:322
  38.3 13.6 %collective-permute-start.18 = (bf16[128,1536]{1,0:T(8,128)(2,1)S(1)}, bf16[128,1536]{1,0:T(8,128)(2,1)S(1)}, u32[]{:S(2)}, u32[]{:S(2)}) collective-permute-start(bf16[128,1536]{1,0:T(8,128)(2,1)S(1)} %collective-permute-done.12.refs_1_.refs_5_), channel_id=1, source_target_pairs={{0,4},{4,0},{8,12},{12,8},{16,20},{20,16},{24,28},{28,24},{1,5},{5... | collective-permute-start | bytes 1179656 | tf_op jit(solution)/shard_map/ppermute | solution.py:322
  38.8 13.1 %collective-permute-start.16 = (bf16[128,1536]{1,0:T(8,128)(2,1)S(1)}, bf16[128,1536]{1,0:T(8,128)(2,1)S(1)}, u32[]{:S(2)}, u32[]{:S(2)}) collective-permute-start(bf16[128,1536]{1,0:T(8,128)(2,1)S(1)} %stitch.1.refs_1_.refs_3_), channel_id=1, source_target_pairs={{0,4},{4,0},{8,12},{12,8},{16,20},{20,16},{24,28},{28,24},{1,5},{5... | collective-permute-start | bytes 1179656 | tf_op jit(solution)/shard_map/ppermute | solution.py:322
  40.0 5.9 %collective-permute-start.20 = (bf16[2,256,128]{2,1,0:T(8,128)(2,1)S(1)}, bf16[2,256,128]{2,1,0:T(8,128)(2,1)S(1)}, u32[]{:S(2)}, u32[]{:S(2)}) collective-permute-start(bf16[2,256,128]{2,1,0:T(8,128)(2,1)S(1)} %get-tuple-element.66), channel_id=1, source_target_pairs={{0,1},{1,0},{2,3},{3,2},{4,5},{5,4},{6,7},{7,6},{8,9},{9,8},{10,11... | collective-permute-start | bytes 393224 | tf_op jit(solution)/shard_map/ppermute | solution.py:319
  40.6 5.8 %collective-permute-start.21 = (bf16[2,256,128]{2,1,0:T(8,128)(2,1)S(1)}, bf16[2,256,128]{2,1,0:T(8,128)(2,1)S(1)}, u32[]{:S(2)}, u32[]{:S(2)}) collective-permute-start(bf16[2,256,128]{2,1,0:T(8,128)(2,1)S(1)} %get-tuple-element.67), channel_id=1, source_target_pairs={{0,2},{1,3},{2,0},{3,1},{4,6},{5,7},{6,4},{7,5},{8,10},{9,11},{10,... | collective-permute-start | bytes 393224 | tf_op jit(solution)/shard_map/ppermute | solution.py:319
  45.9 6.0 %collective-permute-start.19 = (bf16[2,256,128]{2,1,0:T(8,128)(2,1)S(1)}, bf16[2,256,128]{2,1,0:T(8,128)(2,1)S(1)}, u32[]{:S(2)}, u32[]{:S(2)}) collective-permute-start(bf16[2,256,128]{2,1,0:T(8,128)(2,1)S(1)} %get-tuple-element.61), channel_id=1, source_target_pairs={{0,3},{1,2},{2,1},{3,0},{4,7},{5,6},{6,5},{7,4},{8,11},{9,10},{10,... | collective-permute-start | bytes 393224 | tf_op jit(solution)/shard_map/ppermute | solution.py:319
  53.1 5.9 %collective-permute-start.23 = (bf16[144,128]{1,0:T(8,128)(2,1)S(1)}, bf16[144,128]{1,0:T(8,128)(2,1)S(1)}, u32[]{:S(2)}, u32[]{:S(2)}) collective-permute-start(bf16[144,128]{1,0:T(8,128)(2,1)S(1)} %get-tuple-element.79.refs_0_), channel_id=1, source_target_pairs={{8,0},{12,4},{16,8},{20,12},{24,16},{28,20},{9,1},{13,5},{17,9},{2... | collective-permute-start | bytes 110600 | tf_op jit(solution)/shard_map/ppermute | solution.py:328
  54.4 6.4 %collective-permute-start.8 = (bf16[256,128]{1,0:T(8,128)(2,1)S(1)}, bf16[256,128]{1,0:T(8,128)(2,1)S(1)}, u32[]{:S(2)}, u32[]{:S(2)}) collective-permute-start(bf16[256,128]{1,0:T(8,128)(2,1)S(1)} %get-tuple-element.58), channel_id=1, source_target_pairs={{0,4},{4,0},{8,12},{12,8},{16,20},{20,16},{24,28},{28,24},{1,5},{5... | collective-permute-start | bytes 196616 | tf_op jit(solution)/shard_map/ppermute | solution.py:322
  59.5 7.3 %collective-permute-start.24 = (bf16[144,128]{1,0:T(8,128)(2,1)S(1)}, bf16[144,128]{1,0:T(8,128)(2,1)S(1)}, u32[]{:S(2)}, u32[]{:S(2)}) collective-permute-start(bf16[144,128]{1,0:T(8,128)(2,1)S(1)} %join.1), channel_id=1, source_target_pairs={{16,0},{20,4},{24,8},{28,12},{17,1},{21,5},{25,9},{29,13},{18,2},{... | collective-permute-start | bytes 110600 | tf_op jit(solution)/shard_map/ppermute | solution.py:328
  61.4 6.9 %collective-permute-start.13 = (bf16[256,256]{1,0:T(8,128)(2,1)S(1)}, bf16[256,256]{1,0:T(8,128)(2,1)S(1)}, u32[]{:S(2)}, u32[]{:S(2)}) collective-permute-start(bf16[256,256]{1,0:T(8,128)(2,1)S(1)} %order.3.normed_ref), channel_id=1, source_target_pairs={{0,3},{1,2},{2,1},{3,0},{4,7},{5,6},{6,5},{7,4},{8,11},{9,10},{10,... | collective-permute-start | bytes 393224 | tf_op jit(solution)/shard_map/ppermute | solution.py:319
  61.9 6.4 %collective-permute-start.14 = (bf16[256,256]{1,0:T(8,128)(2,1)S(1)}, bf16[256,256]{1,0:T(8,128)(2,1)S(1)}, u32[]{:S(2)}, u32[]{:S(2)}) collective-permute-start(bf16[256,256]{1,0:T(8,128)(2,1)S(1)} %order.3.normed_ref), channel_id=1, source_target_pairs={{0,1},{1,0},{2,3},{3,2},{4,5},{5,4},{6,7},{7,6},{8,9},{9,8},{10,11... | collective-permute-start | bytes 393224 | tf_op jit(solution)/shard_map/ppermute | solution.py:319
  63.4 5.3 %collective-permute-start.15 = (bf16[256,256]{1,0:T(8,128)(2,1)S(1)}, bf16[256,256]{1,0:T(8,128)(2,1)S(1)}, u32[]{:S(2)}, u32[]{:S(2)}) collective-permute-start(bf16[256,256]{1,0:T(8,128)(2,1)S(1)} %order.3.normed_ref), channel_id=1, source_target_pairs={{0,2},{1,3},{2,0},{3,1},{4,6},{5,7},{6,4},{7,5},{8,10},{9,11},{10,... | collective-permute-start | bytes 393224 | tf_op jit(solution)/shard_map/ppermute | solution.py:319
  67.7 5.3 %collective-permute-start.25 = (bf16[256,256]{1,0:T(8,128)(2,1)S(1)}, bf16[256,256]{1,0:T(8,128)(2,1)S(1)}, u32[]{:S(2)}, u32[]{:S(2)}) collective-permute-start(bf16[256,256]{1,0:T(8,128)(2,1)S(1)} %get-tuple-element.81), channel_id=1, source_target_pairs={{0,4},{4,0},{8,12},{12,8},{16,20},{20,16},{24,28},{28,24},{1,5},{5... | collective-permute-start | bytes 393224 | tf_op jit(solution)/shard_map/ppermute | solution.py:322
  (8 other events, 56.5 us)

commit v4 on v3

v4 whole, which is shorter than its diff:
```python
import functools

import jax
import jax.numpy as jnp
from jax import lax
from jax.experimental import pallas as pl
from jax.experimental.pallas import tpu as pltpu
from jax.sharding import PartitionSpec as P

EXACT = lax.Precision.HIGHEST
EPSILON = 1e-05
F32 = jnp.float32
BF16 = jnp.bfloat16
TAIL = 16
HD = 128

NN = (((1,), (0,)), ((), ()))
NT = (((1,), (1,)), ((), ()))
TN = (((0,), (0,)), ((), ()))


def dot(a, b, dims):
    return lax.dot_general(a, b, dims, preferred_element_type=F32)


def split(x):
    high = x.astype(BF16)
    return high, (x - high.astype(F32)).astype(BF16)


def dot_fb(a, b, dims):
    high, low = split(a)
    return dot(high, b, dims) + dot(low, b, dims)


def dot_bf(a, b, dims):
    high, low = split(b)
    return dot(a, high, dims) + dot(a, low, dims)


def dot_ff(a, b, dims):
    ah, al = split(a)
    bh, bl = split(b)
    return dot(ah, bh, dims) + (dot(ah, bl, dims) + dot(al, bh, dims))


def triangle(length):
    rows = lax.broadcasted_iota(jnp.int32, (length, length), 0)
    cols = lax.broadcasted_iota(jnp.int32, (length, length), 1)
    return rows >= cols


def running_columns(decay, lower):
    return lax.dot_general(lower.astype(F32), decay, NT, precision=EXACT, preferred_element_type=F32)


def running_rows(decay, lower):
    return lax.dot_general(decay, lower.astype(F32), NT, precision=EXACT, preferred_element_type=F32)


def put_total(ref, base, total):
    first = total.astype(BF16).astype(F32)
    second = (total - first).astype(BF16).astype(F32)
    third = total - first - second
    at = lax.broadcasted_iota(jnp.int32, (TAIL, 128), 0)
    tail = jnp.where(at == 0, first, jnp.where(at == 1, second, jnp.where(at == 2, third, 0.0)))
    ref[base : base + TAIL, :] = tail.astype(BF16)


def get_total(ref, base):
    tail = ref[base : base + TAIL, :].astype(F32)
    return tail[0:1] + tail[1:2] + tail[2:3]


def total_of(columns, block):
    length = columns.shape[0]
    return jnp.broadcast_to(columns[length - 1 : length, block : block + 1], (1, HD))


def chip_sum(refs):
    summed = jnp.zeros((HD, HD), F32)
    passed = jnp.zeros((1, HD), F32)
    for ref in refs:
        summed = summed + jnp.exp(passed) * ref[0:HD, :].astype(F32)
        passed = passed + get_total(ref, HD)
    return summed


def put_message(ref, state, total):
    ref[0:HD, :] = state.astype(BF16)
    put_total(ref, HD, total)


def lanes_of(number):
    return pl.ds(pl.multiple_of(number * HD, HD), HD)


def rows_of(number, count):
    return pl.ds(pl.multiple_of(number * count, count), count)


def stage_kernel(plan, where_ref, decay_source, weight_ref, q_ref, k_ref, v_ref, *refs):
    *piece_refs, own_ref, send_ref, keep_ref, decay_ref, tail_ref, sems = refs
    core, side, place = where_ref[0], where_ref[1], where_ref[2]
    width = own_ref.shape[1]
    length = keep_ref.shape[0]
    copies = []

    def start(source, target):
        copies.append(pltpu.make_async_copy(source, target, sems.at[len(copies)]))
        copies[-1].start()

    start(decay_source, decay_ref)
    for (step, halves), ref in zip(plan, piece_refs):
        rows = rows_of(core * 2 + side if halves else core, ref.shape[0])
        start(weight_ref.at[rows, rows_of(place ^ step, width)], ref)
    for number, source in enumerate((q_ref, k_ref, v_ref)):
        part = slice(number * HD, (number + 1) * HD)
        start(source.at[:, lanes_of(1 - core)], send_ref.at[0:length, part])
        start(source.at[:, lanes_of(core)], keep_ref.at[:, part])
    start(weight_ref.at[:, rows_of(place, width)], own_ref)
    copies[0].wait()
    decay = jnp.where(core == 0, decay_ref[1:2, :], decay_ref[0:1, :])
    first = decay.astype(BF16).astype(F32)
    second = (decay - first).astype(BF16).astype(F32)
    third = decay - first - second
    at = lax.broadcasted_iota(jnp.int32, (TAIL, length), 0)
    tail = jnp.where(at == 0, first, jnp.where(at == 1, second, jnp.where(at == 2, third, 0.0)))
    tail_ref[...] = jnp.zeros(tail_ref.shape, BF16)
    tail_ref[:, 0:length] = tail.astype(BF16)
    start(tail_ref, send_ref.at[length : length + TAIL, :])
    for copy in copies[1:]:
        copy.wait()


def fresh_kernel(where_ref, keep_ref, got_ref, decay_ref, q_out, k_out, v_out, col_ref, row_ref, first_ref, message_ref):
    core = where_ref[0]
    length = keep_ref.shape[0]
    for number, out in enumerate((q_out, k_out, v_out)):
        part = slice(number * HD, (number + 1) * HD)
        out[core] = keep_ref[:, part]
        out[1 - core] = got_ref[0:length, part]
    mine = jnp.where(core == 0, decay_ref[0:1, :], decay_ref[1:2, :])
    tail = got_ref[length : length + TAIL, 0:length].astype(F32)
    theirs = tail[0:1] + tail[1:2] + tail[2:3]
    block = lax.broadcasted_iota(jnp.int32, (2, length), 0)
    decay = jnp.where(block == core, mine, theirs)
    lower = triangle(length)
    columns = running_columns(decay, lower)
    col_ref[...] = columns
    row_ref[...] = running_rows(decay, lower)
    states = []
    for b in range(2):
        fade = jnp.exp(columns[length - 1 : length, b : b + 1] - columns[:, b : b + 1])
        states.append(dot_bf(k_out[b], fade * v_out[b].astype(F32), TN))
    totals = [total_of(columns, b) for b in range(2)]
    first_ref[...] = states[0]
    put_message(message_ref, jnp.exp(totals[1]) * states[0] + states[1], totals[0] + totals[1])


def weights(columns, across, lower, b):
    return jnp.exp(jnp.where(lower, columns[:, b : b + 1] - across[b : b + 1, :], -1e30))


def inner_kernel(q_ref, k_ref, v_ref, col_ref, row_ref, first_ref, inner_ref):
    columns, across = col_ref[...], row_ref[...]
    lower = triangle(columns.shape[0])
    for b in range(2):
        scores = dot(q_ref[b], k_ref[b], NT) * weights(columns, across, lower, b)
        inner = dot_fb(scores, v_ref[b], NN)
        if b == 1:
            inner = inner + jnp.exp(columns[:, 1:2]) * dot_bf(q_ref[b], first_ref[...], NN)
        inner_ref[b] = inner


def scale_of(mixed):
    return lax.rsqrt(jnp.mean(mixed * mixed, axis=-1, keepdims=True) + EPSILON)


def mixed_kernel(where_ref, q_ref, col_ref, inner_ref, gain_ref, first_ref, *refs):
    chip_refs, (mixed_ref, normed_ref, state_ref) = refs[:-3], refs[-3:]
    core = where_ref[0]
    columns = col_ref[...]
    gain = gain_ref[:, lanes_of(core)]
    state = chip_sum(chip_refs)
    high, low = split(state)
    shrink = jnp.exp(total_of(columns, 0))
    state_ref[0] = state
    state_ref[1] = shrink * state + first_ref[...]
    for b in range(2):
        grow = jnp.exp(columns[:, b : b + 1])
        if b == 1:
            grow = grow * shrink
        mixed = inner_ref[b] + grow * (dot(q_ref[b], high, NN) + dot(q_ref[b], low, NN))
        mixed_ref[b] = mixed
        normed_ref[b] = (mixed * scale_of(mixed) * gain).astype(BF16)


def partial_kernel(kinds, where_ref, grad_ref, got_ref, *refs):
    core, side = where_ref[0], where_ref[1]
    refs = list(refs)
    inputs = [[refs.pop(0) for _ in range(2 if kind == "halves" else 1)] for kind in kinds]
    products = [refs.pop(0), refs.pop(0)]
    weights = []
    for kind, sources in zip(kinds, inputs):
        if kind == "own":
            weights.append(sources[0][rows_of(core, HD), :])
        elif kind == "halves":
            mine, theirs = sources[0][...], sources[1][...]
            weight = jnp.concatenate([jnp.where(side == 0, mine, theirs), jnp.where(side == 0, theirs, mine)], axis=0)
            refs.pop(0)[...] = weight
            weights.append(weight)
        else:
            weights.append(sources[0][...])
    weight = jnp.concatenate(weights, axis=0)
    for block, ref in ((core, grad_ref), (1 - core, got_ref)):
        product = dot(ref[...], weight, NT)
        for number, out in enumerate(products):
            out[block] = product[:, number * HD : (number + 1) * HD].astype(out.dtype)


def grad_mixed_kernel(where_ref, q_ref, col_ref, gain_ref, mixed_ref, own_ref, *refs):
    part_refs, (grad_ref, second_ref, message_ref) = refs[:-3], refs[-3:]
    columns = col_ref[...]
    gain = gain_ref[:, lanes_of(where_ref[0])]
    ups = []
    for b in range(2):
        normed = own_ref[b]
        for ref in part_refs:
            normed = normed + ref[b].astype(F32)
        lifted = normed * gain
        mixed = mixed_ref[b]
        scale = scale_of(mixed)
        unit = mixed * scale
        grad = scale * (lifted - unit * jnp.mean(unit * lifted, axis=-1, keepdims=True))
        grad_ref[b] = grad
        ups.append(dot_bf(q_ref[b], jnp.exp(columns[:, b : b + 1]) * grad, TN))
    second_ref[...] = ups[1]
    totals = [total_of(columns, b) for b in range(2)]
    put_message(message_ref, ups[0] + jnp.exp(totals[0]) * ups[1], totals[0] + totals[1])


def inner_grad_kernel(
    where_ref, q_ref, k_ref, v_ref, col_ref, row_ref, grad_ref, state_ref, second_ref, keep_ref, send_ref
):
    core = where_ref[0]
    columns, across = col_ref[...], row_ref[...]
    length = columns.shape[0]
    lower = triangle(length)
    parts = []
    for b in range(2):
        q, k, v, grad = q_ref[b], k_ref[b], v_ref[b], grad_ref[b]
        weight = weights(columns, across, lower, b)
        scores = dot(q, k, NT) * weight
        grad_scores = dot_fb(grad, v, NT) * weight
        carried = jnp.exp(columns[:, b : b + 1]) * dot_ff(grad, state_ref[b], NT)
        dq = dot_fb(grad_scores, k, NN) + carried
        dk = dot_fb(grad_scores, q, TN)
        dv = dot_ff(scores, grad, TN)
        if b == 0:
            fade = jnp.exp(columns[length - 1 : length, 0:1] - columns[:, 0:1])
            dk = dk + fade * dot_bf(v, second_ref[...], NT)
            dv = dv + fade * dot_bf(k, second_ref[...], NN)
        parts.append((dq, dk, dv))
    for number, (early, late) in enumerate(zip(*parts)):
        part = slice(number * HD, (number + 1) * HD)
        keep_ref[:, part] = jnp.where(core == 0, early, late)
        send_ref[:, part] = jnp.where(core == 0, late, early)


def outer_grad_kernel(count, where_ref, keep_ref, send_ref, col_ref, col_got_ref, inner_ref, inner_got_ref, *refs):
    core = where_ref[0]
    length = keep_ref.shape[0]
    outs = refs[2 * count :]
    for head, rows, cols, inner, chip_refs in (
        (core, keep_ref, col_ref, inner_ref, refs[:count]),
        (1 - core, send_ref, col_got_ref, inner_got_ref, refs[count : 2 * count]),
    ):
        columns = cols[...]
        high, low = split(chip_sum(chip_refs))
        end = columns[length - 1 : length, :]
        block = jnp.where(core == 0, columns[:, 0:1], columns[:, 1:2])
        fade = jnp.exp(jnp.where(core == 0, end[:, 0:1] + end[:, 1:2], end[:, 1:2]) - block)
        k, v = rows[0:length, HD : 2 * HD], rows[0:length, 2 * HD : 3 * HD]
        outs[0][:, lanes_of(head)] = inner[:, 0:HD].astype(BF16)
        key = inner[:, HD : 2 * HD] + fade * (dot(v, high, NT) + dot(v, low, NT))
        outs[1][:, lanes_of(head)] = key.astype(BF16)
        value = inner[:, 2 * HD : 3 * HD] + fade * (dot(k, high, NN) + dot(k, low, NN))
        outs[2][:, lanes_of(head)] = value.astype(BF16)


def layer_kernel(others, where_ref, weight_ref, *refs):
    groups = [refs[number * others : (number + 1) * others] for number in range(2)]
    mine_refs, theirs_refs = groups
    normed_refs = refs[2 * others : 3 * others + 1]
    got_refs = refs[3 * others + 1 : 4 * others + 2]
    out_ref = refs[4 * others + 2]
    core = where_ref[0]
    normed = []
    for mine, theirs in zip(normed_refs, got_refs):
        normed += [mine[core], theirs[core]]
    normed = jnp.concatenate(normed, axis=1)
    width = weight_ref.shape[1]
    step = 512 if width % 512 == 0 else 128
    for begin in range(0, width, step):
        lanes = slice(begin, begin + step)
        weight = [weight_ref[rows_of(core, HD), lanes], weight_ref[rows_of(1 - core, HD), lanes]]
        for mine, theirs in zip(mine_refs, theirs_refs):
            weight += [mine[:, lanes], theirs[:, lanes]]
        out_ref[:, lanes] = dot(normed, jnp.concatenate(weight, axis=0), NN).astype(BF16)


SMEM = pl.BlockSpec(memory_space=pltpu.SMEM)
VMEM = pl.BlockSpec(memory_space=pltpu.VMEM)
HBM = pl.BlockSpec(memory_space=pltpu.HBM)


def call(kernel, name, outs, args, direct=(), copies=0, grant=16, scratch=(), landing=None):
    return pl.pallas_call(
        kernel,
        name=name,
        out_shape=outs,
        in_specs=[SMEM] + [HBM if number in direct else VMEM for number in range(1, len(args))],
        out_specs=[landing or VMEM] * len(outs),
        scratch_shapes=[*scratch] + ([pltpu.SemaphoreType.DMA((copies,))] if copies else []),
        compiler_params=pltpu.CompilerParams(vmem_limit_bytes=grant * 2**20),
        cost_estimate=pl.CostEstimate(flops=1, bytes_accessed=1, transcendentals=0),
    )(*args)


def without_where(kernel):
    return lambda where_ref, *refs: kernel(*refs)


def after(values, *earlier):
    tied = lax.optimization_barrier((tuple(values), earlier))
    return list(tied[0])


def on_device(queries, keys, values, log_decay, norm_gain, out_weight, out_grad):
    length, columns = queries.shape
    seq = lax.axis_size("seq")
    tensor = lax.axis_size("tensor")
    chips = seq // 2
    model = out_weight.shape[1]
    width = model // tensor
    place = lax.axis_index("tensor")
    core = lax.rem(lax.axis_index("seq"), 2)
    side = lax.rem(lax.axis_index("seq") // 2, 2)
    where = jnp.stack([core, side, place]).astype(jnp.int32)
    gain = norm_gain.reshape(1, columns)

    def swap_tensor(value, k):
        return lax.ppermute(value, "tensor", [(i, i ^ k) for i in range(tensor)])

    def swap_core(value):
        return lax.ppermute(value, "seq", [(i, i ^ 1) for i in range(seq)])

    def swap_side(value):
        return lax.ppermute(value, "seq", [(i, i ^ 2) for i in range(seq)])

    def to_chip(value, step):
        return lax.ppermute(
            value, "seq", [(i, i + 2 * step) for i in range(seq) if 0 <= i + 2 * step < seq]
        )

    def shape(dtype, *dims):
        return jax.ShapeDtypeStruct(dims, dtype)

    others = range(1, tensor)
    message = shape(BF16, HD + TAIL, HD)
    pair16 = shape(BF16, 2, length, HD)
    pair32 = shape(F32, 2, length, HD)
    one16 = shape(BF16, length, HD)
    both16 = shape(BF16, length, columns)

    far = [step for step in others if step & (step - 1)]
    near = [step for step in others if not step & (step - 1)]
    order = far + near
    plan = [(step, step in far) for step in order]
    *slices, weight_own, send, keep = call(
        functools.partial(stage_kernel, plan),
        "stage",
        [shape(BF16, HD // 2 if halves else HD, width) for _, halves in plan]
        + [shape(BF16, columns, width), shape(BF16, length + TAIL, 3 * HD), shape(BF16, length, 3 * HD)],
        [where, log_decay, out_weight, queries, keys, values],
        direct=(1, 2, 3, 4, 5),
        copies=len(plan) + 9,
        grant=60,
        scratch=[pltpu.VMEM(log_decay.shape, F32), pltpu.VMEM((TAIL, 3 * HD), BF16)],
        landing=HBM,
    )
    arriving = [swap_tensor(piece, step) for piece, step in zip(slices, order)]
    got = swap_core(send)
    (out_grad,) = after([out_grad], send)
    grad_got = swap_core(out_grad)
    (got,) = after([got], grad_got)
    q, k, v, col, row, first, fresh = call(
        fresh_kernel,
        "fresh",
        [pair16, pair16, pair16, shape(F32, length, 2), shape(F32, 2, length), shape(F32, HD, HD), message],
        [where, keep, got, log_decay],
    )
    arrived = [to_chip(fresh, step) for step in range(1, chips)]
    col_got = swap_core(col)
    (inner,) = call(without_where(inner_kernel), "inner", [pair32], [where, q, k, v, col, row, first])
    mixed, normed, states = call(
        mixed_kernel,
        "mixed",
        [pair32, pair16, shape(F32, 2, HD, HD)],
        [where, q, col, inner, gain, first, *arrived],
    )
    normed_mine = swap_core(normed)
    pieces = [("own", [weight_own])]
    for (step, halves), piece in zip(plan, arriving):
        pieces.append(("halves", [piece, swap_side(piece)]) if halves else ("whole", [piece]))
    partials, mine = [], []
    for number in range(0, tensor, 2):
        kinds, sources = zip(*pieces[number : number + 2])
        sources = sum(sources, [])
        sources = after(sources, normed_mine if number else arrived[-1], col_got, *partials)
        stitched = [shape(BF16, HD, width)] * kinds.count("halves")
        outs = call(
            functools.partial(partial_kernel, kinds),
            "partial",
            [pair16 if number else pair32, pair16, *stitched],
            [where, out_grad, grad_got, *sources],
        )
        partials += outs[:2]
        stitched = list(outs[2:])
        for kind in kinds:
            if kind == "halves":
                mine.append(stitched.pop(0))
                sources = sources[2:]
            else:
                mine.append(sources[0])
                sources = sources[1:]
    mine = mine[1:]
    own_partial, *partials = partials
    sent = [swap_tensor(partial, step) for partial, step in zip(partials, order)]
    (normed_sent,) = after([normed], *partials)
    normed_all = [normed] + [swap_tensor(normed_sent, step) for step in order]
    grad_mixed, second, upward = call(
        grad_mixed_kernel,
        "grad_mixed",
        [pair32, shape(F32, HD, HD), message],
        [where, q, col, gain, mixed, own_partial, *sent],
    )
    returned = [to_chip(upward, -step) for step in range(1, chips)]
    inner_keep, inner_send = call(
        inner_grad_kernel,
        "inner_grad",
        [shape(F32, length, 3 * HD)] * 2,
        [where, q, k, v, col, row, grad_mixed, states, second],
    )
    inner_got = swap_core(inner_send)
    theirs = [swap_core(piece) for piece in after(mine, grad_mixed)]
    normed_got = [normed_mine] + [swap_core(rows) for rows in normed_all[1:]]
    (layer_out,) = call(
        functools.partial(layer_kernel, tensor - 1),
        "layer",
        [shape(BF16, length, width)],
        [where, weight_own, *mine, *theirs, *normed_all, *normed_got],
    )
    returned_got = after([swap_core(rows) for rows in returned], layer_out)
    query_grad, key_grad, value_grad = call(
        functools.partial(outer_grad_kernel, chips - 1),
        "outer_grad",
        [both16] * 3,
        [where, keep, send, col, col_got, inner_keep, inner_got, *returned, *returned_got],
    )
    return layer_out, query_grad, key_grad, value_grad


def solution(mesh):
    in_specs = (
        P("seq", "tensor"),
        P("seq", "tensor"),
        P("seq", "tensor"),
        P("tensor", "seq"),
        P("tensor"),
        P("tensor", None),
        P("seq", "tensor"),
    )
    out_specs = (P("seq", "tensor"), P("seq", "tensor"), P("seq", "tensor"), P("seq", "tensor"))
    return jax.shard_map(
        on_device, mesh=mesh, in_specs=in_specs, out_specs=out_specs, check_vma=False
    )
```

time: 74.7 us -> 136 us (1.82)
  Pallas kernels: 16.9 us -> 80.3 us
  local copies, waits for them, and re-layouts: 8.41 us -> 2.08 us
  starting transfers between devices: 26.6 us -> 28.7 us
  waiting for transfers between devices: 21.4 us -> 23.4 us
    pallas_call x14 -> x10, Pallas kernels: 16.9 us -> 80.3 us  [call(): pl.pallas_call(kernel, name=name, out_shape=outs, in_specs=[SMEM] + [HBM...]
    ppermute x9, waiting for transfers between devices: 15.6 us -> 9.37 us  [swap_tensor(): return lax.ppermute(value, 'tensor', [(i, i ^ k) for i in range(tensor)])]
    ppermute x5 -> x6, waiting for transfers between devices: 4.48 us -> 10.4 us  [to_chip(): lax.ppermute(value, 'seq', [(i, i + 2 * step) for i in range(seq) if 0 <=...]
    dynamic_slice x4 -> x0, local copies, waits for them, and re-layouts: 5 us -> none  [the longest x3 3.81 us: fetch(): lax.dynamic_slice(source, (begin, (place ^ step) * width), (rows, width))]
    ppermute x11 -> x14, waiting for transfers between devices: 1.31 us -> 3.66 us  [swap_core(): return lax.ppermute(value, 'seq', [(i, i ^ 1) for i in range(seq)])]
    unnamed x12 -> x18, local copies, waits for them, and re-layouts: 3.41 us -> 2.08 us
    ppermute x5 -> x6, starting transfers between devices: 10.7 us -> 11.8 us  [to_chip(): lax.ppermute(value, 'seq', [(i, i + 2 * step) for i in range(seq) if 0 <=...]
    ppermute x11 -> x14, starting transfers between devices: 2.48 us -> 3.21 us  [swap_core(): return lax.ppermute(value, 'seq', [(i, i ^ 1) for i in range(seq)])]
  transfers between devices with their start and end apart: 26 -> 30, of which waited for: 6 -> 11; matrix products, arithmetic and copies ran while one was open for 2% -> 0% of each run, Pallas kernels for 19% -> 8%
where the time goes in v4:
time: 136 us
  Pallas kernels  80.3 us (59%)
  starting transfers between devices  28.7 us (21%)
  waiting for transfers between devices  23.4 us (17%)
  local copies, waits for them, and re-layouts  2.08 us (2%)
    pallas_call x10, Pallas kernels, call(): pl.pallas_call(kernel, name=name, out_shape=outs, in_specs=[SMEM] + [HBM...  80.3 us
    ppermute x6, starting transfers between devices, to_chip(): lax.ppermute(value, 'seq', [(i, i + 2 * step) for i in range(seq) if 0 <=...  11.8 us
    ppermute x9, starting transfers between devices, swap_tensor(): return lax.ppermute(value, 'tensor', [(i, i ^ k) for i in range(tensor)])  11.7 us
    ppermute x6, waiting for transfers between devices, to_chip(): lax.ppermute(value, 'seq', [(i, i + 2 * step) for i in range(seq) if 0 <=...  10.4 us
    ppermute x9, waiting for transfers between devices, swap_tensor(): return lax.ppermute(value, 'tensor', [(i, i ^ k) for i in range(tensor)])  9.37 us
    ppermute x14, waiting for transfers between devices, swap_core(): return lax.ppermute(value, 'seq', [(i, i ^ 1) for i in range(seq)])  3.66 us
    ppermute x14, starting transfers between devices, swap_core(): return lax.ppermute(value, 'seq', [(i, i ^ 1) for i in range(seq)])  3.21 us
  transfers between devices with their start and end apart: 30, of which 11 were waited for; matrix products, arithmetic and copies ran while one was open for 0% of the time, Pallas kernels for 8%

profile of v4, /device:TPU:0, one launch (start us, length us, event | category | flops | bytes accessed | tf_op | source)
XLA Modules:
  0.0 136.0 jit_solution(17973059820199552926)
XLA Ops:
  1.3 67.5 %stage.1 = (bf16[64,1536]{1,0:T(8,128)(2,1)}, bf16[128,1536]{1,0:T(8,128)(2,1)}, bf16[128,1536]{1,0:T(8,128)(2,1)}, bf16[256,1536]{1,0:T(8,128)(2,1)}, bf16[272,...) custom-call(s32[3]{0:T(128)} %pad_add_fusion.where_ref, f32[2,256]{1,0:T(2,128)} %decay_ref.1, bf16[256,6144]{1,0:T(8,128)(2,1)} %weight_ref.1, ...), custom_call_target="tpu_custom_call" | custom-call | flops 1 | bytes 1 | tf_op jit(solution)/shard_map/stage/pallas_call | solution.py:319
  69.4 3.5 %collective-permute-start.1 = (bf16[64,1536]{1,0:T(8,128)(2,1)}, bf16[64,1536]{1,0:T(8,128)(2,1)S(1)}, u32[]{:S(2)}, u32[]{:S(2)}) collective-permute-start(bf16[64,1536]{1,0:T(8,128)(2,1)} %get-tuple-element.50), channel_id=1, source_target_pairs={{0,3},{1,2},{2,1},{3,0},{4,7},{5,6},{6,5},{7,4},{8,11},{9,10},{10,... | collective-permute-start | bytes 589832 | tf_op jit(solution)/shard_map/ppermute | solution.py:354
  73.9 5.0 %collective-permute-done.1.refs_1_ = bf16[64,1536]{1,0:T(8,128)(2,1)S(1)} collective-permute-done((bf16[64,1536]{1,0:T(8,128)(2,1)}, bf16[64,1536]{1,0:T(8,128)(2,1)S(1)}, u32[]{:S(2)}, u32[]{:S(2)}) %collective-permute-start.1) | collective-permute-done | bytes 196640 | tf_op jit(solution)/shard_map/ppermute | solution.py:354
  78.9 2.0 %collective-permute-start.2 = (bf16[64,1536]{1,0:T(8,128)(2,1)S(1)}, bf16[64,1536]{1,0:T(8,128)(2,1)S(1)}, u32[]{:S(2)}, u32[]{:S(2)}) collective-permute-start(bf16[64,1536]{1,0:T(8,128)(2,1)S(1)} %collective-permute-done.1.refs_1_), channel_id=1, source_target_pairs={{0,8},{4,12},{8,0},{12,4},{16,24},{20,28},{24,16},{28,20},{1,9},{5... | collective-permute-start | bytes 589832 | tf_op jit(solution)/shard_map/ppermute | solution.py:360
  81.8 1.4 %fresh.1 = (bf16[2,256,128]{2,1,0:T(8,128)(2,1)S(1)}, bf16[2,256,128]{2,1,0:T(8,128)(2,1)S(1)}, bf16[2,256,128]{2,1,0:T(8,128)(2,1)S(1)}, f32[256,2]{1,0:T(8,128...) custom-call(s32[3]{0:T(128)S(1)} %copy-done.6, bf16[256,384]{1,0:T(8,128)(2,1)S(1)} %copy-done.3, ...), custom_call_target="tpu_custom_call" | custom-call | flops 1 | bytes 1 | tf_op jit(solution)/shard_map/fresh/pallas_call | solution.py:319
  83.3 4.4 %collective-permute-start.4 = (bf16[144,128]{1,0:T(8,128)(2,1)S(1)}, bf16[144,128]{1,0:T(8,128)(2,1)S(1)}, u32[]{:S(2)}, u32[]{:S(2)}) collective-permute-start(bf16[144,128]{1,0:T(8,128)(2,1)S(1)} %get-tuple-element.53), channel_id=1, source_target_pairs={{0,24},{4,28},{1,25},{5,29},{2,26},{6,30},{3,27},{7,31}} | collective-permute-start | bytes 110600 | tf_op jit(solution)/shard_map/ppermute | solution.py:363
  87.7 1.3 collective-permute-start.8
  89.3 2.2 %collective-permute-start.9 = (bf16[144,128]{1,0:T(8,128)(2,1)S(1)}, bf16[144,128]{1,0:T(8,128)(2,1)S(1)}, u32[]{:S(2)}, u32[]{:S(2)}) collective-permute-start(bf16[144,128]{1,0:T(8,128)(2,1)S(1)} %get-tuple-element.53), channel_id=1, source_target_pairs={{0,16},{4,20},{8,24},{12,28},{1,17},{5,21},{9,25},{13,29},{2,18},{... | collective-permute-start | bytes 110600 | tf_op jit(solution)/shard_map/ppermute | solution.py:363
  97.9 2.5 %collective-permute-start.11 = (bf16[2,256,128]{2,1,0:T(8,128)(2,1)S(1)}, bf16[2,256,128]{2,1,0:T(8,128)(2,1)S(1)}, u32[]{:S(2)}, u32[]{:S(2)}) collective-permute-start(bf16[2,256,128]{2,1,0:T(8,128)(2,1)S(1)} %get-tuple-element.68), channel_id=1, source_target_pairs={{0,3},{1,2},{2,1},{3,0},{4,7},{5,6},{6,5},{7,4},{8,11},{9,10},{10,... | collective-permute-start | bytes 393224 | tf_op jit(solution)/shard_map/ppermute | solution.py:354
  102.7 2.5 %collective-permute-start.17 = (bf16[2,256,128]{2,1,0:T(8,128)(2,1)S(1)}, bf16[2,256,128]{2,1,0:T(8,128)(2,1)S(1)}, u32[]{:S(2)}, u32[]{:S(2)}) collective-permute-start(bf16[2,256,128]{2,1,0:T(8,128)(2,1)S(1)} %get-tuple-element.78.refs_6_), channel_id=1, source_target_pairs={{0,3},{1,2},{2,1},{3,0},{4,7},{5,6},{6,5},{7,4},{8,11},{9,10},{10,... | collective-permute-start | bytes 393224 | tf_op jit(solution)/shard_map/ppermute | solution.py:354
  106.4 1.6 %collective-permute-done.12.refs_1_ = bf16[2,256,128]{2,1,0:T(8,128)(2,1)S(1)} collective-permute-done((bf16[2,256,128]{2,1,0:T(8,128)(2,1)S(1)}, bf16[2,256,128]{2,1,0:T(8,128)(2,1)S(1)}, u32[]{:S(2)}, u32[]{:S(2)}) %collective-permute-start.12) | collective-permute-done | bytes 131104 | tf_op jit(solution)/shard_map/ppermute | solution.py:354
  108.0 2.7 %collective-permute-done.13.refs_2_ = bf16[2,256,128]{2,1,0:T(8,128)(2,1)S(1)} collective-permute-done((bf16[2,256,128]{2,1,0:T(8,128)(2,1)S(1)}, bf16[2,256,128]{2,1,0:T(8,128)(2,1)S(1)}, u32[]{:S(2)}, u32[]{:S(2)}) %collective-permute-start.13) | collective-permute-done | bytes 131104 | tf_op jit(solution)/shard_map/ppermute | solution.py:354
  110.7 1.2 grad_mixed.1
  111.9 1.4 %collective-permute-start.24 = (bf16[144,128]{1,0:T(8,128)(2,1)S(1)}, bf16[144,128]{1,0:T(8,128)(2,1)S(1)}, u32[]{:S(2)}, u32[]{:S(2)}) collective-permute-start(bf16[144,128]{1,0:T(8,128)(2,1)S(1)} %get-tuple-element.83), channel_id=1, source_target_pairs={{8,0},{12,4},{16,8},{20,12},{24,16},{28,20},{9,1},{13,5},{17,9},{2... | collective-permute-start | bytes 110600 | tf_op jit(solution)/shard_map/ppermute | solution.py:363
  113.4 1.3 collective-permute-start.25
  115.3 5.1 %collective-permute-done.24.refs_0_ = bf16[144,128]{1,0:T(8,128)(2,1)S(1)} collective-permute-done((bf16[144,128]{1,0:T(8,128)(2,1)S(1)}, bf16[144,128]{1,0:T(8,128)(2,1)S(1)}, u32[]{:S(2)}, u32[]{:S(2)}) %collective-permute-start.24) | collective-permute-done | bytes 36896 | tf_op jit(solution)/shard_map/ppermute | solution.py:363
  120.4 1.3 collective-permute-start.26
  121.7 1.5 %collective-permute-done.25.refs_1_ = bf16[144,128]{1,0:T(8,128)(2,1)S(1)} collective-permute-done((bf16[144,128]{1,0:T(8,128)(2,1)S(1)}, bf16[144,128]{1,0:T(8,128)(2,1)S(1)}, u32[]{:S(2)}, u32[]{:S(2)}) %collective-permute-start.25) | collective-permute-done | bytes 36896 | tf_op jit(solution)/shard_map/ppermute | solution.py:363
  123.2 1.9 %inner_grad.1 = (f32[256,384]{1,0:T(8,128)S(1)}, f32[256,384]{1,0:T(8,128)S(1)}) custom-call(s32[3]{0:T(128)S(1)} %copy-done.6, bf16[2,256,128]{2,1,0:T(8,128)(2,1)S(1)} %get-tuple-element.61.refs_0_.q_ref, bf16[2,256,128]{2,1,0:T(8,128)(2,1)S(1)} %get-tuple-element.62.refs_1_.k_ref, bf16[2,256,128]{2,1,0:T(8,128)(2,1)S(1)} %get-tuple-element.63.refs_2_.v_ref, ...), custom_call_target="tpu_custom_call" | custom-call | flops 1 | bytes 1 | tf_op jit(solution)/shard_map/inner_grad/pallas_call | solution.py:319
  125.1 3.0 %collective-permute-done.26.refs_2_ = bf16[144,128]{1,0:T(8,128)(2,1)S(1)} collective-permute-done((bf16[144,128]{1,0:T(8,128)(2,1)S(1)}, bf16[144,128]{1,0:T(8,128)(2,1)S(1)}, u32[]{:S(2)}, u32[]{:S(2)}) %collective-permute-start.26) | collective-permute-done | bytes 36896 | tf_op jit(solution)/shard_map/ppermute | solution.py:363
  128.6 1.4 %collective-permute-done.21.refs_12_ = bf16[2,256,128]{2,1,0:T(8,128)(2,1)S(1)} collective-permute-done((bf16[2,256,128]{2,1,0:T(8,128)(2,1)S(1)}, bf16[2,256,128]{2,1,0:T(8,128)(2,1)S(1)}, u32[]{:S(2)}, u32[]{:S(2)}) %collective-permute-start.21) | collective-permute-done | bytes 131104 | tf_op jit(solution)/shard_map/ppermute | solution.py:357
  130.1 1.2 collective-permute-done.22.refs_13_
  132.0 2.4 %layer.1 = bf16[256,1536]{1,0:T(8,128)(2,1)} custom-call(s32[3]{0:T(128)S(1)} %copy-done.6, bf16[256,1536]{1,0:T(8,128)(2,1)S(1)} %copy-done.2, bf16[128,1536]{1,0:T(8,128)(2,1)S(1)} %get-tuple-element.75.refs_0_, bf16[128,1536]{1,0:T(8,128)(2,1)S(1)} %collective-permute-done.6.refs_0_.refs_1_, bf16[128,1536]{1,0:T(8,128)(2,1)S(1)} %collective-permute-done.7.refs_1_.refs_2_, ...), custom_call_target="tpu_custom_call" | custom-call | flops 1 | bytes 1 | tf_op jit(solution)/shard_map/layer/pallas_call | solution.py:319
  134.4 1.6 %outer_grad.1 = (bf16[256,256]{1,0:T(8,128)(2,1)}, bf16[256,256]{1,0:T(8,128)(2,1)}, bf16[256,256]{1,0:T(8,128)(2,1)}) custom-call(s32[3]{0:T(128)S(1)} %copy-done.6, bf16[256,384]{1,0:T(8,128)(2,1)S(1)} %copy-done.4, bf16[272,384]{1,0:T(8,128)(2,1)S(1)} %copy-done.5, f32[256,2]{1,0:T(8,128)S(1)} %get-tuple-element.54.refs_3_.col_ref, ...), custom_call_target="tpu_custom_call" | custom-call | flops 1 | bytes 1 | tf_op jit(solution)/shard_map/outer_grad/pallas_call | solution.py:319
  (65 shorter events, 15.3 us)
Async XLA Ops:
  68.9 12.0 %collective-permute-start = (bf16[256,1536]{1,0:T(8,128)(2,1)S(1)}, bf16[256,1536]{1,0:T(8,128)(2,1)S(1)}, u32[]{:S(2)}, u32[]{:S(2)}) collective-permute-start(bf16[256,1536]{1,0:T(8,128)(2,1)S(1)} %copy-done), channel_id=1, source_target_pairs={{0,4},{4,0},{8,12},{12,8},{16,20},{20,16},{24,28},{28,24},{1,5},{5... | collective-permute-start | bytes 2359304 | tf_op jit(solution)/shard_map/ppermute | solution.py:357
  69.4 9.5 %collective-permute-start.1 = (bf16[64,1536]{1,0:T(8,128)(2,1)}, bf16[64,1536]{1,0:T(8,128)(2,1)S(1)}, u32[]{:S(2)}, u32[]{:S(2)}) collective-permute-start(bf16[64,1536]{1,0:T(8,128)(2,1)} %get-tuple-element.50), channel_id=1, source_target_pairs={{0,3},{1,2},{2,1},{3,0},{4,7},{5,6},{6,5},{7,4},{8,11},{9,10},{10,... | collective-permute-start | bytes 589832 | tf_op jit(solution)/shard_map/ppermute | solution.py:354
  72.9 8.0 %collective-permute-start.3 = (bf16[272,384]{1,0:T(8,128)(2,1)}, bf16[272,384]{1,0:T(8,128)(2,1)S(1)}, u32[]{:S(2)}, u32[]{:S(2)}) collective-permute-start(bf16[272,384]{1,0:T(8,128)(2,1)} %get-tuple-element.48.send_ref), channel_id=1, source_target_pairs={{0,4},{4,0},{8,12},{12,8},{16,20},{20,16},{24,28},{28,24},{1,5},{5... | collective-permute-start | bytes 626696 | tf_op jit(solution)/shard_map/ppermute | solution.py:357
  73.1 27.3 %collective-permute-start.6 = (bf16[128,1536]{1,0:T(8,128)(2,1)}, bf16[128,1536]{1,0:T(8,128)(2,1)S(1)}, u32[]{:S(2)}, u32[]{:S(2)}) collective-permute-start(bf16[128,1536]{1,0:T(8,128)(2,1)} %get-tuple-element.59), channel_id=1, source_target_pairs={{0,1},{1,0},{2,3},{3,2},{4,5},{5,4},{6,7},{7,6},{8,9},{9,8},{10,11... | collective-permute-start | bytes 1179656 | tf_op jit(solution)/shard_map/ppermute | solution.py:354
  73.6 26.8 %collective-permute-start.7 = (bf16[128,1536]{1,0:T(8,128)(2,1)}, bf16[128,1536]{1,0:T(8,128)(2,1)S(1)}, u32[]{:S(2)}, u32[]{:S(2)}) collective-permute-start(bf16[128,1536]{1,0:T(8,128)(2,1)} %get-tuple-element.60), channel_id=1, source_target_pairs={{0,2},{1,3},{2,0},{3,1},{4,6},{5,7},{6,4},{7,5},{8,10},{9,11},{10,... | collective-permute-start | bytes 1179656 | tf_op jit(solution)/shard_map/ppermute | solution.py:354
  78.9 15.6 %collective-permute-start.2 = (bf16[64,1536]{1,0:T(8,128)(2,1)S(1)}, bf16[64,1536]{1,0:T(8,128)(2,1)S(1)}, u32[]{:S(2)}, u32[]{:S(2)}) collective-permute-start(bf16[64,1536]{1,0:T(8,128)(2,1)S(1)} %collective-permute-done.1.refs_1_), channel_id=1, source_target_pairs={{0,8},{4,12},{8,0},{12,4},{16,24},{20,28},{24,16},{28,20},{1,9},{5... | collective-permute-start | bytes 589832 | tf_op jit(solution)/shard_map/ppermute | solution.py:360
  83.3 6.0 %collective-permute-start.4 = (bf16[144,128]{1,0:T(8,128)(2,1)S(1)}, bf16[144,128]{1,0:T(8,128)(2,1)S(1)}, u32[]{:S(2)}, u32[]{:S(2)}) collective-permute-start(bf16[144,128]{1,0:T(8,128)(2,1)S(1)} %get-tuple-element.53), channel_id=1, source_target_pairs={{0,24},{4,28},{1,25},{5,29},{2,26},{6,30},{3,27},{7,31}} | collective-permute-start | bytes 110600 | tf_op jit(solution)/shard_map/ppermute | solution.py:363
  87.7 4.9 %collective-permute-start.8 = (bf16[144,128]{1,0:T(8,128)(2,1)S(1)}, bf16[144,128]{1,0:T(8,128)(2,1)S(1)}, u32[]{:S(2)}, u32[]{:S(2)}) collective-permute-start(bf16[144,128]{1,0:T(8,128)(2,1)S(1)} %get-tuple-element.53), channel_id=1, source_target_pairs={{0,8},{4,12},{8,16},{12,20},{16,24},{20,28},{1,9},{5,13},{9,17},{1... | collective-permute-start | bytes 110600 | tf_op jit(solution)/shard_map/ppermute | solution.py:363
  89.3 3.8 %collective-permute-start.9 = (bf16[144,128]{1,0:T(8,128)(2,1)S(1)}, bf16[144,128]{1,0:T(8,128)(2,1)S(1)}, u32[]{:S(2)}, u32[]{:S(2)}) collective-permute-start(bf16[144,128]{1,0:T(8,128)(2,1)S(1)} %get-tuple-element.53), channel_id=1, source_target_pairs={{0,16},{4,20},{8,24},{12,28},{1,17},{5,21},{9,25},{13,29},{2,18},{... | collective-permute-start | bytes 110600 | tf_op jit(solution)/shard_map/ppermute | solution.py:363
  94.0 6.4 %collective-permute-start.10 = (bf16[2,256,128]{2,1,0:T(8,128)(2,1)S(1)}, bf16[2,256,128]{2,1,0:T(8,128)(2,1)S(1)}, u32[]{:S(2)}, u32[]{:S(2)}) collective-permute-start(bf16[2,256,128]{2,1,0:T(8,128)(2,1)S(1)} %get-tuple-element.78.refs_6_), channel_id=1, source_target_pairs={{0,4},{4,0},{8,12},{12,8},{16,20},{20,16},{24,28},{28,24},{1,5},{5... | collective-permute-start | bytes 393224 | tf_op jit(solution)/shard_map/ppermute | solution.py:357
  97.9 7.8 %collective-permute-start.11 = (bf16[2,256,128]{2,1,0:T(8,128)(2,1)S(1)}, bf16[2,256,128]{2,1,0:T(8,128)(2,1)S(1)}, u32[]{:S(2)}, u32[]{:S(2)}) collective-permute-start(bf16[2,256,128]{2,1,0:T(8,128)(2,1)S(1)} %get-tuple-element.68), channel_id=1, source_target_pairs={{0,3},{1,2},{2,1},{3,0},{4,7},{5,6},{6,5},{7,4},{8,11},{9,10},{10,... | collective-permute-start | bytes 393224 | tf_op jit(solution)/shard_map/ppermute | solution.py:354
  101.6 6.4 %collective-permute-start.12 = (bf16[2,256,128]{2,1,0:T(8,128)(2,1)S(1)}, bf16[2,256,128]{2,1,0:T(8,128)(2,1)S(1)}, u32[]{:S(2)}, u32[]{:S(2)}) collective-permute-start(bf16[2,256,128]{2,1,0:T(8,128)(2,1)S(1)} %get-tuple-element.72), channel_id=1, source_target_pairs={{0,1},{1,0},{2,3},{3,2},{4,5},{5,4},{6,7},{7,6},{8,9},{9,8},{10,11... | collective-permute-start | bytes 393224 | tf_op jit(solution)/shard_map/ppermute | solution.py:354
  102.2 8.6 %collective-permute-start.13 = (bf16[2,256,128]{2,1,0:T(8,128)(2,1)S(1)}, bf16[2,256,128]{2,1,0:T(8,128)(2,1)S(1)}, u32[]{:S(2)}, u32[]{:S(2)}) collective-permute-start(bf16[2,256,128]{2,1,0:T(8,128)(2,1)S(1)} %get-tuple-element.73), channel_id=1, source_target_pairs={{0,2},{1,3},{2,0},{3,1},{4,6},{5,7},{6,4},{7,5},{8,10},{9,11},{10,... | collective-permute-start | bytes 393224 | tf_op jit(solution)/shard_map/ppermute | solution.py:354
  102.7 12.0 %collective-permute-start.17 = (bf16[2,256,128]{2,1,0:T(8,128)(2,1)S(1)}, bf16[2,256,128]{2,1,0:T(8,128)(2,1)S(1)}, u32[]{:S(2)}, u32[]{:S(2)}) collective-permute-start(bf16[2,256,128]{2,1,0:T(8,128)(2,1)S(1)} %get-tuple-element.78.refs_6_), channel_id=1, source_target_pairs={{0,3},{1,2},{2,1},{3,0},{4,7},{5,6},{6,5},{7,4},{8,11},{9,10},{10,... | collective-permute-start | bytes 393224 | tf_op jit(solution)/shard_map/ppermute | solution.py:354
  105.1 9.6 %collective-permute-start.18 = (bf16[2,256,128]{2,1,0:T(8,128)(2,1)S(1)}, bf16[2,256,128]{2,1,0:T(8,128)(2,1)S(1)}, u32[]{:S(2)}, u32[]{:S(2)}) collective-permute-start(bf16[2,256,128]{2,1,0:T(8,128)(2,1)S(1)} %get-tuple-element.78.refs_6_), channel_id=1, source_target_pairs={{0,1},{1,0},{2,3},{3,2},{4,5},{5,4},{6,7},{7,6},{8,9},{9,8},{10,11... | collective-permute-start | bytes 393224 | tf_op jit(solution)/shard_map/ppermute | solution.py:354
  105.7 9.6 %collective-permute-start.19 = (bf16[2,256,128]{2,1,0:T(8,128)(2,1)S(1)}, bf16[2,256,128]{2,1,0:T(8,128)(2,1)S(1)}, u32[]{:S(2)}, u32[]{:S(2)}) collective-permute-start(bf16[2,256,128]{2,1,0:T(8,128)(2,1)S(1)} %get-tuple-element.78.refs_6_), channel_id=1, source_target_pairs={{0,2},{1,3},{2,0},{3,1},{4,6},{5,7},{6,4},{7,5},{8,10},{9,11},{10,... | collective-permute-start | bytes 393224 | tf_op jit(solution)/shard_map/ppermute | solution.py:354
  111.9 8.5 %collective-permute-start.24 = (bf16[144,128]{1,0:T(8,128)(2,1)S(1)}, bf16[144,128]{1,0:T(8,128)(2,1)S(1)}, u32[]{:S(2)}, u32[]{:S(2)}) collective-permute-start(bf16[144,128]{1,0:T(8,128)(2,1)S(1)} %get-tuple-element.83), channel_id=1, source_target_pairs={{8,0},{12,4},{16,8},{20,12},{24,16},{28,20},{9,1},{13,5},{17,9},{2... | collective-permute-start | bytes 110600 | tf_op jit(solution)/shard_map/ppermute | solution.py:363
  113.4 9.8 %collective-permute-start.25 = (bf16[144,128]{1,0:T(8,128)(2,1)S(1)}, bf16[144,128]{1,0:T(8,128)(2,1)S(1)}, u32[]{:S(2)}, u32[]{:S(2)}) collective-permute-start(bf16[144,128]{1,0:T(8,128)(2,1)S(1)} %get-tuple-element.83), channel_id=1, source_target_pairs={{16,0},{20,4},{24,8},{28,12},{17,1},{21,5},{25,9},{29,13},{18,2},{... | collective-permute-start | bytes 110600 | tf_op jit(solution)/shard_map/ppermute | solution.py:363
  114.7 13.4 %collective-permute-start.20 = (bf16[2,256,128]{2,1,0:T(8,128)(2,1)S(1)}, bf16[2,256,128]{2,1,0:T(8,128)(2,1)S(1)}, u32[]{:S(2)}, u32[]{:S(2)}) collective-permute-start(bf16[2,256,128]{2,1,0:T(8,128)(2,1)S(1)} %collective-permute-done.17.refs_7_), channel_id=1, source_target_pairs={{0,4},{4,0},{8,12},{12,8},{16,20},{20,16},{24,28},{28,24},{1,5},{5... | collective-permute-start | bytes 393224 | tf_op jit(solution)/shard_map/ppermute | solution.py:357
  114.8 16.7 %collective-permute-start.14 = (bf16[128,1536]{1,0:T(8,128)(2,1)S(1)}, bf16[128,1536]{1,0:T(8,128)(2,1)S(1)}, u32[]{:S(2)}, u32[]{:S(2)}) collective-permute-start(bf16[128,1536]{1,0:T(8,128)(2,1)S(1)} %get-tuple-element.75.refs_0_), channel_id=1, source_target_pairs={{0,4},{4,0},{8,12},{12,8},{16,20},{20,16},{24,28},{28,24},{1,5},{5... | collective-permute-start | bytes 1179656 | tf_op jit(solution)/shard_map/ppermute | solution.py:357
  115.3 16.6 %collective-permute-start.15 = (bf16[128,1536]{1,0:T(8,128)(2,1)S(1)}, bf16[128,1536]{1,0:T(8,128)(2,1)S(1)}, u32[]{:S(2)}, u32[]{:S(2)}) collective-permute-start(bf16[128,1536]{1,0:T(8,128)(2,1)S(1)} %collective-permute-done.6.refs_0_.refs_1_), channel_id=1, source_target_pairs={{0,4},{4,0},{8,12},{12,8},{16,20},{20,16},{24,28},{28,24},{1,5},{5... | collective-permute-start | bytes 1179656 | tf_op jit(solution)/shard_map/ppermute | solution.py:357
  120.4 7.6 %collective-permute-start.26 = (bf16[144,128]{1,0:T(8,128)(2,1)S(1)}, bf16[144,128]{1,0:T(8,128)(2,1)S(1)}, u32[]{:S(2)}, u32[]{:S(2)}) collective-permute-start(bf16[144,128]{1,0:T(8,128)(2,1)S(1)} %get-tuple-element.83), channel_id=1, source_target_pairs={{24,0},{28,4},{25,1},{29,5},{26,2},{30,6},{27,3},{31,7}} | collective-permute-start | bytes 110600 | tf_op jit(solution)/shard_map/ppermute | solution.py:363
  123.2 8.8 %collective-permute-start.16 = (bf16[128,1536]{1,0:T(8,128)(2,1)S(1)}, bf16[128,1536]{1,0:T(8,128)(2,1)S(1)}, u32[]{:S(2)}, u32[]{:S(2)}) collective-permute-start(bf16[128,1536]{1,0:T(8,128)(2,1)S(1)} %collective-permute-done.7.refs_1_.refs_2_), channel_id=1, source_target_pairs={{0,4},{4,0},{8,12},{12,8},{16,20},{20,16},{24,28},{28,24},{1,5},{5... | collective-permute-start | bytes 1179656 | tf_op jit(solution)/shard_map/ppermute | solution.py:357
  128.0 6.4 %collective-permute-start.23 = (f32[256,384]{1,0:T(8,128)S(1)}, f32[256,384]{1,0:T(8,128)S(1)}, u32[]{:S(2)}, u32[]{:S(2)}) collective-permute-start(f32[256,384]{1,0:T(8,128)S(1)} %get-tuple-element.82), channel_id=1, source_target_pairs={{0,4},{4,0},{8,12},{12,8},{16,20},{20,16},{24,28},{28,24},{1,5},{5... | collective-permute-start | bytes 1179656 | tf_op jit(solution)/shard_map/ppermute | solution.py:357
  (15 other events, 416.2 us)

commit v5 on v4

--- a/solution.py
+++ b/solution.py
@@ -99,38 +99,21 @@
     return pl.ds(pl.multiple_of(number * count, count), count)
 
 
-def stage_kernel(plan, where_ref, decay_source, weight_ref, q_ref, k_ref, v_ref, *refs):
-    *piece_refs, own_ref, send_ref, keep_ref, decay_ref, tail_ref, sems = refs
-    core, side, place = where_ref[0], where_ref[1], where_ref[2]
-    width = own_ref.shape[1]
+def pack_kernel(where_ref, decay_ref, q_ref, k_ref, v_ref, send_ref, keep_ref):
+    core = where_ref[0]
     length = keep_ref.shape[0]
-    copies = []
-
-    def start(source, target):
-        copies.append(pltpu.make_async_copy(source, target, sems.at[len(copies)]))
-        copies[-1].start()
-
-    start(decay_source, decay_ref)
-    for (step, halves), ref in zip(plan, piece_refs):
-        rows = rows_of(core * 2 + side if halves else core, ref.shape[0])
-        start(weight_ref.at[rows, rows_of(place ^ step, width)], ref)
-    for number, source in enumerate((q_ref, k_ref, v_ref)):
+    for number, ref in enumerate((q_ref, k_ref, v_ref)):
         part = slice(number * HD, (number + 1) * HD)
-        start(source.at[:, lanes_of(1 - core)], send_ref.at[0:length, part])
-        start(source.at[:, lanes_of(core)], keep_ref.at[:, part])
-    start(weight_ref.at[:, rows_of(place, width)], own_ref)
-    copies[0].wait()
+        send_ref[0:length, part] = ref[:, lanes_of(1 - core)]
+        keep_ref[:, part] = ref[:, lanes_of(core)]
     decay = jnp.where(core == 0, decay_ref[1:2, :], decay_ref[0:1, :])
     first = decay.astype(BF16).astype(F32)
     second = (decay - first).astype(BF16).astype(F32)
     third = decay - first - second
     at = lax.broadcasted_iota(jnp.int32, (TAIL, length), 0)
     tail = jnp.where(at == 0, first, jnp.where(at == 1, second, jnp.where(at == 2, third, 0.0)))
-    tail_ref[...] = jnp.zeros(tail_ref.shape, BF16)
-    tail_ref[:, 0:length] = tail.astype(BF16)
-    start(tail_ref, send_ref.at[length : length + TAIL, :])
-    for copy in copies[1:]:
-        copy.wait()
+    send_ref[length : length + TAIL, :] = jnp.zeros((TAIL, send_ref.shape[1]), BF16)
+    send_ref[length : length + TAIL, 0:length] = tail.astype(BF16)
 
 
 def fresh_kernel(where_ref, keep_ref, got_ref, decay_ref, q_out, k_out, v_out, col_ref, row_ref, first_ref, message_ref):
@@ -196,32 +179,38 @@
         normed_ref[b] = (mixed * scale_of(mixed) * gain).astype(BF16)
 
 
-def partial_kernel(kinds, where_ref, grad_ref, got_ref, *refs):
+def partial_kernel(kinds, where_ref, grad_ref, got_ref, normed_ref, *refs):
     core, side = where_ref[0], where_ref[1]
     refs = list(refs)
     inputs = [[refs.pop(0) for _ in range(2 if kind == "halves" else 1)] for kind in kinds]
-    products = [refs.pop(0), refs.pop(0)]
+    *products, weight_out = refs
     weights = []
     for kind, sources in zip(kinds, inputs):
         if kind == "own":
             weights.append(sources[0][rows_of(core, HD), :])
         elif kind == "halves":
             mine, theirs = sources[0][...], sources[1][...]
-            weight = jnp.concatenate([jnp.where(side == 0, mine, theirs), jnp.where(side == 0, theirs, mine)], axis=0)
-            refs.pop(0)[...] = weight
-            weights.append(weight)
+            weights += [jnp.where(side == 0, mine, theirs), jnp.where(side == 0, theirs, mine)]
         else:
             weights.append(sources[0][...])
     weight = jnp.concatenate(weights, axis=0)
+    weight_out[...] = weight[2 * HD - weight_out.shape[0] :]
     for block, ref in ((core, grad_ref), (1 - core, got_ref)):
         product = dot(ref[...], weight, NT)
         for number, out in enumerate(products):
             out[block] = product[:, number * HD : (number + 1) * HD].astype(out.dtype)
-
-
-def grad_mixed_kernel(where_ref, q_ref, col_ref, gain_ref, mixed_ref, own_ref, *refs):
-    part_refs, (grad_ref, second_ref, message_ref) = refs[:-3], refs[-3:]
+    for out in products:
+        if out.shape[0] == 4:
+            out[2:4] = normed_ref[...]
+
+
+def grad_mixed_kernel(where_ref, q_ref, col_ref, gain_ref, mixed_ref, normed_ref, own_ref, *refs):
+    part_refs, (grad_ref, second_ref, message_ref, cross_ref) = refs[:-4], refs[-4:]
     columns = col_ref[...]
+    other = 1 - where_ref[0]
+    cross_ref[0] = normed_ref[other]
+    for number, ref in enumerate(part_refs):
+        cross_ref[number + 1] = ref[2 + other]
     gain = gain_ref[:, lanes_of(where_ref[0])]
     ups = []
     for b in range(2):
@@ -248,6 +237,7 @@
     length = columns.shape[0]
     lower = triangle(length)
     parts = []
+    ends = [columns[length - 1 : length, b : b + 1] for b in range(2)]
     for b in range(2):
         q, k, v, grad = q_ref[b], k_ref[b], v_ref[b], grad_ref[b]
         weight = weights(columns, across, lower, b)
@@ -257,30 +247,28 @@
         dq = dot_fb(grad_scores, k, NN) + carried
         dk = dot_fb(grad_scores, q, TN)
         dv = dot_ff(scores, grad, TN)
+        fade = jnp.exp(ends[b] - columns[:, b : b + 1])
         if b == 0:
-            fade = jnp.exp(columns[length - 1 : length, 0:1] - columns[:, 0:1])
             dk = dk + fade * dot_bf(v, second_ref[...], NT)
             dv = dv + fade * dot_bf(k, second_ref[...], NN)
-        parts.append((dq, dk, dv))
+            fade = fade * jnp.exp(ends[1])
+        parts.append((dq, dk, dv, jnp.broadcast_to(fade, (length, HD))))
     for number, (early, late) in enumerate(zip(*parts)):
         part = slice(number * HD, (number + 1) * HD)
         keep_ref[:, part] = jnp.where(core == 0, early, late)
         send_ref[:, part] = jnp.where(core == 0, late, early)
 
 
-def outer_grad_kernel(count, where_ref, keep_ref, send_ref, col_ref, col_got_ref, inner_ref, inner_got_ref, *refs):
+def outer_grad_kernel(count, where_ref, keep_ref, send_ref, inner_ref, inner_got_ref, *refs):
     core = where_ref[0]
     length = keep_ref.shape[0]
     outs = refs[2 * count :]
-    for head, rows, cols, inner, chip_refs in (
-        (core, keep_ref, col_ref, inner_ref, refs[:count]),
-        (1 - core, send_ref, col_got_ref, inner_got_ref, refs[count : 2 * count]),
+    for head, rows, inner, chip_refs in (
+        (core, keep_ref, inner_ref, refs[:count]),
+        (1 - core, send_ref, inner_got_ref, refs[count : 2 * count]),
     ):
-        columns = cols[...]
         high, low = split(chip_sum(chip_refs))
-        end = columns[length - 1 : length, :]
-        block = jnp.where(core == 0, columns[:, 0:1], columns[:, 1:2])
-        fade = jnp.exp(jnp.where(core == 0, end[:, 0:1] + end[:, 1:2], end[:, 1:2]) - block)
+        fade = inner[:, 3 * HD : 4 * HD]
         k, v = rows[0:length, HD : 2 * HD], rows[0:length, 2 * HD : 3 * HD]
         outs[0][:, lanes_of(head)] = inner[:, 0:HD].astype(BF16)
         key = inner[:, HD : 2 * HD] + fade * (dot(v, high, NT) + dot(v, low, NT))
@@ -289,40 +277,37 @@
         outs[2][:, lanes_of(head)] = value.astype(BF16)
 
 
-def layer_kernel(others, where_ref, weight_ref, *refs):
-    groups = [refs[number * others : (number + 1) * others] for number in range(2)]
-    mine_refs, theirs_refs = groups
-    normed_refs = refs[2 * others : 3 * others + 1]
-    got_refs = refs[3 * others + 1 : 4 * others + 2]
-    out_ref = refs[4 * others + 2]
-    core = where_ref[0]
-    normed = []
-    for mine, theirs in zip(normed_refs, got_refs):
-        normed += [mine[core], theirs[core]]
+def layer_kernel(pairs, where_ref, own_ref, *refs):
+    mine_refs, theirs_refs = refs[:pairs], refs[pairs : 2 * pairs]
+    normed_ref, *sent_refs, got_ref, out_ref = refs[2 * pairs :]
+    core = where_ref[0]
+    mine = [normed_ref[core]] + [ref[2 + core] for ref in sent_refs]
+    theirs = [got_ref[number] for number in range(got_ref.shape[0])]
+    normed = [mine[0], theirs[0], mine[1], theirs[1]]
+    for begin in range(2, len(mine), 2):
+        normed += mine[begin : begin + 2] + theirs[begin : begin + 2]
     normed = jnp.concatenate(normed, axis=1)
-    width = weight_ref.shape[1]
+    width = own_ref.shape[1]
     step = 512 if width % 512 == 0 else 128
     for begin in range(0, width, step):
         lanes = slice(begin, begin + step)
-        weight = [weight_ref[rows_of(core, HD), lanes], weight_ref[rows_of(1 - core, HD), lanes]]
-        for mine, theirs in zip(mine_refs, theirs_refs):
-            weight += [mine[:, lanes], theirs[:, lanes]]
+        weight = [own_ref[rows_of(core, HD), lanes], own_ref[rows_of(1 - core, HD), lanes]]
+        for mine_ref, theirs_ref in zip(mine_refs, theirs_refs):
+            weight += [mine_ref[:, lanes], theirs_ref[:, lanes]]
         out_ref[:, lanes] = dot(normed, jnp.concatenate(weight, axis=0), NN).astype(BF16)
 
 
 SMEM = pl.BlockSpec(memory_space=pltpu.SMEM)
 VMEM = pl.BlockSpec(memory_space=pltpu.VMEM)
-HBM = pl.BlockSpec(memory_space=pltpu.HBM)
-
-
-def call(kernel, name, outs, args, direct=(), copies=0, grant=16, scratch=(), landing=None):
+
+
+def call(kernel, name, outs, args, grant=16):
     return pl.pallas_call(
         kernel,
         name=name,
         out_shape=outs,
-        in_specs=[SMEM] + [HBM if number in direct else VMEM for number in range(1, len(args))],
-        out_specs=[landing or VMEM] * len(outs),
-        scratch_shapes=[*scratch] + ([pltpu.SemaphoreType.DMA((copies,))] if copies else []),
+        in_specs=[SMEM] + [VMEM] * (len(args) - 1),
+        out_specs=[VMEM] * len(outs),
         compiler_params=pltpu.CompilerParams(vmem_limit_bytes=grant * 2**20),
         cost_estimate=pl.CostEstimate(flops=1, bytes_accessed=1, transcendentals=0),
     )(*args)
@@ -347,7 +332,7 @@
     place = lax.axis_index("tensor")
     core = lax.rem(lax.axis_index("seq"), 2)
     side = lax.rem(lax.axis_index("seq") // 2, 2)
-    where = jnp.stack([core, side, place]).astype(jnp.int32)
+    where = jnp.stack([core, side]).astype(jnp.int32)
     gain = norm_gain.reshape(1, columns)
 
     def swap_tensor(value, k):
@@ -378,21 +363,23 @@
     near = [step for step in others if not step & (step - 1)]
     order = far + near
     plan = [(step, step in far) for step in order]
-    *slices, weight_own, send, keep = call(
-        functools.partial(stage_kernel, plan),
-        "stage",
-        [shape(BF16, HD // 2 if halves else HD, width) for _, halves in plan]
-        + [shape(BF16, columns, width), shape(BF16, length + TAIL, 3 * HD), shape(BF16, length, 3 * HD)],
-        [where, log_decay, out_weight, queries, keys, values],
-        direct=(1, 2, 3, 4, 5),
-        copies=len(plan) + 9,
+
+    def slice_for(step, halves):
+        rows = HD // 2 if halves else HD
+        begin = core * HD + side * rows if halves else core * HD
+        return lax.dynamic_slice(out_weight, (begin, (place ^ step) * width), (rows, width))
+
+    slices = [slice_for(step, halves) for step, halves in plan]
+    arriving = [swap_tensor(piece, step) for piece, step in zip(slices, order)]
+    queries, keys, values, out_grad = after([queries, keys, values, out_grad], *slices)
+    send, keep = call(
+        pack_kernel,
+        "pack",
+        [shape(BF16, length + TAIL, 3 * HD), shape(BF16, length, 3 * HD)],
+        [where, log_decay, queries, keys, values],
         grant=60,
-        scratch=[pltpu.VMEM(log_decay.shape, F32), pltpu.VMEM((TAIL, 3 * HD), BF16)],
-        landing=HBM,
-    )
-    arriving = [swap_tensor(piece, step) for piece, step in zip(slices, order)]
+    )
     got = swap_core(send)
-    (out_grad,) = after([out_grad], send)
     grad_got = swap_core(out_grad)
     (got,) = after([got], grad_got)
     q, k, v, col, row, first, fresh = call(
@@ -402,7 +389,6 @@
         [where, keep, got, log_decay],
     )
     arrived = [to_chip(fresh, step) for step in range(1, chips)]
-    col_got = swap_core(col)
     (inner,) = call(without_where(inner_kernel), "inner", [pair32], [where, q, k, v, col, row, first])
     mixed, normed, states = call(
         mixed_kernel,
@@ -410,64 +396,60 @@
         [pair32, pair16, shape(F32, 2, HD, HD)],
         [where, q, col, inner, gain, first, *arrived],
     )
-    normed_mine = swap_core(normed)
+    weight_own = lax.dynamic_slice(out_weight, (0, place * width), (columns, width))
     pieces = [("own", [weight_own])]
     for (step, halves), piece in zip(plan, arriving):
+        if halves:
+            (piece,) = after([piece], fresh)
         pieces.append(("halves", [piece, swap_side(piece)]) if halves else ("whole", [piece]))
-    partials, mine = [], []
+    partials, mine, theirs = [], [], []
     for number in range(0, tensor, 2):
         kinds, sources = zip(*pieces[number : number + 2])
-        sources = sum(sources, [])
-        sources = after(sources, normed_mine if number else arrived[-1], col_got, *partials)
-        stitched = [shape(BF16, HD, width)] * kinds.count("halves")
-        outs = call(
+        sources = after(sum(sources, []), mixed, *partials)
+        *outs, weight = call(
             functools.partial(partial_kernel, kinds),
             "partial",
-            [pair16 if number else pair32, pair16, *stitched],
-            [where, out_grad, grad_got, *sources],
+            [
+                shape(BF16, 4, length, HD) if number else pair32,
+                shape(BF16, 4, length, HD),
+                shape(BF16, 2 * HD if number else HD, width),
+            ],
+            [where, out_grad, grad_got, normed, *sources],
         )
-        partials += outs[:2]
-        stitched = list(outs[2:])
-        for kind in kinds:
-            if kind == "halves":
-                mine.append(stitched.pop(0))
-                sources = sources[2:]
-            else:
-                mine.append(sources[0])
-                sources = sources[1:]
-    mine = mine[1:]
+        partials += outs
+        mine.append(weight)
+        if number == 0:
+            theirs.append(swap_core(weight))
     own_partial, *partials = partials
     sent = [swap_tensor(partial, step) for partial, step in zip(partials, order)]
-    (normed_sent,) = after([normed], *partials)
-    normed_all = [normed] + [swap_tensor(normed_sent, step) for step in order]
-    grad_mixed, second, upward = call(
+    theirs += [swap_core(weight) for weight in mine[1:]]
+    grad_mixed, second, upward, cross = call(
         grad_mixed_kernel,
         "grad_mixed",
-        [pair32, shape(F32, HD, HD), message],
-        [where, q, col, gain, mixed, own_partial, *sent],
+        [pair32, shape(F32, HD, HD), message, shape(BF16, tensor, length, HD)],
+        [where, q, col, gain, mixed, normed, own_partial, *after(sent, *theirs)],
     )
     returned = [to_chip(upward, -step) for step in range(1, chips)]
+    cross_got = swap_core(cross)
     inner_keep, inner_send = call(
         inner_grad_kernel,
         "inner_grad",
-        [shape(F32, length, 3 * HD)] * 2,
+        [shape(F32, length, 4 * HD)] * 2,
         [where, q, k, v, col, row, grad_mixed, states, second],
     )
-    inner_got = swap_core(inner_send)
-    theirs = [swap_core(piece) for piece in after(mine, grad_mixed)]
-    normed_got = [normed_mine] + [swap_core(rows) for rows in normed_all[1:]]
+    inner_got = swap_core(*after([inner_send], *returned))
     (layer_out,) = call(
-        functools.partial(layer_kernel, tensor - 1),
+        functools.partial(layer_kernel, tensor // 2),
         "layer",
         [shape(BF16, length, width)],
-        [where, weight_own, *mine, *theirs, *normed_all, *normed_got],
+        [where, weight_own, *mine, *theirs, normed, *sent, cross_got],
     )
     returned_got = after([swap_core(rows) for rows in returned], layer_out)
     query_grad, key_grad, value_grad = call(
         functools.partial(outer_grad_kernel, chips - 1),
         "outer_grad",
         [both16] * 3,
-        [where, keep, send, col, col_got, inner_keep, inner_got, *returned, *returned_got],
+        [where, keep, send, inner_keep, inner_got, *returned, *returned_got],
     )
     return layer_out, query_grad, key_grad, value_grad
 

time: 136 us -> 68 us (0.50)
  Pallas kernels: 80.3 us -> 14.7 us
  local copies, waits for them, and re-layouts: 2.08 us -> 7.19 us
  starting transfers between devices: 28.7 us -> 23.9 us
  waiting for transfers between devices: 23.4 us -> 20.3 us
    pallas_call x10, Pallas kernels: 80.3 us -> 14.7 us  [call(): pl.pallas_call(kernel, name=name, out_shape=outs, in_specs=[SMEM] + [VMEM...]
    ppermute x6, waiting for transfers between devices: 10.4 us -> 5.63 us  [to_chip(): lax.ppermute(value, 'seq', [(i, i + 2 * step) for i in range(seq) if 0 <=...]
    dynamic_slice x0 -> x3, local copies, waits for them, and re-layouts: none -> 4.26 us  [the longest x2 3.07 us: slice_for(): lax.dynamic_slice(out_weight, (begin, (place ^ step) * width), (rows, wid...]
    ppermute x9 -> x6, starting transfers between devices: 11.7 us -> 7.95 us  [swap_tensor(): return lax.ppermute(value, 'tensor', [(i, i ^ k) for i in range(tensor)])]
    ppermute x14 -> x9, waiting for transfers between devices: 3.66 us -> 1.28 us  [swap_core(): return lax.ppermute(value, 'seq', [(i, i ^ 1) for i in range(seq)])]
    ppermute x9 -> x6, waiting for transfers between devices: 9.37 us -> 11.6 us  [swap_tensor(): return lax.ppermute(value, 'tensor', [(i, i ^ k) for i in range(tensor)])]
    ppermute x6, starting transfers between devices: 11.8 us -> 13.8 us  [to_chip(): lax.ppermute(value, 'seq', [(i, i + 2 * step) for i in range(seq) if 0 <=...]
    ppermute x1, starting transfers between devices: 1.98 us -> 0.07 us  [swap_side(): return lax.ppermute(value, 'seq', [(i, i ^ 2) for i in range(seq)])]
  transfers between devices with their start and end apart: 30 -> 22, of which waited for: 11 -> 7; matrix products, arithmetic and copies ran while one was open for 0% -> 3% of each run, Pallas kernels for 8% -> 16%
where the time goes in v5:
time: 68 us; the launch traced here: 67.6 us
  starting transfers between devices  23.9 us (35%)
  waiting for transfers between devices  20.3 us (30%)
  Pallas kernels  14.7 us (22%)
  local copies, waits for them, and re-layouts  7.19 us (11%)
  between operations  0.95 us (1%)
    pallas_call x10, Pallas kernels, call(): pl.pallas_call(kernel, name=name, out_shape=outs, in_specs=[SMEM] + [VMEM...  14.7 us
    ppermute x6, starting transfers between devices, to_chip(): lax.ppermute(value, 'seq', [(i, i + 2 * step) for i in range(seq) if 0 <=...  13.8 us
    ppermute x6, waiting for transfers between devices, swap_tensor(): return lax.ppermute(value, 'tensor', [(i, i ^ k) for i in range(tensor)])  11.6 us
    ppermute x6, starting transfers between devices, swap_tensor(): return lax.ppermute(value, 'tensor', [(i, i ^ k) for i in range(tensor)])  7.95 us
    ppermute x6, waiting for transfers between devices, to_chip(): lax.ppermute(value, 'seq', [(i, i + 2 * step) for i in range(seq) if 0 <=...  5.63 us
    dynamic_slice x2, local copies, waits for them, and re-layouts, slice_for(): lax.dynamic_slice(out_weight, (begin, (place ^ step) * width), (rows, wid...  3.07 us
    unnamed x16, local copies, waits for them, and re-layouts  2.93 us
    ppermute x9, starting transfers between devices, swap_core(): return lax.ppermute(value, 'seq', [(i, i ^ 1) for i in range(seq)])  2.1 us
  transfers between devices with their start and end apart: 22, of which 7 were waited for; matrix products, arithmetic and copies ran while one was open for 3% of the time, Pallas kernels for 16%

profile of v5, /device:TPU:0, one launch (start us, length us, event | category | flops | bytes accessed | tf_op | source)
XLA Modules:
  0.0 67.6 jit_solution(1968844962882119087)
XLA Ops:
  1.7 2.1 %fusion = (bf16[128,1536]{1,0:T(8,128)(2,1)}, bf16[128,1536]{1,0:T(8,128)(2,1)}) fusion(bf16[256,6144]{1,0:T(8,128)(2,1)} %param.12, s32[]{:T(128)S(6)} %select_n.28, s32[]{:T(128)S(6)} %select_n.30, s32[]{:T(128)S(6)} %select_n.29), kind=kLoop, calls=%fused_computation.2 | loop fusion | bytes 1572876 | tf_op jit(solution)/shard_map/dynamic_slice | solution.py:370
  4.8 1.9 %pack.1 = (bf16[272,384]{1,0:T(8,128)(2,1)}, bf16[256,384]{1,0:T(8,128)(2,1)}) custom-call(s32[2]{0:T(128)} %pad_add_fusion.where_ref, f32[2,256]{1,0:T(2,128)} %decay_ref.3, bf16[256,256]{1,0:T(8,128)(2,1)} %q_ref, bf16[256,256]{1,0:T(8,128)(2,1)} %k_ref, bf16[256,256]{1,0:T(8,128)(2,1)} %v_ref), custom_call_target="tpu_custom_call" | custom-call | flops 1 | bytes 1 | tf_op jit(solution)/shard_map/pack/pallas_call | solution.py:305
  6.8 3.9 %collective-permute-start.5 = (bf16[64,1536]{1,0:T(8,128)(2,1)S(1)}, bf16[64,1536]{1,0:T(8,128)(2,1)S(1)}, u32[]{:S(2)}, u32[]{:S(2)}) collective-permute-start(bf16[64,1536]{1,0:T(8,128)(2,1)S(1)} %dynamic_slice.13), channel_id=1, source_target_pairs={{0,3},{1,2},{2,1},{3,0},{4,7},{5,6},{6,5},{7,4},{8,11},{9,10},{10,... | collective-permute-start | bytes 589832 | tf_op jit(solution)/shard_map/ppermute | solution.py:339
  13.5 1.4 %fresh.1 = (bf16[2,256,128]{2,1,0:T(8,128)(2,1)S(1)}, bf16[2,256,128]{2,1,0:T(8,128)(2,1)S(1)}, bf16[2,256,128]{2,1,0:T(8,128)(2,1)S(1)}, f32[256,2]{1,0:T(8,128...) custom-call(s32[2]{0:T(128)S(1)} %copy-done.4, bf16[256,384]{1,0:T(8,128)(2,1)S(1)} %copy-done.1, ...), custom_call_target="tpu_custom_call" | custom-call | flops 1 | bytes 1 | tf_op jit(solution)/shard_map/fresh/pallas_call | solution.py:305
  14.9 4.0 %collective-permute-start.2 = (bf16[144,128]{1,0:T(8,128)(2,1)S(1)}, bf16[144,128]{1,0:T(8,128)(2,1)S(1)}, u32[]{:S(2)}, u32[]{:S(2)}) collective-permute-start(bf16[144,128]{1,0:T(8,128)(2,1)S(1)} %get-tuple-element.62), channel_id=1, source_target_pairs={{0,8},{4,12},{8,16},{12,20},{16,24},{20,28},{1,9},{5,13},{9,17},{1... | collective-permute-start | bytes 110600 | tf_op jit(solution)/shard_map/ppermute | solution.py:348
  18.9 4.5 %collective-permute-start.3 = (bf16[144,128]{1,0:T(8,128)(2,1)S(1)}, bf16[144,128]{1,0:T(8,128)(2,1)S(1)}, u32[]{:S(2)}, u32[]{:S(2)}) collective-permute-start(bf16[144,128]{1,0:T(8,128)(2,1)S(1)} %get-tuple-element.62), channel_id=1, source_target_pairs={{0,16},{4,20},{8,24},{12,28},{1,17},{5,21},{9,25},{13,29},{2,18},{... | collective-permute-start | bytes 110600 | tf_op jit(solution)/shard_map/ppermute | solution.py:348
  23.4 1.3 %collective-permute-start.4 = (bf16[144,128]{1,0:T(8,128)(2,1)S(1)}, bf16[144,128]{1,0:T(8,128)(2,1)S(1)}, u32[]{:S(2)}, u32[]{:S(2)}) collective-permute-start(bf16[144,128]{1,0:T(8,128)(2,1)S(1)} %get-tuple-element.62), channel_id=1, source_target_pairs={{0,24},{4,28},{1,25},{5,29},{2,26},{6,30},{3,27},{7,31}} | collective-permute-start | bytes 110600 | tf_op jit(solution)/shard_map/ppermute | solution.py:348
  24.8 1.2 %constant_dynamic-slice_fusion.refs_0_.own_ref = bf16[256,1536]{1,0:T(8,128)(2,1)S(1)} fusion(bf16[256,6144]{1,0:T(8,128)(2,1)} %param.12, s32[]{:T(128)S(6)} %select_n.25), kind=kLoop, calls=%fused_computation.1 | loop fusion | bytes 1572868 | tf_op jit(solution)/shard_map/dynamic_slice | solution.py:399
  28.7 1.8 %collective-permute-done.6.refs_2_ = bf16[64,1536]{1,0:T(8,128)(2,1)S(1)} collective-permute-done((bf16[64,1536]{1,0:T(8,128)(2,1)S(1)}, bf16[64,1536]{1,0:T(8,128)(2,1)S(1)}, u32[]{:S(2)}, u32[]{:S(2)}) %collective-permute-start.6) | collective-permute-done | bytes 196640 | tf_op jit(solution)/shard_map/ppermute | solution.py:345
  31.7 1.2 %partial.3 = (bf16[4,256,128]{2,1,0:T(8,128)(2,1)S(1)}, bf16[4,256,128]{2,1,0:T(8,128)(2,1)S(1)}, bf16[256,1536]{1,0:T(8,128)(2,1)S(1)}) custom-call(s32[2]{0:T(128)S(1)} %copy-done.5, bf16[256,1536]{1,0:T(8,128)(2,1)S(1)} %copy-done, bf16[256,1536]{1,0:T(8,128)(2,1)S(1)} %collective-permute-done.got_ref, ...), custom_call_target="tpu_custom_call" | custom-call | flops 1 | bytes 1 | tf_op jit(solution)/shard_map/partial/pallas_call | solution.py:305
  33.4 1.5 %collective-permute-start.12 = (bf16[4,256,128]{2,1,0:T(8,128)(2,1)S(1)}, bf16[4,256,128]{2,1,0:T(8,128)(2,1)S(1)}, u32[]{:S(2)}, u32[]{:S(2)}) collective-permute-start(bf16[4,256,128]{2,1,0:T(8,128)(2,1)S(1)} %get-tuple-element.75), channel_id=1, source_target_pairs={{0,1},{1,0},{2,3},{3,2},{4,5},{5,4},{6,7},{7,6},{8,9},{9,8},{10,11... | collective-permute-start | bytes 786440 | tf_op jit(solution)/shard_map/ppermute | solution.py:339
  34.9 1.5 %collective-permute-start.13 = (bf16[4,256,128]{2,1,0:T(8,128)(2,1)S(1)}, bf16[4,256,128]{2,1,0:T(8,128)(2,1)S(1)}, u32[]{:S(2)}, u32[]{:S(2)}) collective-permute-start(bf16[4,256,128]{2,1,0:T(8,128)(2,1)S(1)} %get-tuple-element.76), channel_id=1, source_target_pairs={{0,2},{1,3},{2,0},{3,1},{4,6},{5,7},{6,4},{7,5},{8,10},{9,11},{10,... | collective-permute-start | bytes 786440 | tf_op jit(solution)/shard_map/ppermute | solution.py:339
  36.9 5.7 %collective-permute-done.12.refs_1_.refs_6_ = bf16[4,256,128]{2,1,0:T(8,128)(2,1)S(1)} collective-permute-done((bf16[4,256,128]{2,1,0:T(8,128)(2,1)S(1)}, bf16[4,256,128]{2,1,0:T(8,128)(2,1)S(1)}, u32[]{:S(2)}, u32[]{:S(2)}) %collective-permute-start.12) | collective-permute-done | bytes 262176 | tf_op jit(solution)/shard_map/ppermute | solution.py:339
  42.6 6.0 %collective-permute-done.13.refs_2_.refs_7_ = bf16[4,256,128]{2,1,0:T(8,128)(2,1)S(1)} collective-permute-done((bf16[4,256,128]{2,1,0:T(8,128)(2,1)S(1)}, bf16[4,256,128]{2,1,0:T(8,128)(2,1)S(1)}, u32[]{:S(2)}, u32[]{:S(2)}) %collective-permute-start.13) | collective-permute-done | bytes 262176 | tf_op jit(solution)/shard_map/ppermute | solution.py:339
  48.6 1.2 %grad_mixed.1 = (f32[2,256,128]{2,1,0:T(8,128)S(1)}, f32[128,128]{1,0:T(8,128)S(1)}, bf16[144,128]{1,0:T(8,128)(2,1)S(1)}, bf16[4,256,128]{2,1,0:T(8,128)(2,1)S(1)}) custom-call(s32[2]{0:T(128)S(1)} %copy-done.5, bf16[2,256,128]{2,1,0:T(8,128)(2,1)S(1)} %get-tuple-element.56.refs_0_.q_ref, f32[256,2]{1,0:T(8,128)S(1)} %get-tuple-element.57.refs_3_.col_ref, ...), custom_call_target="tpu_custom_call" | custom-call | flops 1 | bytes 1 | tf_op jit(solution)/shard_map/grad_mixed/pallas_call | solution.py:305
  49.8 1.4 %collective-permute-start.15 = (bf16[144,128]{1,0:T(8,128)(2,1)S(1)}, bf16[144,128]{1,0:T(8,128)(2,1)S(1)}, u32[]{:S(2)}, u32[]{:S(2)}) collective-permute-start(bf16[144,128]{1,0:T(8,128)(2,1)S(1)} %get-tuple-element.86), channel_id=1, source_target_pairs={{8,0},{12,4},{16,8},{20,12},{24,16},{28,20},{9,1},{13,5},{17,9},{2... | collective-permute-start | bytes 110600 | tf_op jit(solution)/shard_map/ppermute | solution.py:348
  51.2 1.3 %collective-permute-start.16 = (bf16[144,128]{1,0:T(8,128)(2,1)S(1)}, bf16[144,128]{1,0:T(8,128)(2,1)S(1)}, u32[]{:S(2)}, u32[]{:S(2)}) collective-permute-start(bf16[144,128]{1,0:T(8,128)(2,1)S(1)} %get-tuple-element.86), channel_id=1, source_target_pairs={{16,0},{20,4},{24,8},{28,12},{17,1},{21,5},{25,9},{29,13},{18,2},{... | collective-permute-start | bytes 110600 | tf_op jit(solution)/shard_map/ppermute | solution.py:348
  52.5 1.3 %collective-permute-start.17 = (bf16[144,128]{1,0:T(8,128)(2,1)S(1)}, bf16[144,128]{1,0:T(8,128)(2,1)S(1)}, u32[]{:S(2)}, u32[]{:S(2)}) collective-permute-start(bf16[144,128]{1,0:T(8,128)(2,1)S(1)} %get-tuple-element.86), channel_id=1, source_target_pairs={{24,0},{28,4},{25,1},{29,5},{26,2},{30,6},{27,3},{31,7}} | collective-permute-start | bytes 110600 | tf_op jit(solution)/shard_map/ppermute | solution.py:348
  53.8 1.9 %inner_grad.1 = (f32[256,512]{1,0:T(8,128)S(1)}, f32[256,512]{1,0:T(8,128)S(1)}) custom-call(s32[2]{0:T(128)S(1)} %copy-done.5, bf16[2,256,128]{2,1,0:T(8,128)(2,1)S(1)} %get-tuple-element.56.refs_0_.q_ref, bf16[2,256,128]{2,1,0:T(8,128)(2,1)S(1)} %get-tuple-element.58.refs_1_.k_ref, bf16[2,256,128]{2,1,0:T(8,128)(2,1)S(1)} %get-tuple-element.59.refs_2_.v_ref, ...), custom_call_target="tpu_custom_call" | custom-call | flops 1 | bytes 1 | tf_op jit(solution)/shard_map/inner_grad/pallas_call | solution.py:305
  56.1 2.0 %collective-permute-done.16.refs_1_ = bf16[144,128]{1,0:T(8,128)(2,1)S(1)} collective-permute-done((bf16[144,128]{1,0:T(8,128)(2,1)S(1)}, bf16[144,128]{1,0:T(8,128)(2,1)S(1)}, u32[]{:S(2)}, u32[]{:S(2)}) %collective-permute-start.16) | collective-permute-done | bytes 36896 | tf_op jit(solution)/shard_map/ppermute | solution.py:348
  58.2 3.1 %collective-permute-done.17.refs_2_ = bf16[144,128]{1,0:T(8,128)(2,1)S(1)} collective-permute-done((bf16[144,128]{1,0:T(8,128)(2,1)S(1)}, bf16[144,128]{1,0:T(8,128)(2,1)S(1)}, u32[]{:S(2)}, u32[]{:S(2)}) %collective-permute-start.17) | collective-permute-done | bytes 36896 | tf_op jit(solution)/shard_map/ppermute | solution.py:348
  62.4 1.3 %collective-permute-done.14.refs_8_ = bf16[4,256,128]{2,1,0:T(8,128)(2,1)S(1)} collective-permute-done((bf16[4,256,128]{2,1,0:T(8,128)(2,1)S(1)}, bf16[4,256,128]{2,1,0:T(8,128)(2,1)S(1)}, u32[]{:S(2)}, u32[]{:S(2)}) %collective-permute-start.14) | collective-permute-done | bytes 262176 | tf_op jit(solution)/shard_map/ppermute | solution.py:342
  63.6 2.4 %layer.1 = bf16[256,1536]{1,0:T(8,128)(2,1)} custom-call(s32[2]{0:T(128)S(1)} %copy-done.5, bf16[256,1536]{1,0:T(8,128)(2,1)S(1)} %constant_dynamic-slice_fusion.refs_0_.own_ref, bf16[128,1536]{1,0:T(8,128)(2,1)S(1)} %get-tuple-element.69.refs_0_, bf16[256,1536]{1,0:T(8,128)(2,1)S(1)} %get-tuple-element.74.refs_1_, ...), custom_call_target="tpu_custom_call" | custom-call | flops 1 | bytes 1 | tf_op jit(solution)/shard_map/layer/pallas_call | solution.py:305
  66.1 1.5 %outer_grad.1 = (bf16[256,256]{1,0:T(8,128)(2,1)}, bf16[256,256]{1,0:T(8,128)(2,1)}, bf16[256,256]{1,0:T(8,128)(2,1)}) custom-call(s32[2]{0:T(128)S(1)} %copy-done.5, bf16[256,384]{1,0:T(8,128)(2,1)S(1)} %copy-done.2, bf16[272,384]{1,0:T(8,128)(2,1)S(1)} %copy-done.3, f32[256,512]{1,0:T(8,128)S(1)} %get-tuple-element.84.inner_ref, ...), custom_call_target="tpu_custom_call" | custom-call | flops 1 | bytes 1 | tf_op jit(solution)/shard_map/outer_grad/pallas_call | solution.py:305
  (50 shorter events, 11.4 us)
Async XLA Ops:
  0.6 29.8 %copy-start = (bf16[256,1536]{1,0:T(8,128)(2,1)S(1)}, bf16[256,1536]{1,0:T(8,128)(2,1)}, u32[]{:S(2)}) copy-start(bf16[256,1536]{1,0:T(8,128)(2,1)} %grad_ref.1) | copy-start | bytes 2359300
  0.6 27.1 %copy-start.7 = (f32[256]{0:T(256)S(1)}, f32[256]{0:T(256)}, u32[]{:S(2)}) copy-start(f32[256]{0:T(256)} %param.11) | copy-start | bytes 3076
  3.8 7.4 %collective-permute-start = (bf16[256,1536]{1,0:T(8,128)(2,1)}, bf16[256,1536]{1,0:T(8,128)(2,1)S(1)}, u32[]{:S(2)}, u32[]{:S(2)}) collective-permute-start(bf16[256,1536]{1,0:T(8,128)(2,1)} %grad_ref.1), channel_id=1, source_target_pairs={{0,4},{4,0},{8,12},{12,8},{16,20},{20,16},{24,28},{28,24},{1,5},{5... | collective-permute-start | bytes 2359304 | tf_op jit(solution)/shard_map/ppermute | solution.py:342
  6.7 4.5 %collective-permute-start.1 = (bf16[272,384]{1,0:T(8,128)(2,1)}, bf16[272,384]{1,0:T(8,128)(2,1)S(1)}, u32[]{:S(2)}, u32[]{:S(2)}) collective-permute-start(bf16[272,384]{1,0:T(8,128)(2,1)} %get-tuple-element.54.send_ref), channel_id=1, source_target_pairs={{0,4},{4,0},{8,12},{12,8},{16,20},{20,16},{24,28},{28,24},{1,5},{5... | collective-permute-start | bytes 626696 | tf_op jit(solution)/shard_map/ppermute | solution.py:342
  6.8 16.6 %collective-permute-start.5 = (bf16[64,1536]{1,0:T(8,128)(2,1)S(1)}, bf16[64,1536]{1,0:T(8,128)(2,1)S(1)}, u32[]{:S(2)}, u32[]{:S(2)}) collective-permute-start(bf16[64,1536]{1,0:T(8,128)(2,1)S(1)} %dynamic_slice.13), channel_id=1, source_target_pairs={{0,3},{1,2},{2,1},{3,0},{4,7},{5,6},{6,5},{7,4},{8,11},{9,10},{10,... | collective-permute-start | bytes 589832 | tf_op jit(solution)/shard_map/ppermute | solution.py:339
  10.6 21.0 %collective-permute-start.7 = (bf16[128,1536]{1,0:T(8,128)(2,1)}, bf16[128,1536]{1,0:T(8,128)(2,1)S(1)}, u32[]{:S(2)}, u32[]{:S(2)}) collective-permute-start(bf16[128,1536]{1,0:T(8,128)(2,1)} %get-tuple-element.95), channel_id=1, source_target_pairs={{0,1},{1,0},{2,3},{3,2},{4,5},{5,4},{6,7},{7,6},{8,9},{9,8},{10,11... | collective-permute-start | bytes 1179656 | tf_op jit(solution)/shard_map/ppermute | solution.py:339
  11.2 20.5 %collective-permute-start.8 = (bf16[128,1536]{1,0:T(8,128)(2,1)}, bf16[128,1536]{1,0:T(8,128)(2,1)S(1)}, u32[]{:S(2)}, u32[]{:S(2)}) collective-permute-start(bf16[128,1536]{1,0:T(8,128)(2,1)} %get-tuple-element.94), channel_id=1, source_target_pairs={{0,2},{1,3},{2,0},{3,1},{4,6},{5,7},{6,4},{7,5},{8,10},{9,11},{10,... | collective-permute-start | bytes 1179656 | tf_op jit(solution)/shard_map/ppermute | solution.py:339
  14.9 9.8 %collective-permute-start.2 = (bf16[144,128]{1,0:T(8,128)(2,1)S(1)}, bf16[144,128]{1,0:T(8,128)(2,1)S(1)}, u32[]{:S(2)}, u32[]{:S(2)}) collective-permute-start(bf16[144,128]{1,0:T(8,128)(2,1)S(1)} %get-tuple-element.62), channel_id=1, source_target_pairs={{0,8},{4,12},{8,16},{12,20},{16,24},{20,28},{1,9},{5,13},{9,17},{1... | collective-permute-start | bytes 110600 | tf_op jit(solution)/shard_map/ppermute | solution.py:348
  18.9 8.8 %collective-permute-start.3 = (bf16[144,128]{1,0:T(8,128)(2,1)S(1)}, bf16[144,128]{1,0:T(8,128)(2,1)S(1)}, u32[]{:S(2)}, u32[]{:S(2)}) collective-permute-start(bf16[144,128]{1,0:T(8,128)(2,1)S(1)} %get-tuple-element.62), channel_id=1, source_target_pairs={{0,16},{4,20},{8,24},{12,28},{1,17},{5,21},{9,25},{13,29},{2,18},{... | collective-permute-start | bytes 110600 | tf_op jit(solution)/shard_map/ppermute | solution.py:348
  23.4 4.3 %collective-permute-start.4 = (bf16[144,128]{1,0:T(8,128)(2,1)S(1)}, bf16[144,128]{1,0:T(8,128)(2,1)S(1)}, u32[]{:S(2)}, u32[]{:S(2)}) collective-permute-start(bf16[144,128]{1,0:T(8,128)(2,1)S(1)} %get-tuple-element.62), channel_id=1, source_target_pairs={{0,24},{4,28},{1,25},{5,29},{2,26},{6,30},{3,27},{7,31}} | collective-permute-start | bytes 110600 | tf_op jit(solution)/shard_map/ppermute | solution.py:348
  24.7 5.7 %collective-permute-start.6 = (bf16[64,1536]{1,0:T(8,128)(2,1)S(1)}, bf16[64,1536]{1,0:T(8,128)(2,1)S(1)}, u32[]{:S(2)}, u32[]{:S(2)}) collective-permute-start(bf16[64,1536]{1,0:T(8,128)(2,1)S(1)} %collective-permute-done.5.refs_1_), channel_id=1, source_target_pairs={{0,8},{4,12},{8,0},{12,4},{16,24},{20,28},{24,16},{28,20},{1,9},{5... | collective-permute-start | bytes 589832 | tf_op jit(solution)/shard_map/ppermute | solution.py:345
  32.9 15.7 %collective-permute-start.10 = (bf16[256,1536]{1,0:T(8,128)(2,1)S(1)}, bf16[256,1536]{1,0:T(8,128)(2,1)S(1)}, u32[]{:S(2)}, u32[]{:S(2)}) collective-permute-start(bf16[256,1536]{1,0:T(8,128)(2,1)S(1)} %get-tuple-element.74.refs_1_), channel_id=1, source_target_pairs={{0,4},{4,0},{8,12},{12,8},{16,20},{20,16},{24,28},{28,24},{1,5},{5... | collective-permute-start | bytes 2359304 | tf_op jit(solution)/shard_map/ppermute | solution.py:342
  32.9 15.6 %collective-permute-start.9 = (bf16[128,1536]{1,0:T(8,128)(2,1)S(1)}, bf16[128,1536]{1,0:T(8,128)(2,1)S(1)}, u32[]{:S(2)}, u32[]{:S(2)}) collective-permute-start(bf16[128,1536]{1,0:T(8,128)(2,1)S(1)} %get-tuple-element.69.refs_0_), channel_id=1, source_target_pairs={{0,4},{4,0},{8,12},{12,8},{16,20},{20,16},{24,28},{28,24},{1,5},{5... | collective-permute-start | bytes 1179656 | tf_op jit(solution)/shard_map/ppermute | solution.py:342
  33.4 9.2 %collective-permute-start.12 = (bf16[4,256,128]{2,1,0:T(8,128)(2,1)S(1)}, bf16[4,256,128]{2,1,0:T(8,128)(2,1)S(1)}, u32[]{:S(2)}, u32[]{:S(2)}) collective-permute-start(bf16[4,256,128]{2,1,0:T(8,128)(2,1)S(1)} %get-tuple-element.75), channel_id=1, source_target_pairs={{0,1},{1,0},{2,3},{3,2},{4,5},{5,4},{6,7},{7,6},{8,9},{9,8},{10,11... | collective-permute-start | bytes 786440 | tf_op jit(solution)/shard_map/ppermute | solution.py:339
  34.9 13.6 %collective-permute-start.13 = (bf16[4,256,128]{2,1,0:T(8,128)(2,1)S(1)}, bf16[4,256,128]{2,1,0:T(8,128)(2,1)S(1)}, u32[]{:S(2)}, u32[]{:S(2)}) collective-permute-start(bf16[4,256,128]{2,1,0:T(8,128)(2,1)S(1)} %get-tuple-element.76), channel_id=1, source_target_pairs={{0,2},{1,3},{2,0},{3,1},{4,6},{5,7},{6,4},{7,5},{8,10},{9,11},{10,... | collective-permute-start | bytes 786440 | tf_op jit(solution)/shard_map/ppermute | solution.py:339
  36.4 12.1 %collective-permute-start.11 = (bf16[4,256,128]{2,1,0:T(8,128)(2,1)S(1)}, bf16[4,256,128]{2,1,0:T(8,128)(2,1)S(1)}, u32[]{:S(2)}, u32[]{:S(2)}) collective-permute-start(bf16[4,256,128]{2,1,0:T(8,128)(2,1)S(1)} %get-tuple-element.71), channel_id=1, source_target_pairs={{0,3},{1,2},{2,1},{3,0},{4,7},{5,6},{6,5},{7,4},{8,11},{9,10},{10,... | collective-permute-start | bytes 786440 | tf_op jit(solution)/shard_map/ppermute | solution.py:339
  49.8 6.4 %collective-permute-start.15 = (bf16[144,128]{1,0:T(8,128)(2,1)S(1)}, bf16[144,128]{1,0:T(8,128)(2,1)S(1)}, u32[]{:S(2)}, u32[]{:S(2)}) collective-permute-start(bf16[144,128]{1,0:T(8,128)(2,1)S(1)} %get-tuple-element.86), channel_id=1, source_target_pairs={{8,0},{12,4},{16,8},{20,12},{24,16},{28,20},{9,1},{13,5},{17,9},{2... | collective-permute-start | bytes 110600 | tf_op jit(solution)/shard_map/ppermute | solution.py:348
  51.2 7.0 %collective-permute-start.16 = (bf16[144,128]{1,0:T(8,128)(2,1)S(1)}, bf16[144,128]{1,0:T(8,128)(2,1)S(1)}, u32[]{:S(2)}, u32[]{:S(2)}) collective-permute-start(bf16[144,128]{1,0:T(8,128)(2,1)S(1)} %get-tuple-element.86), channel_id=1, source_target_pairs={{16,0},{20,4},{24,8},{28,12},{17,1},{21,5},{25,9},{29,13},{18,2},{... | collective-permute-start | bytes 110600 | tf_op jit(solution)/shard_map/ppermute | solution.py:348
  52.5 8.8 %collective-permute-start.17 = (bf16[144,128]{1,0:T(8,128)(2,1)S(1)}, bf16[144,128]{1,0:T(8,128)(2,1)S(1)}, u32[]{:S(2)}, u32[]{:S(2)}) collective-permute-start(bf16[144,128]{1,0:T(8,128)(2,1)S(1)} %get-tuple-element.86), channel_id=1, source_target_pairs={{24,0},{28,4},{25,1},{29,5},{26,2},{30,6},{27,3},{31,7}} | collective-permute-start | bytes 110600 | tf_op jit(solution)/shard_map/ppermute | solution.py:348
  61.3 4.7 %collective-permute-start.18 = (f32[256,512]{1,0:T(8,128)S(1)}, f32[256,512]{1,0:T(8,128)S(1)}, u32[]{:S(2)}, u32[]{:S(2)}) collective-permute-start(f32[256,512]{1,0:T(8,128)S(1)} %get-tuple-element.87), channel_id=1, source_target_pairs={{0,4},{4,0},{8,12},{12,8},{16,20},{20,16},{24,28},{28,24},{1,5},{5... | collective-permute-start | bytes 1572872 | tf_op jit(solution)/shard_map/ppermute | solution.py:342
  61.3 2.3 %collective-permute-start.14 = (bf16[4,256,128]{2,1,0:T(8,128)(2,1)S(1)}, bf16[4,256,128]{2,1,0:T(8,128)(2,1)S(1)}, u32[]{:S(2)}, u32[]{:S(2)}) collective-permute-start(bf16[4,256,128]{2,1,0:T(8,128)(2,1)S(1)} %get-tuple-element.80), channel_id=1, source_target_pairs={{0,4},{4,0},{8,12},{12,8},{16,20},{20,16},{24,28},{28,24},{1,5},{5... | collective-permute-start | bytes 786440 | tf_op jit(solution)/shard_map/ppermute | solution.py:342
  61.8 4.2 %collective-permute-start.19 = (bf16[144,128]{1,0:T(8,128)(2,1)S(1)}, bf16[144,128]{1,0:T(8,128)(2,1)S(1)}, u32[]{:S(2)}, u32[]{:S(2)}) collective-permute-start(bf16[144,128]{1,0:T(8,128)(2,1)S(1)} %collective-permute-done.15.refs_0_), channel_id=1, source_target_pairs={{0,4},{4,0},{8,12},{12,8},{16,20},{20,16},{24,28},{28,24},{1,5},{5... | collective-permute-start | bytes 110600 | tf_op jit(solution)/shard_map/ppermute | solution.py:342
  61.8 4.2 %collective-permute-start.20 = (bf16[144,128]{1,0:T(8,128)(2,1)S(1)}, bf16[144,128]{1,0:T(8,128)(2,1)S(1)}, u32[]{:S(2)}, u32[]{:S(2)}) collective-permute-start(bf16[144,128]{1,0:T(8,128)(2,1)S(1)} %collective-permute-done.16.refs_1_), channel_id=1, source_target_pairs={{0,4},{4,0},{8,12},{12,8},{16,20},{20,16},{24,28},{28,24},{1,5},{5... | collective-permute-start | bytes 110600 | tf_op jit(solution)/shard_map/ppermute | solution.py:342
  62.3 3.7 %collective-permute-start.21 = (bf16[144,128]{1,0:T(8,128)(2,1)S(1)}, bf16[144,128]{1,0:T(8,128)(2,1)S(1)}, u32[]{:S(2)}, u32[]{:S(2)}) collective-permute-start(bf16[144,128]{1,0:T(8,128)(2,1)S(1)} %collective-permute-done.17.refs_2_), channel_id=1, source_target_pairs={{0,4},{4,0},{8,12},{12,8},{16,20},{20,16},{24,28},{28,24},{1,5},{5... | collective-permute-start | bytes 110600 | tf_op jit(solution)/shard_map/ppermute | solution.py:342
  (6 other events, 35.5 us)

commit v6 on v5

--- a/solution.py
+++ b/solution.py
@@ -99,33 +99,16 @@
     return pl.ds(pl.multiple_of(number * count, count), count)
 
 
-def pack_kernel(where_ref, decay_ref, q_ref, k_ref, v_ref, send_ref, keep_ref):
+def fresh_kernel(
+    where_ref, q_ref, k_ref, v_ref, q_got, k_got, v_got, decay_ref, decay_got, q_out, k_out, v_out, col_ref, row_ref, first_ref, message_ref
+):
     core = where_ref[0]
-    length = keep_ref.shape[0]
-    for number, ref in enumerate((q_ref, k_ref, v_ref)):
-        part = slice(number * HD, (number + 1) * HD)
-        send_ref[0:length, part] = ref[:, lanes_of(1 - core)]
-        keep_ref[:, part] = ref[:, lanes_of(core)]
-    decay = jnp.where(core == 0, decay_ref[1:2, :], decay_ref[0:1, :])
-    first = decay.astype(BF16).astype(F32)
-    second = (decay - first).astype(BF16).astype(F32)
-    third = decay - first - second
-    at = lax.broadcasted_iota(jnp.int32, (TAIL, length), 0)
-    tail = jnp.where(at == 0, first, jnp.where(at == 1, second, jnp.where(at == 2, third, 0.0)))
-    send_ref[length : length + TAIL, :] = jnp.zeros((TAIL, send_ref.shape[1]), BF16)
-    send_ref[length : length + TAIL, 0:length] = tail.astype(BF16)
-
-
-def fresh_kernel(where_ref, keep_ref, got_ref, decay_ref, q_out, k_out, v_out, col_ref, row_ref, first_ref, message_ref):
-    core = where_ref[0]
-    length = keep_ref.shape[0]
-    for number, out in enumerate((q_out, k_out, v_out)):
-        part = slice(number * HD, (number + 1) * HD)
-        out[core] = keep_ref[:, part]
-        out[1 - core] = got_ref[0:length, part]
+    length = q_ref.shape[0]
+    for out, ref, got in ((q_out, q_ref, q_got), (k_out, k_ref, k_got), (v_out, v_ref, v_got)):
+        out[core] = ref[:, lanes_of(core)]
+        out[1 - core] = got[:, lanes_of(core)]
     mine = jnp.where(core == 0, decay_ref[0:1, :], decay_ref[1:2, :])
-    tail = got_ref[length : length + TAIL, 0:length].astype(F32)
-    theirs = tail[0:1] + tail[1:2] + tail[2:3]
+    theirs = jnp.where(core == 0, decay_got[0:1, :], decay_got[1:2, :])
     block = lax.broadcasted_iota(jnp.int32, (2, length), 0)
     decay = jnp.where(block == core, mine, theirs)
     lower = triangle(length)
@@ -179,7 +162,7 @@
         normed_ref[b] = (mixed * scale_of(mixed) * gain).astype(BF16)
 
 
-def partial_kernel(kinds, where_ref, grad_ref, got_ref, normed_ref, *refs):
+def partial_kernel(kinds, where_ref, grad_ref, got_ref, *refs):
     core, side = where_ref[0], where_ref[1]
     refs = list(refs)
     inputs = [[refs.pop(0) for _ in range(2 if kind == "halves" else 1)] for kind in kinds]
@@ -199,18 +182,11 @@
         product = dot(ref[...], weight, NT)
         for number, out in enumerate(products):
             out[block] = product[:, number * HD : (number + 1) * HD].astype(out.dtype)
-    for out in products:
-        if out.shape[0] == 4:
-            out[2:4] = normed_ref[...]
-
-
-def grad_mixed_kernel(where_ref, q_ref, col_ref, gain_ref, mixed_ref, normed_ref, own_ref, *refs):
-    part_refs, (grad_ref, second_ref, message_ref, cross_ref) = refs[:-4], refs[-4:]
+
+
+def grad_mixed_kernel(where_ref, q_ref, col_ref, gain_ref, mixed_ref, own_ref, *refs):
+    part_refs, (grad_ref, second_ref, message_ref) = refs[:-3], refs[-3:]
     columns = col_ref[...]
-    other = 1 - where_ref[0]
-    cross_ref[0] = normed_ref[other]
-    for number, ref in enumerate(part_refs):
-        cross_ref[number + 1] = ref[2 + other]
     gain = gain_ref[:, lanes_of(where_ref[0])]
     ups = []
     for b in range(2):
@@ -230,9 +206,12 @@
 
 
 def inner_grad_kernel(
-    where_ref, q_ref, k_ref, v_ref, col_ref, row_ref, grad_ref, state_ref, second_ref, keep_ref, send_ref
+    where_ref, q_ref, k_ref, v_ref, col_ref, row_ref, grad_ref, state_ref, second_ref, *refs
 ):
+    normed_refs, (keep_ref, send_ref, cross_ref) = refs[:-3], refs[-3:]
     core = where_ref[0]
+    for number, ref in enumerate(normed_refs):
+        cross_ref[number] = ref[1 - core]
     columns, across = col_ref[...], row_ref[...]
     length = columns.shape[0]
     lower = triangle(length)
@@ -259,17 +238,16 @@
         send_ref[:, part] = jnp.where(core == 0, late, early)
 
 
-def outer_grad_kernel(count, where_ref, keep_ref, send_ref, inner_ref, inner_got_ref, *refs):
+def outer_grad_kernel(count, where_ref, k_ref, v_ref, inner_ref, inner_got_ref, *refs):
     core = where_ref[0]
-    length = keep_ref.shape[0]
     outs = refs[2 * count :]
-    for head, rows, inner, chip_refs in (
-        (core, keep_ref, inner_ref, refs[:count]),
-        (1 - core, send_ref, inner_got_ref, refs[count : 2 * count]),
+    for head, inner, chip_refs in (
+        (core, inner_ref, refs[:count]),
+        (1 - core, inner_got_ref, refs[count : 2 * count]),
     ):
         high, low = split(chip_sum(chip_refs))
         fade = inner[:, 3 * HD : 4 * HD]
-        k, v = rows[0:length, HD : 2 * HD], rows[0:length, 2 * HD : 3 * HD]
+        k, v = k_ref[:, lanes_of(head)], v_ref[:, lanes_of(head)]
         outs[0][:, lanes_of(head)] = inner[:, 0:HD].astype(BF16)
         key = inner[:, HD : 2 * HD] + fade * (dot(v, high, NT) + dot(v, low, NT))
         outs[1][:, lanes_of(head)] = key.astype(BF16)
@@ -279,9 +257,9 @@
 
 def layer_kernel(pairs, where_ref, own_ref, *refs):
     mine_refs, theirs_refs = refs[:pairs], refs[pairs : 2 * pairs]
-    normed_ref, *sent_refs, got_ref, out_ref = refs[2 * pairs :]
+    *normed_refs, got_ref, out_ref = refs[2 * pairs :]
     core = where_ref[0]
-    mine = [normed_ref[core]] + [ref[2 + core] for ref in sent_refs]
+    mine = [ref[core] for ref in normed_refs]
     theirs = [got_ref[number] for number in range(got_ref.shape[0])]
     normed = [mine[0], theirs[0], mine[1], theirs[1]]
     for begin in range(2, len(mine), 2):
@@ -371,32 +349,22 @@
 
     slices = [slice_for(step, halves) for step, halves in plan]
     arriving = [swap_tensor(piece, step) for piece, step in zip(slices, order)]
-    queries, keys, values, out_grad = after([queries, keys, values, out_grad], *slices)
-    send, keep = call(
-        pack_kernel,
-        "pack",
-        [shape(BF16, length + TAIL, 3 * HD), shape(BF16, length, 3 * HD)],
-        [where, log_decay, queries, keys, values],
-        grant=60,
-    )
-    got = swap_core(send)
-    grad_got = swap_core(out_grad)
-    (got,) = after([got], grad_got)
+    got = [swap_core(rows) for rows in (queries, keys, values)]
+    got.append(swap_core(log_decay))
+    (weight,) = after([out_weight], *slices)
+    weight_own = lax.dynamic_slice(weight, (0, place * width), (columns, width))
+    got = after(got, weight_own)
+    (grad,) = after([out_grad], *got)
+    grad_got = swap_core(grad)
     q, k, v, col, row, first, fresh = call(
         fresh_kernel,
         "fresh",
         [pair16, pair16, pair16, shape(F32, length, 2), shape(F32, 2, length), shape(F32, HD, HD), message],
-        [where, keep, got, log_decay],
-    )
+        [where, queries, keys, values, *got[:3], log_decay, got[3]],
+    )
+    (fresh,) = after([fresh], grad_got)
     arrived = [to_chip(fresh, step) for step in range(1, chips)]
     (inner,) = call(without_where(inner_kernel), "inner", [pair32], [where, q, k, v, col, row, first])
-    mixed, normed, states = call(
-        mixed_kernel,
-        "mixed",
-        [pair32, pair16, shape(F32, 2, HD, HD)],
-        [where, q, col, inner, gain, first, *arrived],
-    )
-    weight_own = lax.dynamic_slice(out_weight, (0, place * width), (columns, width))
     pieces = [("own", [weight_own])]
     for (step, halves), piece in zip(plan, arriving):
         if halves:
@@ -405,16 +373,12 @@
     partials, mine, theirs = [], [], []
     for number in range(0, tensor, 2):
         kinds, sources = zip(*pieces[number : number + 2])
-        sources = after(sum(sources, []), mixed, *partials)
+        sources = after(sum(sources, []), *arrived, inner, *partials)
         *outs, weight = call(
             functools.partial(partial_kernel, kinds),
             "partial",
-            [
-                shape(BF16, 4, length, HD) if number else pair32,
-                shape(BF16, 4, length, HD),
-                shape(BF16, 2 * HD if number else HD, width),
-            ],
-            [where, out_grad, grad_got, normed, *sources],
+            [pair16 if number else pair32, pair16, shape(BF16, 2 * HD if number else HD, width)],
+            [where, out_grad, grad_got, *sources],
         )
         partials += outs
         mine.append(weight)
@@ -422,34 +386,42 @@
             theirs.append(swap_core(weight))
     own_partial, *partials = partials
     sent = [swap_tensor(partial, step) for partial, step in zip(partials, order)]
-    theirs += [swap_core(weight) for weight in mine[1:]]
-    grad_mixed, second, upward, cross = call(
+    mixed, normed, states = call(
+        mixed_kernel,
+        "mixed",
+        [pair32, pair16, shape(F32, 2, HD, HD)],
+        [where, q, col, inner, gain, first, *after(arrived, *partials)],
+    )
+    normed_all = [normed] + [swap_tensor(normed, step) for step in order]
+    grad_mixed, second, upward = call(
         grad_mixed_kernel,
         "grad_mixed",
-        [pair32, shape(F32, HD, HD), message, shape(BF16, tensor, length, HD)],
-        [where, q, col, gain, mixed, normed, own_partial, *after(sent, *theirs)],
-    )
+        [pair32, shape(F32, HD, HD), message],
+        [where, q, col, gain, mixed, own_partial, *sent],
+    )
+    (upward,) = after([upward], *normed_all)
     returned = [to_chip(upward, -step) for step in range(1, chips)]
-    cross_got = swap_core(cross)
-    inner_keep, inner_send = call(
+    theirs += [swap_core(weight) for weight in after(mine[1:], upward)]
+    inner_keep, inner_send, cross = call(
         inner_grad_kernel,
         "inner_grad",
-        [shape(F32, length, 4 * HD)] * 2,
-        [where, q, k, v, col, row, grad_mixed, states, second],
-    )
+        [shape(F32, length, 4 * HD)] * 2 + [shape(BF16, tensor, length, HD)],
+        [where, q, k, v, col, row, grad_mixed, states, second, *normed_all],
+    )
+    cross_got = swap_core(cross)
     inner_got = swap_core(*after([inner_send], *returned))
     (layer_out,) = call(
         functools.partial(layer_kernel, tensor // 2),
         "layer",
         [shape(BF16, length, width)],
-        [where, weight_own, *mine, *theirs, normed, *sent, cross_got],
+        [where, weight_own, *mine, *theirs, *normed_all, cross_got],
     )
     returned_got = after([swap_core(rows) for rows in returned], layer_out)
     query_grad, key_grad, value_grad = call(
         functools.partial(outer_grad_kernel, chips - 1),
         "outer_grad",
         [both16] * 3,
-        [where, keep, send, inner_keep, inner_got, *returned, *returned_got],
+        [where, keys, values, inner_keep, inner_got, *returned, *returned_got],
     )
     return layer_out, query_grad, key_grad, value_grad
 

time: 68 us -> 64.5 us (0.949)
  starting transfers between devices: 23.9 us -> 31.3 us
  waiting for transfers between devices: 20.3 us -> 15.8 us
  local copies, waits for them, and re-layouts: 7.19 us -> 3.34 us
  Pallas kernels: 14.7 us -> 12.8 us
    ppermute x6 -> x9, waiting for transfers between devices: 11.6 us -> 7.75 us  [swap_tensor(): return lax.ppermute(value, 'tensor', [(i, i ^ k) for i in range(tensor)])]
    ppermute x6 -> x9, starting transfers between devices: 7.95 us -> 11.3 us  [swap_tensor(): return lax.ppermute(value, 'tensor', [(i, i ^ k) for i in range(tensor)])]
    unnamed x16 -> x12, local copies, waits for them, and re-layouts: 2.93 us -> 0.03 us
    ppermute x1, starting transfers between devices: 0.07 us -> 1.98 us  [swap_side(): return lax.ppermute(value, 'seq', [(i, i ^ 2) for i in range(seq)])]
    pallas_call x10 -> x9, Pallas kernels: 14.7 us -> 12.8 us  [call(): pl.pallas_call(kernel, name=name, out_shape=outs, in_specs=[SMEM] + [VMEM...]
    ppermute x1, waiting for transfers between devices: 1.78 us -> 0.01 us  [swap_side(): return lax.ppermute(value, 'seq', [(i, i ^ 2) for i in range(seq)])]
    ppermute x6, starting transfers between devices: 13.8 us -> 15 us  [to_chip(): lax.ppermute(value, 'seq', [(i, i + 2 * step) for i in range(seq) if 0 <=...]
    ppermute x9 -> x12, starting transfers between devices: 2.1 us -> 3.14 us  [swap_core(): return lax.ppermute(value, 'seq', [(i, i ^ 1) for i in range(seq)])]
  transfers between devices with their start and end apart: 22 -> 28, of which waited for: 7 -> 7; matrix products, arithmetic and copies ran while one was open for 3% -> 5% of each run, Pallas kernels for 16% -> 16%
where the time goes in v6:
time: 64.5 us; the launch traced here: 64.2 us
  starting transfers between devices  31.3 us (49%)
  waiting for transfers between devices  15.8 us (24%)
  Pallas kernels  12.8 us (20%)
  local copies, waits for them, and re-layouts  3.34 us (5%)
  between operations  0.92 us (1%)
    ppermute x6, starting transfers between devices, to_chip(): lax.ppermute(value, 'seq', [(i, i + 2 * step) for i in range(seq) if 0 <=...  15 us
    pallas_call x9, Pallas kernels, call(): pl.pallas_call(kernel, name=name, out_shape=outs, in_specs=[SMEM] + [VMEM...  12.8 us
    ppermute x9, starting transfers between devices, swap_tensor(): return lax.ppermute(value, 'tensor', [(i, i ^ k) for i in range(tensor)])  11.3 us
    ppermute x9, waiting for transfers between devices, swap_tensor(): return lax.ppermute(value, 'tensor', [(i, i ^ k) for i in range(tensor)])  7.75 us
    ppermute x6, waiting for transfers between devices, to_chip(): lax.ppermute(value, 'seq', [(i, i + 2 * step) for i in range(seq) if 0 <=...  6.15 us
    ppermute x12, starting transfers between devices, swap_core(): return lax.ppermute(value, 'seq', [(i, i ^ 1) for i in range(seq)])  3.14 us
    dynamic_slice x2, local copies, waits for them, and re-layouts, slice_for(): lax.dynamic_slice(out_weight, (begin, (place ^ step) * width), (rows, wid...  2.12 us
    ppermute x1, starting transfers between devices, swap_side(): return lax.ppermute(value, 'seq', [(i, i ^ 2) for i in range(seq)])  1.98 us
  transfers between devices with their start and end apart: 28, of which 7 were waited for; matrix products, arithmetic and copies ran while one was open for 5% of the time, Pallas kernels for 16%

profile of v6, /device:TPU:0, one launch (start us, length us, event | category | flops | bytes accessed | tf_op | source)
XLA Modules:
  0.0 64.2 jit_solution(5708983273872561491)
XLA Ops:
  2.7 1.2 %fusion = (bf16[128,1536]{1,0:T(8,128)(2,1)S(1)}, bf16[128,1536]{1,0:T(8,128)(2,1)S(1)}) fusion(bf16[256,6144]{1,0:T(8,128)(2,1)} %param.12, s32[]{:T(128)S(6)} %select_n.27, s32[]{:T(128)S(6)} %select_n.29, s32[]{:T(128)S(6)} %select_n.28), kind=kLoop, calls=%fused_computation.2 | loop fusion | bytes 1572876 | tf_op jit(solution)/shard_map/dynamic_slice | solution.py:348
  3.9 1.2 %constant_dynamic-slice_fusion.refs_0_.own_ref = bf16[256,1536]{1,0:T(8,128)(2,1)S(1)} fusion(bf16[256,6144]{1,0:T(8,128)(2,1)} %param.12, s32[]{:T(128)S(6)} %select_n.30), kind=kLoop, calls=%fused_computation.1 | loop fusion | bytes 1572868 | tf_op jit(solution)/shard_map/dynamic_slice | solution.py:355
  5.7 3.5 %collective-permute-start.5 = (bf16[64,1536]{1,0:T(8,128)(2,1)S(1)}, bf16[64,1536]{1,0:T(8,128)(2,1)S(1)}, u32[]{:S(2)}, u32[]{:S(2)}) collective-permute-start(bf16[64,1536]{1,0:T(8,128)(2,1)S(1)} %dynamic_slice.12), channel_id=1, source_target_pairs={{0,3},{1,2},{2,1},{3,0},{4,7},{5,6},{6,5},{7,4},{8,11},{9,10},{10,... | collective-permute-start | bytes 589832 | tf_op jit(solution)/shard_map/ppermute | solution.py:317
  9.9 1.4 %fresh.1 = (bf16[2,256,128]{2,1,0:T(8,128)(2,1)S(1)}, bf16[2,256,128]{2,1,0:T(8,128)(2,1)S(1)}, bf16[2,256,128]{2,1,0:T(8,128)(2,1)S(1)}, f32[256,2]{1,0:T(8,128...) custom-call(s32[2]{0:T(128)S(1)} %pad_add_fusion.where_ref, ...), custom_call_target="tpu_custom_call" | custom-call | flops 1 | bytes 1 | tf_op jit(solution)/shard_map/fresh/pallas_call | solution.py:283
  11.4 3.6 %collective-permute-done.5.refs_1_ = bf16[64,1536]{1,0:T(8,128)(2,1)S(1)} collective-permute-done((bf16[64,1536]{1,0:T(8,128)(2,1)S(1)}, bf16[64,1536]{1,0:T(8,128)(2,1)S(1)}, u32[]{:S(2)}, u32[]{:S(2)}) %collective-permute-start.5) | collective-permute-done | bytes 196640 | tf_op jit(solution)/shard_map/ppermute | solution.py:317
  15.0 2.0 %collective-permute-start.6 = (bf16[64,1536]{1,0:T(8,128)(2,1)S(1)}, bf16[64,1536]{1,0:T(8,128)(2,1)S(1)}, u32[]{:S(2)}, u32[]{:S(2)}) collective-permute-start(bf16[64,1536]{1,0:T(8,128)(2,1)S(1)} %collective-permute-done.5.refs_1_), channel_id=1, source_target_pairs={{0,8},{4,12},{8,0},{12,4},{16,24},{20,28},{24,16},{28,20},{1,9},{5... | collective-permute-start | bytes 589832 | tf_op jit(solution)/shard_map/ppermute | solution.py:323
  17.0 1.9 %collective-permute-start.7 = (bf16[144,128]{1,0:T(8,128)(2,1)S(1)}, bf16[144,128]{1,0:T(8,128)(2,1)S(1)}, u32[]{:S(2)}, u32[]{:S(2)}) collective-permute-start(bf16[144,128]{1,0:T(8,128)(2,1)S(1)} %get-tuple-element.58), channel_id=1, source_target_pairs={{0,8},{4,12},{8,16},{12,20},{16,24},{20,28},{1,9},{5,13},{9,17},{1... | collective-permute-start | bytes 110600 | tf_op jit(solution)/shard_map/ppermute | solution.py:326
  18.9 4.9 %collective-permute-start.8 = (bf16[144,128]{1,0:T(8,128)(2,1)S(1)}, bf16[144,128]{1,0:T(8,128)(2,1)S(1)}, u32[]{:S(2)}, u32[]{:S(2)}) collective-permute-start(bf16[144,128]{1,0:T(8,128)(2,1)S(1)} %get-tuple-element.58), channel_id=1, source_target_pairs={{0,16},{4,20},{8,24},{12,28},{1,17},{5,21},{9,25},{13,29},{2,18},{... | collective-permute-start | bytes 110600 | tf_op jit(solution)/shard_map/ppermute | solution.py:326
  23.8 4.3 %collective-permute-start.9 = (bf16[144,128]{1,0:T(8,128)(2,1)S(1)}, bf16[144,128]{1,0:T(8,128)(2,1)S(1)}, u32[]{:S(2)}, u32[]{:S(2)}) collective-permute-start(bf16[144,128]{1,0:T(8,128)(2,1)S(1)} %get-tuple-element.58), channel_id=1, source_target_pairs={{0,24},{4,28},{1,25},{5,29},{2,26},{6,30},{3,27},{7,31}} | collective-permute-start | bytes 110600 | tf_op jit(solution)/shard_map/ppermute | solution.py:326
  29.7 1.2 %partial.2 = (f32[2,256,128]{2,1,0:T(8,128)S(1)}, bf16[2,256,128]{2,1,0:T(8,128)(2,1)S(1)}, bf16[128,1536]{1,0:T(8,128)(2,1)S(1)}) custom-call(s32[2]{0:T(128)S(1)} %pad_add_fusion.where_ref, bf16[256,1536]{1,0:T(8,128)(2,1)S(1)} %copy-done, bf16[256,1536]{1,0:T(8,128)(2,1)S(1)} %collective-permute-done.4.got_ref, ...), custom_call_target="tpu_custom_call" | custom-call | flops 1 | bytes 1 | tf_op jit(solution)/shard_map/partial/pallas_call | solution.py:283
  32.0 1.6 %collective-permute-start.14 = (bf16[2,256,128]{2,1,0:T(8,128)(2,1)S(1)}, bf16[2,256,128]{2,1,0:T(8,128)(2,1)S(1)}, u32[]{:S(2)}, u32[]{:S(2)}) collective-permute-start(bf16[2,256,128]{2,1,0:T(8,128)(2,1)S(1)} %get-tuple-element.75), channel_id=1, source_target_pairs={{0,1},{1,0},{2,3},{3,2},{4,5},{5,4},{6,7},{7,6},{8,9},{9,8},{10,11... | collective-permute-start | bytes 393224 | tf_op jit(solution)/shard_map/ppermute | solution.py:317
  33.6 1.5 %collective-permute-start.13 = (bf16[2,256,128]{2,1,0:T(8,128)(2,1)S(1)}, bf16[2,256,128]{2,1,0:T(8,128)(2,1)S(1)}, u32[]{:S(2)}, u32[]{:S(2)}) collective-permute-start(bf16[2,256,128]{2,1,0:T(8,128)(2,1)S(1)} %get-tuple-element.71), channel_id=1, source_target_pairs={{0,3},{1,2},{2,1},{3,0},{4,7},{5,6},{6,5},{7,4},{8,11},{9,10},{10,... | collective-permute-start | bytes 393224 | tf_op jit(solution)/shard_map/ppermute | solution.py:317
  36.5 2.5 %collective-permute-start.16 = (bf16[2,256,128]{2,1,0:T(8,128)(2,1)S(1)}, bf16[2,256,128]{2,1,0:T(8,128)(2,1)S(1)}, u32[]{:S(2)}, u32[]{:S(2)}) collective-permute-start(bf16[2,256,128]{2,1,0:T(8,128)(2,1)S(1)} %get-tuple-element.82.refs_0_.refs_4_), channel_id=1, source_target_pairs={{0,3},{1,2},{2,1},{3,0},{4,7},{5,6},{6,5},{7,4},{8,11},{9,10},{10,... | collective-permute-start | bytes 393224 | tf_op jit(solution)/shard_map/ppermute | solution.py:317
  40.1 3.9 %collective-permute-done.15.refs_2_ = bf16[2,256,128]{2,1,0:T(8,128)(2,1)S(1)} collective-permute-done((bf16[2,256,128]{2,1,0:T(8,128)(2,1)S(1)}, bf16[2,256,128]{2,1,0:T(8,128)(2,1)S(1)}, u32[]{:S(2)}, u32[]{:S(2)}) %collective-permute-start.15) | collective-permute-done | bytes 131104 | tf_op jit(solution)/shard_map/ppermute | solution.py:317
  44.0 1.2 %grad_mixed.1 = (f32[2,256,128]{2,1,0:T(8,128)S(1)}, f32[128,128]{1,0:T(8,128)S(1)}, bf16[144,128]{1,0:T(8,128)(2,1)S(1)}) custom-call(s32[2]{0:T(128)S(1)} %pad_add_fusion.where_ref, bf16[2,256,128]{2,1,0:T(8,128)(2,1)S(1)} %get-tuple-element.60.refs_0_.q_ref, f32[256,2]{1,0:T(8,128)S(1)} %get-tuple-element.63.refs_3_.col_ref, f32[1,256]{1,0:T(1,128)S(1)} %bitcast.4, ...), custom_call_target="tpu_custom_call" | custom-call | flops 1 | bytes 1 | tf_op jit(solution)/shard_map/grad_mixed/pallas_call | solution.py:283
  45.4 1.3 %collective-permute-start.21 = (bf16[144,128]{1,0:T(8,128)(2,1)S(1)}, bf16[144,128]{1,0:T(8,128)(2,1)S(1)}, u32[]{:S(2)}, u32[]{:S(2)}) collective-permute-start(bf16[144,128]{1,0:T(8,128)(2,1)S(1)} %get-tuple-element.83), channel_id=1, source_target_pairs={{8,0},{12,4},{16,8},{20,12},{24,16},{28,20},{9,1},{13,5},{17,9},{2... | collective-permute-start | bytes 110600 | tf_op jit(solution)/shard_map/ppermute | solution.py:326
  46.7 1.3 %collective-permute-start.22 = (bf16[144,128]{1,0:T(8,128)(2,1)S(1)}, bf16[144,128]{1,0:T(8,128)(2,1)S(1)}, u32[]{:S(2)}, u32[]{:S(2)}) collective-permute-start(bf16[144,128]{1,0:T(8,128)(2,1)S(1)} %get-tuple-element.83), channel_id=1, source_target_pairs={{16,0},{20,4},{24,8},{28,12},{17,1},{21,5},{25,9},{29,13},{18,2},{... | collective-permute-start | bytes 110600 | tf_op jit(solution)/shard_map/ppermute | solution.py:326
  48.0 1.3 %collective-permute-start.23 = (bf16[144,128]{1,0:T(8,128)(2,1)S(1)}, bf16[144,128]{1,0:T(8,128)(2,1)S(1)}, u32[]{:S(2)}, u32[]{:S(2)}) collective-permute-start(bf16[144,128]{1,0:T(8,128)(2,1)S(1)} %get-tuple-element.83), channel_id=1, source_target_pairs={{24,0},{28,4},{25,1},{29,5},{26,2},{30,6},{27,3},{31,7}} | collective-permute-start | bytes 110600 | tf_op jit(solution)/shard_map/ppermute | solution.py:326
  49.3 1.9 %inner_grad.1 = (f32[256,512]{1,0:T(8,128)S(1)}, f32[256,512]{1,0:T(8,128)S(1)}, bf16[4,256,128]{2,1,0:T(8,128)(2,1)S(1)}) custom-call(s32[2]{0:T(128)S(1)} %pad_add_fusion.where_ref, bf16[2,256,128]{2,1,0:T(8,128)(2,1)S(1)} %get-tuple-element.60.refs_0_.q_ref, bf16[2,256,128]{2,1,0:T(8,128)(2,1)S(1)} %get-tuple-element.61.refs_1_.k_ref, ...), custom_call_target="tpu_custom_call" | custom-call | flops 1 | bytes 1 | tf_op jit(solution)/shard_map/inner_grad/pallas_call | solution.py:283
  51.3 2.2 %collective-permute-done.22.refs_1_ = bf16[144,128]{1,0:T(8,128)(2,1)S(1)} collective-permute-done((bf16[144,128]{1,0:T(8,128)(2,1)S(1)}, bf16[144,128]{1,0:T(8,128)(2,1)S(1)}, u32[]{:S(2)}, u32[]{:S(2)}) %collective-permute-start.22) | collective-permute-done | bytes 36896 | tf_op jit(solution)/shard_map/ppermute | solution.py:326
  53.5 3.4 %collective-permute-done.23.refs_2_ = bf16[144,128]{1,0:T(8,128)(2,1)S(1)} collective-permute-done((bf16[144,128]{1,0:T(8,128)(2,1)S(1)}, bf16[144,128]{1,0:T(8,128)(2,1)S(1)}, u32[]{:S(2)}, u32[]{:S(2)}) %collective-permute-start.23) | collective-permute-done | bytes 36896 | tf_op jit(solution)/shard_map/ppermute | solution.py:326
  57.9 1.8 %collective-permute-done.20.refs_8_ = bf16[4,256,128]{2,1,0:T(8,128)(2,1)S(1)} collective-permute-done((bf16[4,256,128]{2,1,0:T(8,128)(2,1)S(1)}, bf16[4,256,128]{2,1,0:T(8,128)(2,1)S(1)}, u32[]{:S(2)}, u32[]{:S(2)}) %collective-permute-start.20) | collective-permute-done | bytes 262176 | tf_op jit(solution)/shard_map/ppermute | solution.py:320
  60.2 2.4 %layer.1 = bf16[256,1536]{1,0:T(8,128)(2,1)} custom-call(s32[2]{0:T(128)S(1)} %pad_add_fusion.where_ref, bf16[256,1536]{1,0:T(8,128)(2,1)S(1)} %constant_dynamic-slice_fusion.refs_0_.own_ref, bf16[128,1536]{1,0:T(8,128)(2,1)S(1)} %get-tuple-element.69.refs_0_, bf16[256,1536]{1,0:T(8,128)(2,1)S(1)} %get-tuple-element.84.refs_1_, ...), custom_call_target="tpu_custom_call" | custom-call | flops 1 | bytes 1 | tf_op jit(solution)/shard_map/layer/pallas_call | solution.py:283
  62.7 1.6 %outer_grad.1 = (bf16[256,256]{1,0:T(8,128)(2,1)}, bf16[256,256]{1,0:T(8,128)(2,1)}, bf16[256,256]{1,0:T(8,128)(2,1)}) custom-call(s32[2]{0:T(128)S(1)} %pad_add_fusion.where_ref, bf16[256,256]{1,0:T(8,128)(2,1)S(1)} %copy-done.1, bf16[256,256]{1,0:T(8,128)(2,1)S(1)} %copy-done.2, f32[256,512]{1,0:T(8,128)S(1)} %get-tuple-element.89.inner_ref, ...), custom_call_target="tpu_custom_call" | custom-call | flops 1 | bytes 1 | tf_op jit(solution)/shard_map/outer_grad/pallas_call | solution.py:283
  (57 shorter events, 10.3 us)
Async XLA Ops:
  0.7 4.4 %collective-permute-start = (bf16[256,256]{1,0:T(8,128)(2,1)}, bf16[256,256]{1,0:T(8,128)(2,1)S(1)}, u32[]{:S(2)}, u32[]{:S(2)}) collective-permute-start(bf16[256,256]{1,0:T(8,128)(2,1)} %q_ref.1), channel_id=1, source_target_pairs={{0,4},{4,0},{8,12},{12,8},{16,20},{20,16},{24,28},{28,24},{1,5},{5... | collective-permute-start | bytes 393224 | tf_op jit(solution)/shard_map/ppermute | solution.py:320
  1.2 3.9 %collective-permute-start.1 = (bf16[256,256]{1,0:T(8,128)(2,1)}, bf16[256,256]{1,0:T(8,128)(2,1)S(1)}, u32[]{:S(2)}, u32[]{:S(2)}) collective-permute-start(bf16[256,256]{1,0:T(8,128)(2,1)} %k_ref.3), channel_id=1, source_target_pairs={{0,4},{4,0},{8,12},{12,8},{16,20},{20,16},{24,28},{28,24},{1,5},{5... | collective-permute-start | bytes 393224 | tf_op jit(solution)/shard_map/ppermute | solution.py:320
  1.3 3.9 %collective-permute-start.2 = (bf16[256,256]{1,0:T(8,128)(2,1)}, bf16[256,256]{1,0:T(8,128)(2,1)S(1)}, u32[]{:S(2)}, u32[]{:S(2)}) collective-permute-start(bf16[256,256]{1,0:T(8,128)(2,1)} %v_ref.3), channel_id=1, source_target_pairs={{0,4},{4,0},{8,12},{12,8},{16,20},{20,16},{24,28},{28,24},{1,5},{5... | collective-permute-start | bytes 393224 | tf_op jit(solution)/shard_map/ppermute | solution.py:320
  1.7 3.4 %collective-permute-start.3 = (f32[2,256]{1,0:T(2,128)}, f32[2,256]{1,0:T(2,128)S(1)}, u32[]{:S(2)}, u32[]{:S(2)}) collective-permute-start(f32[2,256]{1,0:T(2,128)} %decay_ref.1), channel_id=1, source_target_pairs={{0,4},{4,0},{8,12},{12,8},{16,20},{20,16},{24,28},{28,24},{1,5},{5... | collective-permute-start | bytes 6152 | tf_op jit(solution)/shard_map/ppermute | solution.py:320
  5.2 6.2 %collective-permute-start.4 = (bf16[256,1536]{1,0:T(8,128)(2,1)S(1)}, bf16[256,1536]{1,0:T(8,128)(2,1)S(1)}, u32[]{:S(2)}, u32[]{:S(2)}) collective-permute-start(bf16[256,1536]{1,0:T(8,128)(2,1)S(1)} %copy-done), channel_id=1, source_target_pairs={{0,4},{4,0},{8,12},{12,8},{16,20},{20,16},{24,28},{28,24},{1,5},{5... | collective-permute-start | bytes 2359304 | tf_op jit(solution)/shard_map/ppermute | solution.py:320
  5.7 9.3 %collective-permute-start.5 = (bf16[64,1536]{1,0:T(8,128)(2,1)S(1)}, bf16[64,1536]{1,0:T(8,128)(2,1)S(1)}, u32[]{:S(2)}, u32[]{:S(2)}) collective-permute-start(bf16[64,1536]{1,0:T(8,128)(2,1)S(1)} %dynamic_slice.12), channel_id=1, source_target_pairs={{0,3},{1,2},{2,1},{3,0},{4,7},{5,6},{6,5},{7,4},{8,11},{9,10},{10,... | collective-permute-start | bytes 589832 | tf_op jit(solution)/shard_map/ppermute | solution.py:317
  9.2 21.7 %collective-permute-start.10 = (bf16[128,1536]{1,0:T(8,128)(2,1)S(1)}, bf16[128,1536]{1,0:T(8,128)(2,1)S(1)}, u32[]{:S(2)}, u32[]{:S(2)}) collective-permute-start(bf16[128,1536]{1,0:T(8,128)(2,1)S(1)} %get-tuple-element.99), channel_id=1, source_target_pairs={{0,1},{1,0},{2,3},{3,2},{4,5},{5,4},{6,7},{7,6},{8,9},{9,8},{10,11... | collective-permute-start | bytes 1179656 | tf_op jit(solution)/shard_map/ppermute | solution.py:317
  9.7 21.2 %collective-permute-start.11 = (bf16[128,1536]{1,0:T(8,128)(2,1)S(1)}, bf16[128,1536]{1,0:T(8,128)(2,1)S(1)}, u32[]{:S(2)}, u32[]{:S(2)}) collective-permute-start(bf16[128,1536]{1,0:T(8,128)(2,1)S(1)} %get-tuple-element.98), channel_id=1, source_target_pairs={{0,2},{1,3},{2,0},{3,1},{4,6},{5,7},{6,4},{7,5},{8,10},{9,11},{10,... | collective-permute-start | bytes 1179656 | tf_op jit(solution)/shard_map/ppermute | solution.py:317
  15.0 14.7 %collective-permute-start.6 = (bf16[64,1536]{1,0:T(8,128)(2,1)S(1)}, bf16[64,1536]{1,0:T(8,128)(2,1)S(1)}, u32[]{:S(2)}, u32[]{:S(2)}) collective-permute-start(bf16[64,1536]{1,0:T(8,128)(2,1)S(1)} %collective-permute-done.5.refs_1_), channel_id=1, source_target_pairs={{0,8},{4,12},{8,0},{12,4},{16,24},{20,28},{24,16},{28,20},{1,9},{5... | collective-permute-start | bytes 589832 | tf_op jit(solution)/shard_map/ppermute | solution.py:323
  17.0 6.9 %collective-permute-start.7 = (bf16[144,128]{1,0:T(8,128)(2,1)S(1)}, bf16[144,128]{1,0:T(8,128)(2,1)S(1)}, u32[]{:S(2)}, u32[]{:S(2)}) collective-permute-start(bf16[144,128]{1,0:T(8,128)(2,1)S(1)} %get-tuple-element.58), channel_id=1, source_target_pairs={{0,8},{4,12},{8,16},{12,20},{16,24},{20,28},{1,9},{5,13},{9,17},{1... | collective-permute-start | bytes 110600 | tf_op jit(solution)/shard_map/ppermute | solution.py:326
  18.9 10.3 %collective-permute-start.8 = (bf16[144,128]{1,0:T(8,128)(2,1)S(1)}, bf16[144,128]{1,0:T(8,128)(2,1)S(1)}, u32[]{:S(2)}, u32[]{:S(2)}) collective-permute-start(bf16[144,128]{1,0:T(8,128)(2,1)S(1)} %get-tuple-element.58), channel_id=1, source_target_pairs={{0,16},{4,20},{8,24},{12,28},{1,17},{5,21},{9,25},{13,29},{2,18},{... | collective-permute-start | bytes 110600 | tf_op jit(solution)/shard_map/ppermute | solution.py:326
  23.8 5.9 %collective-permute-start.9 = (bf16[144,128]{1,0:T(8,128)(2,1)S(1)}, bf16[144,128]{1,0:T(8,128)(2,1)S(1)}, u32[]{:S(2)}, u32[]{:S(2)}) collective-permute-start(bf16[144,128]{1,0:T(8,128)(2,1)S(1)} %get-tuple-element.58), channel_id=1, source_target_pairs={{0,24},{4,28},{1,25},{5,29},{2,26},{6,30},{3,27},{7,31}} | collective-permute-start | bytes 110600 | tf_op jit(solution)/shard_map/ppermute | solution.py:326
  32.0 7.5 %collective-permute-start.14 = (bf16[2,256,128]{2,1,0:T(8,128)(2,1)S(1)}, bf16[2,256,128]{2,1,0:T(8,128)(2,1)S(1)}, u32[]{:S(2)}, u32[]{:S(2)}) collective-permute-start(bf16[2,256,128]{2,1,0:T(8,128)(2,1)S(1)} %get-tuple-element.75), channel_id=1, source_target_pairs={{0,1},{1,0},{2,3},{3,2},{4,5},{5,4},{6,7},{7,6},{8,9},{9,8},{10,11... | collective-permute-start | bytes 393224 | tf_op jit(solution)/shard_map/ppermute | solution.py:317
  33.6 10.4 %collective-permute-start.13 = (bf16[2,256,128]{2,1,0:T(8,128)(2,1)S(1)}, bf16[2,256,128]{2,1,0:T(8,128)(2,1)S(1)}, u32[]{:S(2)}, u32[]{:S(2)}) collective-permute-start(bf16[2,256,128]{2,1,0:T(8,128)(2,1)S(1)} %get-tuple-element.71), channel_id=1, source_target_pairs={{0,3},{1,2},{2,1},{3,0},{4,7},{5,6},{6,5},{7,4},{8,11},{9,10},{10,... | collective-permute-start | bytes 393224 | tf_op jit(solution)/shard_map/ppermute | solution.py:317
  35.1 8.9 %collective-permute-start.15 = (bf16[2,256,128]{2,1,0:T(8,128)(2,1)S(1)}, bf16[2,256,128]{2,1,0:T(8,128)(2,1)S(1)}, u32[]{:S(2)}, u32[]{:S(2)}) collective-permute-start(bf16[2,256,128]{2,1,0:T(8,128)(2,1)S(1)} %get-tuple-element.76), channel_id=1, source_target_pairs={{0,2},{1,3},{2,0},{3,1},{4,6},{5,7},{6,4},{7,5},{8,10},{9,11},{10,... | collective-permute-start | bytes 393224 | tf_op jit(solution)/shard_map/ppermute | solution.py:317
  36.5 8.7 %collective-permute-start.16 = (bf16[2,256,128]{2,1,0:T(8,128)(2,1)S(1)}, bf16[2,256,128]{2,1,0:T(8,128)(2,1)S(1)}, u32[]{:S(2)}, u32[]{:S(2)}) collective-permute-start(bf16[2,256,128]{2,1,0:T(8,128)(2,1)S(1)} %get-tuple-element.82.refs_0_.refs_4_), channel_id=1, source_target_pairs={{0,3},{1,2},{2,1},{3,0},{4,7},{5,6},{6,5},{7,4},{8,11},{9,10},{10,... | collective-permute-start | bytes 393224 | tf_op jit(solution)/shard_map/ppermute | solution.py:317
  39.0 6.2 %collective-permute-start.17 = (bf16[2,256,128]{2,1,0:T(8,128)(2,1)S(1)}, bf16[2,256,128]{2,1,0:T(8,128)(2,1)S(1)}, u32[]{:S(2)}, u32[]{:S(2)}) collective-permute-start(bf16[2,256,128]{2,1,0:T(8,128)(2,1)S(1)} %get-tuple-element.82.refs_0_.refs_4_), channel_id=1, source_target_pairs={{0,1},{1,0},{2,3},{3,2},{4,5},{5,4},{6,7},{7,6},{8,9},{9,8},{10,11... | collective-permute-start | bytes 393224 | tf_op jit(solution)/shard_map/ppermute | solution.py:317
  39.6 5.8 %collective-permute-start.18 = (bf16[2,256,128]{2,1,0:T(8,128)(2,1)S(1)}, bf16[2,256,128]{2,1,0:T(8,128)(2,1)S(1)}, u32[]{:S(2)}, u32[]{:S(2)}) collective-permute-start(bf16[2,256,128]{2,1,0:T(8,128)(2,1)S(1)} %get-tuple-element.82.refs_0_.refs_4_), channel_id=1, source_target_pairs={{0,2},{1,3},{2,0},{3,1},{4,6},{5,7},{6,4},{7,5},{8,10},{9,11},{10,... | collective-permute-start | bytes 393224 | tf_op jit(solution)/shard_map/ppermute | solution.py:317
  45.4 14.8 %collective-permute-start.19 = (bf16[256,1536]{1,0:T(8,128)(2,1)S(1)}, bf16[256,1536]{1,0:T(8,128)(2,1)S(1)}, u32[]{:S(2)}, u32[]{:S(2)}) collective-permute-start(bf16[256,1536]{1,0:T(8,128)(2,1)S(1)} %get-tuple-element.84.refs_1_), channel_id=1, source_target_pairs={{0,4},{4,0},{8,12},{12,8},{16,20},{20,16},{24,28},{28,24},{1,5},{5... | collective-permute-start | bytes 2359304 | tf_op jit(solution)/shard_map/ppermute | solution.py:320
  45.4 5.8 %collective-permute-start.21 = (bf16[144,128]{1,0:T(8,128)(2,1)S(1)}, bf16[144,128]{1,0:T(8,128)(2,1)S(1)}, u32[]{:S(2)}, u32[]{:S(2)}) collective-permute-start(bf16[144,128]{1,0:T(8,128)(2,1)S(1)} %get-tuple-element.83), channel_id=1, source_target_pairs={{8,0},{12,4},{16,8},{20,12},{24,16},{28,20},{9,1},{13,5},{17,9},{2... | collective-permute-start | bytes 110600 | tf_op jit(solution)/shard_map/ppermute | solution.py:326
  46.7 6.8 %collective-permute-start.22 = (bf16[144,128]{1,0:T(8,128)(2,1)S(1)}, bf16[144,128]{1,0:T(8,128)(2,1)S(1)}, u32[]{:S(2)}, u32[]{:S(2)}) collective-permute-start(bf16[144,128]{1,0:T(8,128)(2,1)S(1)} %get-tuple-element.83), channel_id=1, source_target_pairs={{16,0},{20,4},{24,8},{28,12},{17,1},{21,5},{25,9},{29,13},{18,2},{... | collective-permute-start | bytes 110600 | tf_op jit(solution)/shard_map/ppermute | solution.py:326
  48.0 8.8 %collective-permute-start.23 = (bf16[144,128]{1,0:T(8,128)(2,1)S(1)}, bf16[144,128]{1,0:T(8,128)(2,1)S(1)}, u32[]{:S(2)}, u32[]{:S(2)}) collective-permute-start(bf16[144,128]{1,0:T(8,128)(2,1)S(1)} %get-tuple-element.83), channel_id=1, source_target_pairs={{24,0},{28,4},{25,1},{29,5},{26,2},{30,6},{27,3},{31,7}} | collective-permute-start | bytes 110600 | tf_op jit(solution)/shard_map/ppermute | solution.py:326
  56.8 5.8 %collective-permute-start.24 = (f32[256,512]{1,0:T(8,128)S(1)}, f32[256,512]{1,0:T(8,128)S(1)}, u32[]{:S(2)}, u32[]{:S(2)}) collective-permute-start(f32[256,512]{1,0:T(8,128)S(1)} %get-tuple-element.91), channel_id=1, source_target_pairs={{0,4},{4,0},{8,12},{12,8},{16,20},{20,16},{24,28},{28,24},{1,5},{5... | collective-permute-start | bytes 1572872 | tf_op jit(solution)/shard_map/ppermute | solution.py:320
  57.4 5.3 %collective-permute-start.25 = (bf16[144,128]{1,0:T(8,128)(2,1)S(1)}, bf16[144,128]{1,0:T(8,128)(2,1)S(1)}, u32[]{:S(2)}, u32[]{:S(2)}) collective-permute-start(bf16[144,128]{1,0:T(8,128)(2,1)S(1)} %collective-permute-done.21.refs_0_), channel_id=1, source_target_pairs={{0,4},{4,0},{8,12},{12,8},{16,20},{20,16},{24,28},{28,24},{1,5},{5... | collective-permute-start | bytes 110600 | tf_op jit(solution)/shard_map/ppermute | solution.py:320
  (10 other events, 76.8 us)

commit v7 on v6

--- a/solution.py
+++ b/solution.py
@@ -348,32 +348,37 @@
         return lax.dynamic_slice(out_weight, (begin, (place ^ step) * width), (rows, width))
 
     slices = [slice_for(step, halves) for step, halves in plan]
-    arriving = [swap_tensor(piece, step) for piece, step in zip(slices, order)]
-    got = [swap_core(rows) for rows in (queries, keys, values)]
-    got.append(swap_core(log_decay))
+    got = [swap_core(rows) for rows in (queries, keys, values, log_decay)]
     (weight,) = after([out_weight], *slices)
     weight_own = lax.dynamic_slice(weight, (0, place * width), (columns, width))
     got = after(got, weight_own)
-    (grad,) = after([out_grad], *got)
-    grad_got = swap_core(grad)
     q, k, v, col, row, first, fresh = call(
         fresh_kernel,
         "fresh",
         [pair16, pair16, pair16, shape(F32, length, 2), shape(F32, 2, length), shape(F32, HD, HD), message],
         [where, queries, keys, values, *got[:3], log_decay, got[3]],
     )
-    (fresh,) = after([fresh], grad_got)
     arrived = [to_chip(fresh, step) for step in range(1, chips)]
+    slices = after(slices, *arrived)
+    arriving = [swap_tensor(piece, step) for piece, step in zip(slices, order)]
+    (grad,) = after([out_grad], *arrived)
+    grad_got = swap_core(grad)
     (inner,) = call(without_where(inner_kernel), "inner", [pair32], [where, q, k, v, col, row, first])
+    mixed, normed, states = call(
+        mixed_kernel,
+        "mixed",
+        [pair32, pair16, shape(F32, 2, HD, HD)],
+        [where, q, col, inner, gain, first, *arrived],
+    )
     pieces = [("own", [weight_own])]
     for (step, halves), piece in zip(plan, arriving):
         if halves:
-            (piece,) = after([piece], fresh)
+            (piece,) = after([piece], mixed)
         pieces.append(("halves", [piece, swap_side(piece)]) if halves else ("whole", [piece]))
     partials, mine, theirs = [], [], []
     for number in range(0, tensor, 2):
         kinds, sources = zip(*pieces[number : number + 2])
-        sources = after(sum(sources, []), *arrived, inner, *partials)
+        sources = after(sum(sources, []), mixed, *partials)
         *outs, weight = call(
             functools.partial(partial_kernel, kinds),
             "partial",
@@ -386,12 +391,6 @@
             theirs.append(swap_core(weight))
     own_partial, *partials = partials
     sent = [swap_tensor(partial, step) for partial, step in zip(partials, order)]
-    mixed, normed, states = call(
-        mixed_kernel,
-        "mixed",
-        [pair32, pair16, shape(F32, 2, HD, HD)],
-        [where, q, col, inner, gain, first, *after(arrived, *partials)],
-    )
     normed_all = [normed] + [swap_tensor(normed, step) for step in order]
     grad_mixed, second, upward = call(
         grad_mixed_kernel,

time: 64.5 us -> 72.3 us (1.12)
  waiting for transfers between devices: 15.8 us -> 26.3 us
  starting transfers between devices: 31.3 us -> 28.5 us
    ppermute x1, waiting for transfers between devices: 0.01 us -> 6.14 us  [swap_side(): return lax.ppermute(value, 'seq', [(i, i ^ 2) for i in range(seq)])]
    ppermute x9, waiting for transfers between devices: 7.75 us -> 11.1 us  [swap_tensor(): return lax.ppermute(value, 'tensor', [(i, i ^ k) for i in range(tensor)])]
    ppermute x1, starting transfers between devices: 1.98 us -> 0.01 us  [swap_side(): return lax.ppermute(value, 'seq', [(i, i ^ 2) for i in range(seq)])]
    ppermute x6, waiting for transfers between devices: 6.15 us -> 7.21 us  [to_chip(): lax.ppermute(value, 'seq', [(i, i + 2 * step) for i in range(seq) if 0 <=...]
  transfers between devices with their start and end apart: 28 -> 28, of which waited for: 7 -> 10; matrix products, arithmetic and copies ran while one was open for 5% -> 5% of each run, Pallas kernels for 16% -> 12%
where the time goes in v7:
time: 72.3 us; the launch traced here: 72 us
  starting transfers between devices  28.5 us (39%)
  waiting for transfers between devices  26.3 us (36%)
  Pallas kernels  12.8 us (18%)
  local copies, waits for them, and re-layouts  3.33 us (5%)
  between operations  0.89 us (1%)
    ppermute x6, starting transfers between devices, to_chip(): lax.ppermute(value, 'seq', [(i, i + 2 * step) for i in range(seq) if 0 <=...  14.6 us
    pallas_call x9, Pallas kernels, call(): pl.pallas_call(kernel, name=name, out_shape=outs, in_specs=[SMEM] + [VMEM...  12.8 us
    ppermute x9, starting transfers between devices, swap_tensor(): return lax.ppermute(value, 'tensor', [(i, i ^ k) for i in range(tensor)])  11.3 us
    ppermute x9, waiting for transfers between devices, swap_tensor(): return lax.ppermute(value, 'tensor', [(i, i ^ k) for i in range(tensor)])  11.1 us
    ppermute x6, waiting for transfers between devices, to_chip(): lax.ppermute(value, 'seq', [(i, i + 2 * step) for i in range(seq) if 0 <=...  7.21 us
    ppermute x1, waiting for transfers between devices, swap_side(): return lax.ppermute(value, 'seq', [(i, i ^ 2) for i in range(seq)])  6.14 us
    ppermute x12, starting transfers between devices, swap_core(): return lax.ppermute(value, 'seq', [(i, i ^ 1) for i in range(seq)])  2.64 us
    dynamic_slice x2, local copies, waits for them, and re-layouts, slice_for(): lax.dynamic_slice(out_weight, (begin, (place ^ step) * width), (rows, wid...  2.12 us
  transfers between devices with their start and end apart: 28, of which 10 were waited for; matrix products, arithmetic and copies ran while one was open for 5% of the time, Pallas kernels for 12%

profile of v7, /device:TPU:0, one launch (start us, length us, event | category | flops | bytes accessed | tf_op | source)
XLA Modules:
  0.0 72.0 jit_solution(43533287826331018)
XLA Ops:
  2.7 1.2 %fusion = (bf16[128,1536]{1,0:T(8,128)(2,1)S(1)}, bf16[128,1536]{1,0:T(8,128)(2,1)S(1)}) fusion(bf16[256,6144]{1,0:T(8,128)(2,1)} %param.12, s32[]{:T(128)S(6)} %select_n.27, s32[]{:T(128)S(6)} %select_n.29, s32[]{:T(128)S(6)} %select_n.28), kind=kLoop, calls=%fused_computation.2 | loop fusion | bytes 1572876 | tf_op jit(solution)/shard_map/dynamic_slice | solution.py:348
  3.9 1.2 %constant_dynamic-slice_fusion.refs_0_.own_ref = bf16[256,1536]{1,0:T(8,128)(2,1)S(1)} fusion(bf16[256,6144]{1,0:T(8,128)(2,1)} %param.12, s32[]{:T(128)S(6)} %select_n.30), kind=kLoop, calls=%fused_computation.1 | loop fusion | bytes 1572868 | tf_op jit(solution)/shard_map/dynamic_slice | solution.py:353
  5.3 1.4 %fresh.1 = (bf16[2,256,128]{2,1,0:T(8,128)(2,1)S(1)}, bf16[2,256,128]{2,1,0:T(8,128)(2,1)S(1)}, bf16[2,256,128]{2,1,0:T(8,128)(2,1)S(1)}, f32[256,2]{1,0:T(8,128...) custom-call(s32[2]{0:T(128)S(1)} %pad_add_fusion.where_ref, ...), custom_call_target="tpu_custom_call" | custom-call | flops 1 | bytes 1 | tf_op jit(solution)/shard_map/fresh/pallas_call | solution.py:283
  6.7 4.9 %collective-permute-start.4 = (bf16[144,128]{1,0:T(8,128)(2,1)S(1)}, bf16[144,128]{1,0:T(8,128)(2,1)S(1)}, u32[]{:S(2)}, u32[]{:S(2)}) collective-permute-start(bf16[144,128]{1,0:T(8,128)(2,1)S(1)} %get-tuple-element.55), channel_id=1, source_target_pairs={{0,8},{4,12},{8,16},{12,20},{16,24},{20,28},{1,9},{5,13},{9,17},{1... | collective-permute-start | bytes 110600 | tf_op jit(solution)/shard_map/ppermute | solution.py:326
  11.6 4.5 %collective-permute-start.5 = (bf16[144,128]{1,0:T(8,128)(2,1)S(1)}, bf16[144,128]{1,0:T(8,128)(2,1)S(1)}, u32[]{:S(2)}, u32[]{:S(2)}) collective-permute-start(bf16[144,128]{1,0:T(8,128)(2,1)S(1)} %get-tuple-element.55), channel_id=1, source_target_pairs={{0,16},{4,20},{8,24},{12,28},{1,17},{5,21},{9,25},{13,29},{2,18},{... | collective-permute-start | bytes 110600 | tf_op jit(solution)/shard_map/ppermute | solution.py:326
  16.1 1.3 %collective-permute-start.6 = (bf16[144,128]{1,0:T(8,128)(2,1)S(1)}, bf16[144,128]{1,0:T(8,128)(2,1)S(1)}, u32[]{:S(2)}, u32[]{:S(2)}) collective-permute-start(bf16[144,128]{1,0:T(8,128)(2,1)S(1)} %get-tuple-element.55), channel_id=1, source_target_pairs={{0,24},{4,28},{1,25},{5,29},{2,26},{6,30},{3,27},{7,31}} | collective-permute-start | bytes 110600 | tf_op jit(solution)/shard_map/ppermute | solution.py:326
  17.8 1.2 %collective-permute-done.6.refs_2_ = bf16[144,128]{1,0:T(8,128)(2,1)S(1)} collective-permute-done((bf16[144,128]{1,0:T(8,128)(2,1)S(1)}, bf16[144,128]{1,0:T(8,128)(2,1)S(1)}, u32[]{:S(2)}, u32[]{:S(2)}) %collective-permute-start.6) | collective-permute-done | bytes 36896 | tf_op jit(solution)/shard_map/ppermute | solution.py:326
  19.0 2.4 %collective-permute-start.8 = (bf16[64,1536]{1,0:T(8,128)(2,1)S(1)}, bf16[64,1536]{1,0:T(8,128)(2,1)S(1)}, u32[]{:S(2)}, u32[]{:S(2)}) collective-permute-start(bf16[64,1536]{1,0:T(8,128)(2,1)S(1)} %dynamic_slice.12), channel_id=1, source_target_pairs={{0,3},{1,2},{2,1},{3,0},{4,7},{5,6},{6,5},{7,4},{8,11},{9,10},{10,... | collective-permute-start | bytes 589832 | tf_op jit(solution)/shard_map/ppermute | solution.py:317
  24.5 3.2 %collective-permute-done.8.refs_1_ = bf16[64,1536]{1,0:T(8,128)(2,1)S(1)} collective-permute-done((bf16[64,1536]{1,0:T(8,128)(2,1)S(1)}, bf16[64,1536]{1,0:T(8,128)(2,1)S(1)}, u32[]{:S(2)}, u32[]{:S(2)}) %collective-permute-start.8) | collective-permute-done | bytes 196640 | tf_op jit(solution)/shard_map/ppermute | solution.py:317
  27.7 6.1 %collective-permute-done.9.refs_2_ = bf16[64,1536]{1,0:T(8,128)(2,1)S(1)} collective-permute-done((bf16[64,1536]{1,0:T(8,128)(2,1)S(1)}, bf16[64,1536]{1,0:T(8,128)(2,1)S(1)}, u32[]{:S(2)}, u32[]{:S(2)}) %collective-permute-start.9) | collective-permute-done | bytes 196640 | tf_op jit(solution)/shard_map/ppermute | solution.py:323
  37.0 1.6 %collective-permute-start.14 = (bf16[2,256,128]{2,1,0:T(8,128)(2,1)S(1)}, bf16[2,256,128]{2,1,0:T(8,128)(2,1)S(1)}, u32[]{:S(2)}, u32[]{:S(2)}) collective-permute-start(bf16[2,256,128]{2,1,0:T(8,128)(2,1)S(1)} %get-tuple-element.77), channel_id=1, source_target_pairs={{0,1},{1,0},{2,3},{3,2},{4,5},{5,4},{6,7},{7,6},{8,9},{9,8},{10,11... | collective-permute-start | bytes 393224 | tf_op jit(solution)/shard_map/ppermute | solution.py:317
  38.5 1.4 %collective-permute-start.13 = (bf16[2,256,128]{2,1,0:T(8,128)(2,1)S(1)}, bf16[2,256,128]{2,1,0:T(8,128)(2,1)S(1)}, u32[]{:S(2)}, u32[]{:S(2)}) collective-permute-start(bf16[2,256,128]{2,1,0:T(8,128)(2,1)S(1)} %get-tuple-element.73), channel_id=1, source_target_pairs={{0,3},{1,2},{2,1},{3,0},{4,7},{5,6},{6,5},{7,4},{8,11},{9,10},{10,... | collective-permute-start | bytes 393224 | tf_op jit(solution)/shard_map/ppermute | solution.py:317
  40.5 2.4 %collective-permute-start.16 = (bf16[2,256,128]{2,1,0:T(8,128)(2,1)S(1)}, bf16[2,256,128]{2,1,0:T(8,128)(2,1)S(1)}, u32[]{:S(2)}, u32[]{:S(2)}) collective-permute-start(bf16[2,256,128]{2,1,0:T(8,128)(2,1)S(1)} %get-tuple-element.80.refs_0_.refs_4_), channel_id=1, source_target_pairs={{0,3},{1,2},{2,1},{3,0},{4,7},{5,6},{6,5},{7,4},{8,11},{9,10},{10,... | collective-permute-start | bytes 393224 | tf_op jit(solution)/shard_map/ppermute | solution.py:317
  43.4 1.4 %collective-permute-start.18 = (bf16[2,256,128]{2,1,0:T(8,128)(2,1)S(1)}, bf16[2,256,128]{2,1,0:T(8,128)(2,1)S(1)}, u32[]{:S(2)}, u32[]{:S(2)}) collective-permute-start(bf16[2,256,128]{2,1,0:T(8,128)(2,1)S(1)} %get-tuple-element.80.refs_0_.refs_4_), channel_id=1, source_target_pairs={{0,2},{1,3},{2,0},{3,1},{4,6},{5,7},{6,4},{7,5},{8,10},{9,11},{10,... | collective-permute-start | bytes 393224 | tf_op jit(solution)/shard_map/ppermute | solution.py:317
  44.8 6.6 %collective-permute-done.15.refs_2_ = bf16[2,256,128]{2,1,0:T(8,128)(2,1)S(1)} collective-permute-done((bf16[2,256,128]{2,1,0:T(8,128)(2,1)S(1)}, bf16[2,256,128]{2,1,0:T(8,128)(2,1)S(1)}, u32[]{:S(2)}, u32[]{:S(2)}) %collective-permute-start.15) | collective-permute-done | bytes 131104 | tf_op jit(solution)/shard_map/ppermute | solution.py:317
  53.2 1.3 %collective-permute-start.21 = (bf16[144,128]{1,0:T(8,128)(2,1)S(1)}, bf16[144,128]{1,0:T(8,128)(2,1)S(1)}, u32[]{:S(2)}, u32[]{:S(2)}) collective-permute-start(bf16[144,128]{1,0:T(8,128)(2,1)S(1)} %get-tuple-element.81), channel_id=1, source_target_pairs={{8,0},{12,4},{16,8},{20,12},{24,16},{28,20},{9,1},{13,5},{17,9},{2... | collective-permute-start | bytes 110600 | tf_op jit(solution)/shard_map/ppermute | solution.py:326
  54.5 1.3 %collective-permute-start.22 = (bf16[144,128]{1,0:T(8,128)(2,1)S(1)}, bf16[144,128]{1,0:T(8,128)(2,1)S(1)}, u32[]{:S(2)}, u32[]{:S(2)}) collective-permute-start(bf16[144,128]{1,0:T(8,128)(2,1)S(1)} %get-tuple-element.81), channel_id=1, source_target_pairs={{16,0},{20,4},{24,8},{28,12},{17,1},{21,5},{25,9},{29,13},{18,2},{... | collective-permute-start | bytes 110600 | tf_op jit(solution)/shard_map/ppermute | solution.py:326
  55.8 1.3 %collective-permute-start.23 = (bf16[144,128]{1,0:T(8,128)(2,1)S(1)}, bf16[144,128]{1,0:T(8,128)(2,1)S(1)}, u32[]{:S(2)}, u32[]{:S(2)}) collective-permute-start(bf16[144,128]{1,0:T(8,128)(2,1)S(1)} %get-tuple-element.81), channel_id=1, source_target_pairs={{24,0},{28,4},{25,1},{29,5},{26,2},{30,6},{27,3},{31,7}} | collective-permute-start | bytes 110600 | tf_op jit(solution)/shard_map/ppermute | solution.py:326
  57.1 1.9 %inner_grad.1 = (f32[256,512]{1,0:T(8,128)S(1)}, f32[256,512]{1,0:T(8,128)S(1)}, bf16[4,256,128]{2,1,0:T(8,128)(2,1)S(1)}) custom-call(s32[2]{0:T(128)S(1)} %pad_add_fusion.where_ref, bf16[2,256,128]{2,1,0:T(8,128)(2,1)S(1)} %get-tuple-element.58.refs_0_.q_ref, bf16[2,256,128]{2,1,0:T(8,128)(2,1)S(1)} %get-tuple-element.60.refs_1_.k_ref, ...), custom_call_target="tpu_custom_call" | custom-call | flops 1 | bytes 1 | tf_op jit(solution)/shard_map/inner_grad/pallas_call | solution.py:283
  59.0 2.2 %collective-permute-done.22.refs_1_ = bf16[144,128]{1,0:T(8,128)(2,1)S(1)} collective-permute-done((bf16[144,128]{1,0:T(8,128)(2,1)S(1)}, bf16[144,128]{1,0:T(8,128)(2,1)S(1)}, u32[]{:S(2)}, u32[]{:S(2)}) %collective-permute-start.22) | collective-permute-done | bytes 36896 | tf_op jit(solution)/shard_map/ppermute | solution.py:326
  61.2 3.4 %collective-permute-done.23.refs_2_ = bf16[144,128]{1,0:T(8,128)(2,1)S(1)} collective-permute-done((bf16[144,128]{1,0:T(8,128)(2,1)S(1)}, bf16[144,128]{1,0:T(8,128)(2,1)S(1)}, u32[]{:S(2)}, u32[]{:S(2)}) %collective-permute-start.23) | collective-permute-done | bytes 36896 | tf_op jit(solution)/shard_map/ppermute | solution.py:326
  65.6 1.8 %collective-permute-done.20.refs_8_ = bf16[4,256,128]{2,1,0:T(8,128)(2,1)S(1)} collective-permute-done((bf16[4,256,128]{2,1,0:T(8,128)(2,1)S(1)}, bf16[4,256,128]{2,1,0:T(8,128)(2,1)S(1)}, u32[]{:S(2)}, u32[]{:S(2)}) %collective-permute-start.20) | collective-permute-done | bytes 262176 | tf_op jit(solution)/shard_map/ppermute | solution.py:320
  68.0 2.4 %layer.1 = bf16[256,1536]{1,0:T(8,128)(2,1)} custom-call(s32[2]{0:T(128)S(1)} %pad_add_fusion.where_ref, bf16[256,1536]{1,0:T(8,128)(2,1)S(1)} %constant_dynamic-slice_fusion.refs_0_.own_ref, bf16[128,1536]{1,0:T(8,128)(2,1)S(1)} %get-tuple-element.69.refs_0_, bf16[256,1536]{1,0:T(8,128)(2,1)S(1)} %get-tuple-element.82.refs_1_, ...), custom_call_target="tpu_custom_call" | custom-call | flops 1 | bytes 1 | tf_op jit(solution)/shard_map/layer/pallas_call | solution.py:283
  70.4 1.6 %outer_grad.1 = (bf16[256,256]{1,0:T(8,128)(2,1)}, bf16[256,256]{1,0:T(8,128)(2,1)}, bf16[256,256]{1,0:T(8,128)(2,1)}) custom-call(s32[2]{0:T(128)S(1)} %pad_add_fusion.where_ref, bf16[256,256]{1,0:T(8,128)(2,1)S(1)} %copy-done.1, bf16[256,256]{1,0:T(8,128)(2,1)S(1)} %copy-done.2, f32[256,512]{1,0:T(8,128)S(1)} %get-tuple-element.87.inner_ref, ...), custom_call_target="tpu_custom_call" | custom-call | flops 1 | bytes 1 | tf_op jit(solution)/shard_map/outer_grad/pallas_call | solution.py:283
  (57 shorter events, 13.2 us)
Async XLA Ops:
  0.7 4.5 %collective-permute-start = (bf16[256,256]{1,0:T(8,128)(2,1)}, bf16[256,256]{1,0:T(8,128)(2,1)S(1)}, u32[]{:S(2)}, u32[]{:S(2)}) collective-permute-start(bf16[256,256]{1,0:T(8,128)(2,1)} %q_ref.1), channel_id=1, source_target_pairs={{0,4},{4,0},{8,12},{12,8},{16,20},{20,16},{24,28},{28,24},{1,5},{5... | collective-permute-start | bytes 393224 | tf_op jit(solution)/shard_map/ppermute | solution.py:320
  1.2 4.0 %collective-permute-start.1 = (bf16[256,256]{1,0:T(8,128)(2,1)}, bf16[256,256]{1,0:T(8,128)(2,1)S(1)}, u32[]{:S(2)}, u32[]{:S(2)}) collective-permute-start(bf16[256,256]{1,0:T(8,128)(2,1)} %k_ref.3), channel_id=1, source_target_pairs={{0,4},{4,0},{8,12},{12,8},{16,20},{20,16},{24,28},{28,24},{1,5},{5... | collective-permute-start | bytes 393224 | tf_op jit(solution)/shard_map/ppermute | solution.py:320
  1.3 3.9 %collective-permute-start.2 = (bf16[256,256]{1,0:T(8,128)(2,1)}, bf16[256,256]{1,0:T(8,128)(2,1)S(1)}, u32[]{:S(2)}, u32[]{:S(2)}) collective-permute-start(bf16[256,256]{1,0:T(8,128)(2,1)} %v_ref.3), channel_id=1, source_target_pairs={{0,4},{4,0},{8,12},{12,8},{16,20},{20,16},{24,28},{28,24},{1,5},{5... | collective-permute-start | bytes 393224 | tf_op jit(solution)/shard_map/ppermute | solution.py:320
  1.7 3.5 %collective-permute-start.3 = (f32[2,256]{1,0:T(2,128)}, f32[2,256]{1,0:T(2,128)S(1)}, u32[]{:S(2)}, u32[]{:S(2)}) collective-permute-start(f32[2,256]{1,0:T(2,128)} %decay_ref.1), channel_id=1, source_target_pairs={{0,4},{4,0},{8,12},{12,8},{16,20},{20,16},{24,28},{28,24},{1,5},{5... | collective-permute-start | bytes 6152 | tf_op jit(solution)/shard_map/ppermute | solution.py:320
  6.7 10.7 %collective-permute-start.4 = (bf16[144,128]{1,0:T(8,128)(2,1)S(1)}, bf16[144,128]{1,0:T(8,128)(2,1)S(1)}, u32[]{:S(2)}, u32[]{:S(2)}) collective-permute-start(bf16[144,128]{1,0:T(8,128)(2,1)S(1)} %get-tuple-element.55), channel_id=1, source_target_pairs={{0,8},{4,12},{8,16},{12,20},{16,24},{20,28},{1,9},{5,13},{9,17},{1... | collective-permute-start | bytes 110600 | tf_op jit(solution)/shard_map/ppermute | solution.py:326
  11.6 6.2 %collective-permute-start.5 = (bf16[144,128]{1,0:T(8,128)(2,1)S(1)}, bf16[144,128]{1,0:T(8,128)(2,1)S(1)}, u32[]{:S(2)}, u32[]{:S(2)}) collective-permute-start(bf16[144,128]{1,0:T(8,128)(2,1)S(1)} %get-tuple-element.55), channel_id=1, source_target_pairs={{0,16},{4,20},{8,24},{12,28},{1,17},{5,21},{9,25},{13,29},{2,18},{... | collective-permute-start | bytes 110600 | tf_op jit(solution)/shard_map/ppermute | solution.py:326
  19.0 14.8 %collective-permute-start.7 = (bf16[256,1536]{1,0:T(8,128)(2,1)S(1)}, bf16[256,1536]{1,0:T(8,128)(2,1)S(1)}, u32[]{:S(2)}, u32[]{:S(2)}) collective-permute-start(bf16[256,1536]{1,0:T(8,128)(2,1)S(1)} %copy-done), channel_id=1, source_target_pairs={{0,4},{4,0},{8,12},{12,8},{16,20},{20,16},{24,28},{28,24},{1,5},{5... | collective-permute-start | bytes 2359304 | tf_op jit(solution)/shard_map/ppermute | solution.py:320
  19.0 8.6 %collective-permute-start.8 = (bf16[64,1536]{1,0:T(8,128)(2,1)S(1)}, bf16[64,1536]{1,0:T(8,128)(2,1)S(1)}, u32[]{:S(2)}, u32[]{:S(2)}) collective-permute-start(bf16[64,1536]{1,0:T(8,128)(2,1)S(1)} %dynamic_slice.12), channel_id=1, source_target_pairs={{0,3},{1,2},{2,1},{3,0},{4,7},{5,6},{6,5},{7,4},{8,11},{9,10},{10,... | collective-permute-start | bytes 589832 | tf_op jit(solution)/shard_map/ppermute | solution.py:317
  21.5 14.3 %collective-permute-start.10 = (bf16[128,1536]{1,0:T(8,128)(2,1)S(1)}, bf16[128,1536]{1,0:T(8,128)(2,1)S(1)}, u32[]{:S(2)}, u32[]{:S(2)}) collective-permute-start(bf16[128,1536]{1,0:T(8,128)(2,1)S(1)} %get-tuple-element.70), channel_id=1, source_target_pairs={{0,1},{1,0},{2,3},{3,2},{4,5},{5,4},{6,7},{7,6},{8,9},{9,8},{10,11... | collective-permute-start | bytes 1179656 | tf_op jit(solution)/shard_map/ppermute | solution.py:317
  22.0 13.8 %collective-permute-start.11 = (bf16[128,1536]{1,0:T(8,128)(2,1)S(1)}, bf16[128,1536]{1,0:T(8,128)(2,1)S(1)}, u32[]{:S(2)}, u32[]{:S(2)}) collective-permute-start(bf16[128,1536]{1,0:T(8,128)(2,1)S(1)} %get-tuple-element.71), channel_id=1, source_target_pairs={{0,2},{1,3},{2,0},{3,1},{4,6},{5,7},{6,4},{7,5},{8,10},{9,11},{10,... | collective-permute-start | bytes 1179656 | tf_op jit(solution)/shard_map/ppermute | solution.py:317
  27.7 6.1 %collective-permute-start.9 = (bf16[64,1536]{1,0:T(8,128)(2,1)S(1)}, bf16[64,1536]{1,0:T(8,128)(2,1)S(1)}, u32[]{:S(2)}, u32[]{:S(2)}) collective-permute-start(bf16[64,1536]{1,0:T(8,128)(2,1)S(1)} %collective-permute-done.8.refs_1_), channel_id=1, source_target_pairs={{0,8},{4,12},{8,0},{12,4},{16,24},{20,28},{24,16},{28,20},{1,9},{5... | collective-permute-start | bytes 589832 | tf_op jit(solution)/shard_map/ppermute | solution.py:323
  37.0 6.4 %collective-permute-start.14 = (bf16[2,256,128]{2,1,0:T(8,128)(2,1)S(1)}, bf16[2,256,128]{2,1,0:T(8,128)(2,1)S(1)}, u32[]{:S(2)}, u32[]{:S(2)}) collective-permute-start(bf16[2,256,128]{2,1,0:T(8,128)(2,1)S(1)} %get-tuple-element.77), channel_id=1, source_target_pairs={{0,1},{1,0},{2,3},{3,2},{4,5},{5,4},{6,7},{7,6},{8,9},{9,8},{10,11... | collective-permute-start | bytes 393224 | tf_op jit(solution)/shard_map/ppermute | solution.py:317
  38.5 12.9 %collective-permute-start.13 = (bf16[2,256,128]{2,1,0:T(8,128)(2,1)S(1)}, bf16[2,256,128]{2,1,0:T(8,128)(2,1)S(1)}, u32[]{:S(2)}, u32[]{:S(2)}) collective-permute-start(bf16[2,256,128]{2,1,0:T(8,128)(2,1)S(1)} %get-tuple-element.73), channel_id=1, source_target_pairs={{0,3},{1,2},{2,1},{3,0},{4,7},{5,6},{6,5},{7,4},{8,11},{9,10},{10,... | collective-permute-start | bytes 393224 | tf_op jit(solution)/shard_map/ppermute | solution.py:317
  39.9 11.5 %collective-permute-start.15 = (bf16[2,256,128]{2,1,0:T(8,128)(2,1)S(1)}, bf16[2,256,128]{2,1,0:T(8,128)(2,1)S(1)}, u32[]{:S(2)}, u32[]{:S(2)}) collective-permute-start(bf16[2,256,128]{2,1,0:T(8,128)(2,1)S(1)} %get-tuple-element.78), channel_id=1, source_target_pairs={{0,2},{1,3},{2,0},{3,1},{4,6},{5,7},{6,4},{7,5},{8,10},{9,11},{10,... | collective-permute-start | bytes 393224 | tf_op jit(solution)/shard_map/ppermute | solution.py:317
  40.5 12.1 %collective-permute-start.16 = (bf16[2,256,128]{2,1,0:T(8,128)(2,1)S(1)}, bf16[2,256,128]{2,1,0:T(8,128)(2,1)S(1)}, u32[]{:S(2)}, u32[]{:S(2)}) collective-permute-start(bf16[2,256,128]{2,1,0:T(8,128)(2,1)S(1)} %get-tuple-element.80.refs_0_.refs_4_), channel_id=1, source_target_pairs={{0,3},{1,2},{2,1},{3,0},{4,7},{5,6},{6,5},{7,4},{8,11},{9,10},{10,... | collective-permute-start | bytes 393224 | tf_op jit(solution)/shard_map/ppermute | solution.py:317
  42.9 9.7 %collective-permute-start.17 = (bf16[2,256,128]{2,1,0:T(8,128)(2,1)S(1)}, bf16[2,256,128]{2,1,0:T(8,128)(2,1)S(1)}, u32[]{:S(2)}, u32[]{:S(2)}) collective-permute-start(bf16[2,256,128]{2,1,0:T(8,128)(2,1)S(1)} %get-tuple-element.80.refs_0_.refs_4_), channel_id=1, source_target_pairs={{0,1},{1,0},{2,3},{3,2},{4,5},{5,4},{6,7},{7,6},{8,9},{9,8},{10,11... | collective-permute-start | bytes 393224 | tf_op jit(solution)/shard_map/ppermute | solution.py:317
  43.4 9.8 %collective-permute-start.18 = (bf16[2,256,128]{2,1,0:T(8,128)(2,1)S(1)}, bf16[2,256,128]{2,1,0:T(8,128)(2,1)S(1)}, u32[]{:S(2)}, u32[]{:S(2)}) collective-permute-start(bf16[2,256,128]{2,1,0:T(8,128)(2,1)S(1)} %get-tuple-element.80.refs_0_.refs_4_), channel_id=1, source_target_pairs={{0,2},{1,3},{2,0},{3,1},{4,6},{5,7},{6,4},{7,5},{8,10},{9,11},{10,... | collective-permute-start | bytes 393224 | tf_op jit(solution)/shard_map/ppermute | solution.py:317
  53.2 14.8 %collective-permute-start.19 = (bf16[256,1536]{1,0:T(8,128)(2,1)S(1)}, bf16[256,1536]{1,0:T(8,128)(2,1)S(1)}, u32[]{:S(2)}, u32[]{:S(2)}) collective-permute-start(bf16[256,1536]{1,0:T(8,128)(2,1)S(1)} %get-tuple-element.82.refs_1_), channel_id=1, source_target_pairs={{0,4},{4,0},{8,12},{12,8},{16,20},{20,16},{24,28},{28,24},{1,5},{5... | collective-permute-start | bytes 2359304 | tf_op jit(solution)/shard_map/ppermute | solution.py:320
  53.2 5.8 %collective-permute-start.21 = (bf16[144,128]{1,0:T(8,128)(2,1)S(1)}, bf16[144,128]{1,0:T(8,128)(2,1)S(1)}, u32[]{:S(2)}, u32[]{:S(2)}) collective-permute-start(bf16[144,128]{1,0:T(8,128)(2,1)S(1)} %get-tuple-element.81), channel_id=1, source_target_pairs={{8,0},{12,4},{16,8},{20,12},{24,16},{28,20},{9,1},{13,5},{17,9},{2... | collective-permute-start | bytes 110600 | tf_op jit(solution)/shard_map/ppermute | solution.py:326
  54.5 6.8 %collective-permute-start.22 = (bf16[144,128]{1,0:T(8,128)(2,1)S(1)}, bf16[144,128]{1,0:T(8,128)(2,1)S(1)}, u32[]{:S(2)}, u32[]{:S(2)}) collective-permute-start(bf16[144,128]{1,0:T(8,128)(2,1)S(1)} %get-tuple-element.81), channel_id=1, source_target_pairs={{16,0},{20,4},{24,8},{28,12},{17,1},{21,5},{25,9},{29,13},{18,2},{... | collective-permute-start | bytes 110600 | tf_op jit(solution)/shard_map/ppermute | solution.py:326
  55.8 8.8 %collective-permute-start.23 = (bf16[144,128]{1,0:T(8,128)(2,1)S(1)}, bf16[144,128]{1,0:T(8,128)(2,1)S(1)}, u32[]{:S(2)}, u32[]{:S(2)}) collective-permute-start(bf16[144,128]{1,0:T(8,128)(2,1)S(1)} %get-tuple-element.81), channel_id=1, source_target_pairs={{24,0},{28,4},{25,1},{29,5},{26,2},{30,6},{27,3},{31,7}} | collective-permute-start | bytes 110600 | tf_op jit(solution)/shard_map/ppermute | solution.py:326
  64.6 5.8 %collective-permute-start.24 = (f32[256,512]{1,0:T(8,128)S(1)}, f32[256,512]{1,0:T(8,128)S(1)}, u32[]{:S(2)}, u32[]{:S(2)}) collective-permute-start(f32[256,512]{1,0:T(8,128)S(1)} %get-tuple-element.89), channel_id=1, source_target_pairs={{0,4},{4,0},{8,12},{12,8},{16,20},{20,16},{24,28},{28,24},{1,5},{5... | collective-permute-start | bytes 1572872 | tf_op jit(solution)/shard_map/ppermute | solution.py:320
  64.6 3.0 %collective-permute-start.12 = (bf16[128,1536]{1,0:T(8,128)(2,1)S(1)}, bf16[128,1536]{1,0:T(8,128)(2,1)S(1)}, u32[]{:S(2)}, u32[]{:S(2)}) collective-permute-start(bf16[128,1536]{1,0:T(8,128)(2,1)S(1)} %get-tuple-element.69.refs_0_), channel_id=1, source_target_pairs={{0,4},{4,0},{8,12},{12,8},{16,20},{20,16},{24,28},{28,24},{1,5},{5... | collective-permute-start | bytes 1179656 | tf_op jit(solution)/shard_map/ppermute | solution.py:320
  65.1 5.3 %collective-permute-start.25 = (bf16[144,128]{1,0:T(8,128)(2,1)S(1)}, bf16[144,128]{1,0:T(8,128)(2,1)S(1)}, u32[]{:S(2)}, u32[]{:S(2)}) collective-permute-start(bf16[144,128]{1,0:T(8,128)(2,1)S(1)} %collective-permute-done.21.refs_0_), channel_id=1, source_target_pairs={{0,4},{4,0},{8,12},{12,8},{16,20},{20,16},{24,28},{28,24},{1,5},{5... | collective-permute-start | bytes 110600 | tf_op jit(solution)/shard_map/ppermute | solution.py:320
  (10 other events, 70.7 us)

commit v8 on v6

--- a/solution.py
+++ b/solution.py
@@ -89,6 +89,18 @@
 def put_message(ref, state, total):
     ref[0:HD, :] = state.astype(BF16)
     put_total(ref, HD, total)
+
+
+def join_kernel(own_ref, got_ref, out_ref):
+    total = get_total(own_ref, HD)
+    state = own_ref[0:HD, :].astype(F32) + jnp.exp(total) * got_ref[0:HD, :].astype(F32)
+    put_message(out_ref, state, total + get_total(got_ref, HD))
+
+
+def cross_kernel(where_ref, *refs):
+    *normed_refs, cross_ref = refs
+    for number, ref in enumerate(normed_refs):
+        cross_ref[number] = ref[1 - where_ref[0]]
 
 
 def lanes_of(number):
@@ -206,12 +218,9 @@
 
 
 def inner_grad_kernel(
-    where_ref, q_ref, k_ref, v_ref, col_ref, row_ref, grad_ref, state_ref, second_ref, *refs
+    where_ref, q_ref, k_ref, v_ref, col_ref, row_ref, grad_ref, state_ref, second_ref, keep_ref, send_ref
 ):
-    normed_refs, (keep_ref, send_ref, cross_ref) = refs[:-3], refs[-3:]
     core = where_ref[0]
-    for number, ref in enumerate(normed_refs):
-        cross_ref[number] = ref[1 - core]
     columns, across = col_ref[...], row_ref[...]
     length = columns.shape[0]
     lower = triangle(length)
@@ -363,17 +372,22 @@
         [where, queries, keys, values, *got[:3], log_decay, got[3]],
     )
     (fresh,) = after([fresh], grad_got)
-    arrived = [to_chip(fresh, step) for step in range(1, chips)]
+    arrived, window, step = [], fresh, 1
+    while step < chips:
+        if arrived:
+            (window,) = call(without_where(join_kernel), "join", [message], [where, window, arrived[-1]])
+        arrived.append(to_chip(window, step))
+        step *= 2
     (inner,) = call(without_where(inner_kernel), "inner", [pair32], [where, q, k, v, col, row, first])
     pieces = [("own", [weight_own])]
     for (step, halves), piece in zip(plan, arriving):
         if halves:
-            (piece,) = after([piece], fresh)
+            (piece,) = after([piece], arrived[0])
         pieces.append(("halves", [piece, swap_side(piece)]) if halves else ("whole", [piece]))
     partials, mine, theirs = [], [], []
     for number in range(0, tensor, 2):
         kinds, sources = zip(*pieces[number : number + 2])
-        sources = after(sum(sources, []), *arrived, inner, *partials)
+        sources = after(sum(sources, []), arrived[0], inner, *partials)
         *outs, weight = call(
             functools.partial(partial_kernel, kinds),
             "partial",
@@ -400,23 +414,25 @@
         [where, q, col, gain, mixed, own_partial, *sent],
     )
     (upward,) = after([upward], *normed_all)
-    returned = [to_chip(upward, -step) for step in range(1, chips)]
+    (cross,) = call(cross_kernel, "cross", [shape(BF16, tensor, length, HD)], [where, *normed_all])
+    cross_got = swap_core(cross)
+    returned = [to_chip(upward, -step) for step in reversed(range(1, chips))][::-1]
     theirs += [swap_core(weight) for weight in after(mine[1:], upward)]
-    inner_keep, inner_send, cross = call(
+    inner_keep, inner_send = call(
         inner_grad_kernel,
         "inner_grad",
-        [shape(F32, length, 4 * HD)] * 2 + [shape(BF16, tensor, length, HD)],
-        [where, q, k, v, col, row, grad_mixed, states, second, *normed_all],
-    )
-    cross_got = swap_core(cross)
-    inner_got = swap_core(*after([inner_send], *returned))
+        [shape(F32, length, 4 * HD)] * 2,
+        [where, q, k, v, col, row, grad_mixed, states, second],
+    )
     (layer_out,) = call(
         functools.partial(layer_kernel, tensor // 2),
         "layer",
         [shape(BF16, length, width)],
         [where, weight_own, *mine, *theirs, *normed_all, cross_got],
     )
-    returned_got = after([swap_core(rows) for rows in returned], layer_out)
+    returned = after(returned, layer_out)
+    inner_got = swap_core(*after([inner_send], *returned))
+    returned_got = [swap_core(rows) for rows in returned]
     query_grad, key_grad, value_grad = call(
         functools.partial(outer_grad_kernel, chips - 1),
         "outer_grad",

time: 64.5 us -> 61.9 us (0.960)
  starting transfers between devices: 31.3 us -> 29.4 us
  waiting for transfers between devices: 15.8 us -> 13.9 us
  Pallas kernels: 12.8 us -> 13.9 us
    ppermute x1, waiting for transfers between devices: 0.01 us -> 2.74 us  [swap_side(): return lax.ppermute(value, 'seq', [(i, i ^ 2) for i in range(seq)])]
    ppermute x6 -> x5, starting transfers between devices: 15 us -> 12.5 us  [to_chip(): lax.ppermute(value, 'seq', [(i, i + 2 * step) for i in range(seq) if 0 <=...]
    ppermute x9, waiting for transfers between devices: 7.75 us -> 5.35 us  [swap_tensor(): return lax.ppermute(value, 'tensor', [(i, i ^ k) for i in range(tensor)])]
    ppermute x6 -> x5, waiting for transfers between devices: 6.15 us -> 4.77 us  [to_chip(): lax.ppermute(value, 'seq', [(i, i + 2 * step) for i in range(seq) if 0 <=...]
    pallas_call x9 -> x11, Pallas kernels: 12.8 us -> 13.9 us  [call(): pl.pallas_call(kernel, name=name, out_shape=outs, in_specs=[SMEM] + [VMEM...]
    ppermute x12, waiting for transfers between devices: 1.85 us -> 1.07 us  [swap_core(): return lax.ppermute(value, 'seq', [(i, i ^ 1) for i in range(seq)])]
  transfers between devices with their start and end apart: 28 -> 27, of which waited for: 7 -> 8; matrix products, arithmetic and copies ran while one was open for 5% -> 5% of each run, Pallas kernels for 16% -> 18%
where the time goes in v8:
time: 61.9 us; the launch traced here: 61.6 us
  starting transfers between devices  29.4 us (47%)
  waiting for transfers between devices  13.9 us (22%)
  Pallas kernels  13.9 us (22%)
  local copies, waits for them, and re-layouts  3.34 us (5%)
  between operations  0.93 us (2%)
    pallas_call x11, Pallas kernels, call(): pl.pallas_call(kernel, name=name, out_shape=outs, in_specs=[SMEM] + [VMEM...  13.9 us
    ppermute x5, starting transfers between devices, to_chip(): lax.ppermute(value, 'seq', [(i, i + 2 * step) for i in range(seq) if 0 <=...  12.5 us
    ppermute x9, starting transfers between devices, swap_tensor(): return lax.ppermute(value, 'tensor', [(i, i ^ k) for i in range(tensor)])  11.3 us
    ppermute x9, waiting for transfers between devices, swap_tensor(): return lax.ppermute(value, 'tensor', [(i, i ^ k) for i in range(tensor)])  5.35 us
    ppermute x5, waiting for transfers between devices, to_chip(): lax.ppermute(value, 'seq', [(i, i + 2 * step) for i in range(seq) if 0 <=...  4.77 us
    ppermute x12, starting transfers between devices, swap_core(): return lax.ppermute(value, 'seq', [(i, i ^ 1) for i in range(seq)])  3.2 us
    ppermute x1, waiting for transfers between devices, swap_side(): return lax.ppermute(value, 'seq', [(i, i ^ 2) for i in range(seq)])  2.74 us
    ppermute x1, starting transfers between devices, swap_side(): return lax.ppermute(value, 'seq', [(i, i ^ 2) for i in range(seq)])  2.32 us
  transfers between devices with their start and end apart: 27, of which 8 were waited for; matrix products, arithmetic and copies ran while one was open for 5% of the time, Pallas kernels for 18%

profile of v8, /device:TPU:0, one launch (start us, length us, event | category | flops | bytes accessed | tf_op | source)
XLA Modules:
  0.0 61.6 jit_solution(16881681785388529409)
XLA Ops:
  2.7 1.2 %fusion = (bf16[128,1536]{1,0:T(8,128)(2,1)S(1)}, bf16[128,1536]{1,0:T(8,128)(2,1)S(1)}) fusion(bf16[256,6144]{1,0:T(8,128)(2,1)} %param.12, s32[]{:T(128)S(6)} %select_n.27, s32[]{:T(128)S(6)} %select_n.29, s32[]{:T(128)S(6)} %select_n.28), kind=kLoop, calls=%fused_computation.2 | loop fusion | bytes 1572876 | tf_op jit(solution)/shard_map/dynamic_slice | solution.py:357
  3.9 1.2 %constant_dynamic-slice_fusion.refs_0_.own_ref = bf16[256,1536]{1,0:T(8,128)(2,1)S(1)} fusion(bf16[256,6144]{1,0:T(8,128)(2,1)} %param.12, s32[]{:T(128)S(6)} %select_n.30), kind=kLoop, calls=%fused_computation.1 | loop fusion | bytes 1572868 | tf_op jit(solution)/shard_map/dynamic_slice | solution.py:364
  5.7 3.5 %collective-permute-start.5 = (bf16[64,1536]{1,0:T(8,128)(2,1)S(1)}, bf16[64,1536]{1,0:T(8,128)(2,1)S(1)}, u32[]{:S(2)}, u32[]{:S(2)}) collective-permute-start(bf16[64,1536]{1,0:T(8,128)(2,1)S(1)} %dynamic_slice.12), channel_id=1, source_target_pairs={{0,3},{1,2},{2,1},{3,0},{4,7},{5,6},{6,5},{7,4},{8,11},{9,10},{10,... | collective-permute-start | bytes 589832 | tf_op jit(solution)/shard_map/ppermute | solution.py:326
  9.9 1.4 %fresh.1 = (bf16[2,256,128]{2,1,0:T(8,128)(2,1)S(1)}, bf16[2,256,128]{2,1,0:T(8,128)(2,1)S(1)}, bf16[2,256,128]{2,1,0:T(8,128)(2,1)S(1)}, f32[256,2]{1,0:T(8,128...) custom-call(s32[2]{0:T(128)S(1)} %pad_add_fusion.where_ref, ...), custom_call_target="tpu_custom_call" | custom-call | flops 1 | bytes 1 | tf_op jit(solution)/shard_map/fresh/pallas_call | solution.py:292
  11.4 3.9 %collective-permute-start.6 = (bf16[144,128]{1,0:T(8,128)(2,1)S(1)}, bf16[144,128]{1,0:T(8,128)(2,1)S(1)}, u32[]{:S(2)}, u32[]{:S(2)}) collective-permute-start(bf16[144,128]{1,0:T(8,128)(2,1)S(1)} %get-tuple-element.56.refs_0_), channel_id=1, source_target_pairs={{0,8},{4,12},{8,16},{12,20},{16,24},{20,28},{1,9},{5,13},{9,17},{1... | collective-permute-start | bytes 110600 | tf_op jit(solution)/shard_map/ppermute | solution.py:335
  15.3 1.6 %collective-permute-done.6.refs_1_.refs_0_ = bf16[144,128]{1,0:T(8,128)(2,1)S(1)} collective-permute-done((bf16[144,128]{1,0:T(8,128)(2,1)S(1)}, bf16[144,128]{1,0:T(8,128)(2,1)S(1)}, u32[]{:S(2)}, u32[]{:S(2)}) %collective-permute-start.6) | collective-permute-done | bytes 36896 | tf_op jit(solution)/shard_map/ppermute | solution.py:335
  16.9 2.3 %collective-permute-start.7 = (bf16[64,1536]{1,0:T(8,128)(2,1)S(1)}, bf16[64,1536]{1,0:T(8,128)(2,1)S(1)}, u32[]{:S(2)}, u32[]{:S(2)}) collective-permute-start(bf16[64,1536]{1,0:T(8,128)(2,1)S(1)} %collective-permute-done.5.refs_1_), channel_id=1, source_target_pairs={{0,8},{4,12},{8,0},{12,4},{16,24},{20,28},{24,16},{28,20},{1,9},{5... | collective-permute-start | bytes 589832 | tf_op jit(solution)/shard_map/ppermute | solution.py:332
  19.2 1.1 %inner.1.inner_ref = f32[2,256,128]{2,1,0:T(8,128)S(1)} custom-call(s32[2]{0:T(128)S(1)} %pad_add_fusion.where_ref, bf16[2,256,128]{2,1,0:T(8,128)(2,1)S(1)} %get-tuple-element.58.refs_0_.q_ref, bf16[2,256,128]{2,1,0:T(8,128)(2,1)S(1)} %get-tuple-element.59.refs_1_.k_ref, bf16[2,256,128]{2,1,0:T(8,128)(2,1)S(1)} %get-tuple-element.60.refs_2_.v_ref, ...), custom_call_target="tpu_custom_call" | custom-call | flops 1 | bytes 1 | tf_op jit(solution)/shard_map/inner/pallas_call | solution.py:292
  20.3 2.7 %collective-permute-done.7.refs_2_ = bf16[64,1536]{1,0:T(8,128)(2,1)S(1)} collective-permute-done((bf16[64,1536]{1,0:T(8,128)(2,1)S(1)}, bf16[64,1536]{1,0:T(8,128)(2,1)S(1)}, u32[]{:S(2)}, u32[]{:S(2)}) %collective-permute-start.7) | collective-permute-done | bytes 196640 | tf_op jit(solution)/shard_map/ppermute | solution.py:332
  23.0 1.2 %partial.2 = (f32[2,256,128]{2,1,0:T(8,128)S(1)}, bf16[2,256,128]{2,1,0:T(8,128)(2,1)S(1)}, bf16[128,1536]{1,0:T(8,128)(2,1)S(1)}) custom-call(s32[2]{0:T(128)S(1)} %pad_add_fusion.where_ref, bf16[256,1536]{1,0:T(8,128)(2,1)S(1)} %copy-done, bf16[256,1536]{1,0:T(8,128)(2,1)S(1)} %collective-permute-done.4.got_ref, ...), custom_call_target="tpu_custom_call" | custom-call | flops 1 | bytes 1 | tf_op jit(solution)/shard_map/partial/pallas_call | solution.py:292
  24.2 1.2 %partial.3 = (bf16[2,256,128]{2,1,0:T(8,128)(2,1)S(1)}, bf16[2,256,128]{2,1,0:T(8,128)(2,1)S(1)}, bf16[256,1536]{1,0:T(8,128)(2,1)S(1)}) custom-call(s32[2]{0:T(128)S(1)} %pad_add_fusion.where_ref, bf16[256,1536]{1,0:T(8,128)(2,1)S(1)} %copy-done, bf16[256,1536]{1,0:T(8,128)(2,1)S(1)} %collective-permute-done.4.got_ref, ...), custom_call_target="tpu_custom_call" | custom-call | flops 1 | bytes 1 | tf_op jit(solution)/shard_map/partial/pallas_call | solution.py:292
  25.4 1.5 %collective-permute-start.13 = (bf16[2,256,128]{2,1,0:T(8,128)(2,1)S(1)}, bf16[2,256,128]{2,1,0:T(8,128)(2,1)S(1)}, u32[]{:S(2)}, u32[]{:S(2)}) collective-permute-start(bf16[2,256,128]{2,1,0:T(8,128)(2,1)S(1)} %get-tuple-element.73), channel_id=1, source_target_pairs={{0,1},{1,0},{2,3},{3,2},{4,5},{5,4},{6,7},{7,6},{8,9},{9,8},{10,11... | collective-permute-start | bytes 393224 | tf_op jit(solution)/shard_map/ppermute | solution.py:326
  27.5 4.8 %collective-permute-start.11 = (bf16[144,128]{1,0:T(8,128)(2,1)S(1)}, bf16[144,128]{1,0:T(8,128)(2,1)S(1)}, u32[]{:S(2)}, u32[]{:S(2)}) collective-permute-start(bf16[144,128]{1,0:T(8,128)(2,1)S(1)} %join.1), channel_id=1, source_target_pairs={{0,16},{4,20},{8,24},{12,28},{1,17},{5,21},{9,25},{13,29},{2,18},{... | collective-permute-start | bytes 110600 | tf_op jit(solution)/shard_map/ppermute | solution.py:335
  32.3 1.6 %collective-permute-start.12 = (bf16[2,256,128]{2,1,0:T(8,128)(2,1)S(1)}, bf16[2,256,128]{2,1,0:T(8,128)(2,1)S(1)}, u32[]{:S(2)}, u32[]{:S(2)}) collective-permute-start(bf16[2,256,128]{2,1,0:T(8,128)(2,1)S(1)} %get-tuple-element.69), channel_id=1, source_target_pairs={{0,3},{1,2},{2,1},{3,0},{4,7},{5,6},{6,5},{7,4},{8,11},{9,10},{10,... | collective-permute-start | bytes 393224 | tf_op jit(solution)/shard_map/ppermute | solution.py:326
  35.2 2.5 %collective-permute-start.15 = (bf16[2,256,128]{2,1,0:T(8,128)(2,1)S(1)}, bf16[2,256,128]{2,1,0:T(8,128)(2,1)S(1)}, u32[]{:S(2)}, u32[]{:S(2)}) collective-permute-start(bf16[2,256,128]{2,1,0:T(8,128)(2,1)S(1)} %get-tuple-element.79.refs_0_.refs_4_), channel_id=1, source_target_pairs={{0,3},{1,2},{2,1},{3,0},{4,7},{5,6},{6,5},{7,4},{8,11},{9,10},{10,... | collective-permute-start | bytes 393224 | tf_op jit(solution)/shard_map/ppermute | solution.py:326
  38.8 4.9 %collective-permute-done.14.refs_2_ = bf16[2,256,128]{2,1,0:T(8,128)(2,1)S(1)} collective-permute-done((bf16[2,256,128]{2,1,0:T(8,128)(2,1)S(1)}, bf16[2,256,128]{2,1,0:T(8,128)(2,1)S(1)}, u32[]{:S(2)}, u32[]{:S(2)}) %collective-permute-start.14) | collective-permute-done | bytes 131104 | tf_op jit(solution)/shard_map/ppermute | solution.py:326
  43.7 1.2 %grad_mixed.1 = (f32[2,256,128]{2,1,0:T(8,128)S(1)}, f32[128,128]{1,0:T(8,128)S(1)}, bf16[144,128]{1,0:T(8,128)(2,1)S(1)}) custom-call(s32[2]{0:T(128)S(1)} %pad_add_fusion.where_ref, bf16[2,256,128]{2,1,0:T(8,128)(2,1)S(1)} %get-tuple-element.58.refs_0_.q_ref, f32[256,2]{1,0:T(8,128)S(1)} %get-tuple-element.61.refs_3_.col_ref, f32[1,256]{1,0:T(1,128)S(1)} %bitcast.4, ...), custom_call_target="tpu_custom_call" | custom-call | flops 1 | bytes 1 | tf_op jit(solution)/shard_map/grad_mixed/pallas_call | solution.py:292
  46.5 1.3 %collective-permute-start.20 = (bf16[144,128]{1,0:T(8,128)(2,1)S(1)}, bf16[144,128]{1,0:T(8,128)(2,1)S(1)}, u32[]{:S(2)}, u32[]{:S(2)}) collective-permute-start(bf16[144,128]{1,0:T(8,128)(2,1)S(1)} %get-tuple-element.80), channel_id=1, source_target_pairs={{8,0},{12,4},{16,8},{20,12},{24,16},{28,20},{9,1},{13,5},{17,9},{2... | collective-permute-start | bytes 110600 | tf_op jit(solution)/shard_map/ppermute | solution.py:335
  47.8 1.3 %collective-permute-start.21 = (bf16[144,128]{1,0:T(8,128)(2,1)S(1)}, bf16[144,128]{1,0:T(8,128)(2,1)S(1)}, u32[]{:S(2)}, u32[]{:S(2)}) collective-permute-start(bf16[144,128]{1,0:T(8,128)(2,1)S(1)} %get-tuple-element.80), channel_id=1, source_target_pairs={{16,0},{20,4},{24,8},{28,12},{17,1},{21,5},{25,9},{29,13},{18,2},{... | collective-permute-start | bytes 110600 | tf_op jit(solution)/shard_map/ppermute | solution.py:335
  49.1 1.3 %collective-permute-start.22 = (bf16[144,128]{1,0:T(8,128)(2,1)S(1)}, bf16[144,128]{1,0:T(8,128)(2,1)S(1)}, u32[]{:S(2)}, u32[]{:S(2)}) collective-permute-start(bf16[144,128]{1,0:T(8,128)(2,1)S(1)} %get-tuple-element.80), channel_id=1, source_target_pairs={{24,0},{28,4},{25,1},{29,5},{26,2},{30,6},{27,3},{31,7}} | collective-permute-start | bytes 110600 | tf_op jit(solution)/shard_map/ppermute | solution.py:335
  50.4 1.9 %inner_grad.1 = (f32[256,512]{1,0:T(8,128)S(1)}, f32[256,512]{1,0:T(8,128)S(1)}) custom-call(s32[2]{0:T(128)S(1)} %pad_add_fusion.where_ref, bf16[2,256,128]{2,1,0:T(8,128)(2,1)S(1)} %get-tuple-element.58.refs_0_.q_ref, bf16[2,256,128]{2,1,0:T(8,128)(2,1)S(1)} %get-tuple-element.59.refs_1_.k_ref, bf16[2,256,128]{2,1,0:T(8,128)(2,1)S(1)} %get-tuple-element.60.refs_2_.v_ref, ...), custom_call_target="tpu_custom_call" | custom-call | flops 1 | bytes 1 | tf_op jit(solution)/shard_map/inner_grad/pallas_call | solution.py:292
  52.3 2.4 %layer.1 = bf16[256,1536]{1,0:T(8,128)(2,1)} custom-call(s32[2]{0:T(128)S(1)} %pad_add_fusion.where_ref, bf16[256,1536]{1,0:T(8,128)(2,1)S(1)} %constant_dynamic-slice_fusion.refs_0_.own_ref, bf16[128,1536]{1,0:T(8,128)(2,1)S(1)} %get-tuple-element.67.refs_0_, bf16[256,1536]{1,0:T(8,128)(2,1)S(1)} %get-tuple-element.81.refs_1_, ...), custom_call_target="tpu_custom_call" | custom-call | flops 1 | bytes 1 | tf_op jit(solution)/shard_map/layer/pallas_call | solution.py:292
  54.8 3.2 %collective-permute-done.22.refs_2_ = bf16[144,128]{1,0:T(8,128)(2,1)S(1)} collective-permute-done((bf16[144,128]{1,0:T(8,128)(2,1)S(1)}, bf16[144,128]{1,0:T(8,128)(2,1)S(1)}, u32[]{:S(2)}, u32[]{:S(2)}) %collective-permute-start.22) | collective-permute-done | bytes 36896 | tf_op jit(solution)/shard_map/ppermute | solution.py:335
  60.0 1.5 %outer_grad.1 = (bf16[256,256]{1,0:T(8,128)(2,1)}, bf16[256,256]{1,0:T(8,128)(2,1)}, bf16[256,256]{1,0:T(8,128)(2,1)}) custom-call(s32[2]{0:T(128)S(1)} %pad_add_fusion.where_ref, bf16[256,256]{1,0:T(8,128)(2,1)S(1)} %copy-done.1, bf16[256,256]{1,0:T(8,128)(2,1)S(1)} %copy-done.2, f32[256,512]{1,0:T(8,128)S(1)} %get-tuple-element.85.inner_ref, ...), custom_call_target="tpu_custom_call" | custom-call | flops 1 | bytes 1 | tf_op jit(solution)/shard_map/outer_grad/pallas_call | solution.py:292
  (57 shorter events, 10.0 us)
Async XLA Ops:
  0.7 4.4 %collective-permute-start = (bf16[256,256]{1,0:T(8,128)(2,1)}, bf16[256,256]{1,0:T(8,128)(2,1)S(1)}, u32[]{:S(2)}, u32[]{:S(2)}) collective-permute-start(bf16[256,256]{1,0:T(8,128)(2,1)} %q_ref.1), channel_id=1, source_target_pairs={{0,4},{4,0},{8,12},{12,8},{16,20},{20,16},{24,28},{28,24},{1,5},{5... | collective-permute-start | bytes 393224 | tf_op jit(solution)/shard_map/ppermute | solution.py:329
  1.2 3.9 %collective-permute-start.1 = (bf16[256,256]{1,0:T(8,128)(2,1)}, bf16[256,256]{1,0:T(8,128)(2,1)S(1)}, u32[]{:S(2)}, u32[]{:S(2)}) collective-permute-start(bf16[256,256]{1,0:T(8,128)(2,1)} %k_ref.3), channel_id=1, source_target_pairs={{0,4},{4,0},{8,12},{12,8},{16,20},{20,16},{24,28},{28,24},{1,5},{5... | collective-permute-start | bytes 393224 | tf_op jit(solution)/shard_map/ppermute | solution.py:329
  1.3 3.9 %collective-permute-start.2 = (bf16[256,256]{1,0:T(8,128)(2,1)}, bf16[256,256]{1,0:T(8,128)(2,1)S(1)}, u32[]{:S(2)}, u32[]{:S(2)}) collective-permute-start(bf16[256,256]{1,0:T(8,128)(2,1)} %v_ref.3), channel_id=1, source_target_pairs={{0,4},{4,0},{8,12},{12,8},{16,20},{20,16},{24,28},{28,24},{1,5},{5... | collective-permute-start | bytes 393224 | tf_op jit(solution)/shard_map/ppermute | solution.py:329
  1.7 3.4 %collective-permute-start.3 = (f32[2,256]{1,0:T(2,128)}, f32[2,256]{1,0:T(2,128)S(1)}, u32[]{:S(2)}, u32[]{:S(2)}) collective-permute-start(f32[2,256]{1,0:T(2,128)} %decay_ref.1), channel_id=1, source_target_pairs={{0,4},{4,0},{8,12},{12,8},{16,20},{20,16},{24,28},{28,24},{1,5},{5... | collective-permute-start | bytes 6152 | tf_op jit(solution)/shard_map/ppermute | solution.py:329
  5.2 6.2 %collective-permute-start.4 = (bf16[256,1536]{1,0:T(8,128)(2,1)S(1)}, bf16[256,1536]{1,0:T(8,128)(2,1)S(1)}, u32[]{:S(2)}, u32[]{:S(2)}) collective-permute-start(bf16[256,1536]{1,0:T(8,128)(2,1)S(1)} %copy-done), channel_id=1, source_target_pairs={{0,4},{4,0},{8,12},{12,8},{16,20},{20,16},{24,28},{28,24},{1,5},{5... | collective-permute-start | bytes 2359304 | tf_op jit(solution)/shard_map/ppermute | solution.py:329
  5.7 9.6 %collective-permute-start.5 = (bf16[64,1536]{1,0:T(8,128)(2,1)S(1)}, bf16[64,1536]{1,0:T(8,128)(2,1)S(1)}, u32[]{:S(2)}, u32[]{:S(2)}) collective-permute-start(bf16[64,1536]{1,0:T(8,128)(2,1)S(1)} %dynamic_slice.12), channel_id=1, source_target_pairs={{0,3},{1,2},{2,1},{3,0},{4,7},{5,6},{6,5},{7,4},{8,11},{9,10},{10,... | collective-permute-start | bytes 589832 | tf_op jit(solution)/shard_map/ppermute | solution.py:326
  9.2 15.0 %collective-permute-start.8 = (bf16[128,1536]{1,0:T(8,128)(2,1)S(1)}, bf16[128,1536]{1,0:T(8,128)(2,1)S(1)}, u32[]{:S(2)}, u32[]{:S(2)}) collective-permute-start(bf16[128,1536]{1,0:T(8,128)(2,1)S(1)} %get-tuple-element.95), channel_id=1, source_target_pairs={{0,1},{1,0},{2,3},{3,2},{4,5},{5,4},{6,7},{7,6},{8,9},{9,8},{10,11... | collective-permute-start | bytes 1179656 | tf_op jit(solution)/shard_map/ppermute | solution.py:326
  9.7 14.5 %collective-permute-start.9 = (bf16[128,1536]{1,0:T(8,128)(2,1)S(1)}, bf16[128,1536]{1,0:T(8,128)(2,1)S(1)}, u32[]{:S(2)}, u32[]{:S(2)}) collective-permute-start(bf16[128,1536]{1,0:T(8,128)(2,1)S(1)} %get-tuple-element.94), channel_id=1, source_target_pairs={{0,2},{1,3},{2,0},{3,1},{4,6},{5,7},{6,4},{7,5},{8,10},{9,11},{10,... | collective-permute-start | bytes 1179656 | tf_op jit(solution)/shard_map/ppermute | solution.py:326
  11.4 5.5 %collective-permute-start.6 = (bf16[144,128]{1,0:T(8,128)(2,1)S(1)}, bf16[144,128]{1,0:T(8,128)(2,1)S(1)}, u32[]{:S(2)}, u32[]{:S(2)}) collective-permute-start(bf16[144,128]{1,0:T(8,128)(2,1)S(1)} %get-tuple-element.56.refs_0_), channel_id=1, source_target_pairs={{0,8},{4,12},{8,16},{12,20},{16,24},{20,28},{1,9},{5,13},{9,17},{1... | collective-permute-start | bytes 110600 | tf_op jit(solution)/shard_map/ppermute | solution.py:335
  16.9 6.1 %collective-permute-start.7 = (bf16[64,1536]{1,0:T(8,128)(2,1)S(1)}, bf16[64,1536]{1,0:T(8,128)(2,1)S(1)}, u32[]{:S(2)}, u32[]{:S(2)}) collective-permute-start(bf16[64,1536]{1,0:T(8,128)(2,1)S(1)} %collective-permute-done.5.refs_1_), channel_id=1, source_target_pairs={{0,8},{4,12},{8,0},{12,4},{16,24},{20,28},{24,16},{28,20},{1,9},{5... | collective-permute-start | bytes 589832 | tf_op jit(solution)/shard_map/ppermute | solution.py:332
  25.4 12.9 %collective-permute-start.13 = (bf16[2,256,128]{2,1,0:T(8,128)(2,1)S(1)}, bf16[2,256,128]{2,1,0:T(8,128)(2,1)S(1)}, u32[]{:S(2)}, u32[]{:S(2)}) collective-permute-start(bf16[2,256,128]{2,1,0:T(8,128)(2,1)S(1)} %get-tuple-element.73), channel_id=1, source_target_pairs={{0,1},{1,0},{2,3},{3,2},{4,5},{5,4},{6,7},{7,6},{8,9},{9,8},{10,11... | collective-permute-start | bytes 393224 | tf_op jit(solution)/shard_map/ppermute | solution.py:326
  27.5 6.8 %collective-permute-start.11 = (bf16[144,128]{1,0:T(8,128)(2,1)S(1)}, bf16[144,128]{1,0:T(8,128)(2,1)S(1)}, u32[]{:S(2)}, u32[]{:S(2)}) collective-permute-start(bf16[144,128]{1,0:T(8,128)(2,1)S(1)} %join.1), channel_id=1, source_target_pairs={{0,16},{4,20},{8,24},{12,28},{1,17},{5,21},{9,25},{13,29},{2,18},{... | collective-permute-start | bytes 110600 | tf_op jit(solution)/shard_map/ppermute | solution.py:335
  32.3 11.4 %collective-permute-start.12 = (bf16[2,256,128]{2,1,0:T(8,128)(2,1)S(1)}, bf16[2,256,128]{2,1,0:T(8,128)(2,1)S(1)}, u32[]{:S(2)}, u32[]{:S(2)}) collective-permute-start(bf16[2,256,128]{2,1,0:T(8,128)(2,1)S(1)} %get-tuple-element.69), channel_id=1, source_target_pairs={{0,3},{1,2},{2,1},{3,0},{4,7},{5,6},{6,5},{7,4},{8,11},{9,10},{10,... | collective-permute-start | bytes 393224 | tf_op jit(solution)/shard_map/ppermute | solution.py:326
  33.8 9.9 %collective-permute-start.14 = (bf16[2,256,128]{2,1,0:T(8,128)(2,1)S(1)}, bf16[2,256,128]{2,1,0:T(8,128)(2,1)S(1)}, u32[]{:S(2)}, u32[]{:S(2)}) collective-permute-start(bf16[2,256,128]{2,1,0:T(8,128)(2,1)S(1)} %get-tuple-element.74), channel_id=1, source_target_pairs={{0,2},{1,3},{2,0},{3,1},{4,6},{5,7},{6,4},{7,5},{8,10},{9,11},{10,... | collective-permute-start | bytes 393224 | tf_op jit(solution)/shard_map/ppermute | solution.py:326
  35.2 9.6 %collective-permute-start.15 = (bf16[2,256,128]{2,1,0:T(8,128)(2,1)S(1)}, bf16[2,256,128]{2,1,0:T(8,128)(2,1)S(1)}, u32[]{:S(2)}, u32[]{:S(2)}) collective-permute-start(bf16[2,256,128]{2,1,0:T(8,128)(2,1)S(1)} %get-tuple-element.79.refs_0_.refs_4_), channel_id=1, source_target_pairs={{0,3},{1,2},{2,1},{3,0},{4,7},{5,6},{6,5},{7,4},{8,11},{9,10},{10,... | collective-permute-start | bytes 393224 | tf_op jit(solution)/shard_map/ppermute | solution.py:326
  37.8 7.2 %collective-permute-start.16 = (bf16[2,256,128]{2,1,0:T(8,128)(2,1)S(1)}, bf16[2,256,128]{2,1,0:T(8,128)(2,1)S(1)}, u32[]{:S(2)}, u32[]{:S(2)}) collective-permute-start(bf16[2,256,128]{2,1,0:T(8,128)(2,1)S(1)} %get-tuple-element.79.refs_0_.refs_4_), channel_id=1, source_target_pairs={{0,1},{1,0},{2,3},{3,2},{4,5},{5,4},{6,7},{7,6},{8,9},{9,8},{10,11... | collective-permute-start | bytes 393224 | tf_op jit(solution)/shard_map/ppermute | solution.py:326
  38.3 7.0 %collective-permute-start.17 = (bf16[2,256,128]{2,1,0:T(8,128)(2,1)S(1)}, bf16[2,256,128]{2,1,0:T(8,128)(2,1)S(1)}, u32[]{:S(2)}, u32[]{:S(2)}) collective-permute-start(bf16[2,256,128]{2,1,0:T(8,128)(2,1)S(1)} %get-tuple-element.79.refs_0_.refs_4_), channel_id=1, source_target_pairs={{0,2},{1,3},{2,0},{3,1},{4,6},{5,7},{6,4},{7,5},{8,10},{9,11},{10,... | collective-permute-start | bytes 393224 | tf_op jit(solution)/shard_map/ppermute | solution.py:326
  45.3 7.0 %collective-permute-start.18 = (bf16[256,1536]{1,0:T(8,128)(2,1)S(1)}, bf16[256,1536]{1,0:T(8,128)(2,1)S(1)}, u32[]{:S(2)}, u32[]{:S(2)}) collective-permute-start(bf16[256,1536]{1,0:T(8,128)(2,1)S(1)} %get-tuple-element.81.refs_1_), channel_id=1, source_target_pairs={{0,4},{4,0},{8,12},{12,8},{16,20},{20,16},{24,28},{28,24},{1,5},{5... | collective-permute-start | bytes 2359304 | tf_op jit(solution)/shard_map/ppermute | solution.py:329
  45.3 7.0 %collective-permute-start.10 = (bf16[128,1536]{1,0:T(8,128)(2,1)S(1)}, bf16[128,1536]{1,0:T(8,128)(2,1)S(1)}, u32[]{:S(2)}, u32[]{:S(2)}) collective-permute-start(bf16[128,1536]{1,0:T(8,128)(2,1)S(1)} %get-tuple-element.67.refs_0_), channel_id=1, source_target_pairs={{0,4},{4,0},{8,12},{12,8},{16,20},{20,16},{24,28},{28,24},{1,5},{5... | collective-permute-start | bytes 1179656 | tf_op jit(solution)/shard_map/ppermute | solution.py:329
  46.4 2.7 %collective-permute-start.19 = (bf16[4,256,128]{2,1,0:T(8,128)(2,1)S(1)}, bf16[4,256,128]{2,1,0:T(8,128)(2,1)S(1)}, u32[]{:S(2)}, u32[]{:S(2)}) collective-permute-start(bf16[4,256,128]{2,1,0:T(8,128)(2,1)S(1)} %cross.1), channel_id=1, source_target_pairs={{0,4},{4,0},{8,12},{12,8},{16,20},{20,16},{24,28},{28,24},{1,5},{5... | collective-permute-start | bytes 786440 | tf_op jit(solution)/shard_map/ppermute | solution.py:329
  46.5 8.3 %collective-permute-start.20 = (bf16[144,128]{1,0:T(8,128)(2,1)S(1)}, bf16[144,128]{1,0:T(8,128)(2,1)S(1)}, u32[]{:S(2)}, u32[]{:S(2)}) collective-permute-start(bf16[144,128]{1,0:T(8,128)(2,1)S(1)} %get-tuple-element.80), channel_id=1, source_target_pairs={{8,0},{12,4},{16,8},{20,12},{24,16},{28,20},{9,1},{13,5},{17,9},{2... | collective-permute-start | bytes 110600 | tf_op jit(solution)/shard_map/ppermute | solution.py:335
  47.8 7.0 %collective-permute-start.21 = (bf16[144,128]{1,0:T(8,128)(2,1)S(1)}, bf16[144,128]{1,0:T(8,128)(2,1)S(1)}, u32[]{:S(2)}, u32[]{:S(2)}) collective-permute-start(bf16[144,128]{1,0:T(8,128)(2,1)S(1)} %get-tuple-element.80), channel_id=1, source_target_pairs={{16,0},{20,4},{24,8},{28,12},{17,1},{21,5},{25,9},{29,13},{18,2},{... | collective-permute-start | bytes 110600 | tf_op jit(solution)/shard_map/ppermute | solution.py:335
  49.1 8.8 %collective-permute-start.22 = (bf16[144,128]{1,0:T(8,128)(2,1)S(1)}, bf16[144,128]{1,0:T(8,128)(2,1)S(1)}, u32[]{:S(2)}, u32[]{:S(2)}) collective-permute-start(bf16[144,128]{1,0:T(8,128)(2,1)S(1)} %get-tuple-element.80), channel_id=1, source_target_pairs={{24,0},{28,4},{25,1},{29,5},{26,2},{30,6},{27,3},{31,7}} | collective-permute-start | bytes 110600 | tf_op jit(solution)/shard_map/ppermute | solution.py:335
  57.9 2.1 %collective-permute-start.23 = (f32[256,512]{1,0:T(8,128)S(1)}, f32[256,512]{1,0:T(8,128)S(1)}, u32[]{:S(2)}, u32[]{:S(2)}) collective-permute-start(f32[256,512]{1,0:T(8,128)S(1)} %get-tuple-element.90), channel_id=1, source_target_pairs={{0,4},{4,0},{8,12},{12,8},{16,20},{20,16},{24,28},{28,24},{1,5},{5... | collective-permute-start | bytes 1572872 | tf_op jit(solution)/shard_map/ppermute | solution.py:329
  (9 other events, 69.5 us)

commit v9 on v8

--- a/solution.py
+++ b/solution.py
@@ -251,8 +251,8 @@
     core = where_ref[0]
     outs = refs[2 * count :]
     for head, inner, chip_refs in (
-        (core, inner_ref, refs[:count]),
-        (1 - core, inner_got_ref, refs[count : 2 * count]),
+        (core, inner_ref, refs[:count][::-1]),
+        (1 - core, inner_got_ref, refs[count : 2 * count][::-1]),
     ):
         high, low = split(chip_sum(chip_refs))
         fade = inner[:, 3 * HD : 4 * HD]
@@ -387,7 +387,7 @@
     partials, mine, theirs = [], [], []
     for number in range(0, tensor, 2):
         kinds, sources = zip(*pieces[number : number + 2])
-        sources = after(sum(sources, []), arrived[0], inner, *partials)
+        sources = after(sum(sources, []), *arrived, inner, *partials)
         *outs, weight = call(
             functools.partial(partial_kernel, kinds),
             "partial",
@@ -416,7 +416,7 @@
     (upward,) = after([upward], *normed_all)
     (cross,) = call(cross_kernel, "cross", [shape(BF16, tensor, length, HD)], [where, *normed_all])
     cross_got = swap_core(cross)
-    returned = [to_chip(upward, -step) for step in reversed(range(1, chips))][::-1]
+    returned = [to_chip(upward, -step) for step in reversed(range(1, chips))]
     theirs += [swap_core(weight) for weight in after(mine[1:], upward)]
     inner_keep, inner_send = call(
         inner_grad_kernel,

time: 61.9 us -> 56.6 us (0.914)
  waiting for transfers between devices: 13.9 us -> 8.95 us
    ppermute x1, waiting for transfers between devices: 2.74 us -> 0.01 us  [swap_side(): return lax.ppermute(value, 'seq', [(i, i ^ 2) for i in range(seq)])]
    ppermute x5, waiting for transfers between devices: 4.77 us -> 3.04 us  [to_chip(): lax.ppermute(value, 'seq', [(i, i + 2 * step) for i in range(seq) if 0 <=...]
  transfers between devices with their start and end apart: 27 -> 27, of which waited for: 8 -> 8; matrix products, arithmetic and copies ran while one was open for 5% -> 6% of each run, Pallas kernels for 18% -> 20%
where the time goes in v9:
time: 56.6 us; the launch traced here: 56.2 us
  starting transfers between devices  29.1 us (51%)
  Pallas kernels  13.9 us (25%)
  waiting for transfers between devices  8.95 us (16%)
  local copies, waits for them, and re-layouts  3.34 us (6%)
  between operations  0.93 us (2%)
    pallas_call x11, Pallas kernels, call(): pl.pallas_call(kernel, name=name, out_shape=outs, in_specs=[SMEM] + [VMEM...  13.9 us
    ppermute x5, starting transfers between devices, to_chip(): lax.ppermute(value, 'seq', [(i, i + 2 * step) for i in range(seq) if 0 <=...  12.3 us
    ppermute x9, starting transfers between devices, swap_tensor(): return lax.ppermute(value, 'tensor', [(i, i ^ k) for i in range(tensor)])  11.3 us
    ppermute x9, waiting for transfers between devices, swap_tensor(): return lax.ppermute(value, 'tensor', [(i, i ^ k) for i in range(tensor)])  4.84 us
    ppermute x12, starting transfers between devices, swap_core(): return lax.ppermute(value, 'seq', [(i, i ^ 1) for i in range(seq)])  3.21 us
    ppermute x5, waiting for transfers between devices, to_chip(): lax.ppermute(value, 'seq', [(i, i + 2 * step) for i in range(seq) if 0 <=...  3.04 us
    ppermute x1, starting transfers between devices, swap_side(): return lax.ppermute(value, 'seq', [(i, i ^ 2) for i in range(seq)])  2.32 us
    dynamic_slice x2, local copies, waits for them, and re-layouts, slice_for(): lax.dynamic_slice(out_weight, (begin, (place ^ step) * width), (rows, wid...  2.12 us
  transfers between devices with their start and end apart: 27, of which 8 were waited for; matrix products, arithmetic and copies ran while one was open for 6% of the time, Pallas kernels for 20%

profile of v9, /device:TPU:0, one launch (start us, length us, event | category | flops | bytes accessed | tf_op | source)
XLA Modules:
  0.0 56.2 jit_solution(6056414183941072339)
XLA Ops:
  1.8 0.9 %dynamic_slice.12 = bf16[64,1536]{1,0:T(8,128)(2,1)S(1)} dynamic-slice(bf16[256,6144]{1,0:T(8,128)(2,1)} %param.12, s32[]{:T(128)S(6)} %select_n.25, s32[]{:T(128)S(6)} %select_n.26), dynamic_slice_sizes={64,1536} | dynamic-slice | bytes 393220 | tf_op jit(solution)/shard_map/dynamic_slice | solution.py:357
  2.7 1.2 %fusion = (bf16[128,1536]{1,0:T(8,128)(2,1)S(1)}, bf16[128,1536]{1,0:T(8,128)(2,1)S(1)}) fusion(bf16[256,6144]{1,0:T(8,128)(2,1)} %param.12, s32[]{:T(128)S(6)} %select_n.27, s32[]{:T(128)S(6)} %select_n.29, s32[]{:T(128)S(6)} %select_n.28), kind=kLoop, calls=%fused_computation.2 | loop fusion | bytes 1572876 | tf_op jit(solution)/shard_map/dynamic_slice | solution.py:357
  3.9 1.2 %constant_dynamic-slice_fusion.refs_0_.own_ref = bf16[256,1536]{1,0:T(8,128)(2,1)S(1)} fusion(bf16[256,6144]{1,0:T(8,128)(2,1)} %param.12, s32[]{:T(128)S(6)} %select_n.30), kind=kLoop, calls=%fused_computation.1 | loop fusion | bytes 1572868 | tf_op jit(solution)/shard_map/dynamic_slice | solution.py:364
  5.7 3.5 %collective-permute-start.5 = (bf16[64,1536]{1,0:T(8,128)(2,1)S(1)}, bf16[64,1536]{1,0:T(8,128)(2,1)S(1)}, u32[]{:S(2)}, u32[]{:S(2)}) collective-permute-start(bf16[64,1536]{1,0:T(8,128)(2,1)S(1)} %dynamic_slice.12), channel_id=1, source_target_pairs={{0,3},{1,2},{2,1},{3,0},{4,7},{5,6},{6,5},{7,4},{8,11},{9,10},{10,... | collective-permute-start | bytes 589832 | tf_op jit(solution)/shard_map/ppermute | solution.py:326
  9.9 1.4 %fresh.1 = (bf16[2,256,128]{2,1,0:T(8,128)(2,1)S(1)}, bf16[2,256,128]{2,1,0:T(8,128)(2,1)S(1)}, bf16[2,256,128]{2,1,0:T(8,128)(2,1)S(1)}, f32[256,2]{1,0:T(8,128...) custom-call(s32[2]{0:T(128)S(1)} %pad_add_fusion.where_ref, ...), custom_call_target="tpu_custom_call" | custom-call | flops 1 | bytes 1 | tf_op jit(solution)/shard_map/fresh/pallas_call | solution.py:292
  11.4 3.9 %collective-permute-start.6 = (bf16[144,128]{1,0:T(8,128)(2,1)S(1)}, bf16[144,128]{1,0:T(8,128)(2,1)S(1)}, u32[]{:S(2)}, u32[]{:S(2)}) collective-permute-start(bf16[144,128]{1,0:T(8,128)(2,1)S(1)} %get-tuple-element.56.refs_0_), channel_id=1, source_target_pairs={{0,8},{4,12},{8,16},{12,20},{16,24},{20,28},{1,9},{5,13},{9,17},{1... | collective-permute-start | bytes 110600 | tf_op jit(solution)/shard_map/ppermute | solution.py:335
  15.3 1.6 %collective-permute-done.6.refs_1_.refs_0_ = bf16[144,128]{1,0:T(8,128)(2,1)S(1)} collective-permute-done((bf16[144,128]{1,0:T(8,128)(2,1)S(1)}, bf16[144,128]{1,0:T(8,128)(2,1)S(1)}, u32[]{:S(2)}, u32[]{:S(2)}) %collective-permute-start.6) | collective-permute-done | bytes 36896 | tf_op jit(solution)/shard_map/ppermute | solution.py:335
  16.9 2.3 %collective-permute-start.7 = (bf16[64,1536]{1,0:T(8,128)(2,1)S(1)}, bf16[64,1536]{1,0:T(8,128)(2,1)S(1)}, u32[]{:S(2)}, u32[]{:S(2)}) collective-permute-start(bf16[64,1536]{1,0:T(8,128)(2,1)S(1)} %collective-permute-done.5.refs_1_), channel_id=1, source_target_pairs={{0,8},{4,12},{8,0},{12,4},{16,24},{20,28},{24,16},{28,20},{1,9},{5... | collective-permute-start | bytes 589832 | tf_op jit(solution)/shard_map/ppermute | solution.py:332
  19.8 4.5 %collective-permute-start.8 = (bf16[144,128]{1,0:T(8,128)(2,1)S(1)}, bf16[144,128]{1,0:T(8,128)(2,1)S(1)}, u32[]{:S(2)}, u32[]{:S(2)}) collective-permute-start(bf16[144,128]{1,0:T(8,128)(2,1)S(1)} %join.1), channel_id=1, source_target_pairs={{0,16},{4,20},{8,24},{12,28},{1,17},{5,21},{9,25},{13,29},{2,18},{... | collective-permute-start | bytes 110600 | tf_op jit(solution)/shard_map/ppermute | solution.py:335
  24.3 1.1 %inner.1.inner_ref = f32[2,256,128]{2,1,0:T(8,128)S(1)} custom-call(s32[2]{0:T(128)S(1)} %pad_add_fusion.where_ref, bf16[2,256,128]{2,1,0:T(8,128)(2,1)S(1)} %get-tuple-element.58.refs_0_.q_ref, bf16[2,256,128]{2,1,0:T(8,128)(2,1)S(1)} %get-tuple-element.59.refs_1_.k_ref, bf16[2,256,128]{2,1,0:T(8,128)(2,1)S(1)} %get-tuple-element.60.refs_2_.v_ref, ...), custom_call_target="tpu_custom_call" | custom-call | flops 1 | bytes 1 | tf_op jit(solution)/shard_map/inner/pallas_call | solution.py:292
  25.9 1.2 %partial.2 = (f32[2,256,128]{2,1,0:T(8,128)S(1)}, bf16[2,256,128]{2,1,0:T(8,128)(2,1)S(1)}, bf16[128,1536]{1,0:T(8,128)(2,1)S(1)}) custom-call(s32[2]{0:T(128)S(1)} %pad_add_fusion.where_ref, bf16[256,1536]{1,0:T(8,128)(2,1)S(1)} %copy-done, bf16[256,1536]{1,0:T(8,128)(2,1)S(1)} %collective-permute-done.4.got_ref, ...), custom_call_target="tpu_custom_call" | custom-call | flops 1 | bytes 1 | tf_op jit(solution)/shard_map/partial/pallas_call | solution.py:292
  27.1 1.2 %partial.3 = (bf16[2,256,128]{2,1,0:T(8,128)(2,1)S(1)}, bf16[2,256,128]{2,1,0:T(8,128)(2,1)S(1)}, bf16[256,1536]{1,0:T(8,128)(2,1)S(1)}) custom-call(s32[2]{0:T(128)S(1)} %pad_add_fusion.where_ref, bf16[256,1536]{1,0:T(8,128)(2,1)S(1)} %copy-done, bf16[256,1536]{1,0:T(8,128)(2,1)S(1)} %collective-permute-done.4.got_ref, ...), custom_call_target="tpu_custom_call" | custom-call | flops 1 | bytes 1 | tf_op jit(solution)/shard_map/partial/pallas_call | solution.py:292
  28.2 1.6 %collective-permute-start.13 = (bf16[2,256,128]{2,1,0:T(8,128)(2,1)S(1)}, bf16[2,256,128]{2,1,0:T(8,128)(2,1)S(1)}, u32[]{:S(2)}, u32[]{:S(2)}) collective-permute-start(bf16[2,256,128]{2,1,0:T(8,128)(2,1)S(1)} %get-tuple-element.73), channel_id=1, source_target_pairs={{0,1},{1,0},{2,3},{3,2},{4,5},{5,4},{6,7},{7,6},{8,9},{9,8},{10,11... | collective-permute-start | bytes 393224 | tf_op jit(solution)/shard_map/ppermute | solution.py:326
  29.8 1.5 %collective-permute-start.12 = (bf16[2,256,128]{2,1,0:T(8,128)(2,1)S(1)}, bf16[2,256,128]{2,1,0:T(8,128)(2,1)S(1)}, u32[]{:S(2)}, u32[]{:S(2)}) collective-permute-start(bf16[2,256,128]{2,1,0:T(8,128)(2,1)S(1)} %get-tuple-element.69), channel_id=1, source_target_pairs={{0,3},{1,2},{2,1},{3,0},{4,7},{5,6},{6,5},{7,4},{8,11},{9,10},{10,... | collective-permute-start | bytes 393224 | tf_op jit(solution)/shard_map/ppermute | solution.py:326
  32.7 2.5 %collective-permute-start.15 = (bf16[2,256,128]{2,1,0:T(8,128)(2,1)S(1)}, bf16[2,256,128]{2,1,0:T(8,128)(2,1)S(1)}, u32[]{:S(2)}, u32[]{:S(2)}) collective-permute-start(bf16[2,256,128]{2,1,0:T(8,128)(2,1)S(1)} %get-tuple-element.79.refs_0_.refs_4_), channel_id=1, source_target_pairs={{0,3},{1,2},{2,1},{3,0},{4,7},{5,6},{6,5},{7,4},{8,11},{9,10},{10,... | collective-permute-start | bytes 393224 | tf_op jit(solution)/shard_map/ppermute | solution.py:326
  36.3 4.6 %collective-permute-done.14.refs_2_ = bf16[2,256,128]{2,1,0:T(8,128)(2,1)S(1)} collective-permute-done((bf16[2,256,128]{2,1,0:T(8,128)(2,1)S(1)}, bf16[2,256,128]{2,1,0:T(8,128)(2,1)S(1)}, u32[]{:S(2)}, u32[]{:S(2)}) %collective-permute-start.14) | collective-permute-done | bytes 131104 | tf_op jit(solution)/shard_map/ppermute | solution.py:326
  40.9 1.2 %grad_mixed.1 = (f32[2,256,128]{2,1,0:T(8,128)S(1)}, f32[128,128]{1,0:T(8,128)S(1)}, bf16[144,128]{1,0:T(8,128)(2,1)S(1)}) custom-call(s32[2]{0:T(128)S(1)} %pad_add_fusion.where_ref, bf16[2,256,128]{2,1,0:T(8,128)(2,1)S(1)} %get-tuple-element.58.refs_0_.q_ref, f32[256,2]{1,0:T(8,128)S(1)} %get-tuple-element.61.refs_3_.col_ref, f32[1,256]{1,0:T(1,128)S(1)} %bitcast.4, ...), custom_call_target="tpu_custom_call" | custom-call | flops 1 | bytes 1 | tf_op jit(solution)/shard_map/grad_mixed/pallas_call | solution.py:292
  43.4 1.3 %collective-permute-start.20 = (bf16[144,128]{1,0:T(8,128)(2,1)S(1)}, bf16[144,128]{1,0:T(8,128)(2,1)S(1)}, u32[]{:S(2)}, u32[]{:S(2)}) collective-permute-start(bf16[144,128]{1,0:T(8,128)(2,1)S(1)} %get-tuple-element.80), channel_id=1, source_target_pairs={{24,0},{28,4},{25,1},{29,5},{26,2},{30,6},{27,3},{31,7}} | collective-permute-start | bytes 110600 | tf_op jit(solution)/shard_map/ppermute | solution.py:335
  44.7 1.3 %collective-permute-start.21 = (bf16[144,128]{1,0:T(8,128)(2,1)S(1)}, bf16[144,128]{1,0:T(8,128)(2,1)S(1)}, u32[]{:S(2)}, u32[]{:S(2)}) collective-permute-start(bf16[144,128]{1,0:T(8,128)(2,1)S(1)} %get-tuple-element.80), channel_id=1, source_target_pairs={{16,0},{20,4},{24,8},{28,12},{17,1},{21,5},{25,9},{29,13},{18,2},{... | collective-permute-start | bytes 110600 | tf_op jit(solution)/shard_map/ppermute | solution.py:335
  46.1 1.3 %collective-permute-start.22 = (bf16[144,128]{1,0:T(8,128)(2,1)S(1)}, bf16[144,128]{1,0:T(8,128)(2,1)S(1)}, u32[]{:S(2)}, u32[]{:S(2)}) collective-permute-start(bf16[144,128]{1,0:T(8,128)(2,1)S(1)} %get-tuple-element.80), channel_id=1, source_target_pairs={{8,0},{12,4},{16,8},{20,12},{24,16},{28,20},{9,1},{13,5},{17,9},{2... | collective-permute-start | bytes 110600 | tf_op jit(solution)/shard_map/ppermute | solution.py:335
  47.4 1.9 %inner_grad.1 = (f32[256,512]{1,0:T(8,128)S(1)}, f32[256,512]{1,0:T(8,128)S(1)}) custom-call(s32[2]{0:T(128)S(1)} %pad_add_fusion.where_ref, bf16[2,256,128]{2,1,0:T(8,128)(2,1)S(1)} %get-tuple-element.58.refs_0_.q_ref, bf16[2,256,128]{2,1,0:T(8,128)(2,1)S(1)} %get-tuple-element.59.refs_1_.k_ref, bf16[2,256,128]{2,1,0:T(8,128)(2,1)S(1)} %get-tuple-element.60.refs_2_.v_ref, ...), custom_call_target="tpu_custom_call" | custom-call | flops 1 | bytes 1 | tf_op jit(solution)/shard_map/inner_grad/pallas_call | solution.py:292
  49.3 2.4 %layer.1 = bf16[256,1536]{1,0:T(8,128)(2,1)} custom-call(s32[2]{0:T(128)S(1)} %pad_add_fusion.where_ref, bf16[256,1536]{1,0:T(8,128)(2,1)S(1)} %constant_dynamic-slice_fusion.refs_0_.own_ref, bf16[128,1536]{1,0:T(8,128)(2,1)S(1)} %get-tuple-element.67.refs_0_, bf16[256,1536]{1,0:T(8,128)(2,1)S(1)} %get-tuple-element.81.refs_1_, ...), custom_call_target="tpu_custom_call" | custom-call | flops 1 | bytes 1 | tf_op jit(solution)/shard_map/layer/pallas_call | solution.py:292
  53.6 0.9 %collective-permute-done.24.refs_3_ = bf16[144,128]{1,0:T(8,128)(2,1)S(1)} collective-permute-done((bf16[144,128]{1,0:T(8,128)(2,1)S(1)}, bf16[144,128]{1,0:T(8,128)(2,1)S(1)}, u32[]{:S(2)}, u32[]{:S(2)}) %collective-permute-start.24) | collective-permute-done | bytes 36896 | tf_op jit(solution)/shard_map/ppermute | solution.py:329
  54.7 1.5 %outer_grad.1 = (bf16[256,256]{1,0:T(8,128)(2,1)}, bf16[256,256]{1,0:T(8,128)(2,1)}, bf16[256,256]{1,0:T(8,128)(2,1)}) custom-call(s32[2]{0:T(128)S(1)} %pad_add_fusion.where_ref, bf16[256,256]{1,0:T(8,128)(2,1)S(1)} %copy-done.1, bf16[256,256]{1,0:T(8,128)(2,1)S(1)} %copy-done.2, f32[256,512]{1,0:T(8,128)S(1)} %get-tuple-element.85.inner_ref, ...), custom_call_target="tpu_custom_call" | custom-call | flops 1 | bytes 1 | tf_op jit(solution)/shard_map/outer_grad/pallas_call | solution.py:292
  (57 shorter events, 9.3 us)
Async XLA Ops:
  0.7 4.4 %collective-permute-start = (bf16[256,256]{1,0:T(8,128)(2,1)}, bf16[256,256]{1,0:T(8,128)(2,1)S(1)}, u32[]{:S(2)}, u32[]{:S(2)}) collective-permute-start(bf16[256,256]{1,0:T(8,128)(2,1)} %q_ref.1), channel_id=1, source_target_pairs={{0,4},{4,0},{8,12},{12,8},{16,20},{20,16},{24,28},{28,24},{1,5},{5... | collective-permute-start | bytes 393224 | tf_op jit(solution)/shard_map/ppermute | solution.py:329
  1.2 3.9 %collective-permute-start.1 = (bf16[256,256]{1,0:T(8,128)(2,1)}, bf16[256,256]{1,0:T(8,128)(2,1)S(1)}, u32[]{:S(2)}, u32[]{:S(2)}) collective-permute-start(bf16[256,256]{1,0:T(8,128)(2,1)} %k_ref.3), channel_id=1, source_target_pairs={{0,4},{4,0},{8,12},{12,8},{16,20},{20,16},{24,28},{28,24},{1,5},{5... | collective-permute-start | bytes 393224 | tf_op jit(solution)/shard_map/ppermute | solution.py:329
  1.3 3.9 %collective-permute-start.2 = (bf16[256,256]{1,0:T(8,128)(2,1)}, bf16[256,256]{1,0:T(8,128)(2,1)S(1)}, u32[]{:S(2)}, u32[]{:S(2)}) collective-permute-start(bf16[256,256]{1,0:T(8,128)(2,1)} %v_ref.3), channel_id=1, source_target_pairs={{0,4},{4,0},{8,12},{12,8},{16,20},{20,16},{24,28},{28,24},{1,5},{5... | collective-permute-start | bytes 393224 | tf_op jit(solution)/shard_map/ppermute | solution.py:329
  1.7 3.4 %collective-permute-start.3 = (f32[2,256]{1,0:T(2,128)}, f32[2,256]{1,0:T(2,128)S(1)}, u32[]{:S(2)}, u32[]{:S(2)}) collective-permute-start(f32[2,256]{1,0:T(2,128)} %decay_ref.1), channel_id=1, source_target_pairs={{0,4},{4,0},{8,12},{12,8},{16,20},{20,16},{24,28},{28,24},{1,5},{5... | collective-permute-start | bytes 6152 | tf_op jit(solution)/shard_map/ppermute | solution.py:329
  5.2 6.2 %collective-permute-start.4 = (bf16[256,1536]{1,0:T(8,128)(2,1)S(1)}, bf16[256,1536]{1,0:T(8,128)(2,1)S(1)}, u32[]{:S(2)}, u32[]{:S(2)}) collective-permute-start(bf16[256,1536]{1,0:T(8,128)(2,1)S(1)} %copy-done), channel_id=1, source_target_pairs={{0,4},{4,0},{8,12},{12,8},{16,20},{20,16},{24,28},{28,24},{1,5},{5... | collective-permute-start | bytes 2359304 | tf_op jit(solution)/shard_map/ppermute | solution.py:329
  5.7 9.6 %collective-permute-start.5 = (bf16[64,1536]{1,0:T(8,128)(2,1)S(1)}, bf16[64,1536]{1,0:T(8,128)(2,1)S(1)}, u32[]{:S(2)}, u32[]{:S(2)}) collective-permute-start(bf16[64,1536]{1,0:T(8,128)(2,1)S(1)} %dynamic_slice.12), channel_id=1, source_target_pairs={{0,3},{1,2},{2,1},{3,0},{4,7},{5,6},{6,5},{7,4},{8,11},{9,10},{10,... | collective-permute-start | bytes 589832 | tf_op jit(solution)/shard_map/ppermute | solution.py:326
  9.2 17.9 %collective-permute-start.10 = (bf16[128,1536]{1,0:T(8,128)(2,1)S(1)}, bf16[128,1536]{1,0:T(8,128)(2,1)S(1)}, u32[]{:S(2)}, u32[]{:S(2)}) collective-permute-start(bf16[128,1536]{1,0:T(8,128)(2,1)S(1)} %get-tuple-element.94), channel_id=1, source_target_pairs={{0,2},{1,3},{2,0},{3,1},{4,6},{5,7},{6,4},{7,5},{8,10},{9,11},{10,... | collective-permute-start | bytes 1179656 | tf_op jit(solution)/shard_map/ppermute | solution.py:326
  9.7 17.4 %collective-permute-start.9 = (bf16[128,1536]{1,0:T(8,128)(2,1)S(1)}, bf16[128,1536]{1,0:T(8,128)(2,1)S(1)}, u32[]{:S(2)}, u32[]{:S(2)}) collective-permute-start(bf16[128,1536]{1,0:T(8,128)(2,1)S(1)} %get-tuple-element.95), channel_id=1, source_target_pairs={{0,1},{1,0},{2,3},{3,2},{4,5},{5,4},{6,7},{7,6},{8,9},{9,8},{10,11... | collective-permute-start | bytes 1179656 | tf_op jit(solution)/shard_map/ppermute | solution.py:326
  11.4 5.5 %collective-permute-start.6 = (bf16[144,128]{1,0:T(8,128)(2,1)S(1)}, bf16[144,128]{1,0:T(8,128)(2,1)S(1)}, u32[]{:S(2)}, u32[]{:S(2)}) collective-permute-start(bf16[144,128]{1,0:T(8,128)(2,1)S(1)} %get-tuple-element.56.refs_0_), channel_id=1, source_target_pairs={{0,8},{4,12},{8,16},{12,20},{16,24},{20,28},{1,9},{5,13},{9,17},{1... | collective-permute-start | bytes 110600 | tf_op jit(solution)/shard_map/ppermute | solution.py:335
  16.9 9.0 %collective-permute-start.7 = (bf16[64,1536]{1,0:T(8,128)(2,1)S(1)}, bf16[64,1536]{1,0:T(8,128)(2,1)S(1)}, u32[]{:S(2)}, u32[]{:S(2)}) collective-permute-start(bf16[64,1536]{1,0:T(8,128)(2,1)S(1)} %collective-permute-done.5.refs_1_), channel_id=1, source_target_pairs={{0,8},{4,12},{8,0},{12,4},{16,24},{20,28},{24,16},{28,20},{1,9},{5... | collective-permute-start | bytes 589832 | tf_op jit(solution)/shard_map/ppermute | solution.py:332
  19.8 6.1 %collective-permute-start.8 = (bf16[144,128]{1,0:T(8,128)(2,1)S(1)}, bf16[144,128]{1,0:T(8,128)(2,1)S(1)}, u32[]{:S(2)}, u32[]{:S(2)}) collective-permute-start(bf16[144,128]{1,0:T(8,128)(2,1)S(1)} %join.1), channel_id=1, source_target_pairs={{0,16},{4,20},{8,24},{12,28},{1,17},{5,21},{9,25},{13,29},{2,18},{... | collective-permute-start | bytes 110600 | tf_op jit(solution)/shard_map/ppermute | solution.py:335
  28.2 7.5 %collective-permute-start.13 = (bf16[2,256,128]{2,1,0:T(8,128)(2,1)S(1)}, bf16[2,256,128]{2,1,0:T(8,128)(2,1)S(1)}, u32[]{:S(2)}, u32[]{:S(2)}) collective-permute-start(bf16[2,256,128]{2,1,0:T(8,128)(2,1)S(1)} %get-tuple-element.73), channel_id=1, source_target_pairs={{0,1},{1,0},{2,3},{3,2},{4,5},{5,4},{6,7},{7,6},{8,9},{9,8},{10,11... | collective-permute-start | bytes 393224 | tf_op jit(solution)/shard_map/ppermute | solution.py:326
  29.8 11.1 %collective-permute-start.12 = (bf16[2,256,128]{2,1,0:T(8,128)(2,1)S(1)}, bf16[2,256,128]{2,1,0:T(8,128)(2,1)S(1)}, u32[]{:S(2)}, u32[]{:S(2)}) collective-permute-start(bf16[2,256,128]{2,1,0:T(8,128)(2,1)S(1)} %get-tuple-element.69), channel_id=1, source_target_pairs={{0,3},{1,2},{2,1},{3,0},{4,7},{5,6},{6,5},{7,4},{8,11},{9,10},{10,... | collective-permute-start | bytes 393224 | tf_op jit(solution)/shard_map/ppermute | solution.py:326
  31.3 9.6 %collective-permute-start.14 = (bf16[2,256,128]{2,1,0:T(8,128)(2,1)S(1)}, bf16[2,256,128]{2,1,0:T(8,128)(2,1)S(1)}, u32[]{:S(2)}, u32[]{:S(2)}) collective-permute-start(bf16[2,256,128]{2,1,0:T(8,128)(2,1)S(1)} %get-tuple-element.74), channel_id=1, source_target_pairs={{0,2},{1,3},{2,0},{3,1},{4,6},{5,7},{6,4},{7,5},{8,10},{9,11},{10,... | collective-permute-start | bytes 393224 | tf_op jit(solution)/shard_map/ppermute | solution.py:326
  32.7 9.4 %collective-permute-start.15 = (bf16[2,256,128]{2,1,0:T(8,128)(2,1)S(1)}, bf16[2,256,128]{2,1,0:T(8,128)(2,1)S(1)}, u32[]{:S(2)}, u32[]{:S(2)}) collective-permute-start(bf16[2,256,128]{2,1,0:T(8,128)(2,1)S(1)} %get-tuple-element.79.refs_0_.refs_4_), channel_id=1, source_target_pairs={{0,3},{1,2},{2,1},{3,0},{4,7},{5,6},{6,5},{7,4},{8,11},{9,10},{10,... | collective-permute-start | bytes 393224 | tf_op jit(solution)/shard_map/ppermute | solution.py:326
  35.2 6.9 %collective-permute-start.16 = (bf16[2,256,128]{2,1,0:T(8,128)(2,1)S(1)}, bf16[2,256,128]{2,1,0:T(8,128)(2,1)S(1)}, u32[]{:S(2)}, u32[]{:S(2)}) collective-permute-start(bf16[2,256,128]{2,1,0:T(8,128)(2,1)S(1)} %get-tuple-element.79.refs_0_.refs_4_), channel_id=1, source_target_pairs={{0,1},{1,0},{2,3},{3,2},{4,5},{5,4},{6,7},{7,6},{8,9},{9,8},{10,11... | collective-permute-start | bytes 393224 | tf_op jit(solution)/shard_map/ppermute | solution.py:326
  35.8 6.5 %collective-permute-start.17 = (bf16[2,256,128]{2,1,0:T(8,128)(2,1)S(1)}, bf16[2,256,128]{2,1,0:T(8,128)(2,1)S(1)}, u32[]{:S(2)}, u32[]{:S(2)}) collective-permute-start(bf16[2,256,128]{2,1,0:T(8,128)(2,1)S(1)} %get-tuple-element.79.refs_0_.refs_4_), channel_id=1, source_target_pairs={{0,2},{1,3},{2,0},{3,1},{4,6},{5,7},{6,4},{7,5},{8,10},{9,11},{10,... | collective-permute-start | bytes 393224 | tf_op jit(solution)/shard_map/ppermute | solution.py:326
  42.3 7.0 %collective-permute-start.18 = (bf16[256,1536]{1,0:T(8,128)(2,1)S(1)}, bf16[256,1536]{1,0:T(8,128)(2,1)S(1)}, u32[]{:S(2)}, u32[]{:S(2)}) collective-permute-start(bf16[256,1536]{1,0:T(8,128)(2,1)S(1)} %get-tuple-element.81.refs_1_), channel_id=1, source_target_pairs={{0,4},{4,0},{8,12},{12,8},{16,20},{20,16},{24,28},{28,24},{1,5},{5... | collective-permute-start | bytes 2359304 | tf_op jit(solution)/shard_map/ppermute | solution.py:329
  42.3 7.0 %collective-permute-start.11 = (bf16[128,1536]{1,0:T(8,128)(2,1)S(1)}, bf16[128,1536]{1,0:T(8,128)(2,1)S(1)}, u32[]{:S(2)}, u32[]{:S(2)}) collective-permute-start(bf16[128,1536]{1,0:T(8,128)(2,1)S(1)} %get-tuple-element.67.refs_0_), channel_id=1, source_target_pairs={{0,4},{4,0},{8,12},{12,8},{16,20},{20,16},{24,28},{28,24},{1,5},{5... | collective-permute-start | bytes 1179656 | tf_op jit(solution)/shard_map/ppermute | solution.py:329
  43.4 2.7 %collective-permute-start.19 = (bf16[4,256,128]{2,1,0:T(8,128)(2,1)S(1)}, bf16[4,256,128]{2,1,0:T(8,128)(2,1)S(1)}, u32[]{:S(2)}, u32[]{:S(2)}) collective-permute-start(bf16[4,256,128]{2,1,0:T(8,128)(2,1)S(1)} %cross.1), channel_id=1, source_target_pairs={{0,4},{4,0},{8,12},{12,8},{16,20},{20,16},{24,28},{28,24},{1,5},{5... | collective-permute-start | bytes 786440 | tf_op jit(solution)/shard_map/ppermute | solution.py:329
  43.4 8.3 %collective-permute-start.20 = (bf16[144,128]{1,0:T(8,128)(2,1)S(1)}, bf16[144,128]{1,0:T(8,128)(2,1)S(1)}, u32[]{:S(2)}, u32[]{:S(2)}) collective-permute-start(bf16[144,128]{1,0:T(8,128)(2,1)S(1)} %get-tuple-element.80), channel_id=1, source_target_pairs={{24,0},{28,4},{25,1},{29,5},{26,2},{30,6},{27,3},{31,7}} | collective-permute-start | bytes 110600 | tf_op jit(solution)/shard_map/ppermute | solution.py:335
  44.7 7.8 %collective-permute-start.21 = (bf16[144,128]{1,0:T(8,128)(2,1)S(1)}, bf16[144,128]{1,0:T(8,128)(2,1)S(1)}, u32[]{:S(2)}, u32[]{:S(2)}) collective-permute-start(bf16[144,128]{1,0:T(8,128)(2,1)S(1)} %get-tuple-element.80), channel_id=1, source_target_pairs={{16,0},{20,4},{24,8},{28,12},{17,1},{21,5},{25,9},{29,13},{18,2},{... | collective-permute-start | bytes 110600 | tf_op jit(solution)/shard_map/ppermute | solution.py:335
  46.1 6.5 %collective-permute-start.22 = (bf16[144,128]{1,0:T(8,128)(2,1)S(1)}, bf16[144,128]{1,0:T(8,128)(2,1)S(1)}, u32[]{:S(2)}, u32[]{:S(2)}) collective-permute-start(bf16[144,128]{1,0:T(8,128)(2,1)S(1)} %get-tuple-element.80), channel_id=1, source_target_pairs={{8,0},{12,4},{16,8},{20,12},{24,16},{28,20},{9,1},{13,5},{17,9},{2... | collective-permute-start | bytes 110600 | tf_op jit(solution)/shard_map/ppermute | solution.py:335
  52.6 2.1 %collective-permute-start.23 = (f32[256,512]{1,0:T(8,128)S(1)}, f32[256,512]{1,0:T(8,128)S(1)}, u32[]{:S(2)}, u32[]{:S(2)}) collective-permute-start(f32[256,512]{1,0:T(8,128)S(1)} %get-tuple-element.90), channel_id=1, source_target_pairs={{0,4},{4,0},{8,12},{12,8},{16,20},{20,16},{24,28},{28,24},{1,5},{5... | collective-permute-start | bytes 1572872 | tf_op jit(solution)/shard_map/ppermute | solution.py:329
  (9 other events, 67.0 us)

commit v10 on v9

--- a/solution.py
+++ b/solution.py
@@ -406,38 +406,40 @@
         [pair32, pair16, shape(F32, 2, HD, HD)],
         [where, q, col, inner, gain, first, *after(arrived, *partials)],
     )
-    normed_all = [normed] + [swap_tensor(normed, step) for step in order]
+    theirs += [swap_core(weight) for weight in mine[1:]]
+    sent = after(sent, *theirs)
+    (normed_sent,) = after([normed], *sent)
+    normed_all = [normed] + [swap_tensor(normed_sent, step) for step in order]
     grad_mixed, second, upward = call(
         grad_mixed_kernel,
         "grad_mixed",
         [pair32, shape(F32, HD, HD), message],
         [where, q, col, gain, mixed, own_partial, *sent],
     )
-    (upward,) = after([upward], *normed_all)
     (cross,) = call(cross_kernel, "cross", [shape(BF16, tensor, length, HD)], [where, *normed_all])
     cross_got = swap_core(cross)
+    (upward,) = after([upward], normed_all[-1])
     returned = [to_chip(upward, -step) for step in reversed(range(1, chips))]
-    theirs += [swap_core(weight) for weight in after(mine[1:], upward)]
     inner_keep, inner_send = call(
         inner_grad_kernel,
         "inner_grad",
         [shape(F32, length, 4 * HD)] * 2,
         [where, q, k, v, col, row, grad_mixed, states, second],
     )
-    (layer_out,) = call(
-        functools.partial(layer_kernel, tensor // 2),
-        "layer",
-        [shape(BF16, length, width)],
-        [where, weight_own, *mine, *theirs, *normed_all, cross_got],
-    )
-    returned = after(returned, layer_out)
-    inner_got = swap_core(*after([inner_send], *returned))
+    inner_got = swap_core(*after([inner_send], *returned, *normed_all))
     returned_got = [swap_core(rows) for rows in returned]
     query_grad, key_grad, value_grad = call(
         functools.partial(outer_grad_kernel, chips - 1),
         "outer_grad",
         [both16] * 3,
         [where, keys, values, inner_keep, inner_got, *returned, *returned_got],
+    )
+    (cross_got,) = after([cross_got], key_grad)
+    (layer_out,) = call(
+        functools.partial(layer_kernel, tensor // 2),
+        "layer",
+        [shape(BF16, length, width)],
+        [where, weight_own, *mine, *theirs, *normed_all, cross_got],
     )
     return layer_out, query_grad, key_grad, value_grad
 

time: 56.6 us -> 60.9 us (1.076)
  the two profiles are of different devices: /device:TPU:0 before, /device:TPU:19 now
where the time goes in v10:
time: 60.9 us; the launch traced here: 60.6 us
  starting transfers between devices  28.8 us (47%)
  Pallas kernels  13.9 us (23%)
  waiting for transfers between devices  13.6 us (22%)
  local copies, waits for them, and re-layouts  3.34 us (5%)
  between operations  0.93 us (2%)
    pallas_call x11, Pallas kernels, call(): pl.pallas_call(kernel, name=name, out_shape=outs, in_specs=[SMEM] + [VMEM...  13.9 us
    ppermute x12, starting transfers between devices, swap_core(): return lax.ppermute(value, 'seq', [(i, i ^ 1) for i in range(seq)])  10.5 us
    ppermute x5, starting transfers between devices, to_chip(): lax.ppermute(value, 'seq', [(i, i + 2 * step) for i in range(seq) if 0 <=...  9.02 us
    ppermute x9, starting transfers between devices, swap_tensor(): return lax.ppermute(value, 'tensor', [(i, i ^ k) for i in range(tensor)])  7.96 us
    ppermute x9, waiting for transfers between devices, swap_tensor(): return lax.ppermute(value, 'tensor', [(i, i ^ k) for i in range(tensor)])  6.63 us
    ppermute x5, waiting for transfers between devices, to_chip(): lax.ppermute(value, 'seq', [(i, i + 2 * step) for i in range(seq) if 0 <=...  6.12 us
    dynamic_slice x2, local copies, waits for them, and re-layouts, slice_for(): lax.dynamic_slice(out_weight, (begin, (place ^ step) * width), (rows, wid...  2.12 us
    ppermute x1, starting transfers between devices, swap_side(): return lax.ppermute(value, 'seq', [(i, i ^ 2) for i in range(seq)])  1.3 us
  transfers between devices with their start and end apart: 27, of which 9 were waited for; matrix products, arithmetic and copies ran while one was open for 6% of the time, Pallas kernels for 17%

profile of v10, /device:TPU:19, one launch (start us, length us, event | category | flops | bytes accessed | tf_op | source)
XLA Modules:
  0.0 60.6 jit_solution(17787835847481581193)
XLA Ops:
  3.0 1.2 %fusion = (bf16[128,1536]{1,0:T(8,128)(2,1)S(1)}, bf16[128,1536]{1,0:T(8,128)(2,1)S(1)}) fusion(bf16[256,6144]{1,0:T(8,128)(2,1)} %param.12, s32[]{:T(128)S(6)} %select_n.27, s32[]{:T(128)S(6)} %select_n.29, s32[]{:T(128)S(6)} %select_n.28), kind=kLoop, calls=%fused_computation.2 | loop fusion | bytes 1572876 | tf_op jit(solution)/shard_map/dynamic_slice | solution.py:357
  4.1 1.2 %constant_dynamic-slice_fusion.refs_0_.own_ref = bf16[256,1536]{1,0:T(8,128)(2,1)S(1)} fusion(bf16[256,6144]{1,0:T(8,128)(2,1)} %param.12, s32[]{:T(128)S(6)} %select_n.30), kind=kLoop, calls=%fused_computation.1 | loop fusion | bytes 1572868 | tf_op jit(solution)/shard_map/dynamic_slice | solution.py:364
  5.9 1.2 %collective-permute-start.5 = (bf16[64,1536]{1,0:T(8,128)(2,1)S(1)}, bf16[64,1536]{1,0:T(8,128)(2,1)S(1)}, u32[]{:S(2)}, u32[]{:S(2)}) collective-permute-start(bf16[64,1536]{1,0:T(8,128)(2,1)S(1)} %dynamic_slice.12), channel_id=1, source_target_pairs={{0,3},{1,2},{2,1},{3,0},{4,7},{5,6},{6,5},{7,4},{8,11},{9,10},{10,... | collective-permute-start | bytes 589832 | tf_op jit(solution)/shard_map/ppermute | solution.py:326
  7.3 1.2 %collective-permute-start.9 = (bf16[128,1536]{1,0:T(8,128)(2,1)S(1)}, bf16[128,1536]{1,0:T(8,128)(2,1)S(1)}, u32[]{:S(2)}, u32[]{:S(2)}) collective-permute-start(bf16[128,1536]{1,0:T(8,128)(2,1)S(1)} %get-tuple-element.97), channel_id=1, source_target_pairs={{0,1},{1,0},{2,3},{3,2},{4,5},{5,4},{6,7},{7,6},{8,9},{9,8},{10,11... | collective-permute-start | bytes 1179656 | tf_op jit(solution)/shard_map/ppermute | solution.py:326
  8.6 1.4 %fresh.1 = (bf16[2,256,128]{2,1,0:T(8,128)(2,1)S(1)}, bf16[2,256,128]{2,1,0:T(8,128)(2,1)S(1)}, bf16[2,256,128]{2,1,0:T(8,128)(2,1)S(1)}, f32[256,2]{1,0:T(8,128...) custom-call(s32[2]{0:T(128)S(1)} %pad_add_fusion.where_ref, ...), custom_call_target="tpu_custom_call" | custom-call | flops 1 | bytes 1 | tf_op jit(solution)/shard_map/fresh/pallas_call | solution.py:292
  10.1 3.2 %collective-permute-start.6 = (bf16[144,128]{1,0:T(8,128)(2,1)S(1)}, bf16[144,128]{1,0:T(8,128)(2,1)S(1)}, u32[]{:S(2)}, u32[]{:S(2)}) collective-permute-start(bf16[144,128]{1,0:T(8,128)(2,1)S(1)} %get-tuple-element.57.refs_0_), channel_id=1, source_target_pairs={{0,8},{4,12},{8,16},{12,20},{16,24},{20,28},{1,9},{5,13},{9,17},{1... | collective-permute-start | bytes 110600 | tf_op jit(solution)/shard_map/ppermute | solution.py:335
  13.3 1.8 %collective-permute-done.6.refs_1_.refs_0_ = bf16[144,128]{1,0:T(8,128)(2,1)S(1)} collective-permute-done((bf16[144,128]{1,0:T(8,128)(2,1)S(1)}, bf16[144,128]{1,0:T(8,128)(2,1)S(1)}, u32[]{:S(2)}, u32[]{:S(2)}) %collective-permute-start.6) | collective-permute-done | bytes 36896 | tf_op jit(solution)/shard_map/ppermute | solution.py:335
  15.1 1.3 %collective-permute-start.7 = (bf16[64,1536]{1,0:T(8,128)(2,1)S(1)}, bf16[64,1536]{1,0:T(8,128)(2,1)S(1)}, u32[]{:S(2)}, u32[]{:S(2)}) collective-permute-start(bf16[64,1536]{1,0:T(8,128)(2,1)S(1)} %collective-permute-done.5.refs_1_), channel_id=1, source_target_pairs={{0,8},{4,12},{8,0},{12,4},{16,24},{20,28},{24,16},{28,20},{1,9},{5... | collective-permute-start | bytes 589832 | tf_op jit(solution)/shard_map/ppermute | solution.py:332
  17.0 1.3 %collective-permute-start.8 = (bf16[144,128]{1,0:T(8,128)(2,1)S(1)}, bf16[144,128]{1,0:T(8,128)(2,1)S(1)}, u32[]{:S(2)}, u32[]{:S(2)}) collective-permute-start(bf16[144,128]{1,0:T(8,128)(2,1)S(1)} %join.1), channel_id=1, source_target_pairs={{0,16},{4,20},{8,24},{12,28},{1,17},{5,21},{9,25},{13,29},{2,18},{... | collective-permute-start | bytes 110600 | tf_op jit(solution)/shard_map/ppermute | solution.py:335
  19.3 3.2 %collective-permute-done.8.refs_1_ = bf16[144,128]{1,0:T(8,128)(2,1)S(1)} collective-permute-done((bf16[144,128]{1,0:T(8,128)(2,1)S(1)}, bf16[144,128]{1,0:T(8,128)(2,1)S(1)}, u32[]{:S(2)}, u32[]{:S(2)}) %collective-permute-start.8) | collective-permute-done | bytes 36896 | tf_op jit(solution)/shard_map/ppermute | solution.py:335
  22.6 1.2 %partial.2 = (f32[2,256,128]{2,1,0:T(8,128)S(1)}, bf16[2,256,128]{2,1,0:T(8,128)(2,1)S(1)}, bf16[128,1536]{1,0:T(8,128)(2,1)S(1)}) custom-call(s32[2]{0:T(128)S(1)} %pad_add_fusion.where_ref, bf16[256,1536]{1,0:T(8,128)(2,1)S(1)} %copy-done, bf16[256,1536]{1,0:T(8,128)(2,1)S(1)} %collective-permute-done.4.got_ref, ...), custom_call_target="tpu_custom_call" | custom-call | flops 1 | bytes 1 | tf_op jit(solution)/shard_map/partial/pallas_call | solution.py:292
  23.8 1.2 %partial.3 = (bf16[2,256,128]{2,1,0:T(8,128)(2,1)S(1)}, bf16[2,256,128]{2,1,0:T(8,128)(2,1)S(1)}, bf16[256,1536]{1,0:T(8,128)(2,1)S(1)}) custom-call(s32[2]{0:T(128)S(1)} %pad_add_fusion.where_ref, bf16[256,1536]{1,0:T(8,128)(2,1)S(1)} %copy-done, bf16[256,1536]{1,0:T(8,128)(2,1)S(1)} %collective-permute-done.4.got_ref, ...), custom_call_target="tpu_custom_call" | custom-call | flops 1 | bytes 1 | tf_op jit(solution)/shard_map/partial/pallas_call | solution.py:292
  24.9 3.2 %collective-permute-start.12 = (bf16[256,1536]{1,0:T(8,128)(2,1)S(1)}, bf16[256,1536]{1,0:T(8,128)(2,1)S(1)}, u32[]{:S(2)}, u32[]{:S(2)}) collective-permute-start(bf16[256,1536]{1,0:T(8,128)(2,1)S(1)} %get-tuple-element.73.refs_1_), channel_id=1, source_target_pairs={{0,4},{4,0},{8,12},{12,8},{16,20},{20,16},{24,28},{28,24},{1,5},{5... | collective-permute-start | bytes 2359304 | tf_op jit(solution)/shard_map/ppermute | solution.py:329
  28.5 1.2 %collective-permute-start.15 = (bf16[2,256,128]{2,1,0:T(8,128)(2,1)S(1)}, bf16[2,256,128]{2,1,0:T(8,128)(2,1)S(1)}, u32[]{:S(2)}, u32[]{:S(2)}) collective-permute-start(bf16[2,256,128]{2,1,0:T(8,128)(2,1)S(1)} %get-tuple-element.75), channel_id=1, source_target_pairs={{0,2},{1,3},{2,0},{3,1},{4,6},{5,7},{6,4},{7,5},{8,10},{9,11},{10,... | collective-permute-start | bytes 393224 | tf_op jit(solution)/shard_map/ppermute | solution.py:326
  32.9 3.8 %collective-permute-done.13.refs_0_ = bf16[2,256,128]{2,1,0:T(8,128)(2,1)S(1)} collective-permute-done((bf16[2,256,128]{2,1,0:T(8,128)(2,1)S(1)}, bf16[2,256,128]{2,1,0:T(8,128)(2,1)S(1)}, u32[]{:S(2)}, u32[]{:S(2)}) %collective-permute-start.13) | collective-permute-done | bytes 131104 | tf_op jit(solution)/shard_map/ppermute | solution.py:326
  37.9 1.4 %collective-permute-start.17 = (bf16[2,256,128]{2,1,0:T(8,128)(2,1)S(1)}, bf16[2,256,128]{2,1,0:T(8,128)(2,1)S(1)}, u32[]{:S(2)}, u32[]{:S(2)}) collective-permute-start(bf16[2,256,128]{2,1,0:T(8,128)(2,1)S(1)} %get-tuple-element.82.refs_0_.refs_4_), channel_id=1, source_target_pairs={{0,1},{1,0},{2,3},{3,2},{4,5},{5,4},{6,7},{7,6},{8,9},{9,8},{10,11... | collective-permute-start | bytes 393224 | tf_op jit(solution)/shard_map/ppermute | solution.py:326
  39.3 1.2 %grad_mixed.1 = (f32[2,256,128]{2,1,0:T(8,128)S(1)}, f32[128,128]{1,0:T(8,128)S(1)}, bf16[144,128]{1,0:T(8,128)(2,1)S(1)}) custom-call(s32[2]{0:T(128)S(1)} %pad_add_fusion.where_ref, bf16[2,256,128]{2,1,0:T(8,128)(2,1)S(1)} %get-tuple-element.59.refs_0_.q_ref, f32[256,2]{1,0:T(8,128)S(1)} %get-tuple-element.62.refs_3_.col_ref, f32[1,256]{1,0:T(1,128)S(1)} %bitcast.4, ...), custom_call_target="tpu_custom_call" | custom-call | flops 1 | bytes 1 | tf_op jit(solution)/shard_map/grad_mixed/pallas_call | solution.py:292
  40.5 1.8 %collective-permute-done.18.refs_3_.refs_7_ = bf16[2,256,128]{2,1,0:T(8,128)(2,1)S(1)} collective-permute-done((bf16[2,256,128]{2,1,0:T(8,128)(2,1)S(1)}, bf16[2,256,128]{2,1,0:T(8,128)(2,1)S(1)}, u32[]{:S(2)}, u32[]{:S(2)}) %collective-permute-start.18) | collective-permute-done | bytes 131104 | tf_op jit(solution)/shard_map/ppermute | solution.py:326
  42.9 2.0 %collective-permute-start.21 = (bf16[144,128]{1,0:T(8,128)(2,1)S(1)}, bf16[144,128]{1,0:T(8,128)(2,1)S(1)}, u32[]{:S(2)}, u32[]{:S(2)}) collective-permute-start(bf16[144,128]{1,0:T(8,128)(2,1)S(1)} %get-tuple-element.90), channel_id=1, source_target_pairs={{16,0},{20,4},{24,8},{28,12},{17,1},{21,5},{25,9},{29,13},{18,2},{... | collective-permute-start | bytes 110600 | tf_op jit(solution)/shard_map/ppermute | solution.py:335
  44.9 1.9 %collective-permute-start.22 = (bf16[144,128]{1,0:T(8,128)(2,1)S(1)}, bf16[144,128]{1,0:T(8,128)(2,1)S(1)}, u32[]{:S(2)}, u32[]{:S(2)}) collective-permute-start(bf16[144,128]{1,0:T(8,128)(2,1)S(1)} %get-tuple-element.90), channel_id=1, source_target_pairs={{8,0},{12,4},{16,8},{20,12},{24,16},{28,20},{9,1},{13,5},{17,9},{2... | collective-permute-start | bytes 110600 | tf_op jit(solution)/shard_map/ppermute | solution.py:335
  46.8 1.9 %inner_grad.1 = (f32[256,512]{1,0:T(8,128)S(1)}, f32[256,512]{1,0:T(8,128)S(1)}) custom-call(s32[2]{0:T(128)S(1)} %pad_add_fusion.where_ref, bf16[2,256,128]{2,1,0:T(8,128)(2,1)S(1)} %get-tuple-element.59.refs_0_.q_ref, bf16[2,256,128]{2,1,0:T(8,128)(2,1)S(1)} %get-tuple-element.60.refs_1_.k_ref, bf16[2,256,128]{2,1,0:T(8,128)(2,1)S(1)} %get-tuple-element.61.refs_2_.v_ref, ...), custom_call_target="tpu_custom_call" | custom-call | flops 1 | bytes 1 | tf_op jit(solution)/shard_map/inner_grad/pallas_call | solution.py:292
  49.9 4.3 %collective-permute-start.23 = (f32[256,512]{1,0:T(8,128)S(1)}, f32[256,512]{1,0:T(8,128)S(1)}, u32[]{:S(2)}, u32[]{:S(2)}) collective-permute-start(f32[256,512]{1,0:T(8,128)S(1)} %get-tuple-element.91), channel_id=1, source_target_pairs={{0,4},{4,0},{8,12},{12,8},{16,20},{20,16},{24,28},{28,24},{1,5},{5... | collective-permute-start | bytes 1572872 | tf_op jit(solution)/shard_map/ppermute | solution.py:329
  56.7 1.5 %outer_grad.1 = (bf16[256,256]{1,0:T(8,128)(2,1)}, bf16[256,256]{1,0:T(8,128)(2,1)}, bf16[256,256]{1,0:T(8,128)(2,1)}) custom-call(s32[2]{0:T(128)S(1)} %pad_add_fusion.where_ref, bf16[256,256]{1,0:T(8,128)(2,1)S(1)} %copy-done.1, bf16[256,256]{1,0:T(8,128)(2,1)S(1)} %copy-done.2, f32[256,512]{1,0:T(8,128)S(1)} %get-tuple-element.87.inner_ref, ...), custom_call_target="tpu_custom_call" | custom-call | flops 1 | bytes 1 | tf_op jit(solution)/shard_map/outer_grad/pallas_call | solution.py:292
  58.2 2.4 %layer.1 = bf16[256,1536]{1,0:T(8,128)(2,1)} custom-call(s32[2]{0:T(128)S(1)} %pad_add_fusion.where_ref, bf16[256,1536]{1,0:T(8,128)(2,1)S(1)} %constant_dynamic-slice_fusion.refs_0_.own_ref, bf16[128,1536]{1,0:T(8,128)(2,1)S(1)} %get-tuple-element.68.refs_0_, bf16[256,1536]{1,0:T(8,128)(2,1)S(1)} %get-tuple-element.73.refs_1_, ...), custom_call_target="tpu_custom_call" | custom-call | flops 1 | bytes 1 | tf_op jit(solution)/shard_map/layer/pallas_call | solution.py:292
  (57 shorter events, 13.8 us)
Async XLA Ops:
  0.7 4.7 %collective-permute-start = (bf16[256,256]{1,0:T(8,128)(2,1)}, bf16[256,256]{1,0:T(8,128)(2,1)S(1)}, u32[]{:S(2)}, u32[]{:S(2)}) collective-permute-start(bf16[256,256]{1,0:T(8,128)(2,1)} %q_ref.1), channel_id=1, source_target_pairs={{0,4},{4,0},{8,12},{12,8},{16,20},{20,16},{24,28},{28,24},{1,5},{5... | collective-permute-start | bytes 393224 | tf_op jit(solution)/shard_map/ppermute | solution.py:329
  1.4 3.9 %collective-permute-start.1 = (bf16[256,256]{1,0:T(8,128)(2,1)}, bf16[256,256]{1,0:T(8,128)(2,1)S(1)}, u32[]{:S(2)}, u32[]{:S(2)}) collective-permute-start(bf16[256,256]{1,0:T(8,128)(2,1)} %k_ref.3), channel_id=1, source_target_pairs={{0,4},{4,0},{8,12},{12,8},{16,20},{20,16},{24,28},{28,24},{1,5},{5... | collective-permute-start | bytes 393224 | tf_op jit(solution)/shard_map/ppermute | solution.py:329
  1.5 3.9 %collective-permute-start.2 = (bf16[256,256]{1,0:T(8,128)(2,1)}, bf16[256,256]{1,0:T(8,128)(2,1)S(1)}, u32[]{:S(2)}, u32[]{:S(2)}) collective-permute-start(bf16[256,256]{1,0:T(8,128)(2,1)} %v_ref.3), channel_id=1, source_target_pairs={{0,4},{4,0},{8,12},{12,8},{16,20},{20,16},{24,28},{28,24},{1,5},{5... | collective-permute-start | bytes 393224 | tf_op jit(solution)/shard_map/ppermute | solution.py:329
  1.9 3.4 %collective-permute-start.3 = (f32[2,256]{1,0:T(2,128)}, f32[2,256]{1,0:T(2,128)S(1)}, u32[]{:S(2)}, u32[]{:S(2)}) collective-permute-start(f32[2,256]{1,0:T(2,128)} %decay_ref.1), channel_id=1, source_target_pairs={{0,4},{4,0},{8,12},{12,8},{16,20},{20,16},{24,28},{28,24},{1,5},{5... | collective-permute-start | bytes 6152 | tf_op jit(solution)/shard_map/ppermute | solution.py:329
  5.4 4.7 %collective-permute-start.4 = (bf16[256,1536]{1,0:T(8,128)(2,1)S(1)}, bf16[256,1536]{1,0:T(8,128)(2,1)S(1)}, u32[]{:S(2)}, u32[]{:S(2)}) collective-permute-start(bf16[256,1536]{1,0:T(8,128)(2,1)S(1)} %copy-done), channel_id=1, source_target_pairs={{0,4},{4,0},{8,12},{12,8},{16,20},{20,16},{24,28},{28,24},{1,5},{5... | collective-permute-start | bytes 2359304 | tf_op jit(solution)/shard_map/ppermute | solution.py:329
  5.9 7.4 %collective-permute-start.5 = (bf16[64,1536]{1,0:T(8,128)(2,1)S(1)}, bf16[64,1536]{1,0:T(8,128)(2,1)S(1)}, u32[]{:S(2)}, u32[]{:S(2)}) collective-permute-start(bf16[64,1536]{1,0:T(8,128)(2,1)S(1)} %dynamic_slice.12), channel_id=1, source_target_pairs={{0,3},{1,2},{2,1},{3,0},{4,7},{5,6},{6,5},{7,4},{8,11},{9,10},{10,... | collective-permute-start | bytes 589832 | tf_op jit(solution)/shard_map/ppermute | solution.py:326
  7.1 16.6 %collective-permute-start.10 = (bf16[128,1536]{1,0:T(8,128)(2,1)S(1)}, bf16[128,1536]{1,0:T(8,128)(2,1)S(1)}, u32[]{:S(2)}, u32[]{:S(2)}) collective-permute-start(bf16[128,1536]{1,0:T(8,128)(2,1)S(1)} %get-tuple-element.96), channel_id=1, source_target_pairs={{0,2},{1,3},{2,0},{3,1},{4,6},{5,7},{6,4},{7,5},{8,10},{9,11},{10,... | collective-permute-start | bytes 1179656 | tf_op jit(solution)/shard_map/ppermute | solution.py:326
  7.3 16.4 %collective-permute-start.9 = (bf16[128,1536]{1,0:T(8,128)(2,1)S(1)}, bf16[128,1536]{1,0:T(8,128)(2,1)S(1)}, u32[]{:S(2)}, u32[]{:S(2)}) collective-permute-start(bf16[128,1536]{1,0:T(8,128)(2,1)S(1)} %get-tuple-element.97), channel_id=1, source_target_pairs={{0,1},{1,0},{2,3},{3,2},{4,5},{5,4},{6,7},{7,6},{8,9},{9,8},{10,11... | collective-permute-start | bytes 1179656 | tf_op jit(solution)/shard_map/ppermute | solution.py:326
  10.1 5.0 %collective-permute-start.6 = (bf16[144,128]{1,0:T(8,128)(2,1)S(1)}, bf16[144,128]{1,0:T(8,128)(2,1)S(1)}, u32[]{:S(2)}, u32[]{:S(2)}) collective-permute-start(bf16[144,128]{1,0:T(8,128)(2,1)S(1)} %get-tuple-element.57.refs_0_), channel_id=1, source_target_pairs={{0,8},{4,12},{8,16},{12,20},{16,24},{20,28},{1,9},{5,13},{9,17},{1... | collective-permute-start | bytes 110600 | tf_op jit(solution)/shard_map/ppermute | solution.py:335
  15.1 7.5 %collective-permute-start.7 = (bf16[64,1536]{1,0:T(8,128)(2,1)S(1)}, bf16[64,1536]{1,0:T(8,128)(2,1)S(1)}, u32[]{:S(2)}, u32[]{:S(2)}) collective-permute-start(bf16[64,1536]{1,0:T(8,128)(2,1)S(1)} %collective-permute-done.5.refs_1_), channel_id=1, source_target_pairs={{0,8},{4,12},{8,0},{12,4},{16,24},{20,28},{24,16},{28,20},{1,9},{5... | collective-permute-start | bytes 589832 | tf_op jit(solution)/shard_map/ppermute | solution.py:332
  17.0 5.6 %collective-permute-start.8 = (bf16[144,128]{1,0:T(8,128)(2,1)S(1)}, bf16[144,128]{1,0:T(8,128)(2,1)S(1)}, u32[]{:S(2)}, u32[]{:S(2)}) collective-permute-start(bf16[144,128]{1,0:T(8,128)(2,1)S(1)} %join.1), channel_id=1, source_target_pairs={{0,16},{4,20},{8,24},{12,28},{1,17},{5,21},{9,25},{13,29},{2,18},{... | collective-permute-start | bytes 110600 | tf_op jit(solution)/shard_map/ppermute | solution.py:335
  24.9 11.7 %collective-permute-start.12 = (bf16[256,1536]{1,0:T(8,128)(2,1)S(1)}, bf16[256,1536]{1,0:T(8,128)(2,1)S(1)}, u32[]{:S(2)}, u32[]{:S(2)}) collective-permute-start(bf16[256,1536]{1,0:T(8,128)(2,1)S(1)} %get-tuple-element.73.refs_1_), channel_id=1, source_target_pairs={{0,4},{4,0},{8,12},{12,8},{16,20},{20,16},{24,28},{28,24},{1,5},{5... | collective-permute-start | bytes 2359304 | tf_op jit(solution)/shard_map/ppermute | solution.py:329
  28.2 8.5 %collective-permute-start.11 = (bf16[128,1536]{1,0:T(8,128)(2,1)S(1)}, bf16[128,1536]{1,0:T(8,128)(2,1)S(1)}, u32[]{:S(2)}, u32[]{:S(2)}) collective-permute-start(bf16[128,1536]{1,0:T(8,128)(2,1)S(1)} %get-tuple-element.68.refs_0_), channel_id=1, source_target_pairs={{0,4},{4,0},{8,12},{12,8},{16,20},{20,16},{24,28},{28,24},{1,5},{5... | collective-permute-start | bytes 1179656 | tf_op jit(solution)/shard_map/ppermute | solution.py:329
  28.2 4.6 %collective-permute-start.14 = (bf16[2,256,128]{2,1,0:T(8,128)(2,1)S(1)}, bf16[2,256,128]{2,1,0:T(8,128)(2,1)S(1)}, u32[]{:S(2)}, u32[]{:S(2)}) collective-permute-start(bf16[2,256,128]{2,1,0:T(8,128)(2,1)S(1)} %get-tuple-element.74), channel_id=1, source_target_pairs={{0,1},{1,0},{2,3},{3,2},{4,5},{5,4},{6,7},{7,6},{8,9},{9,8},{10,11... | collective-permute-start | bytes 393224 | tf_op jit(solution)/shard_map/ppermute | solution.py:326
  28.5 4.4 %collective-permute-start.15 = (bf16[2,256,128]{2,1,0:T(8,128)(2,1)S(1)}, bf16[2,256,128]{2,1,0:T(8,128)(2,1)S(1)}, u32[]{:S(2)}, u32[]{:S(2)}) collective-permute-start(bf16[2,256,128]{2,1,0:T(8,128)(2,1)S(1)} %get-tuple-element.75), channel_id=1, source_target_pairs={{0,2},{1,3},{2,0},{3,1},{4,6},{5,7},{6,4},{7,5},{8,10},{9,11},{10,... | collective-permute-start | bytes 393224 | tf_op jit(solution)/shard_map/ppermute | solution.py:326
  29.7 6.9 %collective-permute-start.13 = (bf16[2,256,128]{2,1,0:T(8,128)(2,1)S(1)}, bf16[2,256,128]{2,1,0:T(8,128)(2,1)S(1)}, u32[]{:S(2)}, u32[]{:S(2)}) collective-permute-start(bf16[2,256,128]{2,1,0:T(8,128)(2,1)S(1)} %get-tuple-element.70), channel_id=1, source_target_pairs={{0,3},{1,2},{2,1},{3,0},{4,7},{5,6},{6,5},{7,4},{8,11},{9,10},{10,... | collective-permute-start | bytes 393224 | tf_op jit(solution)/shard_map/ppermute | solution.py:326
  36.7 5.6 %collective-permute-start.18 = (bf16[2,256,128]{2,1,0:T(8,128)(2,1)S(1)}, bf16[2,256,128]{2,1,0:T(8,128)(2,1)S(1)}, u32[]{:S(2)}, u32[]{:S(2)}) collective-permute-start(bf16[2,256,128]{2,1,0:T(8,128)(2,1)S(1)} %get-tuple-element.82.refs_0_.refs_4_), channel_id=1, source_target_pairs={{0,2},{1,3},{2,0},{3,1},{4,6},{5,7},{6,4},{7,5},{8,10},{9,11},{10,... | collective-permute-start | bytes 393224 | tf_op jit(solution)/shard_map/ppermute | solution.py:326
  36.9 11.8 %collective-permute-start.16 = (bf16[2,256,128]{2,1,0:T(8,128)(2,1)S(1)}, bf16[2,256,128]{2,1,0:T(8,128)(2,1)S(1)}, u32[]{:S(2)}, u32[]{:S(2)}) collective-permute-start(bf16[2,256,128]{2,1,0:T(8,128)(2,1)S(1)} %get-tuple-element.82.refs_0_.refs_4_), channel_id=1, source_target_pairs={{0,3},{1,2},{2,1},{3,0},{4,7},{5,6},{6,5},{7,4},{8,11},{9,10},{10,... | collective-permute-start | bytes 393224 | tf_op jit(solution)/shard_map/ppermute | solution.py:326
  37.9 10.8 %collective-permute-start.17 = (bf16[2,256,128]{2,1,0:T(8,128)(2,1)S(1)}, bf16[2,256,128]{2,1,0:T(8,128)(2,1)S(1)}, u32[]{:S(2)}, u32[]{:S(2)}) collective-permute-start(bf16[2,256,128]{2,1,0:T(8,128)(2,1)S(1)} %get-tuple-element.82.refs_0_.refs_4_), channel_id=1, source_target_pairs={{0,1},{1,0},{2,3},{3,2},{4,5},{5,4},{6,7},{7,6},{8,9},{9,8},{10,11... | collective-permute-start | bytes 393224 | tf_op jit(solution)/shard_map/ppermute | solution.py:326
  42.2 6.5 %collective-permute-start.20 = (bf16[144,128]{1,0:T(8,128)(2,1)S(1)}, bf16[144,128]{1,0:T(8,128)(2,1)S(1)}, u32[]{:S(2)}, u32[]{:S(2)}) collective-permute-start(bf16[144,128]{1,0:T(8,128)(2,1)S(1)} %get-tuple-element.90), channel_id=1, source_target_pairs={{24,0},{28,4},{25,1},{29,5},{26,2},{30,6},{27,3},{31,7}} | collective-permute-start | bytes 110600 | tf_op jit(solution)/shard_map/ppermute | solution.py:335
  42.9 5.8 %collective-permute-start.21 = (bf16[144,128]{1,0:T(8,128)(2,1)S(1)}, bf16[144,128]{1,0:T(8,128)(2,1)S(1)}, u32[]{:S(2)}, u32[]{:S(2)}) collective-permute-start(bf16[144,128]{1,0:T(8,128)(2,1)S(1)} %get-tuple-element.90), channel_id=1, source_target_pairs={{16,0},{20,4},{24,8},{28,12},{17,1},{21,5},{25,9},{29,13},{18,2},{... | collective-permute-start | bytes 110600 | tf_op jit(solution)/shard_map/ppermute | solution.py:335
  44.9 5.0 %collective-permute-start.22 = (bf16[144,128]{1,0:T(8,128)(2,1)S(1)}, bf16[144,128]{1,0:T(8,128)(2,1)S(1)}, u32[]{:S(2)}, u32[]{:S(2)}) collective-permute-start(bf16[144,128]{1,0:T(8,128)(2,1)S(1)} %get-tuple-element.90), channel_id=1, source_target_pairs={{8,0},{12,4},{16,8},{20,12},{24,16},{28,20},{9,1},{13,5},{17,9},{2... | collective-permute-start | bytes 110600 | tf_op jit(solution)/shard_map/ppermute | solution.py:335
  49.9 6.8 %collective-permute-start.23 = (f32[256,512]{1,0:T(8,128)S(1)}, f32[256,512]{1,0:T(8,128)S(1)}, u32[]{:S(2)}, u32[]{:S(2)}) collective-permute-start(f32[256,512]{1,0:T(8,128)S(1)} %get-tuple-element.91), channel_id=1, source_target_pairs={{0,4},{4,0},{8,12},{12,8},{16,20},{20,16},{24,28},{28,24},{1,5},{5... | collective-permute-start | bytes 1572872 | tf_op jit(solution)/shard_map/ppermute | solution.py:329
  54.7 3.5 %collective-permute-start.19 = (bf16[4,256,128]{2,1,0:T(8,128)(2,1)S(1)}, bf16[4,256,128]{2,1,0:T(8,128)(2,1)S(1)}, u32[]{:S(2)}, u32[]{:S(2)}) collective-permute-start(bf16[4,256,128]{2,1,0:T(8,128)(2,1)S(1)} %cross.1), channel_id=1, source_target_pairs={{0,4},{4,0},{8,12},{12,8},{16,20},{20,16},{24,28},{28,24},{1,5},{5... | collective-permute-start | bytes 786440 | tf_op jit(solution)/shard_map/ppermute | solution.py:329
  (9 other events, 61.5 us)

commit v11 on v9

--- a/solution.py
+++ b/solution.py
@@ -305,8 +305,8 @@
 
 
 def after(values, *earlier):
-    tied = lax.optimization_barrier((tuple(values), earlier))
-    return list(tied[0])
+    tied = lax.optimization_barrier((earlier, tuple(values)))
+    return list(tied[1])
 
 
 def on_device(queries, keys, values, log_decay, norm_gain, out_weight, out_grad):
@@ -378,16 +378,15 @@
             (window,) = call(without_where(join_kernel), "join", [message], [where, window, arrived[-1]])
         arrived.append(to_chip(window, step))
         step *= 2
-    (inner,) = call(without_where(inner_kernel), "inner", [pair32], [where, q, k, v, col, row, first])
     pieces = [("own", [weight_own])]
     for (step, halves), piece in zip(plan, arriving):
         if halves:
-            (piece,) = after([piece], arrived[0])
+            (piece,) = after([piece], window)
         pieces.append(("halves", [piece, swap_side(piece)]) if halves else ("whole", [piece]))
     partials, mine, theirs = [], [], []
     for number in range(0, tensor, 2):
         kinds, sources = zip(*pieces[number : number + 2])
-        sources = after(sum(sources, []), *arrived, inner, *partials)
+        sources = after(sum(sources, []), *arrived, *partials)
         *outs, weight = call(
             functools.partial(partial_kernel, kinds),
             "partial",
@@ -400,6 +399,7 @@
             theirs.append(swap_core(weight))
     own_partial, *partials = partials
     sent = [swap_tensor(partial, step) for partial, step in zip(partials, order)]
+    (inner,) = call(without_where(inner_kernel), "inner", [pair32], [where, q, k, v, col, row, *after([first], *partials)])
     mixed, normed, states = call(
         mixed_kernel,
         "mixed",

time: 56.6 us -> 57 us (level)
    ppermute x5, waiting for transfers between devices: 3.04 us -> 4.13 us  [to_chip(): lax.ppermute(value, 'seq', [(i, i + 2 * step) for i in range(seq) if 0 <=...]
    ppermute x9, waiting for transfers between devices: 4.84 us -> 4.11 us  [swap_tensor(): return lax.ppermute(value, 'tensor', [(i, i ^ k) for i in range(tensor)])]
where the time goes in v11:
time: 57 us; the launch traced here: 56.6 us
  starting transfers between devices  29.1 us (51%)
  Pallas kernels  13.9 us (24%)
  waiting for transfers between devices  9.32 us (16%)
  local copies, waits for them, and re-layouts  3.34 us (6%)
  between operations  0.94 us (2%)
    pallas_call x11, Pallas kernels, call(): pl.pallas_call(kernel, name=name, out_shape=outs, in_specs=[SMEM] + [VMEM...  13.9 us
    ppermute x5, starting transfers between devices, to_chip(): lax.ppermute(value, 'seq', [(i, i + 2 * step) for i in range(seq) if 0 <=...  12.2 us
    ppermute x9, starting transfers between devices, swap_tensor(): return lax.ppermute(value, 'tensor', [(i, i ^ k) for i in range(tensor)])  11.3 us
    ppermute x5, waiting for transfers between devices, to_chip(): lax.ppermute(value, 'seq', [(i, i + 2 * step) for i in range(seq) if 0 <=...  4.13 us
    ppermute x9, waiting for transfers between devices, swap_tensor(): return lax.ppermute(value, 'tensor', [(i, i ^ k) for i in range(tensor)])  4.11 us
    ppermute x12, starting transfers between devices, swap_core(): return lax.ppermute(value, 'seq', [(i, i ^ 1) for i in range(seq)])  3.21 us
    ppermute x1, starting transfers between devices, swap_side(): return lax.ppermute(value, 'seq', [(i, i ^ 2) for i in range(seq)])  2.39 us
    dynamic_slice x2, local copies, waits for them, and re-layouts, slice_for(): lax.dynamic_slice(out_weight, (begin, (place ^ step) * width), (rows, wid...  2.12 us
  transfers between devices with their start and end apart: 27, of which 8 were waited for; matrix products, arithmetic and copies ran while one was open for 6% of the time, Pallas kernels for 20%

profile of v11, /device:TPU:0, one launch (start us, length us, event | category | flops | bytes accessed | tf_op | source)
XLA Modules:
  0.0 56.6 jit_solution(12229656431843230049)
XLA Ops:
  2.7 1.2 %fusion = (bf16[128,1536]{1,0:T(8,128)(2,1)S(1)}, bf16[128,1536]{1,0:T(8,128)(2,1)S(1)}) fusion(bf16[256,6144]{1,0:T(8,128)(2,1)} %param.12, s32[]{:T(128)S(6)} %select_n.27, s32[]{:T(128)S(6)} %select_n.29, s32[]{:T(128)S(6)} %select_n.28), kind=kLoop, calls=%fused_computation.2 | loop fusion | bytes 1572876 | tf_op jit(solution)/shard_map/dynamic_slice | solution.py:357
  3.9 1.2 %constant_dynamic-slice_fusion.refs_0_.own_ref = bf16[256,1536]{1,0:T(8,128)(2,1)S(1)} fusion(bf16[256,6144]{1,0:T(8,128)(2,1)} %param.12, s32[]{:T(128)S(6)} %select_n.30), kind=kLoop, calls=%fused_computation.1 | loop fusion | bytes 1572868 | tf_op jit(solution)/shard_map/dynamic_slice | solution.py:364
  5.7 3.5 %collective-permute-start.7 = (bf16[64,1536]{1,0:T(8,128)(2,1)S(1)}, bf16[64,1536]{1,0:T(8,128)(2,1)S(1)}, u32[]{:S(2)}, u32[]{:S(2)}) collective-permute-start(bf16[64,1536]{1,0:T(8,128)(2,1)S(1)} %dynamic_slice.12), channel_id=1, source_target_pairs={{0,3},{1,2},{2,1},{3,0},{4,7},{5,6},{6,5},{7,4},{8,11},{9,10},{10,... | collective-permute-start | bytes 589832 | tf_op jit(solution)/shard_map/ppermute | solution.py:326
  9.9 1.4 %fresh.1 = (bf16[2,256,128]{2,1,0:T(8,128)(2,1)S(1)}, bf16[2,256,128]{2,1,0:T(8,128)(2,1)S(1)}, bf16[2,256,128]{2,1,0:T(8,128)(2,1)S(1)}, f32[256,2]{1,0:T(8,128...) custom-call(s32[2]{0:T(128)S(1)} %pad_add_fusion.where_ref, ...), custom_call_target="tpu_custom_call" | custom-call | flops 1 | bytes 1 | tf_op jit(solution)/shard_map/fresh/pallas_call | solution.py:292
  11.4 3.9 %collective-permute-start.5 = (bf16[144,128]{1,0:T(8,128)(2,1)S(1)}, bf16[144,128]{1,0:T(8,128)(2,1)S(1)}, u32[]{:S(2)}, u32[]{:S(2)}) collective-permute-start(bf16[144,128]{1,0:T(8,128)(2,1)S(1)} %get-tuple-element.57.refs_0_), channel_id=1, source_target_pairs={{0,8},{4,12},{8,16},{12,20},{16,24},{20,28},{1,9},{5,13},{9,17},{1... | collective-permute-start | bytes 110600 | tf_op jit(solution)/shard_map/ppermute | solution.py:335
  15.3 1.6 %collective-permute-done.5.refs_1_.refs_0_ = bf16[144,128]{1,0:T(8,128)(2,1)S(1)} collective-permute-done((bf16[144,128]{1,0:T(8,128)(2,1)S(1)}, bf16[144,128]{1,0:T(8,128)(2,1)S(1)}, u32[]{:S(2)}, u32[]{:S(2)}) %collective-permute-start.5) | collective-permute-done | bytes 36896 | tf_op jit(solution)/shard_map/ppermute | solution.py:335
  17.5 2.4 %collective-permute-start.8 = (bf16[64,1536]{1,0:T(8,128)(2,1)S(1)}, bf16[64,1536]{1,0:T(8,128)(2,1)S(1)}, u32[]{:S(2)}, u32[]{:S(2)}) collective-permute-start(bf16[64,1536]{1,0:T(8,128)(2,1)S(1)} %collective-permute-done.7.refs_1_), channel_id=1, source_target_pairs={{0,8},{4,12},{8,0},{12,4},{16,24},{20,28},{24,16},{28,20},{1,9},{5... | collective-permute-start | bytes 589832 | tf_op jit(solution)/shard_map/ppermute | solution.py:332
  19.8 4.5 %collective-permute-start.6 = (bf16[144,128]{1,0:T(8,128)(2,1)S(1)}, bf16[144,128]{1,0:T(8,128)(2,1)S(1)}, u32[]{:S(2)}, u32[]{:S(2)}) collective-permute-start(bf16[144,128]{1,0:T(8,128)(2,1)S(1)} %join.1), channel_id=1, source_target_pairs={{0,16},{4,20},{8,24},{12,28},{1,17},{5,21},{9,25},{13,29},{2,18},{... | collective-permute-start | bytes 110600 | tf_op jit(solution)/shard_map/ppermute | solution.py:335
  24.3 1.6 %collective-permute-done.6.refs_1_ = bf16[144,128]{1,0:T(8,128)(2,1)S(1)} collective-permute-done((bf16[144,128]{1,0:T(8,128)(2,1)S(1)}, bf16[144,128]{1,0:T(8,128)(2,1)S(1)}, u32[]{:S(2)}, u32[]{:S(2)}) %collective-permute-start.6) | collective-permute-done | bytes 36896 | tf_op jit(solution)/shard_map/ppermute | solution.py:335
  26.0 1.2 %partial.2 = (f32[2,256,128]{2,1,0:T(8,128)S(1)}, bf16[2,256,128]{2,1,0:T(8,128)(2,1)S(1)}, bf16[128,1536]{1,0:T(8,128)(2,1)S(1)}) custom-call(s32[2]{0:T(128)S(1)} %pad_add_fusion.where_ref, bf16[256,1536]{1,0:T(8,128)(2,1)S(1)} %copy-done, bf16[256,1536]{1,0:T(8,128)(2,1)S(1)} %collective-permute-done.4.got_ref, ...), custom_call_target="tpu_custom_call" | custom-call | flops 1 | bytes 1 | tf_op jit(solution)/shard_map/partial/pallas_call | solution.py:292
  27.1 1.2 %partial.3 = (bf16[2,256,128]{2,1,0:T(8,128)(2,1)S(1)}, bf16[2,256,128]{2,1,0:T(8,128)(2,1)S(1)}, bf16[256,1536]{1,0:T(8,128)(2,1)S(1)}) custom-call(s32[2]{0:T(128)S(1)} %pad_add_fusion.where_ref, bf16[256,1536]{1,0:T(8,128)(2,1)S(1)} %copy-done, bf16[256,1536]{1,0:T(8,128)(2,1)S(1)} %collective-permute-done.4.got_ref, ...), custom_call_target="tpu_custom_call" | custom-call | flops 1 | bytes 1 | tf_op jit(solution)/shard_map/partial/pallas_call | solution.py:292
  28.3 1.5 %collective-permute-start.16 = (bf16[2,256,128]{2,1,0:T(8,128)(2,1)S(1)}, bf16[2,256,128]{2,1,0:T(8,128)(2,1)S(1)}, u32[]{:S(2)}, u32[]{:S(2)}) collective-permute-start(bf16[2,256,128]{2,1,0:T(8,128)(2,1)S(1)} %get-tuple-element.73), channel_id=1, source_target_pairs={{0,1},{1,0},{2,3},{3,2},{4,5},{5,4},{6,7},{7,6},{8,9},{9,8},{10,11... | collective-permute-start | bytes 393224 | tf_op jit(solution)/shard_map/ppermute | solution.py:326
  29.9 1.5 %collective-permute-start.15 = (bf16[2,256,128]{2,1,0:T(8,128)(2,1)S(1)}, bf16[2,256,128]{2,1,0:T(8,128)(2,1)S(1)}, u32[]{:S(2)}, u32[]{:S(2)}) collective-permute-start(bf16[2,256,128]{2,1,0:T(8,128)(2,1)S(1)} %get-tuple-element.64), channel_id=1, source_target_pairs={{0,3},{1,2},{2,1},{3,0},{4,7},{5,6},{6,5},{7,4},{8,11},{9,10},{10,... | collective-permute-start | bytes 393224 | tf_op jit(solution)/shard_map/ppermute | solution.py:326
  31.9 1.1 %inner.1.inner_ref = f32[2,256,128]{2,1,0:T(8,128)S(1)} custom-call(s32[2]{0:T(128)S(1)} %pad_add_fusion.where_ref, bf16[2,256,128]{2,1,0:T(8,128)(2,1)S(1)} %get-tuple-element.68.refs_0_.q_ref, bf16[2,256,128]{2,1,0:T(8,128)(2,1)S(1)} %get-tuple-element.70.refs_1_.k_ref, bf16[2,256,128]{2,1,0:T(8,128)(2,1)S(1)} %get-tuple-element.71.refs_2_.v_ref, ...), custom_call_target="tpu_custom_call" | custom-call | flops 1 | bytes 1 | tf_op jit(solution)/shard_map/inner/pallas_call | solution.py:292
  33.9 2.5 %collective-permute-start.12 = (bf16[2,256,128]{2,1,0:T(8,128)(2,1)S(1)}, bf16[2,256,128]{2,1,0:T(8,128)(2,1)S(1)}, u32[]{:S(2)}, u32[]{:S(2)}) collective-permute-start(bf16[2,256,128]{2,1,0:T(8,128)(2,1)S(1)} %get-tuple-element.79.refs_0_.refs_4_), channel_id=1, source_target_pairs={{0,3},{1,2},{2,1},{3,0},{4,7},{5,6},{6,5},{7,4},{8,11},{9,10},{10,... | collective-permute-start | bytes 393224 | tf_op jit(solution)/shard_map/ppermute | solution.py:326
  37.4 3.8 %collective-permute-done.17.refs_2_ = bf16[2,256,128]{2,1,0:T(8,128)(2,1)S(1)} collective-permute-done((bf16[2,256,128]{2,1,0:T(8,128)(2,1)S(1)}, bf16[2,256,128]{2,1,0:T(8,128)(2,1)S(1)}, u32[]{:S(2)}, u32[]{:S(2)}) %collective-permute-start.17) | collective-permute-done | bytes 131104 | tf_op jit(solution)/shard_map/ppermute | solution.py:326
  41.2 1.2 %grad_mixed.1 = (f32[2,256,128]{2,1,0:T(8,128)S(1)}, f32[128,128]{1,0:T(8,128)S(1)}, bf16[144,128]{1,0:T(8,128)(2,1)S(1)}) custom-call(s32[2]{0:T(128)S(1)} %pad_add_fusion.where_ref, bf16[2,256,128]{2,1,0:T(8,128)(2,1)S(1)} %get-tuple-element.68.refs_0_.q_ref, f32[256,2]{1,0:T(8,128)S(1)} %get-tuple-element.69.refs_3_.col_ref, f32[1,256]{1,0:T(1,128)S(1)} %bitcast.4, ...), custom_call_target="tpu_custom_call" | custom-call | flops 1 | bytes 1 | tf_op jit(solution)/shard_map/grad_mixed/pallas_call | solution.py:292
  43.9 1.3 %collective-permute-start.20 = (bf16[144,128]{1,0:T(8,128)(2,1)S(1)}, bf16[144,128]{1,0:T(8,128)(2,1)S(1)}, u32[]{:S(2)}, u32[]{:S(2)}) collective-permute-start(bf16[144,128]{1,0:T(8,128)(2,1)S(1)} %get-tuple-element.82), channel_id=1, source_target_pairs={{24,0},{28,4},{25,1},{29,5},{26,2},{30,6},{27,3},{31,7}} | collective-permute-start | bytes 110600 | tf_op jit(solution)/shard_map/ppermute | solution.py:335
  45.2 1.3 %collective-permute-start.21 = (bf16[144,128]{1,0:T(8,128)(2,1)S(1)}, bf16[144,128]{1,0:T(8,128)(2,1)S(1)}, u32[]{:S(2)}, u32[]{:S(2)}) collective-permute-start(bf16[144,128]{1,0:T(8,128)(2,1)S(1)} %get-tuple-element.82), channel_id=1, source_target_pairs={{16,0},{20,4},{24,8},{28,12},{17,1},{21,5},{25,9},{29,13},{18,2},{... | collective-permute-start | bytes 110600 | tf_op jit(solution)/shard_map/ppermute | solution.py:335
  46.5 1.3 %collective-permute-start.22 = (bf16[144,128]{1,0:T(8,128)(2,1)S(1)}, bf16[144,128]{1,0:T(8,128)(2,1)S(1)}, u32[]{:S(2)}, u32[]{:S(2)}) collective-permute-start(bf16[144,128]{1,0:T(8,128)(2,1)S(1)} %get-tuple-element.82), channel_id=1, source_target_pairs={{8,0},{12,4},{16,8},{20,12},{24,16},{28,20},{9,1},{13,5},{17,9},{2... | collective-permute-start | bytes 110600 | tf_op jit(solution)/shard_map/ppermute | solution.py:335
  47.8 1.9 %inner_grad.1 = (f32[256,512]{1,0:T(8,128)S(1)}, f32[256,512]{1,0:T(8,128)S(1)}) custom-call(s32[2]{0:T(128)S(1)} %pad_add_fusion.where_ref, bf16[2,256,128]{2,1,0:T(8,128)(2,1)S(1)} %get-tuple-element.68.refs_0_.q_ref, bf16[2,256,128]{2,1,0:T(8,128)(2,1)S(1)} %get-tuple-element.70.refs_1_.k_ref, bf16[2,256,128]{2,1,0:T(8,128)(2,1)S(1)} %get-tuple-element.71.refs_2_.v_ref, ...), custom_call_target="tpu_custom_call" | custom-call | flops 1 | bytes 1 | tf_op jit(solution)/shard_map/inner_grad/pallas_call | solution.py:292
  49.7 2.4 %layer.1 = bf16[256,1536]{1,0:T(8,128)(2,1)} custom-call(s32[2]{0:T(128)S(1)} %pad_add_fusion.where_ref, bf16[256,1536]{1,0:T(8,128)(2,1)S(1)} %constant_dynamic-slice_fusion.refs_0_.own_ref, bf16[128,1536]{1,0:T(8,128)(2,1)S(1)} %get-tuple-element.62.refs_0_, bf16[256,1536]{1,0:T(8,128)(2,1)S(1)} %get-tuple-element.83.refs_1_, ...), custom_call_target="tpu_custom_call" | custom-call | flops 1 | bytes 1 | tf_op jit(solution)/shard_map/layer/pallas_call | solution.py:292
  54.0 0.9 %collective-permute-done.24.refs_3_ = bf16[144,128]{1,0:T(8,128)(2,1)S(1)} collective-permute-done((bf16[144,128]{1,0:T(8,128)(2,1)S(1)}, bf16[144,128]{1,0:T(8,128)(2,1)S(1)}, u32[]{:S(2)}, u32[]{:S(2)}) %collective-permute-start.24) | collective-permute-done | bytes 36896 | tf_op jit(solution)/shard_map/ppermute | solution.py:329
  55.1 1.5 %outer_grad.1 = (bf16[256,256]{1,0:T(8,128)(2,1)}, bf16[256,256]{1,0:T(8,128)(2,1)}, bf16[256,256]{1,0:T(8,128)(2,1)}) custom-call(s32[2]{0:T(128)S(1)} %pad_add_fusion.where_ref, bf16[256,256]{1,0:T(8,128)(2,1)S(1)} %copy-done.1, bf16[256,256]{1,0:T(8,128)(2,1)S(1)} %copy-done.2, f32[256,512]{1,0:T(8,128)S(1)} %get-tuple-element.87.inner_ref, ...), custom_call_target="tpu_custom_call" | custom-call | flops 1 | bytes 1 | tf_op jit(solution)/shard_map/outer_grad/pallas_call | solution.py:292
  (57 shorter events, 9.8 us)
Async XLA Ops:
  0.7 4.4 %collective-permute-start = (bf16[256,256]{1,0:T(8,128)(2,1)}, bf16[256,256]{1,0:T(8,128)(2,1)S(1)}, u32[]{:S(2)}, u32[]{:S(2)}) collective-permute-start(bf16[256,256]{1,0:T(8,128)(2,1)} %q_ref.1), channel_id=1, source_target_pairs={{0,4},{4,0},{8,12},{12,8},{16,20},{20,16},{24,28},{28,24},{1,5},{5... | collective-permute-start | bytes 393224 | tf_op jit(solution)/shard_map/ppermute | solution.py:329
  1.2 3.9 %collective-permute-start.1 = (bf16[256,256]{1,0:T(8,128)(2,1)}, bf16[256,256]{1,0:T(8,128)(2,1)S(1)}, u32[]{:S(2)}, u32[]{:S(2)}) collective-permute-start(bf16[256,256]{1,0:T(8,128)(2,1)} %k_ref.3), channel_id=1, source_target_pairs={{0,4},{4,0},{8,12},{12,8},{16,20},{20,16},{24,28},{28,24},{1,5},{5... | collective-permute-start | bytes 393224 | tf_op jit(solution)/shard_map/ppermute | solution.py:329
  1.3 3.9 %collective-permute-start.2 = (bf16[256,256]{1,0:T(8,128)(2,1)}, bf16[256,256]{1,0:T(8,128)(2,1)S(1)}, u32[]{:S(2)}, u32[]{:S(2)}) collective-permute-start(bf16[256,256]{1,0:T(8,128)(2,1)} %v_ref.3), channel_id=1, source_target_pairs={{0,4},{4,0},{8,12},{12,8},{16,20},{20,16},{24,28},{28,24},{1,5},{5... | collective-permute-start | bytes 393224 | tf_op jit(solution)/shard_map/ppermute | solution.py:329
  1.7 3.4 %collective-permute-start.3 = (f32[2,256]{1,0:T(2,128)}, f32[2,256]{1,0:T(2,128)S(1)}, u32[]{:S(2)}, u32[]{:S(2)}) collective-permute-start(f32[2,256]{1,0:T(2,128)} %decay_ref.1), channel_id=1, source_target_pairs={{0,4},{4,0},{8,12},{12,8},{16,20},{20,16},{24,28},{28,24},{1,5},{5... | collective-permute-start | bytes 6152 | tf_op jit(solution)/shard_map/ppermute | solution.py:329
  5.2 6.2 %collective-permute-start.4 = (bf16[256,1536]{1,0:T(8,128)(2,1)S(1)}, bf16[256,1536]{1,0:T(8,128)(2,1)S(1)}, u32[]{:S(2)}, u32[]{:S(2)}) collective-permute-start(bf16[256,1536]{1,0:T(8,128)(2,1)S(1)} %copy-done), channel_id=1, source_target_pairs={{0,4},{4,0},{8,12},{12,8},{16,20},{20,16},{24,28},{28,24},{1,5},{5... | collective-permute-start | bytes 2359304 | tf_op jit(solution)/shard_map/ppermute | solution.py:329
  5.7 11.8 %collective-permute-start.7 = (bf16[64,1536]{1,0:T(8,128)(2,1)S(1)}, bf16[64,1536]{1,0:T(8,128)(2,1)S(1)}, u32[]{:S(2)}, u32[]{:S(2)}) collective-permute-start(bf16[64,1536]{1,0:T(8,128)(2,1)S(1)} %dynamic_slice.12), channel_id=1, source_target_pairs={{0,3},{1,2},{2,1},{3,0},{4,7},{5,6},{6,5},{7,4},{8,11},{9,10},{10,... | collective-permute-start | bytes 589832 | tf_op jit(solution)/shard_map/ppermute | solution.py:326
  9.2 17.9 %collective-permute-start.10 = (bf16[128,1536]{1,0:T(8,128)(2,1)S(1)}, bf16[128,1536]{1,0:T(8,128)(2,1)S(1)}, u32[]{:S(2)}, u32[]{:S(2)}) collective-permute-start(bf16[128,1536]{1,0:T(8,128)(2,1)S(1)} %get-tuple-element.96), channel_id=1, source_target_pairs={{0,2},{1,3},{2,0},{3,1},{4,6},{5,7},{6,4},{7,5},{8,10},{9,11},{10,... | collective-permute-start | bytes 1179656 | tf_op jit(solution)/shard_map/ppermute | solution.py:326
  9.7 17.5 %collective-permute-start.9 = (bf16[128,1536]{1,0:T(8,128)(2,1)S(1)}, bf16[128,1536]{1,0:T(8,128)(2,1)S(1)}, u32[]{:S(2)}, u32[]{:S(2)}) collective-permute-start(bf16[128,1536]{1,0:T(8,128)(2,1)S(1)} %get-tuple-element.97), channel_id=1, source_target_pairs={{0,1},{1,0},{2,3},{3,2},{4,5},{5,4},{6,7},{7,6},{8,9},{9,8},{10,11... | collective-permute-start | bytes 1179656 | tf_op jit(solution)/shard_map/ppermute | solution.py:326
  11.4 5.5 %collective-permute-start.5 = (bf16[144,128]{1,0:T(8,128)(2,1)S(1)}, bf16[144,128]{1,0:T(8,128)(2,1)S(1)}, u32[]{:S(2)}, u32[]{:S(2)}) collective-permute-start(bf16[144,128]{1,0:T(8,128)(2,1)S(1)} %get-tuple-element.57.refs_0_), channel_id=1, source_target_pairs={{0,8},{4,12},{8,16},{12,20},{16,24},{20,28},{1,9},{5,13},{9,17},{1... | collective-permute-start | bytes 110600 | tf_op jit(solution)/shard_map/ppermute | solution.py:335
  17.5 8.5 %collective-permute-start.8 = (bf16[64,1536]{1,0:T(8,128)(2,1)S(1)}, bf16[64,1536]{1,0:T(8,128)(2,1)S(1)}, u32[]{:S(2)}, u32[]{:S(2)}) collective-permute-start(bf16[64,1536]{1,0:T(8,128)(2,1)S(1)} %collective-permute-done.7.refs_1_), channel_id=1, source_target_pairs={{0,8},{4,12},{8,0},{12,4},{16,24},{20,28},{24,16},{28,20},{1,9},{5... | collective-permute-start | bytes 589832 | tf_op jit(solution)/shard_map/ppermute | solution.py:332
  19.8 6.1 %collective-permute-start.6 = (bf16[144,128]{1,0:T(8,128)(2,1)S(1)}, bf16[144,128]{1,0:T(8,128)(2,1)S(1)}, u32[]{:S(2)}, u32[]{:S(2)}) collective-permute-start(bf16[144,128]{1,0:T(8,128)(2,1)S(1)} %join.1), channel_id=1, source_target_pairs={{0,16},{4,20},{8,24},{12,28},{1,17},{5,21},{9,25},{13,29},{2,18},{... | collective-permute-start | bytes 110600 | tf_op jit(solution)/shard_map/ppermute | solution.py:335
  28.3 8.6 %collective-permute-start.16 = (bf16[2,256,128]{2,1,0:T(8,128)(2,1)S(1)}, bf16[2,256,128]{2,1,0:T(8,128)(2,1)S(1)}, u32[]{:S(2)}, u32[]{:S(2)}) collective-permute-start(bf16[2,256,128]{2,1,0:T(8,128)(2,1)S(1)} %get-tuple-element.73), channel_id=1, source_target_pairs={{0,1},{1,0},{2,3},{3,2},{4,5},{5,4},{6,7},{7,6},{8,9},{9,8},{10,11... | collective-permute-start | bytes 393224 | tf_op jit(solution)/shard_map/ppermute | solution.py:326
  29.9 11.4 %collective-permute-start.15 = (bf16[2,256,128]{2,1,0:T(8,128)(2,1)S(1)}, bf16[2,256,128]{2,1,0:T(8,128)(2,1)S(1)}, u32[]{:S(2)}, u32[]{:S(2)}) collective-permute-start(bf16[2,256,128]{2,1,0:T(8,128)(2,1)S(1)} %get-tuple-element.64), channel_id=1, source_target_pairs={{0,3},{1,2},{2,1},{3,0},{4,7},{5,6},{6,5},{7,4},{8,11},{9,10},{10,... | collective-permute-start | bytes 393224 | tf_op jit(solution)/shard_map/ppermute | solution.py:326
  31.3 9.9 %collective-permute-start.17 = (bf16[2,256,128]{2,1,0:T(8,128)(2,1)S(1)}, bf16[2,256,128]{2,1,0:T(8,128)(2,1)S(1)}, u32[]{:S(2)}, u32[]{:S(2)}) collective-permute-start(bf16[2,256,128]{2,1,0:T(8,128)(2,1)S(1)} %get-tuple-element.74), channel_id=1, source_target_pairs={{0,2},{1,3},{2,0},{3,1},{4,6},{5,7},{6,4},{7,5},{8,10},{9,11},{10,... | collective-permute-start | bytes 393224 | tf_op jit(solution)/shard_map/ppermute | solution.py:326
  33.9 8.6 %collective-permute-start.12 = (bf16[2,256,128]{2,1,0:T(8,128)(2,1)S(1)}, bf16[2,256,128]{2,1,0:T(8,128)(2,1)S(1)}, u32[]{:S(2)}, u32[]{:S(2)}) collective-permute-start(bf16[2,256,128]{2,1,0:T(8,128)(2,1)S(1)} %get-tuple-element.79.refs_0_.refs_4_), channel_id=1, source_target_pairs={{0,3},{1,2},{2,1},{3,0},{4,7},{5,6},{6,5},{7,4},{8,11},{9,10},{10,... | collective-permute-start | bytes 393224 | tf_op jit(solution)/shard_map/ppermute | solution.py:326
  36.4 6.1 %collective-permute-start.13 = (bf16[2,256,128]{2,1,0:T(8,128)(2,1)S(1)}, bf16[2,256,128]{2,1,0:T(8,128)(2,1)S(1)}, u32[]{:S(2)}, u32[]{:S(2)}) collective-permute-start(bf16[2,256,128]{2,1,0:T(8,128)(2,1)S(1)} %get-tuple-element.79.refs_0_.refs_4_), channel_id=1, source_target_pairs={{0,1},{1,0},{2,3},{3,2},{4,5},{5,4},{6,7},{7,6},{8,9},{9,8},{10,11... | collective-permute-start | bytes 393224 | tf_op jit(solution)/shard_map/ppermute | solution.py:326
  36.9 5.8 %collective-permute-start.14 = (bf16[2,256,128]{2,1,0:T(8,128)(2,1)S(1)}, bf16[2,256,128]{2,1,0:T(8,128)(2,1)S(1)}, u32[]{:S(2)}, u32[]{:S(2)}) collective-permute-start(bf16[2,256,128]{2,1,0:T(8,128)(2,1)S(1)} %get-tuple-element.79.refs_0_.refs_4_), channel_id=1, source_target_pairs={{0,2},{1,3},{2,0},{3,1},{4,6},{5,7},{6,4},{7,5},{8,10},{9,11},{10,... | collective-permute-start | bytes 393224 | tf_op jit(solution)/shard_map/ppermute | solution.py:326
  42.7 7.0 %collective-permute-start.18 = (bf16[256,1536]{1,0:T(8,128)(2,1)S(1)}, bf16[256,1536]{1,0:T(8,128)(2,1)S(1)}, u32[]{:S(2)}, u32[]{:S(2)}) collective-permute-start(bf16[256,1536]{1,0:T(8,128)(2,1)S(1)} %get-tuple-element.83.refs_1_), channel_id=1, source_target_pairs={{0,4},{4,0},{8,12},{12,8},{16,20},{20,16},{24,28},{28,24},{1,5},{5... | collective-permute-start | bytes 2359304 | tf_op jit(solution)/shard_map/ppermute | solution.py:329
  42.7 7.0 %collective-permute-start.11 = (bf16[128,1536]{1,0:T(8,128)(2,1)S(1)}, bf16[128,1536]{1,0:T(8,128)(2,1)S(1)}, u32[]{:S(2)}, u32[]{:S(2)}) collective-permute-start(bf16[128,1536]{1,0:T(8,128)(2,1)S(1)} %get-tuple-element.62.refs_0_), channel_id=1, source_target_pairs={{0,4},{4,0},{8,12},{12,8},{16,20},{20,16},{24,28},{28,24},{1,5},{5... | collective-permute-start | bytes 1179656 | tf_op jit(solution)/shard_map/ppermute | solution.py:329
  43.8 2.7 %collective-permute-start.19 = (bf16[4,256,128]{2,1,0:T(8,128)(2,1)S(1)}, bf16[4,256,128]{2,1,0:T(8,128)(2,1)S(1)}, u32[]{:S(2)}, u32[]{:S(2)}) collective-permute-start(bf16[4,256,128]{2,1,0:T(8,128)(2,1)S(1)} %cross.1), channel_id=1, source_target_pairs={{0,4},{4,0},{8,12},{12,8},{16,20},{20,16},{24,28},{28,24},{1,5},{5... | collective-permute-start | bytes 786440 | tf_op jit(solution)/shard_map/ppermute | solution.py:329
  43.9 8.3 %collective-permute-start.20 = (bf16[144,128]{1,0:T(8,128)(2,1)S(1)}, bf16[144,128]{1,0:T(8,128)(2,1)S(1)}, u32[]{:S(2)}, u32[]{:S(2)}) collective-permute-start(bf16[144,128]{1,0:T(8,128)(2,1)S(1)} %get-tuple-element.82), channel_id=1, source_target_pairs={{24,0},{28,4},{25,1},{29,5},{26,2},{30,6},{27,3},{31,7}} | collective-permute-start | bytes 110600 | tf_op jit(solution)/shard_map/ppermute | solution.py:335
  45.2 7.8 %collective-permute-start.21 = (bf16[144,128]{1,0:T(8,128)(2,1)S(1)}, bf16[144,128]{1,0:T(8,128)(2,1)S(1)}, u32[]{:S(2)}, u32[]{:S(2)}) collective-permute-start(bf16[144,128]{1,0:T(8,128)(2,1)S(1)} %get-tuple-element.82), channel_id=1, source_target_pairs={{16,0},{20,4},{24,8},{28,12},{17,1},{21,5},{25,9},{29,13},{18,2},{... | collective-permute-start | bytes 110600 | tf_op jit(solution)/shard_map/ppermute | solution.py:335
  46.5 6.5 %collective-permute-start.22 = (bf16[144,128]{1,0:T(8,128)(2,1)S(1)}, bf16[144,128]{1,0:T(8,128)(2,1)S(1)}, u32[]{:S(2)}, u32[]{:S(2)}) collective-permute-start(bf16[144,128]{1,0:T(8,128)(2,1)S(1)} %get-tuple-element.82), channel_id=1, source_target_pairs={{8,0},{12,4},{16,8},{20,12},{24,16},{28,20},{9,1},{13,5},{17,9},{2... | collective-permute-start | bytes 110600 | tf_op jit(solution)/shard_map/ppermute | solution.py:335
  53.0 2.1 %collective-permute-start.23 = (f32[256,512]{1,0:T(8,128)S(1)}, f32[256,512]{1,0:T(8,128)S(1)}, u32[]{:S(2)}, u32[]{:S(2)}) collective-permute-start(f32[256,512]{1,0:T(8,128)S(1)} %get-tuple-element.92), channel_id=1, source_target_pairs={{0,4},{4,0},{8,12},{12,8},{16,20},{20,16},{24,28},{28,24},{1,5},{5... | collective-permute-start | bytes 1572872 | tf_op jit(solution)/shard_map/ppermute | solution.py:329
  (9 other events, 68.1 us)

commit v12 on v9

--- a/solution.py
+++ b/solution.py
@@ -36,12 +36,6 @@
 def dot_bf(a, b, dims):
     high, low = split(b)
     return dot(a, high, dims) + dot(a, low, dims)
-
-
-def dot_ff(a, b, dims):
-    ah, al = split(a)
-    bh, bl = split(b)
-    return dot(ah, bh, dims) + (dot(ah, bl, dims) + dot(al, bh, dims))
 
 
 def triangle(length):
@@ -130,7 +124,7 @@
     states = []
     for b in range(2):
         fade = jnp.exp(columns[length - 1 : length, b : b + 1] - columns[:, b : b + 1])
-        states.append(dot_bf(k_out[b], fade * v_out[b].astype(F32), TN))
+        states.append(dot(k_out[b], (fade * v_out[b].astype(F32)).astype(BF16), TN))
     totals = [total_of(columns, b) for b in range(2)]
     first_ref[...] = states[0]
     put_message(message_ref, jnp.exp(totals[1]) * states[0] + states[1], totals[0] + totals[1])
@@ -190,10 +184,12 @@
             weights.append(sources[0][...])
     weight = jnp.concatenate(weights, axis=0)
     weight_out[...] = weight[2 * HD - weight_out.shape[0] :]
-    for block, ref in ((core, grad_ref), (1 - core, got_ref)):
-        product = dot(ref[...], weight, NT)
+    length = grad_ref.shape[0]
+    product = dot(jnp.concatenate([grad_ref[...], got_ref[...]], axis=0), weight, NT)
+    for begin, block in ((0, core), (length, 1 - core)):
         for number, out in enumerate(products):
-            out[block] = product[:, number * HD : (number + 1) * HD].astype(out.dtype)
+            part = product[begin : begin + length, number * HD : (number + 1) * HD]
+            out[block] = part.astype(out.dtype)
 
 
 def grad_mixed_kernel(where_ref, q_ref, col_ref, gain_ref, mixed_ref, own_ref, *refs):
@@ -211,7 +207,7 @@
         unit = mixed * scale
         grad = scale * (lifted - unit * jnp.mean(unit * lifted, axis=-1, keepdims=True))
         grad_ref[b] = grad
-        ups.append(dot_bf(q_ref[b], jnp.exp(columns[:, b : b + 1]) * grad, TN))
+        ups.append(dot(q_ref[b], (jnp.exp(columns[:, b : b + 1]) * grad).astype(BF16), TN))
     second_ref[...] = ups[1]
     totals = [total_of(columns, b) for b in range(2)]
     put_message(message_ref, ups[0] + jnp.exp(totals[0]) * ups[1], totals[0] + totals[1])
@@ -229,16 +225,18 @@
     for b in range(2):
         q, k, v, grad = q_ref[b], k_ref[b], v_ref[b], grad_ref[b]
         weight = weights(columns, across, lower, b)
-        scores = dot(q, k, NT) * weight
-        grad_scores = dot_fb(grad, v, NT) * weight
-        carried = jnp.exp(columns[:, b : b + 1]) * dot_ff(grad, state_ref[b], NT)
-        dq = dot_fb(grad_scores, k, NN) + carried
-        dk = dot_fb(grad_scores, q, TN)
-        dv = dot_ff(scores, grad, TN)
+        narrow = grad.astype(BF16)
+        scores = (dot(q, k, NT) * weight).astype(BF16)
+        grad_scores = (dot(narrow, v, NT) * weight).astype(BF16)
+        carried = jnp.exp(columns[:, b : b + 1]) * dot(narrow, state_ref[b].astype(BF16), NT)
+        dq = dot(grad_scores, k, NN) + carried
+        dk = dot(grad_scores, q, TN)
+        dv = dot(scores, narrow, TN)
         fade = jnp.exp(ends[b] - columns[:, b : b + 1])
         if b == 0:
-            dk = dk + fade * dot_bf(v, second_ref[...], NT)
-            dv = dv + fade * dot_bf(k, second_ref[...], NN)
+            second = second_ref[...].astype(BF16)
+            dk = dk + fade * dot(v, second, NT)
+            dv = dv + fade * dot(k, second, NN)
             fade = fade * jnp.exp(ends[1])
         parts.append((dq, dk, dv, jnp.broadcast_to(fade, (length, HD))))
     for number, (early, late) in enumerate(zip(*parts)):
@@ -254,13 +252,13 @@
         (core, inner_ref, refs[:count][::-1]),
         (1 - core, inner_got_ref, refs[count : 2 * count][::-1]),
     ):
-        high, low = split(chip_sum(chip_refs))
+        state = chip_sum(chip_refs).astype(BF16)
         fade = inner[:, 3 * HD : 4 * HD]
         k, v = k_ref[:, lanes_of(head)], v_ref[:, lanes_of(head)]
         outs[0][:, lanes_of(head)] = inner[:, 0:HD].astype(BF16)
-        key = inner[:, HD : 2 * HD] + fade * (dot(v, high, NT) + dot(v, low, NT))
+        key = inner[:, HD : 2 * HD] + fade * dot(v, state, NT)
         outs[1][:, lanes_of(head)] = key.astype(BF16)
-        value = inner[:, 2 * HD : 3 * HD] + fade * (dot(k, high, NN) + dot(k, low, NN))
+        value = inner[:, 2 * HD : 3 * HD] + fade * dot(k, state, NN)
         outs[2][:, lanes_of(head)] = value.astype(BF16)
 
 

time: 56.6 us -> 56.4 us (level)
  Pallas kernels: 13.9 us -> 13.2 us
    pallas_call x11, Pallas kernels: 13.9 us -> 13.2 us  [call(): pl.pallas_call(kernel, name=name, out_shape=outs, in_specs=[SMEM] + [VMEM...]
  transfers between devices with their start and end apart: 27 -> 27, of which waited for: 8 -> 8; matrix products, arithmetic and copies ran while one was open for 6% -> 6% of each run, Pallas kernels for 20% -> 19%
where the time goes in v12:
time: 56.4 us; the launch traced here: 56.1 us
  starting transfers between devices  29.1 us (52%)
  Pallas kernels  13.2 us (23%)
  waiting for transfers between devices  9.5 us (17%)
  local copies, waits for them, and re-layouts  3.34 us (6%)
  between operations  0.93 us (2%)
    pallas_call x11, Pallas kernels, call(): pl.pallas_call(kernel, name=name, out_shape=outs, in_specs=[SMEM] + [VMEM...  13.2 us
    ppermute x5, starting transfers between devices, to_chip(): lax.ppermute(value, 'seq', [(i, i + 2 * step) for i in range(seq) if 0 <=...  12.3 us
    ppermute x9, starting transfers between devices, swap_tensor(): return lax.ppermute(value, 'tensor', [(i, i ^ k) for i in range(tensor)])  11.3 us
    ppermute x9, waiting for transfers between devices, swap_tensor(): return lax.ppermute(value, 'tensor', [(i, i ^ k) for i in range(tensor)])  4.86 us
    ppermute x5, waiting for transfers between devices, to_chip(): lax.ppermute(value, 'seq', [(i, i + 2 * step) for i in range(seq) if 0 <=...  3.57 us
    ppermute x12, starting transfers between devices, swap_core(): return lax.ppermute(value, 'seq', [(i, i ^ 1) for i in range(seq)])  3.21 us
    ppermute x1, starting transfers between devices, swap_side(): return lax.ppermute(value, 'seq', [(i, i ^ 2) for i in range(seq)])  2.32 us
    dynamic_slice x2, local copies, waits for them, and re-layouts, slice_for(): lax.dynamic_slice(out_weight, (begin, (place ^ step) * width), (rows, wid...  2.12 us
  transfers between devices with their start and end apart: 27, of which 8 were waited for; matrix products, arithmetic and copies ran while one was open for 6% of the time, Pallas kernels for 19%

profile of v12, /device:TPU:0, one launch (start us, length us, event | category | flops | bytes accessed | tf_op | source)
XLA Modules:
  0.0 56.1 jit_solution(1672063151768169968)
XLA Ops:
  2.7 1.2 %fusion = (bf16[128,1536]{1,0:T(8,128)(2,1)S(1)}, bf16[128,1536]{1,0:T(8,128)(2,1)S(1)}) fusion(bf16[256,6144]{1,0:T(8,128)(2,1)} %param.12, s32[]{:T(128)S(6)} %select_n.27, s32[]{:T(128)S(6)} %select_n.29, s32[]{:T(128)S(6)} %select_n.28), kind=kLoop, calls=%fused_computation.2 | loop fusion | bytes 1572876 | tf_op jit(solution)/shard_map/dynamic_slice | solution.py:355
  3.9 1.2 %constant_dynamic-slice_fusion.refs_0_.own_ref = bf16[256,1536]{1,0:T(8,128)(2,1)S(1)} fusion(bf16[256,6144]{1,0:T(8,128)(2,1)} %param.12, s32[]{:T(128)S(6)} %select_n.30), kind=kLoop, calls=%fused_computation.1 | loop fusion | bytes 1572868 | tf_op jit(solution)/shard_map/dynamic_slice | solution.py:362
  5.7 3.5 %collective-permute-start.5 = (bf16[64,1536]{1,0:T(8,128)(2,1)S(1)}, bf16[64,1536]{1,0:T(8,128)(2,1)S(1)}, u32[]{:S(2)}, u32[]{:S(2)}) collective-permute-start(bf16[64,1536]{1,0:T(8,128)(2,1)S(1)} %dynamic_slice.12), channel_id=1, source_target_pairs={{0,3},{1,2},{2,1},{3,0},{4,7},{5,6},{6,5},{7,4},{8,11},{9,10},{10,... | collective-permute-start | bytes 589832 | tf_op jit(solution)/shard_map/ppermute | solution.py:324
  9.9 1.4 %fresh.1 = (bf16[2,256,128]{2,1,0:T(8,128)(2,1)S(1)}, bf16[2,256,128]{2,1,0:T(8,128)(2,1)S(1)}, bf16[2,256,128]{2,1,0:T(8,128)(2,1)S(1)}, f32[256,2]{1,0:T(8,128...) custom-call(s32[2]{0:T(128)S(1)} %pad_add_fusion.where_ref, ...), custom_call_target="tpu_custom_call" | custom-call | flops 1 | bytes 1 | tf_op jit(solution)/shard_map/fresh/pallas_call | solution.py:290
  11.4 3.9 %collective-permute-start.6 = (bf16[144,128]{1,0:T(8,128)(2,1)S(1)}, bf16[144,128]{1,0:T(8,128)(2,1)S(1)}, u32[]{:S(2)}, u32[]{:S(2)}) collective-permute-start(bf16[144,128]{1,0:T(8,128)(2,1)S(1)} %get-tuple-element.56.refs_0_), channel_id=1, source_target_pairs={{0,8},{4,12},{8,16},{12,20},{16,24},{20,28},{1,9},{5,13},{9,17},{1... | collective-permute-start | bytes 110600 | tf_op jit(solution)/shard_map/ppermute | solution.py:333
  15.3 1.6 %collective-permute-done.6.refs_1_.refs_0_ = bf16[144,128]{1,0:T(8,128)(2,1)S(1)} collective-permute-done((bf16[144,128]{1,0:T(8,128)(2,1)S(1)}, bf16[144,128]{1,0:T(8,128)(2,1)S(1)}, u32[]{:S(2)}, u32[]{:S(2)}) %collective-permute-start.6) | collective-permute-done | bytes 36896 | tf_op jit(solution)/shard_map/ppermute | solution.py:333
  16.9 2.3 %collective-permute-start.7 = (bf16[64,1536]{1,0:T(8,128)(2,1)S(1)}, bf16[64,1536]{1,0:T(8,128)(2,1)S(1)}, u32[]{:S(2)}, u32[]{:S(2)}) collective-permute-start(bf16[64,1536]{1,0:T(8,128)(2,1)S(1)} %collective-permute-done.5.refs_1_), channel_id=1, source_target_pairs={{0,8},{4,12},{8,0},{12,4},{16,24},{20,28},{24,16},{28,20},{1,9},{5... | collective-permute-start | bytes 589832 | tf_op jit(solution)/shard_map/ppermute | solution.py:330
  19.8 4.5 %collective-permute-start.8 = (bf16[144,128]{1,0:T(8,128)(2,1)S(1)}, bf16[144,128]{1,0:T(8,128)(2,1)S(1)}, u32[]{:S(2)}, u32[]{:S(2)}) collective-permute-start(bf16[144,128]{1,0:T(8,128)(2,1)S(1)} %join.1), channel_id=1, source_target_pairs={{0,16},{4,20},{8,24},{12,28},{1,17},{5,21},{9,25},{13,29},{2,18},{... | collective-permute-start | bytes 110600 | tf_op jit(solution)/shard_map/ppermute | solution.py:333
  24.3 1.1 %inner.1.inner_ref = f32[2,256,128]{2,1,0:T(8,128)S(1)} custom-call(s32[2]{0:T(128)S(1)} %pad_add_fusion.where_ref, bf16[2,256,128]{2,1,0:T(8,128)(2,1)S(1)} %get-tuple-element.58.refs_0_.q_ref, bf16[2,256,128]{2,1,0:T(8,128)(2,1)S(1)} %get-tuple-element.59.refs_1_.k_ref, bf16[2,256,128]{2,1,0:T(8,128)(2,1)S(1)} %get-tuple-element.60.refs_2_.v_ref, ...), custom_call_target="tpu_custom_call" | custom-call | flops 1 | bytes 1 | tf_op jit(solution)/shard_map/inner/pallas_call | solution.py:290
  25.9 1.2 %partial.2 = (f32[2,256,128]{2,1,0:T(8,128)S(1)}, bf16[2,256,128]{2,1,0:T(8,128)(2,1)S(1)}, bf16[128,1536]{1,0:T(8,128)(2,1)S(1)}) custom-call(s32[2]{0:T(128)S(1)} %pad_add_fusion.where_ref, bf16[256,1536]{1,0:T(8,128)(2,1)S(1)} %copy-done, bf16[256,1536]{1,0:T(8,128)(2,1)S(1)} %collective-permute-done.4.got_ref, ...), custom_call_target="tpu_custom_call" | custom-call | flops 1 | bytes 1 | tf_op jit(solution)/shard_map/partial/pallas_call | solution.py:290
  27.1 1.1 %partial.3 = (bf16[2,256,128]{2,1,0:T(8,128)(2,1)S(1)}, bf16[2,256,128]{2,1,0:T(8,128)(2,1)S(1)}, bf16[256,1536]{1,0:T(8,128)(2,1)S(1)}) custom-call(s32[2]{0:T(128)S(1)} %pad_add_fusion.where_ref, bf16[256,1536]{1,0:T(8,128)(2,1)S(1)} %copy-done, bf16[256,1536]{1,0:T(8,128)(2,1)S(1)} %collective-permute-done.4.got_ref, ...), custom_call_target="tpu_custom_call" | custom-call | flops 1 | bytes 1 | tf_op jit(solution)/shard_map/partial/pallas_call | solution.py:290
  28.2 1.6 %collective-permute-start.13 = (bf16[2,256,128]{2,1,0:T(8,128)(2,1)S(1)}, bf16[2,256,128]{2,1,0:T(8,128)(2,1)S(1)}, u32[]{:S(2)}, u32[]{:S(2)}) collective-permute-start(bf16[2,256,128]{2,1,0:T(8,128)(2,1)S(1)} %get-tuple-element.73), channel_id=1, source_target_pairs={{0,1},{1,0},{2,3},{3,2},{4,5},{5,4},{6,7},{7,6},{8,9},{9,8},{10,11... | collective-permute-start | bytes 393224 | tf_op jit(solution)/shard_map/ppermute | solution.py:324
  29.8 1.5 %collective-permute-start.12 = (bf16[2,256,128]{2,1,0:T(8,128)(2,1)S(1)}, bf16[2,256,128]{2,1,0:T(8,128)(2,1)S(1)}, u32[]{:S(2)}, u32[]{:S(2)}) collective-permute-start(bf16[2,256,128]{2,1,0:T(8,128)(2,1)S(1)} %get-tuple-element.69), channel_id=1, source_target_pairs={{0,3},{1,2},{2,1},{3,0},{4,7},{5,6},{6,5},{7,4},{8,11},{9,10},{10,... | collective-permute-start | bytes 393224 | tf_op jit(solution)/shard_map/ppermute | solution.py:324
  32.7 2.5 %collective-permute-start.15 = (bf16[2,256,128]{2,1,0:T(8,128)(2,1)S(1)}, bf16[2,256,128]{2,1,0:T(8,128)(2,1)S(1)}, u32[]{:S(2)}, u32[]{:S(2)}) collective-permute-start(bf16[2,256,128]{2,1,0:T(8,128)(2,1)S(1)} %get-tuple-element.79.refs_0_.refs_4_), channel_id=1, source_target_pairs={{0,3},{1,2},{2,1},{3,0},{4,7},{5,6},{6,5},{7,4},{8,11},{9,10},{10,... | collective-permute-start | bytes 393224 | tf_op jit(solution)/shard_map/ppermute | solution.py:324
  36.2 4.6 %collective-permute-done.14.refs_2_ = bf16[2,256,128]{2,1,0:T(8,128)(2,1)S(1)} collective-permute-done((bf16[2,256,128]{2,1,0:T(8,128)(2,1)S(1)}, bf16[2,256,128]{2,1,0:T(8,128)(2,1)S(1)}, u32[]{:S(2)}, u32[]{:S(2)}) %collective-permute-start.14) | collective-permute-done | bytes 131104 | tf_op jit(solution)/shard_map/ppermute | solution.py:324
  40.9 1.2 %grad_mixed.1 = (f32[2,256,128]{2,1,0:T(8,128)S(1)}, f32[128,128]{1,0:T(8,128)S(1)}, bf16[144,128]{1,0:T(8,128)(2,1)S(1)}) custom-call(s32[2]{0:T(128)S(1)} %pad_add_fusion.where_ref, bf16[2,256,128]{2,1,0:T(8,128)(2,1)S(1)} %get-tuple-element.58.refs_0_.q_ref, f32[256,2]{1,0:T(8,128)S(1)} %get-tuple-element.61.refs_3_.col_ref, f32[1,256]{1,0:T(1,128)S(1)} %bitcast.4, ...), custom_call_target="tpu_custom_call" | custom-call | flops 1 | bytes 1 | tf_op jit(solution)/shard_map/grad_mixed/pallas_call | solution.py:290
  43.4 1.3 %collective-permute-start.20 = (bf16[144,128]{1,0:T(8,128)(2,1)S(1)}, bf16[144,128]{1,0:T(8,128)(2,1)S(1)}, u32[]{:S(2)}, u32[]{:S(2)}) collective-permute-start(bf16[144,128]{1,0:T(8,128)(2,1)S(1)} %get-tuple-element.80), channel_id=1, source_target_pairs={{24,0},{28,4},{25,1},{29,5},{26,2},{30,6},{27,3},{31,7}} | collective-permute-start | bytes 110600 | tf_op jit(solution)/shard_map/ppermute | solution.py:333
  44.7 1.3 %collective-permute-start.21 = (bf16[144,128]{1,0:T(8,128)(2,1)S(1)}, bf16[144,128]{1,0:T(8,128)(2,1)S(1)}, u32[]{:S(2)}, u32[]{:S(2)}) collective-permute-start(bf16[144,128]{1,0:T(8,128)(2,1)S(1)} %get-tuple-element.80), channel_id=1, source_target_pairs={{16,0},{20,4},{24,8},{28,12},{17,1},{21,5},{25,9},{29,13},{18,2},{... | collective-permute-start | bytes 110600 | tf_op jit(solution)/shard_map/ppermute | solution.py:333
  46.0 1.3 %collective-permute-start.22 = (bf16[144,128]{1,0:T(8,128)(2,1)S(1)}, bf16[144,128]{1,0:T(8,128)(2,1)S(1)}, u32[]{:S(2)}, u32[]{:S(2)}) collective-permute-start(bf16[144,128]{1,0:T(8,128)(2,1)S(1)} %get-tuple-element.80), channel_id=1, source_target_pairs={{8,0},{12,4},{16,8},{20,12},{24,16},{28,20},{9,1},{13,5},{17,9},{2... | collective-permute-start | bytes 110600 | tf_op jit(solution)/shard_map/ppermute | solution.py:333
  47.3 1.4 %inner_grad.1 = (f32[256,512]{1,0:T(8,128)S(1)}, f32[256,512]{1,0:T(8,128)S(1)}) custom-call(s32[2]{0:T(128)S(1)} %pad_add_fusion.where_ref, bf16[2,256,128]{2,1,0:T(8,128)(2,1)S(1)} %get-tuple-element.58.refs_0_.q_ref, bf16[2,256,128]{2,1,0:T(8,128)(2,1)S(1)} %get-tuple-element.59.refs_1_.k_ref, bf16[2,256,128]{2,1,0:T(8,128)(2,1)S(1)} %get-tuple-element.60.refs_2_.v_ref, ...), custom_call_target="tpu_custom_call" | custom-call | flops 1 | bytes 1 | tf_op jit(solution)/shard_map/inner_grad/pallas_call | solution.py:290
  48.7 2.4 %layer.1 = bf16[256,1536]{1,0:T(8,128)(2,1)} custom-call(s32[2]{0:T(128)S(1)} %pad_add_fusion.where_ref, bf16[256,1536]{1,0:T(8,128)(2,1)S(1)} %constant_dynamic-slice_fusion.refs_0_.own_ref, bf16[128,1536]{1,0:T(8,128)(2,1)S(1)} %get-tuple-element.67.refs_0_, bf16[256,1536]{1,0:T(8,128)(2,1)S(1)} %get-tuple-element.81.refs_1_, ...), custom_call_target="tpu_custom_call" | custom-call | flops 1 | bytes 1 | tf_op jit(solution)/shard_map/layer/pallas_call | solution.py:290
  51.2 1.4 %collective-permute-done.21.refs_1_ = bf16[144,128]{1,0:T(8,128)(2,1)S(1)} collective-permute-done((bf16[144,128]{1,0:T(8,128)(2,1)S(1)}, bf16[144,128]{1,0:T(8,128)(2,1)S(1)}, u32[]{:S(2)}, u32[]{:S(2)}) %collective-permute-start.21) | collective-permute-done | bytes 36896 | tf_op jit(solution)/shard_map/ppermute | solution.py:333
  53.6 0.9 %collective-permute-done.24.refs_3_ = bf16[144,128]{1,0:T(8,128)(2,1)S(1)} collective-permute-done((bf16[144,128]{1,0:T(8,128)(2,1)S(1)}, bf16[144,128]{1,0:T(8,128)(2,1)S(1)}, u32[]{:S(2)}, u32[]{:S(2)}) %collective-permute-start.24) | collective-permute-done | bytes 36896 | tf_op jit(solution)/shard_map/ppermute | solution.py:327
  54.6 1.5 %outer_grad.1 = (bf16[256,256]{1,0:T(8,128)(2,1)}, bf16[256,256]{1,0:T(8,128)(2,1)}, bf16[256,256]{1,0:T(8,128)(2,1)}) custom-call(s32[2]{0:T(128)S(1)} %pad_add_fusion.where_ref, bf16[256,256]{1,0:T(8,128)(2,1)S(1)} %copy-done.1, bf16[256,256]{1,0:T(8,128)(2,1)S(1)} %copy-done.2, f32[256,512]{1,0:T(8,128)S(1)} %get-tuple-element.85.inner_ref, ...), custom_call_target="tpu_custom_call" | custom-call | flops 1 | bytes 1 | tf_op jit(solution)/shard_map/outer_grad/pallas_call | solution.py:290
  (57 shorter events, 9.4 us)
Async XLA Ops:
  0.7 4.4 %collective-permute-start = (bf16[256,256]{1,0:T(8,128)(2,1)}, bf16[256,256]{1,0:T(8,128)(2,1)S(1)}, u32[]{:S(2)}, u32[]{:S(2)}) collective-permute-start(bf16[256,256]{1,0:T(8,128)(2,1)} %q_ref.1), channel_id=1, source_target_pairs={{0,4},{4,0},{8,12},{12,8},{16,20},{20,16},{24,28},{28,24},{1,5},{5... | collective-permute-start | bytes 393224 | tf_op jit(solution)/shard_map/ppermute | solution.py:327
  1.2 3.9 %collective-permute-start.1 = (bf16[256,256]{1,0:T(8,128)(2,1)}, bf16[256,256]{1,0:T(8,128)(2,1)S(1)}, u32[]{:S(2)}, u32[]{:S(2)}) collective-permute-start(bf16[256,256]{1,0:T(8,128)(2,1)} %k_ref.3), channel_id=1, source_target_pairs={{0,4},{4,0},{8,12},{12,8},{16,20},{20,16},{24,28},{28,24},{1,5},{5... | collective-permute-start | bytes 393224 | tf_op jit(solution)/shard_map/ppermute | solution.py:327
  1.3 3.9 %collective-permute-start.2 = (bf16[256,256]{1,0:T(8,128)(2,1)}, bf16[256,256]{1,0:T(8,128)(2,1)S(1)}, u32[]{:S(2)}, u32[]{:S(2)}) collective-permute-start(bf16[256,256]{1,0:T(8,128)(2,1)} %v_ref.3), channel_id=1, source_target_pairs={{0,4},{4,0},{8,12},{12,8},{16,20},{20,16},{24,28},{28,24},{1,5},{5... | collective-permute-start | bytes 393224 | tf_op jit(solution)/shard_map/ppermute | solution.py:327
  1.7 3.4 %collective-permute-start.3 = (f32[2,256]{1,0:T(2,128)}, f32[2,256]{1,0:T(2,128)S(1)}, u32[]{:S(2)}, u32[]{:S(2)}) collective-permute-start(f32[2,256]{1,0:T(2,128)} %decay_ref.1), channel_id=1, source_target_pairs={{0,4},{4,0},{8,12},{12,8},{16,20},{20,16},{24,28},{28,24},{1,5},{5... | collective-permute-start | bytes 6152 | tf_op jit(solution)/shard_map/ppermute | solution.py:327
  5.2 6.2 %collective-permute-start.4 = (bf16[256,1536]{1,0:T(8,128)(2,1)S(1)}, bf16[256,1536]{1,0:T(8,128)(2,1)S(1)}, u32[]{:S(2)}, u32[]{:S(2)}) collective-permute-start(bf16[256,1536]{1,0:T(8,128)(2,1)S(1)} %copy-done), channel_id=1, source_target_pairs={{0,4},{4,0},{8,12},{12,8},{16,20},{20,16},{24,28},{28,24},{1,5},{5... | collective-permute-start | bytes 2359304 | tf_op jit(solution)/shard_map/ppermute | solution.py:327
  5.7 9.6 %collective-permute-start.5 = (bf16[64,1536]{1,0:T(8,128)(2,1)S(1)}, bf16[64,1536]{1,0:T(8,128)(2,1)S(1)}, u32[]{:S(2)}, u32[]{:S(2)}) collective-permute-start(bf16[64,1536]{1,0:T(8,128)(2,1)S(1)} %dynamic_slice.12), channel_id=1, source_target_pairs={{0,3},{1,2},{2,1},{3,0},{4,7},{5,6},{6,5},{7,4},{8,11},{9,10},{10,... | collective-permute-start | bytes 589832 | tf_op jit(solution)/shard_map/ppermute | solution.py:324
  9.2 17.9 %collective-permute-start.10 = (bf16[128,1536]{1,0:T(8,128)(2,1)S(1)}, bf16[128,1536]{1,0:T(8,128)(2,1)S(1)}, u32[]{:S(2)}, u32[]{:S(2)}) collective-permute-start(bf16[128,1536]{1,0:T(8,128)(2,1)S(1)} %get-tuple-element.94), channel_id=1, source_target_pairs={{0,2},{1,3},{2,0},{3,1},{4,6},{5,7},{6,4},{7,5},{8,10},{9,11},{10,... | collective-permute-start | bytes 1179656 | tf_op jit(solution)/shard_map/ppermute | solution.py:324
  9.7 17.4 %collective-permute-start.9 = (bf16[128,1536]{1,0:T(8,128)(2,1)S(1)}, bf16[128,1536]{1,0:T(8,128)(2,1)S(1)}, u32[]{:S(2)}, u32[]{:S(2)}) collective-permute-start(bf16[128,1536]{1,0:T(8,128)(2,1)S(1)} %get-tuple-element.95), channel_id=1, source_target_pairs={{0,1},{1,0},{2,3},{3,2},{4,5},{5,4},{6,7},{7,6},{8,9},{9,8},{10,11... | collective-permute-start | bytes 1179656 | tf_op jit(solution)/shard_map/ppermute | solution.py:324
  11.4 5.5 %collective-permute-start.6 = (bf16[144,128]{1,0:T(8,128)(2,1)S(1)}, bf16[144,128]{1,0:T(8,128)(2,1)S(1)}, u32[]{:S(2)}, u32[]{:S(2)}) collective-permute-start(bf16[144,128]{1,0:T(8,128)(2,1)S(1)} %get-tuple-element.56.refs_0_), channel_id=1, source_target_pairs={{0,8},{4,12},{8,16},{12,20},{16,24},{20,28},{1,9},{5,13},{9,17},{1... | collective-permute-start | bytes 110600 | tf_op jit(solution)/shard_map/ppermute | solution.py:333
  16.9 9.0 %collective-permute-start.7 = (bf16[64,1536]{1,0:T(8,128)(2,1)S(1)}, bf16[64,1536]{1,0:T(8,128)(2,1)S(1)}, u32[]{:S(2)}, u32[]{:S(2)}) collective-permute-start(bf16[64,1536]{1,0:T(8,128)(2,1)S(1)} %collective-permute-done.5.refs_1_), channel_id=1, source_target_pairs={{0,8},{4,12},{8,0},{12,4},{16,24},{20,28},{24,16},{28,20},{1,9},{5... | collective-permute-start | bytes 589832 | tf_op jit(solution)/shard_map/ppermute | solution.py:330
  19.8 6.1 %collective-permute-start.8 = (bf16[144,128]{1,0:T(8,128)(2,1)S(1)}, bf16[144,128]{1,0:T(8,128)(2,1)S(1)}, u32[]{:S(2)}, u32[]{:S(2)}) collective-permute-start(bf16[144,128]{1,0:T(8,128)(2,1)S(1)} %join.1), channel_id=1, source_target_pairs={{0,16},{4,20},{8,24},{12,28},{1,17},{5,21},{9,25},{13,29},{2,18},{... | collective-permute-start | bytes 110600 | tf_op jit(solution)/shard_map/ppermute | solution.py:333
  28.2 7.5 %collective-permute-start.13 = (bf16[2,256,128]{2,1,0:T(8,128)(2,1)S(1)}, bf16[2,256,128]{2,1,0:T(8,128)(2,1)S(1)}, u32[]{:S(2)}, u32[]{:S(2)}) collective-permute-start(bf16[2,256,128]{2,1,0:T(8,128)(2,1)S(1)} %get-tuple-element.73), channel_id=1, source_target_pairs={{0,1},{1,0},{2,3},{3,2},{4,5},{5,4},{6,7},{7,6},{8,9},{9,8},{10,11... | collective-permute-start | bytes 393224 | tf_op jit(solution)/shard_map/ppermute | solution.py:324
  29.8 11.1 %collective-permute-start.12 = (bf16[2,256,128]{2,1,0:T(8,128)(2,1)S(1)}, bf16[2,256,128]{2,1,0:T(8,128)(2,1)S(1)}, u32[]{:S(2)}, u32[]{:S(2)}) collective-permute-start(bf16[2,256,128]{2,1,0:T(8,128)(2,1)S(1)} %get-tuple-element.69), channel_id=1, source_target_pairs={{0,3},{1,2},{2,1},{3,0},{4,7},{5,6},{6,5},{7,4},{8,11},{9,10},{10,... | collective-permute-start | bytes 393224 | tf_op jit(solution)/shard_map/ppermute | solution.py:324
  31.3 9.6 %collective-permute-start.14 = (bf16[2,256,128]{2,1,0:T(8,128)(2,1)S(1)}, bf16[2,256,128]{2,1,0:T(8,128)(2,1)S(1)}, u32[]{:S(2)}, u32[]{:S(2)}) collective-permute-start(bf16[2,256,128]{2,1,0:T(8,128)(2,1)S(1)} %get-tuple-element.74), channel_id=1, source_target_pairs={{0,2},{1,3},{2,0},{3,1},{4,6},{5,7},{6,4},{7,5},{8,10},{9,11},{10,... | collective-permute-start | bytes 393224 | tf_op jit(solution)/shard_map/ppermute | solution.py:324
  32.7 9.3 %collective-permute-start.15 = (bf16[2,256,128]{2,1,0:T(8,128)(2,1)S(1)}, bf16[2,256,128]{2,1,0:T(8,128)(2,1)S(1)}, u32[]{:S(2)}, u32[]{:S(2)}) collective-permute-start(bf16[2,256,128]{2,1,0:T(8,128)(2,1)S(1)} %get-tuple-element.79.refs_0_.refs_4_), channel_id=1, source_target_pairs={{0,3},{1,2},{2,1},{3,0},{4,7},{5,6},{6,5},{7,4},{8,11},{9,10},{10,... | collective-permute-start | bytes 393224 | tf_op jit(solution)/shard_map/ppermute | solution.py:324
  35.2 6.8 %collective-permute-start.16 = (bf16[2,256,128]{2,1,0:T(8,128)(2,1)S(1)}, bf16[2,256,128]{2,1,0:T(8,128)(2,1)S(1)}, u32[]{:S(2)}, u32[]{:S(2)}) collective-permute-start(bf16[2,256,128]{2,1,0:T(8,128)(2,1)S(1)} %get-tuple-element.79.refs_0_.refs_4_), channel_id=1, source_target_pairs={{0,1},{1,0},{2,3},{3,2},{4,5},{5,4},{6,7},{7,6},{8,9},{9,8},{10,11... | collective-permute-start | bytes 393224 | tf_op jit(solution)/shard_map/ppermute | solution.py:324
  35.7 6.5 %collective-permute-start.17 = (bf16[2,256,128]{2,1,0:T(8,128)(2,1)S(1)}, bf16[2,256,128]{2,1,0:T(8,128)(2,1)S(1)}, u32[]{:S(2)}, u32[]{:S(2)}) collective-permute-start(bf16[2,256,128]{2,1,0:T(8,128)(2,1)S(1)} %get-tuple-element.79.refs_0_.refs_4_), channel_id=1, source_target_pairs={{0,2},{1,3},{2,0},{3,1},{4,6},{5,7},{6,4},{7,5},{8,10},{9,11},{10,... | collective-permute-start | bytes 393224 | tf_op jit(solution)/shard_map/ppermute | solution.py:324
  42.3 6.5 %collective-permute-start.18 = (bf16[256,1536]{1,0:T(8,128)(2,1)S(1)}, bf16[256,1536]{1,0:T(8,128)(2,1)S(1)}, u32[]{:S(2)}, u32[]{:S(2)}) collective-permute-start(bf16[256,1536]{1,0:T(8,128)(2,1)S(1)} %get-tuple-element.81.refs_1_), channel_id=1, source_target_pairs={{0,4},{4,0},{8,12},{12,8},{16,20},{20,16},{24,28},{28,24},{1,5},{5... | collective-permute-start | bytes 2359304 | tf_op jit(solution)/shard_map/ppermute | solution.py:327
  42.3 6.4 %collective-permute-start.11 = (bf16[128,1536]{1,0:T(8,128)(2,1)S(1)}, bf16[128,1536]{1,0:T(8,128)(2,1)S(1)}, u32[]{:S(2)}, u32[]{:S(2)}) collective-permute-start(bf16[128,1536]{1,0:T(8,128)(2,1)S(1)} %get-tuple-element.67.refs_0_), channel_id=1, source_target_pairs={{0,4},{4,0},{8,12},{12,8},{16,20},{20,16},{24,28},{28,24},{1,5},{5... | collective-permute-start | bytes 1179656 | tf_op jit(solution)/shard_map/ppermute | solution.py:327
  43.3 2.7 %collective-permute-start.19 = (bf16[4,256,128]{2,1,0:T(8,128)(2,1)S(1)}, bf16[4,256,128]{2,1,0:T(8,128)(2,1)S(1)}, u32[]{:S(2)}, u32[]{:S(2)}) collective-permute-start(bf16[4,256,128]{2,1,0:T(8,128)(2,1)S(1)} %cross.1), channel_id=1, source_target_pairs={{0,4},{4,0},{8,12},{12,8},{16,20},{20,16},{24,28},{28,24},{1,5},{5... | collective-permute-start | bytes 786440 | tf_op jit(solution)/shard_map/ppermute | solution.py:327
  43.4 7.8 %collective-permute-start.20 = (bf16[144,128]{1,0:T(8,128)(2,1)S(1)}, bf16[144,128]{1,0:T(8,128)(2,1)S(1)}, u32[]{:S(2)}, u32[]{:S(2)}) collective-permute-start(bf16[144,128]{1,0:T(8,128)(2,1)S(1)} %get-tuple-element.80), channel_id=1, source_target_pairs={{24,0},{28,4},{25,1},{29,5},{26,2},{30,6},{27,3},{31,7}} | collective-permute-start | bytes 110600 | tf_op jit(solution)/shard_map/ppermute | solution.py:333
  44.7 7.8 %collective-permute-start.21 = (bf16[144,128]{1,0:T(8,128)(2,1)S(1)}, bf16[144,128]{1,0:T(8,128)(2,1)S(1)}, u32[]{:S(2)}, u32[]{:S(2)}) collective-permute-start(bf16[144,128]{1,0:T(8,128)(2,1)S(1)} %get-tuple-element.80), channel_id=1, source_target_pairs={{16,0},{20,4},{24,8},{28,12},{17,1},{21,5},{25,9},{29,13},{18,2},{... | collective-permute-start | bytes 110600 | tf_op jit(solution)/shard_map/ppermute | solution.py:333
  46.0 6.5 %collective-permute-start.22 = (bf16[144,128]{1,0:T(8,128)(2,1)S(1)}, bf16[144,128]{1,0:T(8,128)(2,1)S(1)}, u32[]{:S(2)}, u32[]{:S(2)}) collective-permute-start(bf16[144,128]{1,0:T(8,128)(2,1)S(1)} %get-tuple-element.80), channel_id=1, source_target_pairs={{8,0},{12,4},{16,8},{20,12},{24,16},{28,20},{9,1},{13,5},{17,9},{2... | collective-permute-start | bytes 110600 | tf_op jit(solution)/shard_map/ppermute | solution.py:333
  52.6 2.1 %collective-permute-start.23 = (f32[256,512]{1,0:T(8,128)S(1)}, f32[256,512]{1,0:T(8,128)S(1)}, u32[]{:S(2)}, u32[]{:S(2)}) collective-permute-start(f32[256,512]{1,0:T(8,128)S(1)} %get-tuple-element.90), channel_id=1, source_target_pairs={{0,4},{4,0},{8,12},{12,8},{16,20},{20,16},{24,28},{28,24},{1,5},{5... | collective-permute-start | bytes 1572872 | tf_op jit(solution)/shard_map/ppermute | solution.py:327
  (9 other events, 67.0 us)

commit v13 on v12

--- a/solution.py
+++ b/solution.py
@@ -7,7 +7,6 @@
 from jax.experimental.pallas import tpu as pltpu
 from jax.sharding import PartitionSpec as P
 
-EXACT = lax.Precision.HIGHEST
 EPSILON = 1e-05
 F32 = jnp.float32
 BF16 = jnp.bfloat16
@@ -44,12 +43,15 @@
     return rows >= cols
 
 
-def running_columns(decay, lower):
-    return lax.dot_general(lower.astype(F32), decay, NT, precision=EXACT, preferred_element_type=F32)
-
-
-def running_rows(decay, lower):
-    return lax.dot_general(decay, lower.astype(F32), NT, precision=EXACT, preferred_element_type=F32)
+def running_sums(decay, lower):
+    ones = lower.astype(BF16)
+    columns = rows = 0.0
+    for _ in range(3):
+        part = decay.astype(BF16)
+        decay = decay - part.astype(F32)
+        columns = columns + dot(ones, part, NT)
+        rows = rows + dot(part, ones, NT)
+    return columns, rows
 
 
 def put_total(ref, base, total):
@@ -118,9 +120,9 @@
     block = lax.broadcasted_iota(jnp.int32, (2, length), 0)
     decay = jnp.where(block == core, mine, theirs)
     lower = triangle(length)
-    columns = running_columns(decay, lower)
+    columns, rows = running_sums(decay, lower)
     col_ref[...] = columns
-    row_ref[...] = running_rows(decay, lower)
+    row_ref[...] = rows
     states = []
     for b in range(2):
         fade = jnp.exp(columns[length - 1 : length, b : b + 1] - columns[:, b : b + 1])

time: 56.4 us -> 56.2 us (level)
  transfers between devices with their start and end apart: 27 -> 27, of which waited for: 8 -> 8; matrix products, arithmetic and copies ran while one was open for 6% -> 6% of each run, Pallas kernels for 19% -> 18%
where the time goes in v13:
time: 56.2 us; the launch traced here: 55.9 us
  starting transfers between devices  29 us (52%)
  Pallas kernels  13 us (23%)
  waiting for transfers between devices  9.51 us (17%)
  local copies, waits for them, and re-layouts  3.34 us (6%)
  between operations  0.93 us (2%)
    pallas_call x11, Pallas kernels, call(): pl.pallas_call(kernel, name=name, out_shape=outs, in_specs=[SMEM] + [VMEM...  13 us
    ppermute x5, starting transfers between devices, to_chip(): lax.ppermute(value, 'seq', [(i, i + 2 * step) for i in range(seq) if 0 <=...  12.3 us
    ppermute x9, starting transfers between devices, swap_tensor(): return lax.ppermute(value, 'tensor', [(i, i ^ k) for i in range(tensor)])  11.3 us
    ppermute x9, waiting for transfers between devices, swap_tensor(): return lax.ppermute(value, 'tensor', [(i, i ^ k) for i in range(tensor)])  4.86 us
    ppermute x5, waiting for transfers between devices, to_chip(): lax.ppermute(value, 'seq', [(i, i + 2 * step) for i in range(seq) if 0 <=...  3.57 us
    ppermute x12, starting transfers between devices, swap_core(): return lax.ppermute(value, 'seq', [(i, i ^ 1) for i in range(seq)])  3.21 us
    ppermute x1, starting transfers between devices, swap_side(): return lax.ppermute(value, 'seq', [(i, i ^ 2) for i in range(seq)])  2.32 us
    dynamic_slice x2, local copies, waits for them, and re-layouts, slice_for(): lax.dynamic_slice(out_weight, (begin, (place ^ step) * width), (rows, wid...  2.12 us
  transfers between devices with their start and end apart: 27, of which 8 were waited for; matrix products, arithmetic and copies ran while one was open for 6% of the time, Pallas kernels for 18%

profile of v13, /device:TPU:0, one launch (start us, length us, event | category | flops | bytes accessed | tf_op | source)
XLA Modules:
  0.0 55.9 jit_solution(14153613781739791404)
XLA Ops:
  2.7 1.2 %fusion = (bf16[128,1536]{1,0:T(8,128)(2,1)S(1)}, bf16[128,1536]{1,0:T(8,128)(2,1)S(1)}) fusion(bf16[256,6144]{1,0:T(8,128)(2,1)} %param.12, s32[]{:T(128)S(6)} %select_n.27, s32[]{:T(128)S(6)} %select_n.29, s32[]{:T(128)S(6)} %select_n.28), kind=kLoop, calls=%fused_computation.2 | loop fusion | bytes 1572876 | tf_op jit(solution)/shard_map/dynamic_slice | solution.py:357
  3.9 1.2 %constant_dynamic-slice_fusion.refs_0_.own_ref = bf16[256,1536]{1,0:T(8,128)(2,1)S(1)} fusion(bf16[256,6144]{1,0:T(8,128)(2,1)} %param.12, s32[]{:T(128)S(6)} %select_n.30), kind=kLoop, calls=%fused_computation.1 | loop fusion | bytes 1572868 | tf_op jit(solution)/shard_map/dynamic_slice | solution.py:364
  5.7 3.5 %collective-permute-start.5 = (bf16[64,1536]{1,0:T(8,128)(2,1)S(1)}, bf16[64,1536]{1,0:T(8,128)(2,1)S(1)}, u32[]{:S(2)}, u32[]{:S(2)}) collective-permute-start(bf16[64,1536]{1,0:T(8,128)(2,1)S(1)} %dynamic_slice.12), channel_id=1, source_target_pairs={{0,3},{1,2},{2,1},{3,0},{4,7},{5,6},{6,5},{7,4},{8,11},{9,10},{10,... | collective-permute-start | bytes 589832 | tf_op jit(solution)/shard_map/ppermute | solution.py:326
  9.9 1.2 %fresh.1 = (bf16[2,256,128]{2,1,0:T(8,128)(2,1)S(1)}, bf16[2,256,128]{2,1,0:T(8,128)(2,1)S(1)}, bf16[2,256,128]{2,1,0:T(8,128)(2,1)S(1)}, f32[256,2]{1,0:T(8,128...) custom-call(s32[2]{0:T(128)S(1)} %pad_add_fusion.where_ref, ...), custom_call_target="tpu_custom_call" | custom-call | flops 1 | bytes 1 | tf_op jit(solution)/shard_map/fresh/pallas_call | solution.py:292
  11.1 3.9 %collective-permute-start.6 = (bf16[144,128]{1,0:T(8,128)(2,1)S(1)}, bf16[144,128]{1,0:T(8,128)(2,1)S(1)}, u32[]{:S(2)}, u32[]{:S(2)}) collective-permute-start(bf16[144,128]{1,0:T(8,128)(2,1)S(1)} %get-tuple-element.56.refs_0_), channel_id=1, source_target_pairs={{0,8},{4,12},{8,16},{12,20},{16,24},{20,28},{1,9},{5,13},{9,17},{1... | collective-permute-start | bytes 110600 | tf_op jit(solution)/shard_map/ppermute | solution.py:335
  15.0 1.6 %collective-permute-done.6.refs_1_.refs_0_ = bf16[144,128]{1,0:T(8,128)(2,1)S(1)} collective-permute-done((bf16[144,128]{1,0:T(8,128)(2,1)S(1)}, bf16[144,128]{1,0:T(8,128)(2,1)S(1)}, u32[]{:S(2)}, u32[]{:S(2)}) %collective-permute-start.6) | collective-permute-done | bytes 36896 | tf_op jit(solution)/shard_map/ppermute | solution.py:335
  16.6 2.3 %collective-permute-start.7 = (bf16[64,1536]{1,0:T(8,128)(2,1)S(1)}, bf16[64,1536]{1,0:T(8,128)(2,1)S(1)}, u32[]{:S(2)}, u32[]{:S(2)}) collective-permute-start(bf16[64,1536]{1,0:T(8,128)(2,1)S(1)} %collective-permute-done.5.refs_1_), channel_id=1, source_target_pairs={{0,8},{4,12},{8,0},{12,4},{16,24},{20,28},{24,16},{28,20},{1,9},{5... | collective-permute-start | bytes 589832 | tf_op jit(solution)/shard_map/ppermute | solution.py:332
  19.5 4.5 %collective-permute-start.8 = (bf16[144,128]{1,0:T(8,128)(2,1)S(1)}, bf16[144,128]{1,0:T(8,128)(2,1)S(1)}, u32[]{:S(2)}, u32[]{:S(2)}) collective-permute-start(bf16[144,128]{1,0:T(8,128)(2,1)S(1)} %join.1), channel_id=1, source_target_pairs={{0,16},{4,20},{8,24},{12,28},{1,17},{5,21},{9,25},{13,29},{2,18},{... | collective-permute-start | bytes 110600 | tf_op jit(solution)/shard_map/ppermute | solution.py:335
  24.0 1.1 %inner.1.inner_ref = f32[2,256,128]{2,1,0:T(8,128)S(1)} custom-call(s32[2]{0:T(128)S(1)} %pad_add_fusion.where_ref, bf16[2,256,128]{2,1,0:T(8,128)(2,1)S(1)} %get-tuple-element.58.refs_0_.q_ref, bf16[2,256,128]{2,1,0:T(8,128)(2,1)S(1)} %get-tuple-element.59.refs_1_.k_ref, bf16[2,256,128]{2,1,0:T(8,128)(2,1)S(1)} %get-tuple-element.60.refs_2_.v_ref, ...), custom_call_target="tpu_custom_call" | custom-call | flops 1 | bytes 1 | tf_op jit(solution)/shard_map/inner/pallas_call | solution.py:292
  25.6 1.1 %partial.2 = (f32[2,256,128]{2,1,0:T(8,128)S(1)}, bf16[2,256,128]{2,1,0:T(8,128)(2,1)S(1)}, bf16[128,1536]{1,0:T(8,128)(2,1)S(1)}) custom-call(s32[2]{0:T(128)S(1)} %pad_add_fusion.where_ref, bf16[256,1536]{1,0:T(8,128)(2,1)S(1)} %copy-done, bf16[256,1536]{1,0:T(8,128)(2,1)S(1)} %collective-permute-done.4.got_ref, ...), custom_call_target="tpu_custom_call" | custom-call | flops 1 | bytes 1 | tf_op jit(solution)/shard_map/partial/pallas_call | solution.py:292
  26.8 1.1 %partial.3 = (bf16[2,256,128]{2,1,0:T(8,128)(2,1)S(1)}, bf16[2,256,128]{2,1,0:T(8,128)(2,1)S(1)}, bf16[256,1536]{1,0:T(8,128)(2,1)S(1)}) custom-call(s32[2]{0:T(128)S(1)} %pad_add_fusion.where_ref, bf16[256,1536]{1,0:T(8,128)(2,1)S(1)} %copy-done, bf16[256,1536]{1,0:T(8,128)(2,1)S(1)} %collective-permute-done.4.got_ref, ...), custom_call_target="tpu_custom_call" | custom-call | flops 1 | bytes 1 | tf_op jit(solution)/shard_map/partial/pallas_call | solution.py:292
  27.9 1.6 %collective-permute-start.13 = (bf16[2,256,128]{2,1,0:T(8,128)(2,1)S(1)}, bf16[2,256,128]{2,1,0:T(8,128)(2,1)S(1)}, u32[]{:S(2)}, u32[]{:S(2)}) collective-permute-start(bf16[2,256,128]{2,1,0:T(8,128)(2,1)S(1)} %get-tuple-element.73), channel_id=1, source_target_pairs={{0,1},{1,0},{2,3},{3,2},{4,5},{5,4},{6,7},{7,6},{8,9},{9,8},{10,11... | collective-permute-start | bytes 393224 | tf_op jit(solution)/shard_map/ppermute | solution.py:326
  29.5 1.5 %collective-permute-start.12 = (bf16[2,256,128]{2,1,0:T(8,128)(2,1)S(1)}, bf16[2,256,128]{2,1,0:T(8,128)(2,1)S(1)}, u32[]{:S(2)}, u32[]{:S(2)}) collective-permute-start(bf16[2,256,128]{2,1,0:T(8,128)(2,1)S(1)} %get-tuple-element.69), channel_id=1, source_target_pairs={{0,3},{1,2},{2,1},{3,0},{4,7},{5,6},{6,5},{7,4},{8,11},{9,10},{10,... | collective-permute-start | bytes 393224 | tf_op jit(solution)/shard_map/ppermute | solution.py:326
  32.4 2.5 %collective-permute-start.15 = (bf16[2,256,128]{2,1,0:T(8,128)(2,1)S(1)}, bf16[2,256,128]{2,1,0:T(8,128)(2,1)S(1)}, u32[]{:S(2)}, u32[]{:S(2)}) collective-permute-start(bf16[2,256,128]{2,1,0:T(8,128)(2,1)S(1)} %get-tuple-element.79.refs_0_.refs_4_), channel_id=1, source_target_pairs={{0,3},{1,2},{2,1},{3,0},{4,7},{5,6},{6,5},{7,4},{8,11},{9,10},{10,... | collective-permute-start | bytes 393224 | tf_op jit(solution)/shard_map/ppermute | solution.py:326
  36.0 4.6 %collective-permute-done.14.refs_2_ = bf16[2,256,128]{2,1,0:T(8,128)(2,1)S(1)} collective-permute-done((bf16[2,256,128]{2,1,0:T(8,128)(2,1)S(1)}, bf16[2,256,128]{2,1,0:T(8,128)(2,1)S(1)}, u32[]{:S(2)}, u32[]{:S(2)}) %collective-permute-start.14) | collective-permute-done | bytes 131104 | tf_op jit(solution)/shard_map/ppermute | solution.py:326
  40.6 1.2 %grad_mixed.1 = (f32[2,256,128]{2,1,0:T(8,128)S(1)}, f32[128,128]{1,0:T(8,128)S(1)}, bf16[144,128]{1,0:T(8,128)(2,1)S(1)}) custom-call(s32[2]{0:T(128)S(1)} %pad_add_fusion.where_ref, bf16[2,256,128]{2,1,0:T(8,128)(2,1)S(1)} %get-tuple-element.58.refs_0_.q_ref, f32[256,2]{1,0:T(8,128)S(1)} %get-tuple-element.61.refs_3_.col_ref, f32[1,256]{1,0:T(1,128)S(1)} %bitcast.4, ...), custom_call_target="tpu_custom_call" | custom-call | flops 1 | bytes 1 | tf_op jit(solution)/shard_map/grad_mixed/pallas_call | solution.py:292
  43.2 1.3 %collective-permute-start.20 = (bf16[144,128]{1,0:T(8,128)(2,1)S(1)}, bf16[144,128]{1,0:T(8,128)(2,1)S(1)}, u32[]{:S(2)}, u32[]{:S(2)}) collective-permute-start(bf16[144,128]{1,0:T(8,128)(2,1)S(1)} %get-tuple-element.80), channel_id=1, source_target_pairs={{24,0},{28,4},{25,1},{29,5},{26,2},{30,6},{27,3},{31,7}} | collective-permute-start | bytes 110600 | tf_op jit(solution)/shard_map/ppermute | solution.py:335
  44.5 1.3 %collective-permute-start.21 = (bf16[144,128]{1,0:T(8,128)(2,1)S(1)}, bf16[144,128]{1,0:T(8,128)(2,1)S(1)}, u32[]{:S(2)}, u32[]{:S(2)}) collective-permute-start(bf16[144,128]{1,0:T(8,128)(2,1)S(1)} %get-tuple-element.80), channel_id=1, source_target_pairs={{16,0},{20,4},{24,8},{28,12},{17,1},{21,5},{25,9},{29,13},{18,2},{... | collective-permute-start | bytes 110600 | tf_op jit(solution)/shard_map/ppermute | solution.py:335
  45.8 1.3 %collective-permute-start.22 = (bf16[144,128]{1,0:T(8,128)(2,1)S(1)}, bf16[144,128]{1,0:T(8,128)(2,1)S(1)}, u32[]{:S(2)}, u32[]{:S(2)}) collective-permute-start(bf16[144,128]{1,0:T(8,128)(2,1)S(1)} %get-tuple-element.80), channel_id=1, source_target_pairs={{8,0},{12,4},{16,8},{20,12},{24,16},{28,20},{9,1},{13,5},{17,9},{2... | collective-permute-start | bytes 110600 | tf_op jit(solution)/shard_map/ppermute | solution.py:335
  47.1 1.4 %inner_grad.1 = (f32[256,512]{1,0:T(8,128)S(1)}, f32[256,512]{1,0:T(8,128)S(1)}) custom-call(s32[2]{0:T(128)S(1)} %pad_add_fusion.where_ref, bf16[2,256,128]{2,1,0:T(8,128)(2,1)S(1)} %get-tuple-element.58.refs_0_.q_ref, bf16[2,256,128]{2,1,0:T(8,128)(2,1)S(1)} %get-tuple-element.59.refs_1_.k_ref, bf16[2,256,128]{2,1,0:T(8,128)(2,1)S(1)} %get-tuple-element.60.refs_2_.v_ref, ...), custom_call_target="tpu_custom_call" | custom-call | flops 1 | bytes 1 | tf_op jit(solution)/shard_map/inner_grad/pallas_call | solution.py:292
  48.5 2.4 %layer.1 = bf16[256,1536]{1,0:T(8,128)(2,1)} custom-call(s32[2]{0:T(128)S(1)} %pad_add_fusion.where_ref, bf16[256,1536]{1,0:T(8,128)(2,1)S(1)} %constant_dynamic-slice_fusion.refs_0_.own_ref, bf16[128,1536]{1,0:T(8,128)(2,1)S(1)} %get-tuple-element.67.refs_0_, bf16[256,1536]{1,0:T(8,128)(2,1)S(1)} %get-tuple-element.81.refs_1_, ...), custom_call_target="tpu_custom_call" | custom-call | flops 1 | bytes 1 | tf_op jit(solution)/shard_map/layer/pallas_call | solution.py:292
  50.9 1.4 %collective-permute-done.21.refs_1_ = bf16[144,128]{1,0:T(8,128)(2,1)S(1)} collective-permute-done((bf16[144,128]{1,0:T(8,128)(2,1)S(1)}, bf16[144,128]{1,0:T(8,128)(2,1)S(1)}, u32[]{:S(2)}, u32[]{:S(2)}) %collective-permute-start.21) | collective-permute-done | bytes 36896 | tf_op jit(solution)/shard_map/ppermute | solution.py:335
  53.3 0.9 %collective-permute-done.24.refs_3_ = bf16[144,128]{1,0:T(8,128)(2,1)S(1)} collective-permute-done((bf16[144,128]{1,0:T(8,128)(2,1)S(1)}, bf16[144,128]{1,0:T(8,128)(2,1)S(1)}, u32[]{:S(2)}, u32[]{:S(2)}) %collective-permute-start.24) | collective-permute-done | bytes 36896 | tf_op jit(solution)/shard_map/ppermute | solution.py:329
  54.4 1.5 %outer_grad.1 = (bf16[256,256]{1,0:T(8,128)(2,1)}, bf16[256,256]{1,0:T(8,128)(2,1)}, bf16[256,256]{1,0:T(8,128)(2,1)}) custom-call(s32[2]{0:T(128)S(1)} %pad_add_fusion.where_ref, bf16[256,256]{1,0:T(8,128)(2,1)S(1)} %copy-done.1, bf16[256,256]{1,0:T(8,128)(2,1)S(1)} %copy-done.2, f32[256,512]{1,0:T(8,128)S(1)} %get-tuple-element.85.inner_ref, ...), custom_call_target="tpu_custom_call" | custom-call | flops 1 | bytes 1 | tf_op jit(solution)/shard_map/outer_grad/pallas_call | solution.py:292
  (57 shorter events, 9.4 us)
Async XLA Ops:
  0.7 4.4 %collective-permute-start = (bf16[256,256]{1,0:T(8,128)(2,1)}, bf16[256,256]{1,0:T(8,128)(2,1)S(1)}, u32[]{:S(2)}, u32[]{:S(2)}) collective-permute-start(bf16[256,256]{1,0:T(8,128)(2,1)} %q_ref.1), channel_id=1, source_target_pairs={{0,4},{4,0},{8,12},{12,8},{16,20},{20,16},{24,28},{28,24},{1,5},{5... | collective-permute-start | bytes 393224 | tf_op jit(solution)/shard_map/ppermute | solution.py:329
  1.2 3.9 %collective-permute-start.1 = (bf16[256,256]{1,0:T(8,128)(2,1)}, bf16[256,256]{1,0:T(8,128)(2,1)S(1)}, u32[]{:S(2)}, u32[]{:S(2)}) collective-permute-start(bf16[256,256]{1,0:T(8,128)(2,1)} %k_ref.3), channel_id=1, source_target_pairs={{0,4},{4,0},{8,12},{12,8},{16,20},{20,16},{24,28},{28,24},{1,5},{5... | collective-permute-start | bytes 393224 | tf_op jit(solution)/shard_map/ppermute | solution.py:329
  1.3 3.9 %collective-permute-start.2 = (bf16[256,256]{1,0:T(8,128)(2,1)}, bf16[256,256]{1,0:T(8,128)(2,1)S(1)}, u32[]{:S(2)}, u32[]{:S(2)}) collective-permute-start(bf16[256,256]{1,0:T(8,128)(2,1)} %v_ref.3), channel_id=1, source_target_pairs={{0,4},{4,0},{8,12},{12,8},{16,20},{20,16},{24,28},{28,24},{1,5},{5... | collective-permute-start | bytes 393224 | tf_op jit(solution)/shard_map/ppermute | solution.py:329
  1.7 3.4 %collective-permute-start.3 = (f32[2,256]{1,0:T(2,128)}, f32[2,256]{1,0:T(2,128)S(1)}, u32[]{:S(2)}, u32[]{:S(2)}) collective-permute-start(f32[2,256]{1,0:T(2,128)} %decay_ref.1), channel_id=1, source_target_pairs={{0,4},{4,0},{8,12},{12,8},{16,20},{20,16},{24,28},{28,24},{1,5},{5... | collective-permute-start | bytes 6152 | tf_op jit(solution)/shard_map/ppermute | solution.py:329
  5.2 5.9 %collective-permute-start.4 = (bf16[256,1536]{1,0:T(8,128)(2,1)S(1)}, bf16[256,1536]{1,0:T(8,128)(2,1)S(1)}, u32[]{:S(2)}, u32[]{:S(2)}) collective-permute-start(bf16[256,1536]{1,0:T(8,128)(2,1)S(1)} %copy-done), channel_id=1, source_target_pairs={{0,4},{4,0},{8,12},{12,8},{16,20},{20,16},{24,28},{28,24},{1,5},{5... | collective-permute-start | bytes 2359304 | tf_op jit(solution)/shard_map/ppermute | solution.py:329
  5.7 9.3 %collective-permute-start.5 = (bf16[64,1536]{1,0:T(8,128)(2,1)S(1)}, bf16[64,1536]{1,0:T(8,128)(2,1)S(1)}, u32[]{:S(2)}, u32[]{:S(2)}) collective-permute-start(bf16[64,1536]{1,0:T(8,128)(2,1)S(1)} %dynamic_slice.12), channel_id=1, source_target_pairs={{0,3},{1,2},{2,1},{3,0},{4,7},{5,6},{6,5},{7,4},{8,11},{9,10},{10,... | collective-permute-start | bytes 589832 | tf_op jit(solution)/shard_map/ppermute | solution.py:326
  9.2 17.6 %collective-permute-start.10 = (bf16[128,1536]{1,0:T(8,128)(2,1)S(1)}, bf16[128,1536]{1,0:T(8,128)(2,1)S(1)}, u32[]{:S(2)}, u32[]{:S(2)}) collective-permute-start(bf16[128,1536]{1,0:T(8,128)(2,1)S(1)} %get-tuple-element.94), channel_id=1, source_target_pairs={{0,2},{1,3},{2,0},{3,1},{4,6},{5,7},{6,4},{7,5},{8,10},{9,11},{10,... | collective-permute-start | bytes 1179656 | tf_op jit(solution)/shard_map/ppermute | solution.py:326
  9.7 17.1 %collective-permute-start.9 = (bf16[128,1536]{1,0:T(8,128)(2,1)S(1)}, bf16[128,1536]{1,0:T(8,128)(2,1)S(1)}, u32[]{:S(2)}, u32[]{:S(2)}) collective-permute-start(bf16[128,1536]{1,0:T(8,128)(2,1)S(1)} %get-tuple-element.95), channel_id=1, source_target_pairs={{0,1},{1,0},{2,3},{3,2},{4,5},{5,4},{6,7},{7,6},{8,9},{9,8},{10,11... | collective-permute-start | bytes 1179656 | tf_op jit(solution)/shard_map/ppermute | solution.py:326
  11.1 5.5 %collective-permute-start.6 = (bf16[144,128]{1,0:T(8,128)(2,1)S(1)}, bf16[144,128]{1,0:T(8,128)(2,1)S(1)}, u32[]{:S(2)}, u32[]{:S(2)}) collective-permute-start(bf16[144,128]{1,0:T(8,128)(2,1)S(1)} %get-tuple-element.56.refs_0_), channel_id=1, source_target_pairs={{0,8},{4,12},{8,16},{12,20},{16,24},{20,28},{1,9},{5,13},{9,17},{1... | collective-permute-start | bytes 110600 | tf_op jit(solution)/shard_map/ppermute | solution.py:335
  16.6 9.0 %collective-permute-start.7 = (bf16[64,1536]{1,0:T(8,128)(2,1)S(1)}, bf16[64,1536]{1,0:T(8,128)(2,1)S(1)}, u32[]{:S(2)}, u32[]{:S(2)}) collective-permute-start(bf16[64,1536]{1,0:T(8,128)(2,1)S(1)} %collective-permute-done.5.refs_1_), channel_id=1, source_target_pairs={{0,8},{4,12},{8,0},{12,4},{16,24},{20,28},{24,16},{28,20},{1,9},{5... | collective-permute-start | bytes 589832 | tf_op jit(solution)/shard_map/ppermute | solution.py:332
  19.5 6.1 %collective-permute-start.8 = (bf16[144,128]{1,0:T(8,128)(2,1)S(1)}, bf16[144,128]{1,0:T(8,128)(2,1)S(1)}, u32[]{:S(2)}, u32[]{:S(2)}) collective-permute-start(bf16[144,128]{1,0:T(8,128)(2,1)S(1)} %join.1), channel_id=1, source_target_pairs={{0,16},{4,20},{8,24},{12,28},{1,17},{5,21},{9,25},{13,29},{2,18},{... | collective-permute-start | bytes 110600 | tf_op jit(solution)/shard_map/ppermute | solution.py:335
  27.9 7.5 %collective-permute-start.13 = (bf16[2,256,128]{2,1,0:T(8,128)(2,1)S(1)}, bf16[2,256,128]{2,1,0:T(8,128)(2,1)S(1)}, u32[]{:S(2)}, u32[]{:S(2)}) collective-permute-start(bf16[2,256,128]{2,1,0:T(8,128)(2,1)S(1)} %get-tuple-element.73), channel_id=1, source_target_pairs={{0,1},{1,0},{2,3},{3,2},{4,5},{5,4},{6,7},{7,6},{8,9},{9,8},{10,11... | collective-permute-start | bytes 393224 | tf_op jit(solution)/shard_map/ppermute | solution.py:326
  29.5 11.1 %collective-permute-start.12 = (bf16[2,256,128]{2,1,0:T(8,128)(2,1)S(1)}, bf16[2,256,128]{2,1,0:T(8,128)(2,1)S(1)}, u32[]{:S(2)}, u32[]{:S(2)}) collective-permute-start(bf16[2,256,128]{2,1,0:T(8,128)(2,1)S(1)} %get-tuple-element.69), channel_id=1, source_target_pairs={{0,3},{1,2},{2,1},{3,0},{4,7},{5,6},{6,5},{7,4},{8,11},{9,10},{10,... | collective-permute-start | bytes 393224 | tf_op jit(solution)/shard_map/ppermute | solution.py:326
  31.0 9.6 %collective-permute-start.14 = (bf16[2,256,128]{2,1,0:T(8,128)(2,1)S(1)}, bf16[2,256,128]{2,1,0:T(8,128)(2,1)S(1)}, u32[]{:S(2)}, u32[]{:S(2)}) collective-permute-start(bf16[2,256,128]{2,1,0:T(8,128)(2,1)S(1)} %get-tuple-element.74), channel_id=1, source_target_pairs={{0,2},{1,3},{2,0},{3,1},{4,6},{5,7},{6,4},{7,5},{8,10},{9,11},{10,... | collective-permute-start | bytes 393224 | tf_op jit(solution)/shard_map/ppermute | solution.py:326
  32.4 9.3 %collective-permute-start.15 = (bf16[2,256,128]{2,1,0:T(8,128)(2,1)S(1)}, bf16[2,256,128]{2,1,0:T(8,128)(2,1)S(1)}, u32[]{:S(2)}, u32[]{:S(2)}) collective-permute-start(bf16[2,256,128]{2,1,0:T(8,128)(2,1)S(1)} %get-tuple-element.79.refs_0_.refs_4_), channel_id=1, source_target_pairs={{0,3},{1,2},{2,1},{3,0},{4,7},{5,6},{6,5},{7,4},{8,11},{9,10},{10,... | collective-permute-start | bytes 393224 | tf_op jit(solution)/shard_map/ppermute | solution.py:326
  34.9 6.8 %collective-permute-start.16 = (bf16[2,256,128]{2,1,0:T(8,128)(2,1)S(1)}, bf16[2,256,128]{2,1,0:T(8,128)(2,1)S(1)}, u32[]{:S(2)}, u32[]{:S(2)}) collective-permute-start(bf16[2,256,128]{2,1,0:T(8,128)(2,1)S(1)} %get-tuple-element.79.refs_0_.refs_4_), channel_id=1, source_target_pairs={{0,1},{1,0},{2,3},{3,2},{4,5},{5,4},{6,7},{7,6},{8,9},{9,8},{10,11... | collective-permute-start | bytes 393224 | tf_op jit(solution)/shard_map/ppermute | solution.py:326
  35.5 6.5 %collective-permute-start.17 = (bf16[2,256,128]{2,1,0:T(8,128)(2,1)S(1)}, bf16[2,256,128]{2,1,0:T(8,128)(2,1)S(1)}, u32[]{:S(2)}, u32[]{:S(2)}) collective-permute-start(bf16[2,256,128]{2,1,0:T(8,128)(2,1)S(1)} %get-tuple-element.79.refs_0_.refs_4_), channel_id=1, source_target_pairs={{0,2},{1,3},{2,0},{3,1},{4,6},{5,7},{6,4},{7,5},{8,10},{9,11},{10,... | collective-permute-start | bytes 393224 | tf_op jit(solution)/shard_map/ppermute | solution.py:326
  42.0 6.5 %collective-permute-start.18 = (bf16[256,1536]{1,0:T(8,128)(2,1)S(1)}, bf16[256,1536]{1,0:T(8,128)(2,1)S(1)}, u32[]{:S(2)}, u32[]{:S(2)}) collective-permute-start(bf16[256,1536]{1,0:T(8,128)(2,1)S(1)} %get-tuple-element.81.refs_1_), channel_id=1, source_target_pairs={{0,4},{4,0},{8,12},{12,8},{16,20},{20,16},{24,28},{28,24},{1,5},{5... | collective-permute-start | bytes 2359304 | tf_op jit(solution)/shard_map/ppermute | solution.py:329
  42.0 6.4 %collective-permute-start.11 = (bf16[128,1536]{1,0:T(8,128)(2,1)S(1)}, bf16[128,1536]{1,0:T(8,128)(2,1)S(1)}, u32[]{:S(2)}, u32[]{:S(2)}) collective-permute-start(bf16[128,1536]{1,0:T(8,128)(2,1)S(1)} %get-tuple-element.67.refs_0_), channel_id=1, source_target_pairs={{0,4},{4,0},{8,12},{12,8},{16,20},{20,16},{24,28},{28,24},{1,5},{5... | collective-permute-start | bytes 1179656 | tf_op jit(solution)/shard_map/ppermute | solution.py:329
  43.1 2.7 %collective-permute-start.19 = (bf16[4,256,128]{2,1,0:T(8,128)(2,1)S(1)}, bf16[4,256,128]{2,1,0:T(8,128)(2,1)S(1)}, u32[]{:S(2)}, u32[]{:S(2)}) collective-permute-start(bf16[4,256,128]{2,1,0:T(8,128)(2,1)S(1)} %cross.1), channel_id=1, source_target_pairs={{0,4},{4,0},{8,12},{12,8},{16,20},{20,16},{24,28},{28,24},{1,5},{5... | collective-permute-start | bytes 786440 | tf_op jit(solution)/shard_map/ppermute | solution.py:329
  43.2 7.8 %collective-permute-start.20 = (bf16[144,128]{1,0:T(8,128)(2,1)S(1)}, bf16[144,128]{1,0:T(8,128)(2,1)S(1)}, u32[]{:S(2)}, u32[]{:S(2)}) collective-permute-start(bf16[144,128]{1,0:T(8,128)(2,1)S(1)} %get-tuple-element.80), channel_id=1, source_target_pairs={{24,0},{28,4},{25,1},{29,5},{26,2},{30,6},{27,3},{31,7}} | collective-permute-start | bytes 110600 | tf_op jit(solution)/shard_map/ppermute | solution.py:335
  44.5 7.8 %collective-permute-start.21 = (bf16[144,128]{1,0:T(8,128)(2,1)S(1)}, bf16[144,128]{1,0:T(8,128)(2,1)S(1)}, u32[]{:S(2)}, u32[]{:S(2)}) collective-permute-start(bf16[144,128]{1,0:T(8,128)(2,1)S(1)} %get-tuple-element.80), channel_id=1, source_target_pairs={{16,0},{20,4},{24,8},{28,12},{17,1},{21,5},{25,9},{29,13},{18,2},{... | collective-permute-start | bytes 110600 | tf_op jit(solution)/shard_map/ppermute | solution.py:335
  45.8 6.5 %collective-permute-start.22 = (bf16[144,128]{1,0:T(8,128)(2,1)S(1)}, bf16[144,128]{1,0:T(8,128)(2,1)S(1)}, u32[]{:S(2)}, u32[]{:S(2)}) collective-permute-start(bf16[144,128]{1,0:T(8,128)(2,1)S(1)} %get-tuple-element.80), channel_id=1, source_target_pairs={{8,0},{12,4},{16,8},{20,12},{24,16},{28,20},{9,1},{13,5},{17,9},{2... | collective-permute-start | bytes 110600 | tf_op jit(solution)/shard_map/ppermute | solution.py:335
  52.3 2.1 %collective-permute-start.23 = (f32[256,512]{1,0:T(8,128)S(1)}, f32[256,512]{1,0:T(8,128)S(1)}, u32[]{:S(2)}, u32[]{:S(2)}) collective-permute-start(f32[256,512]{1,0:T(8,128)S(1)} %get-tuple-element.90), channel_id=1, source_target_pairs={{0,4},{4,0},{8,12},{12,8},{16,20},{20,16},{24,28},{28,24},{1,5},{5... | collective-permute-start | bytes 1572872 | tf_op jit(solution)/shard_map/ppermute | solution.py:329
  (9 other events, 67.0 us)

commit v14 on v13

--- a/solution.py
+++ b/solution.py
@@ -270,18 +270,17 @@
     core = where_ref[0]
     mine = [ref[core] for ref in normed_refs]
     theirs = [got_ref[number] for number in range(got_ref.shape[0])]
-    normed = [mine[0], theirs[0], mine[1], theirs[1]]
-    for begin in range(2, len(mine), 2):
-        normed += mine[begin : begin + 2] + theirs[begin : begin + 2]
-    normed = jnp.concatenate(normed, axis=1)
+    first = core == 0
+    own = jnp.concatenate([jnp.where(first, mine[0], theirs[0]), jnp.where(first, theirs[0], mine[0])], axis=1)
+    pieces = [(own, own_ref), (mine[1], mine_refs[0]), (theirs[1], theirs_refs[0])]
+    for pair in range(1, pairs):
+        for rows, refs in ((mine, mine_refs), (theirs, theirs_refs)):
+            pieces.append((jnp.concatenate(rows[2 * pair : 2 * pair + 2], axis=1), refs[pair]))
     width = own_ref.shape[1]
     step = 512 if width % 512 == 0 else 128
     for begin in range(0, width, step):
         lanes = slice(begin, begin + step)
-        weight = [own_ref[rows_of(core, HD), lanes], own_ref[rows_of(1 - core, HD), lanes]]
-        for mine_ref, theirs_ref in zip(mine_refs, theirs_refs):
-            weight += [mine_ref[:, lanes], theirs_ref[:, lanes]]
-        out_ref[:, lanes] = dot(normed, jnp.concatenate(weight, axis=0), NN).astype(BF16)
+        out_ref[:, lanes] = sum(dot(rows, ref[:, lanes], NN) for rows, ref in pieces).astype(BF16)
 
 
 SMEM = pl.BlockSpec(memory_space=pltpu.SMEM)

time: 56.2 us -> 56.2 us (level)
  transfers between devices with their start and end apart: 27 -> 27, of which waited for: 8 -> 8; matrix products, arithmetic and copies ran while one was open for 6% -> 6% of each run, Pallas kernels for 18% -> 19%
where the time goes in v14:
time: 56.2 us; the launch traced here: 55.9 us
  starting transfers between devices  29 us (52%)
  Pallas kernels  13.1 us (23%)
  waiting for transfers between devices  9.32 us (17%)
  local copies, waits for them, and re-layouts  3.34 us (6%)
  between operations  0.93 us (2%)
    pallas_call x11, Pallas kernels, call(): pl.pallas_call(kernel, name=name, out_shape=outs, in_specs=[SMEM] + [VMEM...  13.1 us
    ppermute x5, starting transfers between devices, to_chip(): lax.ppermute(value, 'seq', [(i, i + 2 * step) for i in range(seq) if 0 <=...  12.3 us
    ppermute x9, starting transfers between devices, swap_tensor(): return lax.ppermute(value, 'tensor', [(i, i ^ k) for i in range(tensor)])  11.3 us
    ppermute x9, waiting for transfers between devices, swap_tensor(): return lax.ppermute(value, 'tensor', [(i, i ^ k) for i in range(tensor)])  4.86 us
    ppermute x5, waiting for transfers between devices, to_chip(): lax.ppermute(value, 'seq', [(i, i + 2 * step) for i in range(seq) if 0 <=...  3.39 us
    ppermute x12, starting transfers between devices, swap_core(): return lax.ppermute(value, 'seq', [(i, i ^ 1) for i in range(seq)])  3.21 us
    ppermute x1, starting transfers between devices, swap_side(): return lax.ppermute(value, 'seq', [(i, i ^ 2) for i in range(seq)])  2.32 us
    dynamic_slice x2, local copies, waits for them, and re-layouts, slice_for(): lax.dynamic_slice(out_weight, (begin, (place ^ step) * width), (rows, wid...  2.12 us
  transfers between devices with their start and end apart: 27, of which 8 were waited for; matrix products, arithmetic and copies ran while one was open for 6% of the time, Pallas kernels for 19%

profile of v14, /device:TPU:0, one launch (start us, length us, event | category | flops | bytes accessed | tf_op | source)
XLA Modules:
  0.0 55.9 jit_solution(195300798954762530)
XLA Ops:
  2.7 1.2 %fusion = (bf16[128,1536]{1,0:T(8,128)(2,1)S(1)}, bf16[128,1536]{1,0:T(8,128)(2,1)S(1)}) fusion(bf16[256,6144]{1,0:T(8,128)(2,1)} %param.12, s32[]{:T(128)S(6)} %select_n.27, s32[]{:T(128)S(6)} %select_n.29, s32[]{:T(128)S(6)} %select_n.28), kind=kLoop, calls=%fused_computation.2 | loop fusion | bytes 1572876 | tf_op jit(solution)/shard_map/dynamic_slice | solution.py:356
  3.9 1.2 %constant_dynamic-slice_fusion.refs_0_.own_ref = bf16[256,1536]{1,0:T(8,128)(2,1)S(1)} fusion(bf16[256,6144]{1,0:T(8,128)(2,1)} %param.12, s32[]{:T(128)S(6)} %select_n.30), kind=kLoop, calls=%fused_computation.1 | loop fusion | bytes 1572868 | tf_op jit(solution)/shard_map/dynamic_slice | solution.py:363
  5.7 3.5 %collective-permute-start.5 = (bf16[64,1536]{1,0:T(8,128)(2,1)S(1)}, bf16[64,1536]{1,0:T(8,128)(2,1)S(1)}, u32[]{:S(2)}, u32[]{:S(2)}) collective-permute-start(bf16[64,1536]{1,0:T(8,128)(2,1)S(1)} %dynamic_slice.12), channel_id=1, source_target_pairs={{0,3},{1,2},{2,1},{3,0},{4,7},{5,6},{6,5},{7,4},{8,11},{9,10},{10,... | collective-permute-start | bytes 589832 | tf_op jit(solution)/shard_map/ppermute | solution.py:325
  9.9 1.2 %fresh.1 = (bf16[2,256,128]{2,1,0:T(8,128)(2,1)S(1)}, bf16[2,256,128]{2,1,0:T(8,128)(2,1)S(1)}, bf16[2,256,128]{2,1,0:T(8,128)(2,1)S(1)}, f32[256,2]{1,0:T(8,128...) custom-call(s32[2]{0:T(128)S(1)} %pad_add_fusion.where_ref, ...), custom_call_target="tpu_custom_call" | custom-call | flops 1 | bytes 1 | tf_op jit(solution)/shard_map/fresh/pallas_call | solution.py:291
  11.1 3.9 %collective-permute-start.6 = (bf16[144,128]{1,0:T(8,128)(2,1)S(1)}, bf16[144,128]{1,0:T(8,128)(2,1)S(1)}, u32[]{:S(2)}, u32[]{:S(2)}) collective-permute-start(bf16[144,128]{1,0:T(8,128)(2,1)S(1)} %get-tuple-element.56.refs_0_), channel_id=1, source_target_pairs={{0,8},{4,12},{8,16},{12,20},{16,24},{20,28},{1,9},{5,13},{9,17},{1... | collective-permute-start | bytes 110600 | tf_op jit(solution)/shard_map/ppermute | solution.py:334
  15.0 1.6 %collective-permute-done.6.refs_1_.refs_0_ = bf16[144,128]{1,0:T(8,128)(2,1)S(1)} collective-permute-done((bf16[144,128]{1,0:T(8,128)(2,1)S(1)}, bf16[144,128]{1,0:T(8,128)(2,1)S(1)}, u32[]{:S(2)}, u32[]{:S(2)}) %collective-permute-start.6) | collective-permute-done | bytes 36896 | tf_op jit(solution)/shard_map/ppermute | solution.py:334
  16.6 2.3 %collective-permute-start.7 = (bf16[64,1536]{1,0:T(8,128)(2,1)S(1)}, bf16[64,1536]{1,0:T(8,128)(2,1)S(1)}, u32[]{:S(2)}, u32[]{:S(2)}) collective-permute-start(bf16[64,1536]{1,0:T(8,128)(2,1)S(1)} %collective-permute-done.5.refs_1_), channel_id=1, source_target_pairs={{0,8},{4,12},{8,0},{12,4},{16,24},{20,28},{24,16},{28,20},{1,9},{5... | collective-permute-start | bytes 589832 | tf_op jit(solution)/shard_map/ppermute | solution.py:331
  19.5 4.5 %collective-permute-start.8 = (bf16[144,128]{1,0:T(8,128)(2,1)S(1)}, bf16[144,128]{1,0:T(8,128)(2,1)S(1)}, u32[]{:S(2)}, u32[]{:S(2)}) collective-permute-start(bf16[144,128]{1,0:T(8,128)(2,1)S(1)} %join.1), channel_id=1, source_target_pairs={{0,16},{4,20},{8,24},{12,28},{1,17},{5,21},{9,25},{13,29},{2,18},{... | collective-permute-start | bytes 110600 | tf_op jit(solution)/shard_map/ppermute | solution.py:334
  24.0 1.1 %inner.1.inner_ref = f32[2,256,128]{2,1,0:T(8,128)S(1)} custom-call(s32[2]{0:T(128)S(1)} %pad_add_fusion.where_ref, bf16[2,256,128]{2,1,0:T(8,128)(2,1)S(1)} %get-tuple-element.58.refs_0_.q_ref, bf16[2,256,128]{2,1,0:T(8,128)(2,1)S(1)} %get-tuple-element.59.refs_1_.k_ref, bf16[2,256,128]{2,1,0:T(8,128)(2,1)S(1)} %get-tuple-element.60.refs_2_.v_ref, ...), custom_call_target="tpu_custom_call" | custom-call | flops 1 | bytes 1 | tf_op jit(solution)/shard_map/inner/pallas_call | solution.py:291
  25.6 1.1 %partial.2 = (f32[2,256,128]{2,1,0:T(8,128)S(1)}, bf16[2,256,128]{2,1,0:T(8,128)(2,1)S(1)}, bf16[128,1536]{1,0:T(8,128)(2,1)S(1)}) custom-call(s32[2]{0:T(128)S(1)} %pad_add_fusion.where_ref, bf16[256,1536]{1,0:T(8,128)(2,1)S(1)} %copy-done, bf16[256,1536]{1,0:T(8,128)(2,1)S(1)} %collective-permute-done.4.got_ref, ...), custom_call_target="tpu_custom_call" | custom-call | flops 1 | bytes 1 | tf_op jit(solution)/shard_map/partial/pallas_call | solution.py:291
  26.8 1.1 %partial.3 = (bf16[2,256,128]{2,1,0:T(8,128)(2,1)S(1)}, bf16[2,256,128]{2,1,0:T(8,128)(2,1)S(1)}, bf16[256,1536]{1,0:T(8,128)(2,1)S(1)}) custom-call(s32[2]{0:T(128)S(1)} %pad_add_fusion.where_ref, bf16[256,1536]{1,0:T(8,128)(2,1)S(1)} %copy-done, bf16[256,1536]{1,0:T(8,128)(2,1)S(1)} %collective-permute-done.4.got_ref, ...), custom_call_target="tpu_custom_call" | custom-call | flops 1 | bytes 1 | tf_op jit(solution)/shard_map/partial/pallas_call | solution.py:291
  27.9 1.6 %collective-permute-start.13 = (bf16[2,256,128]{2,1,0:T(8,128)(2,1)S(1)}, bf16[2,256,128]{2,1,0:T(8,128)(2,1)S(1)}, u32[]{:S(2)}, u32[]{:S(2)}) collective-permute-start(bf16[2,256,128]{2,1,0:T(8,128)(2,1)S(1)} %get-tuple-element.73), channel_id=1, source_target_pairs={{0,1},{1,0},{2,3},{3,2},{4,5},{5,4},{6,7},{7,6},{8,9},{9,8},{10,11... | collective-permute-start | bytes 393224 | tf_op jit(solution)/shard_map/ppermute | solution.py:325
  29.5 1.5 %collective-permute-start.12 = (bf16[2,256,128]{2,1,0:T(8,128)(2,1)S(1)}, bf16[2,256,128]{2,1,0:T(8,128)(2,1)S(1)}, u32[]{:S(2)}, u32[]{:S(2)}) collective-permute-start(bf16[2,256,128]{2,1,0:T(8,128)(2,1)S(1)} %get-tuple-element.69), channel_id=1, source_target_pairs={{0,3},{1,2},{2,1},{3,0},{4,7},{5,6},{6,5},{7,4},{8,11},{9,10},{10,... | collective-permute-start | bytes 393224 | tf_op jit(solution)/shard_map/ppermute | solution.py:325
  32.4 2.5 %collective-permute-start.15 = (bf16[2,256,128]{2,1,0:T(8,128)(2,1)S(1)}, bf16[2,256,128]{2,1,0:T(8,128)(2,1)S(1)}, u32[]{:S(2)}, u32[]{:S(2)}) collective-permute-start(bf16[2,256,128]{2,1,0:T(8,128)(2,1)S(1)} %get-tuple-element.79.refs_0_.refs_4_), channel_id=1, source_target_pairs={{0,3},{1,2},{2,1},{3,0},{4,7},{5,6},{6,5},{7,4},{8,11},{9,10},{10,... | collective-permute-start | bytes 393224 | tf_op jit(solution)/shard_map/ppermute | solution.py:325
  36.0 4.6 %collective-permute-done.14.refs_2_ = bf16[2,256,128]{2,1,0:T(8,128)(2,1)S(1)} collective-permute-done((bf16[2,256,128]{2,1,0:T(8,128)(2,1)S(1)}, bf16[2,256,128]{2,1,0:T(8,128)(2,1)S(1)}, u32[]{:S(2)}, u32[]{:S(2)}) %collective-permute-start.14) | collective-permute-done | bytes 131104 | tf_op jit(solution)/shard_map/ppermute | solution.py:325
  40.6 1.2 %grad_mixed.1 = (f32[2,256,128]{2,1,0:T(8,128)S(1)}, f32[128,128]{1,0:T(8,128)S(1)}, bf16[144,128]{1,0:T(8,128)(2,1)S(1)}) custom-call(s32[2]{0:T(128)S(1)} %pad_add_fusion.where_ref, bf16[2,256,128]{2,1,0:T(8,128)(2,1)S(1)} %get-tuple-element.58.refs_0_.q_ref, f32[256,2]{1,0:T(8,128)S(1)} %get-tuple-element.61.refs_3_.col_ref, f32[1,256]{1,0:T(1,128)S(1)} %bitcast.4, ...), custom_call_target="tpu_custom_call" | custom-call | flops 1 | bytes 1 | tf_op jit(solution)/shard_map/grad_mixed/pallas_call | solution.py:291
  43.2 1.3 %collective-permute-start.20 = (bf16[144,128]{1,0:T(8,128)(2,1)S(1)}, bf16[144,128]{1,0:T(8,128)(2,1)S(1)}, u32[]{:S(2)}, u32[]{:S(2)}) collective-permute-start(bf16[144,128]{1,0:T(8,128)(2,1)S(1)} %get-tuple-element.80), channel_id=1, source_target_pairs={{24,0},{28,4},{25,1},{29,5},{26,2},{30,6},{27,3},{31,7}} | collective-permute-start | bytes 110600 | tf_op jit(solution)/shard_map/ppermute | solution.py:334
  44.5 1.3 %collective-permute-start.21 = (bf16[144,128]{1,0:T(8,128)(2,1)S(1)}, bf16[144,128]{1,0:T(8,128)(2,1)S(1)}, u32[]{:S(2)}, u32[]{:S(2)}) collective-permute-start(bf16[144,128]{1,0:T(8,128)(2,1)S(1)} %get-tuple-element.80), channel_id=1, source_target_pairs={{16,0},{20,4},{24,8},{28,12},{17,1},{21,5},{25,9},{29,13},{18,2},{... | collective-permute-start | bytes 110600 | tf_op jit(solution)/shard_map/ppermute | solution.py:334
  45.8 1.3 %collective-permute-start.22 = (bf16[144,128]{1,0:T(8,128)(2,1)S(1)}, bf16[144,128]{1,0:T(8,128)(2,1)S(1)}, u32[]{:S(2)}, u32[]{:S(2)}) collective-permute-start(bf16[144,128]{1,0:T(8,128)(2,1)S(1)} %get-tuple-element.80), channel_id=1, source_target_pairs={{8,0},{12,4},{16,8},{20,12},{24,16},{28,20},{9,1},{13,5},{17,9},{2... | collective-permute-start | bytes 110600 | tf_op jit(solution)/shard_map/ppermute | solution.py:334
  47.1 1.4 %inner_grad.1 = (f32[256,512]{1,0:T(8,128)S(1)}, f32[256,512]{1,0:T(8,128)S(1)}) custom-call(s32[2]{0:T(128)S(1)} %pad_add_fusion.where_ref, bf16[2,256,128]{2,1,0:T(8,128)(2,1)S(1)} %get-tuple-element.58.refs_0_.q_ref, bf16[2,256,128]{2,1,0:T(8,128)(2,1)S(1)} %get-tuple-element.59.refs_1_.k_ref, bf16[2,256,128]{2,1,0:T(8,128)(2,1)S(1)} %get-tuple-element.60.refs_2_.v_ref, ...), custom_call_target="tpu_custom_call" | custom-call | flops 1 | bytes 1 | tf_op jit(solution)/shard_map/inner_grad/pallas_call | solution.py:291
  48.5 2.6 %layer.1 = bf16[256,1536]{1,0:T(8,128)(2,1)} custom-call(s32[2]{0:T(128)S(1)} %pad_add_fusion.where_ref, bf16[256,1536]{1,0:T(8,128)(2,1)S(1)} %constant_dynamic-slice_fusion.refs_0_.own_ref, bf16[128,1536]{1,0:T(8,128)(2,1)S(1)} %get-tuple-element.67.refs_0_, bf16[256,1536]{1,0:T(8,128)(2,1)S(1)} %get-tuple-element.81.refs_1_, ...), custom_call_target="tpu_custom_call" | custom-call | flops 1 | bytes 1 | tf_op jit(solution)/shard_map/layer/pallas_call | solution.py:291
  51.1 1.2 %collective-permute-done.21.refs_1_ = bf16[144,128]{1,0:T(8,128)(2,1)S(1)} collective-permute-done((bf16[144,128]{1,0:T(8,128)(2,1)S(1)}, bf16[144,128]{1,0:T(8,128)(2,1)S(1)}, u32[]{:S(2)}, u32[]{:S(2)}) %collective-permute-start.21) | collective-permute-done | bytes 36896 | tf_op jit(solution)/shard_map/ppermute | solution.py:334
  53.3 0.9 %collective-permute-done.24.refs_3_ = bf16[144,128]{1,0:T(8,128)(2,1)S(1)} collective-permute-done((bf16[144,128]{1,0:T(8,128)(2,1)S(1)}, bf16[144,128]{1,0:T(8,128)(2,1)S(1)}, u32[]{:S(2)}, u32[]{:S(2)}) %collective-permute-start.24) | collective-permute-done | bytes 36896 | tf_op jit(solution)/shard_map/ppermute | solution.py:328
  54.4 1.5 %outer_grad.1 = (bf16[256,256]{1,0:T(8,128)(2,1)}, bf16[256,256]{1,0:T(8,128)(2,1)}, bf16[256,256]{1,0:T(8,128)(2,1)}) custom-call(s32[2]{0:T(128)S(1)} %pad_add_fusion.where_ref, bf16[256,256]{1,0:T(8,128)(2,1)S(1)} %copy-done.1, bf16[256,256]{1,0:T(8,128)(2,1)S(1)} %copy-done.2, f32[256,512]{1,0:T(8,128)S(1)} %get-tuple-element.85.inner_ref, ...), custom_call_target="tpu_custom_call" | custom-call | flops 1 | bytes 1 | tf_op jit(solution)/shard_map/outer_grad/pallas_call | solution.py:291
  (57 shorter events, 9.4 us)
Async XLA Ops:
  0.7 4.4 %collective-permute-start = (bf16[256,256]{1,0:T(8,128)(2,1)}, bf16[256,256]{1,0:T(8,128)(2,1)S(1)}, u32[]{:S(2)}, u32[]{:S(2)}) collective-permute-start(bf16[256,256]{1,0:T(8,128)(2,1)} %q_ref.1), channel_id=1, source_target_pairs={{0,4},{4,0},{8,12},{12,8},{16,20},{20,16},{24,28},{28,24},{1,5},{5... | collective-permute-start | bytes 393224 | tf_op jit(solution)/shard_map/ppermute | solution.py:328
  1.2 3.9 %collective-permute-start.1 = (bf16[256,256]{1,0:T(8,128)(2,1)}, bf16[256,256]{1,0:T(8,128)(2,1)S(1)}, u32[]{:S(2)}, u32[]{:S(2)}) collective-permute-start(bf16[256,256]{1,0:T(8,128)(2,1)} %k_ref.3), channel_id=1, source_target_pairs={{0,4},{4,0},{8,12},{12,8},{16,20},{20,16},{24,28},{28,24},{1,5},{5... | collective-permute-start | bytes 393224 | tf_op jit(solution)/shard_map/ppermute | solution.py:328
  1.3 3.9 %collective-permute-start.2 = (bf16[256,256]{1,0:T(8,128)(2,1)}, bf16[256,256]{1,0:T(8,128)(2,1)S(1)}, u32[]{:S(2)}, u32[]{:S(2)}) collective-permute-start(bf16[256,256]{1,0:T(8,128)(2,1)} %v_ref.3), channel_id=1, source_target_pairs={{0,4},{4,0},{8,12},{12,8},{16,20},{20,16},{24,28},{28,24},{1,5},{5... | collective-permute-start | bytes 393224 | tf_op jit(solution)/shard_map/ppermute | solution.py:328
  1.7 3.4 %collective-permute-start.3 = (f32[2,256]{1,0:T(2,128)}, f32[2,256]{1,0:T(2,128)S(1)}, u32[]{:S(2)}, u32[]{:S(2)}) collective-permute-start(f32[2,256]{1,0:T(2,128)} %decay_ref.1), channel_id=1, source_target_pairs={{0,4},{4,0},{8,12},{12,8},{16,20},{20,16},{24,28},{28,24},{1,5},{5... | collective-permute-start | bytes 6152 | tf_op jit(solution)/shard_map/ppermute | solution.py:328
  5.2 5.9 %collective-permute-start.4 = (bf16[256,1536]{1,0:T(8,128)(2,1)S(1)}, bf16[256,1536]{1,0:T(8,128)(2,1)S(1)}, u32[]{:S(2)}, u32[]{:S(2)}) collective-permute-start(bf16[256,1536]{1,0:T(8,128)(2,1)S(1)} %copy-done), channel_id=1, source_target_pairs={{0,4},{4,0},{8,12},{12,8},{16,20},{20,16},{24,28},{28,24},{1,5},{5... | collective-permute-start | bytes 2359304 | tf_op jit(solution)/shard_map/ppermute | solution.py:328
  5.7 9.3 %collective-permute-start.5 = (bf16[64,1536]{1,0:T(8,128)(2,1)S(1)}, bf16[64,1536]{1,0:T(8,128)(2,1)S(1)}, u32[]{:S(2)}, u32[]{:S(2)}) collective-permute-start(bf16[64,1536]{1,0:T(8,128)(2,1)S(1)} %dynamic_slice.12), channel_id=1, source_target_pairs={{0,3},{1,2},{2,1},{3,0},{4,7},{5,6},{6,5},{7,4},{8,11},{9,10},{10,... | collective-permute-start | bytes 589832 | tf_op jit(solution)/shard_map/ppermute | solution.py:325
  9.2 17.6 %collective-permute-start.10 = (bf16[128,1536]{1,0:T(8,128)(2,1)S(1)}, bf16[128,1536]{1,0:T(8,128)(2,1)S(1)}, u32[]{:S(2)}, u32[]{:S(2)}) collective-permute-start(bf16[128,1536]{1,0:T(8,128)(2,1)S(1)} %get-tuple-element.94), channel_id=1, source_target_pairs={{0,2},{1,3},{2,0},{3,1},{4,6},{5,7},{6,4},{7,5},{8,10},{9,11},{10,... | collective-permute-start | bytes 1179656 | tf_op jit(solution)/shard_map/ppermute | solution.py:325
  9.7 17.1 %collective-permute-start.9 = (bf16[128,1536]{1,0:T(8,128)(2,1)S(1)}, bf16[128,1536]{1,0:T(8,128)(2,1)S(1)}, u32[]{:S(2)}, u32[]{:S(2)}) collective-permute-start(bf16[128,1536]{1,0:T(8,128)(2,1)S(1)} %get-tuple-element.95), channel_id=1, source_target_pairs={{0,1},{1,0},{2,3},{3,2},{4,5},{5,4},{6,7},{7,6},{8,9},{9,8},{10,11... | collective-permute-start | bytes 1179656 | tf_op jit(solution)/shard_map/ppermute | solution.py:325
  11.1 5.5 %collective-permute-start.6 = (bf16[144,128]{1,0:T(8,128)(2,1)S(1)}, bf16[144,128]{1,0:T(8,128)(2,1)S(1)}, u32[]{:S(2)}, u32[]{:S(2)}) collective-permute-start(bf16[144,128]{1,0:T(8,128)(2,1)S(1)} %get-tuple-element.56.refs_0_), channel_id=1, source_target_pairs={{0,8},{4,12},{8,16},{12,20},{16,24},{20,28},{1,9},{5,13},{9,17},{1... | collective-permute-start | bytes 110600 | tf_op jit(solution)/shard_map/ppermute | solution.py:334
  16.6 9.0 %collective-permute-start.7 = (bf16[64,1536]{1,0:T(8,128)(2,1)S(1)}, bf16[64,1536]{1,0:T(8,128)(2,1)S(1)}, u32[]{:S(2)}, u32[]{:S(2)}) collective-permute-start(bf16[64,1536]{1,0:T(8,128)(2,1)S(1)} %collective-permute-done.5.refs_1_), channel_id=1, source_target_pairs={{0,8},{4,12},{8,0},{12,4},{16,24},{20,28},{24,16},{28,20},{1,9},{5... | collective-permute-start | bytes 589832 | tf_op jit(solution)/shard_map/ppermute | solution.py:331
  19.5 6.1 %collective-permute-start.8 = (bf16[144,128]{1,0:T(8,128)(2,1)S(1)}, bf16[144,128]{1,0:T(8,128)(2,1)S(1)}, u32[]{:S(2)}, u32[]{:S(2)}) collective-permute-start(bf16[144,128]{1,0:T(8,128)(2,1)S(1)} %join.1), channel_id=1, source_target_pairs={{0,16},{4,20},{8,24},{12,28},{1,17},{5,21},{9,25},{13,29},{2,18},{... | collective-permute-start | bytes 110600 | tf_op jit(solution)/shard_map/ppermute | solution.py:334
  27.9 7.5 %collective-permute-start.13 = (bf16[2,256,128]{2,1,0:T(8,128)(2,1)S(1)}, bf16[2,256,128]{2,1,0:T(8,128)(2,1)S(1)}, u32[]{:S(2)}, u32[]{:S(2)}) collective-permute-start(bf16[2,256,128]{2,1,0:T(8,128)(2,1)S(1)} %get-tuple-element.73), channel_id=1, source_target_pairs={{0,1},{1,0},{2,3},{3,2},{4,5},{5,4},{6,7},{7,6},{8,9},{9,8},{10,11... | collective-permute-start | bytes 393224 | tf_op jit(solution)/shard_map/ppermute | solution.py:325
  29.5 11.1 %collective-permute-start.12 = (bf16[2,256,128]{2,1,0:T(8,128)(2,1)S(1)}, bf16[2,256,128]{2,1,0:T(8,128)(2,1)S(1)}, u32[]{:S(2)}, u32[]{:S(2)}) collective-permute-start(bf16[2,256,128]{2,1,0:T(8,128)(2,1)S(1)} %get-tuple-element.69), channel_id=1, source_target_pairs={{0,3},{1,2},{2,1},{3,0},{4,7},{5,6},{6,5},{7,4},{8,11},{9,10},{10,... | collective-permute-start | bytes 393224 | tf_op jit(solution)/shard_map/ppermute | solution.py:325
  31.0 9.6 %collective-permute-start.14 = (bf16[2,256,128]{2,1,0:T(8,128)(2,1)S(1)}, bf16[2,256,128]{2,1,0:T(8,128)(2,1)S(1)}, u32[]{:S(2)}, u32[]{:S(2)}) collective-permute-start(bf16[2,256,128]{2,1,0:T(8,128)(2,1)S(1)} %get-tuple-element.74), channel_id=1, source_target_pairs={{0,2},{1,3},{2,0},{3,1},{4,6},{5,7},{6,4},{7,5},{8,10},{9,11},{10,... | collective-permute-start | bytes 393224 | tf_op jit(solution)/shard_map/ppermute | solution.py:325
  32.4 9.3 %collective-permute-start.15 = (bf16[2,256,128]{2,1,0:T(8,128)(2,1)S(1)}, bf16[2,256,128]{2,1,0:T(8,128)(2,1)S(1)}, u32[]{:S(2)}, u32[]{:S(2)}) collective-permute-start(bf16[2,256,128]{2,1,0:T(8,128)(2,1)S(1)} %get-tuple-element.79.refs_0_.refs_4_), channel_id=1, source_target_pairs={{0,3},{1,2},{2,1},{3,0},{4,7},{5,6},{6,5},{7,4},{8,11},{9,10},{10,... | collective-permute-start | bytes 393224 | tf_op jit(solution)/shard_map/ppermute | solution.py:325
  34.9 6.8 %collective-permute-start.16 = (bf16[2,256,128]{2,1,0:T(8,128)(2,1)S(1)}, bf16[2,256,128]{2,1,0:T(8,128)(2,1)S(1)}, u32[]{:S(2)}, u32[]{:S(2)}) collective-permute-start(bf16[2,256,128]{2,1,0:T(8,128)(2,1)S(1)} %get-tuple-element.79.refs_0_.refs_4_), channel_id=1, source_target_pairs={{0,1},{1,0},{2,3},{3,2},{4,5},{5,4},{6,7},{7,6},{8,9},{9,8},{10,11... | collective-permute-start | bytes 393224 | tf_op jit(solution)/shard_map/ppermute | solution.py:325
  35.5 6.5 %collective-permute-start.17 = (bf16[2,256,128]{2,1,0:T(8,128)(2,1)S(1)}, bf16[2,256,128]{2,1,0:T(8,128)(2,1)S(1)}, u32[]{:S(2)}, u32[]{:S(2)}) collective-permute-start(bf16[2,256,128]{2,1,0:T(8,128)(2,1)S(1)} %get-tuple-element.79.refs_0_.refs_4_), channel_id=1, source_target_pairs={{0,2},{1,3},{2,0},{3,1},{4,6},{5,7},{6,4},{7,5},{8,10},{9,11},{10,... | collective-permute-start | bytes 393224 | tf_op jit(solution)/shard_map/ppermute | solution.py:325
  42.0 6.5 %collective-permute-start.18 = (bf16[256,1536]{1,0:T(8,128)(2,1)S(1)}, bf16[256,1536]{1,0:T(8,128)(2,1)S(1)}, u32[]{:S(2)}, u32[]{:S(2)}) collective-permute-start(bf16[256,1536]{1,0:T(8,128)(2,1)S(1)} %get-tuple-element.81.refs_1_), channel_id=1, source_target_pairs={{0,4},{4,0},{8,12},{12,8},{16,20},{20,16},{24,28},{28,24},{1,5},{5... | collective-permute-start | bytes 2359304 | tf_op jit(solution)/shard_map/ppermute | solution.py:328
  42.0 6.4 %collective-permute-start.11 = (bf16[128,1536]{1,0:T(8,128)(2,1)S(1)}, bf16[128,1536]{1,0:T(8,128)(2,1)S(1)}, u32[]{:S(2)}, u32[]{:S(2)}) collective-permute-start(bf16[128,1536]{1,0:T(8,128)(2,1)S(1)} %get-tuple-element.67.refs_0_), channel_id=1, source_target_pairs={{0,4},{4,0},{8,12},{12,8},{16,20},{20,16},{24,28},{28,24},{1,5},{5... | collective-permute-start | bytes 1179656 | tf_op jit(solution)/shard_map/ppermute | solution.py:328
  43.1 2.7 %collective-permute-start.19 = (bf16[4,256,128]{2,1,0:T(8,128)(2,1)S(1)}, bf16[4,256,128]{2,1,0:T(8,128)(2,1)S(1)}, u32[]{:S(2)}, u32[]{:S(2)}) collective-permute-start(bf16[4,256,128]{2,1,0:T(8,128)(2,1)S(1)} %cross.1), channel_id=1, source_target_pairs={{0,4},{4,0},{8,12},{12,8},{16,20},{20,16},{24,28},{28,24},{1,5},{5... | collective-permute-start | bytes 786440 | tf_op jit(solution)/shard_map/ppermute | solution.py:328
  43.2 7.9 %collective-permute-start.20 = (bf16[144,128]{1,0:T(8,128)(2,1)S(1)}, bf16[144,128]{1,0:T(8,128)(2,1)S(1)}, u32[]{:S(2)}, u32[]{:S(2)}) collective-permute-start(bf16[144,128]{1,0:T(8,128)(2,1)S(1)} %get-tuple-element.80), channel_id=1, source_target_pairs={{24,0},{28,4},{25,1},{29,5},{26,2},{30,6},{27,3},{31,7}} | collective-permute-start | bytes 110600 | tf_op jit(solution)/shard_map/ppermute | solution.py:334
  44.5 7.8 %collective-permute-start.21 = (bf16[144,128]{1,0:T(8,128)(2,1)S(1)}, bf16[144,128]{1,0:T(8,128)(2,1)S(1)}, u32[]{:S(2)}, u32[]{:S(2)}) collective-permute-start(bf16[144,128]{1,0:T(8,128)(2,1)S(1)} %get-tuple-element.80), channel_id=1, source_target_pairs={{16,0},{20,4},{24,8},{28,12},{17,1},{21,5},{25,9},{29,13},{18,2},{... | collective-permute-start | bytes 110600 | tf_op jit(solution)/shard_map/ppermute | solution.py:334
  45.8 6.5 %collective-permute-start.22 = (bf16[144,128]{1,0:T(8,128)(2,1)S(1)}, bf16[144,128]{1,0:T(8,128)(2,1)S(1)}, u32[]{:S(2)}, u32[]{:S(2)}) collective-permute-start(bf16[144,128]{1,0:T(8,128)(2,1)S(1)} %get-tuple-element.80), channel_id=1, source_target_pairs={{8,0},{12,4},{16,8},{20,12},{24,16},{28,20},{9,1},{13,5},{17,9},{2... | collective-permute-start | bytes 110600 | tf_op jit(solution)/shard_map/ppermute | solution.py:334
  52.3 2.1 %collective-permute-start.23 = (f32[256,512]{1,0:T(8,128)S(1)}, f32[256,512]{1,0:T(8,128)S(1)}, u32[]{:S(2)}, u32[]{:S(2)}) collective-permute-start(f32[256,512]{1,0:T(8,128)S(1)} %get-tuple-element.90), channel_id=1, source_target_pairs={{0,4},{4,0},{8,12},{12,8},{16,20},{20,16},{24,28},{28,24},{1,5},{5... | collective-permute-start | bytes 1572872 | tf_op jit(solution)/shard_map/ppermute | solution.py:328
  (9 other events, 67.0 us)

commit v15 on v13

--- a/solution.py
+++ b/solution.py
@@ -244,7 +244,7 @@
     for number, (early, late) in enumerate(zip(*parts)):
         part = slice(number * HD, (number + 1) * HD)
         keep_ref[:, part] = jnp.where(core == 0, early, late)
-        send_ref[:, part] = jnp.where(core == 0, late, early)
+        send_ref[:, part] = jnp.where(core == 0, late, early).astype(BF16)
 
 
 def outer_grad_kernel(count, where_ref, k_ref, v_ref, inner_ref, inner_got_ref, *refs):
@@ -255,12 +255,12 @@
         (1 - core, inner_got_ref, refs[count : 2 * count][::-1]),
     ):
         state = chip_sum(chip_refs).astype(BF16)
-        fade = inner[:, 3 * HD : 4 * HD]
+        fade = inner[:, 3 * HD : 4 * HD].astype(F32)
         k, v = k_ref[:, lanes_of(head)], v_ref[:, lanes_of(head)]
         outs[0][:, lanes_of(head)] = inner[:, 0:HD].astype(BF16)
-        key = inner[:, HD : 2 * HD] + fade * dot(v, state, NT)
+        key = inner[:, HD : 2 * HD].astype(F32) + fade * dot(v, state, NT)
         outs[1][:, lanes_of(head)] = key.astype(BF16)
-        value = inner[:, 2 * HD : 3 * HD] + fade * dot(k, state, NN)
+        value = inner[:, 2 * HD : 3 * HD].astype(F32) + fade * dot(k, state, NN)
         outs[2][:, lanes_of(head)] = value.astype(BF16)
 
 
@@ -421,7 +421,7 @@
     inner_keep, inner_send = call(
         inner_grad_kernel,
         "inner_grad",
-        [shape(F32, length, 4 * HD)] * 2,
+        [shape(F32, length, 4 * HD), shape(BF16, length, 4 * HD)],
         [where, q, k, v, col, row, grad_mixed, states, second],
     )
     (layer_out,) = call(

time: 56.2 us -> 58.2 us (1.036)
  waiting for transfers between devices: 9.51 us -> 11.1 us
    ppermute x5, waiting for transfers between devices: 3.57 us -> 5.84 us  [to_chip(): lax.ppermute(value, 'seq', [(i, i + 2 * step) for i in range(seq) if 0 <=...]
  transfers between devices with their start and end apart: 27 -> 27, of which waited for: 8 -> 9; matrix products, arithmetic and copies ran while one was open for 6% -> 6% of each run, Pallas kernels for 18% -> 18%
where the time goes in v15:
time: 58.2 us; the launch traced here: 57.9 us
  starting transfers between devices  29.5 us (51%)
  Pallas kernels  13 us (22%)
  waiting for transfers between devices  11.1 us (19%)
  local copies, waits for them, and re-layouts  3.34 us (6%)
  between operations  0.92 us (2%)
    pallas_call x11, Pallas kernels, call(): pl.pallas_call(kernel, name=name, out_shape=outs, in_specs=[SMEM] + [VMEM...  13 us
    ppermute x5, starting transfers between devices, to_chip(): lax.ppermute(value, 'seq', [(i, i + 2 * step) for i in range(seq) if 0 <=...  12.2 us
    ppermute x9, starting transfers between devices, swap_tensor(): return lax.ppermute(value, 'tensor', [(i, i ^ k) for i in range(tensor)])  11.7 us
    ppermute x5, waiting for transfers between devices, to_chip(): lax.ppermute(value, 'seq', [(i, i + 2 * step) for i in range(seq) if 0 <=...  5.84 us
    ppermute x9, waiting for transfers between devices, swap_tensor(): return lax.ppermute(value, 'tensor', [(i, i ^ k) for i in range(tensor)])  4.37 us
    ppermute x12, starting transfers between devices, swap_core(): return lax.ppermute(value, 'seq', [(i, i ^ 1) for i in range(seq)])  3.27 us
    ppermute x1, starting transfers between devices, swap_side(): return lax.ppermute(value, 'seq', [(i, i ^ 2) for i in range(seq)])  2.32 us
    dynamic_slice x2, local copies, waits for them, and re-layouts, slice_for(): lax.dynamic_slice(out_weight, (begin, (place ^ step) * width), (rows, wid...  2.12 us
  transfers between devices with their start and end apart: 27, of which 9 were waited for; matrix products, arithmetic and copies ran while one was open for 6% of the time, Pallas kernels for 18%

profile of v15, /device:TPU:0, one launch (start us, length us, event | category | flops | bytes accessed | tf_op | source)
XLA Modules:
  0.0 57.9 jit_solution(16534252426091989109)
XLA Ops:
  2.7 1.2 %fusion = (bf16[128,1536]{1,0:T(8,128)(2,1)S(1)}, bf16[128,1536]{1,0:T(8,128)(2,1)S(1)}) fusion(bf16[256,6144]{1,0:T(8,128)(2,1)} %param.12, s32[]{:T(128)S(6)} %select_n.27, s32[]{:T(128)S(6)} %select_n.29, s32[]{:T(128)S(6)} %select_n.28), kind=kLoop, calls=%fused_computation.2 | loop fusion | bytes 1572876 | tf_op jit(solution)/shard_map/dynamic_slice | solution.py:357
  3.9 1.2 %constant_dynamic-slice_fusion.refs_0_.own_ref = bf16[256,1536]{1,0:T(8,128)(2,1)S(1)} fusion(bf16[256,6144]{1,0:T(8,128)(2,1)} %param.12, s32[]{:T(128)S(6)} %select_n.30), kind=kLoop, calls=%fused_computation.1 | loop fusion | bytes 1572868 | tf_op jit(solution)/shard_map/dynamic_slice | solution.py:364
  5.7 3.5 %collective-permute-start.5 = (bf16[64,1536]{1,0:T(8,128)(2,1)S(1)}, bf16[64,1536]{1,0:T(8,128)(2,1)S(1)}, u32[]{:S(2)}, u32[]{:S(2)}) collective-permute-start(bf16[64,1536]{1,0:T(8,128)(2,1)S(1)} %dynamic_slice.12), channel_id=1, source_target_pairs={{0,3},{1,2},{2,1},{3,0},{4,7},{5,6},{6,5},{7,4},{8,11},{9,10},{10,... | collective-permute-start | bytes 589832 | tf_op jit(solution)/shard_map/ppermute | solution.py:326
  9.9 1.2 %fresh.1 = (bf16[2,256,128]{2,1,0:T(8,128)(2,1)S(1)}, bf16[2,256,128]{2,1,0:T(8,128)(2,1)S(1)}, bf16[2,256,128]{2,1,0:T(8,128)(2,1)S(1)}, f32[256,2]{1,0:T(8,128...) custom-call(s32[2]{0:T(128)S(1)} %pad_add_fusion.where_ref, ...), custom_call_target="tpu_custom_call" | custom-call | flops 1 | bytes 1 | tf_op jit(solution)/shard_map/fresh/pallas_call | solution.py:292
  11.1 3.9 %collective-permute-start.6 = (bf16[144,128]{1,0:T(8,128)(2,1)S(1)}, bf16[144,128]{1,0:T(8,128)(2,1)S(1)}, u32[]{:S(2)}, u32[]{:S(2)}) collective-permute-start(bf16[144,128]{1,0:T(8,128)(2,1)S(1)} %get-tuple-element.56.refs_0_), channel_id=1, source_target_pairs={{0,8},{4,12},{8,16},{12,20},{16,24},{20,28},{1,9},{5,13},{9,17},{1... | collective-permute-start | bytes 110600 | tf_op jit(solution)/shard_map/ppermute | solution.py:335
  15.0 1.6 %collective-permute-done.6.refs_1_.refs_0_ = bf16[144,128]{1,0:T(8,128)(2,1)S(1)} collective-permute-done((bf16[144,128]{1,0:T(8,128)(2,1)S(1)}, bf16[144,128]{1,0:T(8,128)(2,1)S(1)}, u32[]{:S(2)}, u32[]{:S(2)}) %collective-permute-start.6) | collective-permute-done | bytes 36896 | tf_op jit(solution)/shard_map/ppermute | solution.py:335
  16.6 2.3 %collective-permute-start.7 = (bf16[64,1536]{1,0:T(8,128)(2,1)S(1)}, bf16[64,1536]{1,0:T(8,128)(2,1)S(1)}, u32[]{:S(2)}, u32[]{:S(2)}) collective-permute-start(bf16[64,1536]{1,0:T(8,128)(2,1)S(1)} %collective-permute-done.5.refs_1_), channel_id=1, source_target_pairs={{0,8},{4,12},{8,0},{12,4},{16,24},{20,28},{24,16},{28,20},{1,9},{5... | collective-permute-start | bytes 589832 | tf_op jit(solution)/shard_map/ppermute | solution.py:332
  19.5 4.5 %collective-permute-start.8 = (bf16[144,128]{1,0:T(8,128)(2,1)S(1)}, bf16[144,128]{1,0:T(8,128)(2,1)S(1)}, u32[]{:S(2)}, u32[]{:S(2)}) collective-permute-start(bf16[144,128]{1,0:T(8,128)(2,1)S(1)} %join.1), channel_id=1, source_target_pairs={{0,16},{4,20},{8,24},{12,28},{1,17},{5,21},{9,25},{13,29},{2,18},{... | collective-permute-start | bytes 110600 | tf_op jit(solution)/shard_map/ppermute | solution.py:335
  25.6 1.1 %partial.2 = (f32[2,256,128]{2,1,0:T(8,128)S(1)}, bf16[2,256,128]{2,1,0:T(8,128)(2,1)S(1)}, bf16[128,1536]{1,0:T(8,128)(2,1)S(1)}) custom-call(s32[2]{0:T(128)S(1)} %pad_add_fusion.where_ref, bf16[256,1536]{1,0:T(8,128)(2,1)S(1)} %copy-done, bf16[256,1536]{1,0:T(8,128)(2,1)S(1)} %collective-permute-done.4.got_ref, ...), custom_call_target="tpu_custom_call" | custom-call | flops 1 | bytes 1 | tf_op jit(solution)/shard_map/partial/pallas_call | solution.py:292
  26.8 1.1 %partial.3 = (bf16[2,256,128]{2,1,0:T(8,128)(2,1)S(1)}, bf16[2,256,128]{2,1,0:T(8,128)(2,1)S(1)}, bf16[256,1536]{1,0:T(8,128)(2,1)S(1)}) custom-call(s32[2]{0:T(128)S(1)} %pad_add_fusion.where_ref, bf16[256,1536]{1,0:T(8,128)(2,1)S(1)} %copy-done, bf16[256,1536]{1,0:T(8,128)(2,1)S(1)} %collective-permute-done.4.got_ref, ...), custom_call_target="tpu_custom_call" | custom-call | flops 1 | bytes 1 | tf_op jit(solution)/shard_map/partial/pallas_call | solution.py:292
  27.9 1.6 %collective-permute-start.13 = (bf16[2,256,128]{2,1,0:T(8,128)(2,1)S(1)}, bf16[2,256,128]{2,1,0:T(8,128)(2,1)S(1)}, u32[]{:S(2)}, u32[]{:S(2)}) collective-permute-start(bf16[2,256,128]{2,1,0:T(8,128)(2,1)S(1)} %get-tuple-element.73), channel_id=1, source_target_pairs={{0,1},{1,0},{2,3},{3,2},{4,5},{5,4},{6,7},{7,6},{8,9},{9,8},{10,11... | collective-permute-start | bytes 393224 | tf_op jit(solution)/shard_map/ppermute | solution.py:326
  29.5 1.5 %collective-permute-start.12 = (bf16[2,256,128]{2,1,0:T(8,128)(2,1)S(1)}, bf16[2,256,128]{2,1,0:T(8,128)(2,1)S(1)}, u32[]{:S(2)}, u32[]{:S(2)}) collective-permute-start(bf16[2,256,128]{2,1,0:T(8,128)(2,1)S(1)} %get-tuple-element.69), channel_id=1, source_target_pairs={{0,3},{1,2},{2,1},{3,0},{4,7},{5,6},{6,5},{7,4},{8,11},{9,10},{10,... | collective-permute-start | bytes 393224 | tf_op jit(solution)/shard_map/ppermute | solution.py:326
  32.4 1.6 %collective-permute-start.17 = (bf16[2,256,128]{2,1,0:T(8,128)(2,1)S(1)}, bf16[2,256,128]{2,1,0:T(8,128)(2,1)S(1)}, u32[]{:S(2)}, u32[]{:S(2)}) collective-permute-start(bf16[2,256,128]{2,1,0:T(8,128)(2,1)S(1)} %get-tuple-element.79.refs_0_.refs_4_), channel_id=1, source_target_pairs={{0,2},{1,3},{2,0},{3,1},{4,6},{5,7},{6,4},{7,5},{8,10},{9,11},{10,... | collective-permute-start | bytes 393224 | tf_op jit(solution)/shard_map/ppermute | solution.py:326
  34.0 1.5 %collective-permute-start.16 = (bf16[2,256,128]{2,1,0:T(8,128)(2,1)S(1)}, bf16[2,256,128]{2,1,0:T(8,128)(2,1)S(1)}, u32[]{:S(2)}, u32[]{:S(2)}) collective-permute-start(bf16[2,256,128]{2,1,0:T(8,128)(2,1)S(1)} %get-tuple-element.79.refs_0_.refs_4_), channel_id=1, source_target_pairs={{0,1},{1,0},{2,3},{3,2},{4,5},{5,4},{6,7},{7,6},{8,9},{9,8},{10,11... | collective-permute-start | bytes 393224 | tf_op jit(solution)/shard_map/ppermute | solution.py:326
  36.4 2.7 %collective-permute-done.14.refs_2_ = bf16[2,256,128]{2,1,0:T(8,128)(2,1)S(1)} collective-permute-done((bf16[2,256,128]{2,1,0:T(8,128)(2,1)S(1)}, bf16[2,256,128]{2,1,0:T(8,128)(2,1)S(1)}, u32[]{:S(2)}, u32[]{:S(2)}) %collective-permute-start.14) | collective-permute-done | bytes 131104 | tf_op jit(solution)/shard_map/ppermute | solution.py:326
  39.1 1.2 %grad_mixed.1 = (f32[2,256,128]{2,1,0:T(8,128)S(1)}, f32[128,128]{1,0:T(8,128)S(1)}, bf16[144,128]{1,0:T(8,128)(2,1)S(1)}) custom-call(s32[2]{0:T(128)S(1)} %pad_add_fusion.where_ref, bf16[2,256,128]{2,1,0:T(8,128)(2,1)S(1)} %get-tuple-element.58.refs_0_.q_ref, f32[256,2]{1,0:T(8,128)S(1)} %get-tuple-element.61.refs_3_.col_ref, f32[1,256]{1,0:T(1,128)S(1)} %bitcast.4, ...), custom_call_target="tpu_custom_call" | custom-call | flops 1 | bytes 1 | tf_op jit(solution)/shard_map/grad_mixed/pallas_call | solution.py:292
  40.2 1.6 %collective-permute-done.17.refs_3_.refs_7_ = bf16[2,256,128]{2,1,0:T(8,128)(2,1)S(1)} collective-permute-done((bf16[2,256,128]{2,1,0:T(8,128)(2,1)S(1)}, bf16[2,256,128]{2,1,0:T(8,128)(2,1)S(1)}, u32[]{:S(2)}, u32[]{:S(2)}) %collective-permute-start.17) | collective-permute-done | bytes 131104 | tf_op jit(solution)/shard_map/ppermute | solution.py:326
  43.1 1.3 %collective-permute-start.22 = (bf16[144,128]{1,0:T(8,128)(2,1)S(1)}, bf16[144,128]{1,0:T(8,128)(2,1)S(1)}, u32[]{:S(2)}, u32[]{:S(2)}) collective-permute-start(bf16[144,128]{1,0:T(8,128)(2,1)S(1)} %get-tuple-element.80), channel_id=1, source_target_pairs={{8,0},{12,4},{16,8},{20,12},{24,16},{28,20},{9,1},{13,5},{17,9},{2... | collective-permute-start | bytes 110600 | tf_op jit(solution)/shard_map/ppermute | solution.py:335
  44.4 1.3 %collective-permute-start.21 = (bf16[144,128]{1,0:T(8,128)(2,1)S(1)}, bf16[144,128]{1,0:T(8,128)(2,1)S(1)}, u32[]{:S(2)}, u32[]{:S(2)}) collective-permute-start(bf16[144,128]{1,0:T(8,128)(2,1)S(1)} %get-tuple-element.80), channel_id=1, source_target_pairs={{16,0},{20,4},{24,8},{28,12},{17,1},{21,5},{25,9},{29,13},{18,2},{... | collective-permute-start | bytes 110600 | tf_op jit(solution)/shard_map/ppermute | solution.py:335
  45.7 1.3 %collective-permute-start.20 = (bf16[144,128]{1,0:T(8,128)(2,1)S(1)}, bf16[144,128]{1,0:T(8,128)(2,1)S(1)}, u32[]{:S(2)}, u32[]{:S(2)}) collective-permute-start(bf16[144,128]{1,0:T(8,128)(2,1)S(1)} %get-tuple-element.80), channel_id=1, source_target_pairs={{24,0},{28,4},{25,1},{29,5},{26,2},{30,6},{27,3},{31,7}} | collective-permute-start | bytes 110600 | tf_op jit(solution)/shard_map/ppermute | solution.py:335
  47.0 1.4 %inner_grad.1 = (f32[256,512]{1,0:T(8,128)S(1)}, bf16[256,512]{1,0:T(8,128)(2,1)S(1)}) custom-call(s32[2]{0:T(128)S(1)} %pad_add_fusion.where_ref, bf16[2,256,128]{2,1,0:T(8,128)(2,1)S(1)} %get-tuple-element.58.refs_0_.q_ref, bf16[2,256,128]{2,1,0:T(8,128)(2,1)S(1)} %get-tuple-element.59.refs_1_.k_ref, ...), custom_call_target="tpu_custom_call" | custom-call | flops 1 | bytes 1 | tf_op jit(solution)/shard_map/inner_grad/pallas_call | solution.py:292
  48.4 2.4 %layer.1 = bf16[256,1536]{1,0:T(8,128)(2,1)} custom-call(s32[2]{0:T(128)S(1)} %pad_add_fusion.where_ref, bf16[256,1536]{1,0:T(8,128)(2,1)S(1)} %constant_dynamic-slice_fusion.refs_0_.own_ref, bf16[128,1536]{1,0:T(8,128)(2,1)S(1)} %get-tuple-element.67.refs_0_, bf16[256,1536]{1,0:T(8,128)(2,1)S(1)} %get-tuple-element.81.refs_1_, ...), custom_call_target="tpu_custom_call" | custom-call | flops 1 | bytes 1 | tf_op jit(solution)/shard_map/layer/pallas_call | solution.py:292
  51.3 3.2 %collective-permute-done.20.refs_0_ = bf16[144,128]{1,0:T(8,128)(2,1)S(1)} collective-permute-done((bf16[144,128]{1,0:T(8,128)(2,1)S(1)}, bf16[144,128]{1,0:T(8,128)(2,1)S(1)}, u32[]{:S(2)}, u32[]{:S(2)}) %collective-permute-start.20) | collective-permute-done | bytes 36896 | tf_op jit(solution)/shard_map/ppermute | solution.py:335
  56.4 1.5 %outer_grad.1 = (bf16[256,256]{1,0:T(8,128)(2,1)}, bf16[256,256]{1,0:T(8,128)(2,1)}, bf16[256,256]{1,0:T(8,128)(2,1)}) custom-call(s32[2]{0:T(128)S(1)} %pad_add_fusion.where_ref, bf16[256,256]{1,0:T(8,128)(2,1)S(1)} %copy-done.1, bf16[256,256]{1,0:T(8,128)(2,1)S(1)} %copy-done.2, f32[256,512]{1,0:T(8,128)S(1)} %get-tuple-element.85.inner_ref, ...), custom_call_target="tpu_custom_call" | custom-call | flops 1 | bytes 1 | tf_op jit(solution)/shard_map/outer_grad/pallas_call | solution.py:292
  (57 shorter events, 11.3 us)
Async XLA Ops:
  0.7 4.4 %collective-permute-start.3 = (f32[2,256]{1,0:T(2,128)}, f32[2,256]{1,0:T(2,128)S(1)}, u32[]{:S(2)}, u32[]{:S(2)}) collective-permute-start(f32[2,256]{1,0:T(2,128)} %decay_ref.1), channel_id=1, source_target_pairs={{0,4},{4,0},{8,12},{12,8},{16,20},{20,16},{24,28},{28,24},{1,5},{5... | collective-permute-start | bytes 6152 | tf_op jit(solution)/shard_map/ppermute | solution.py:329
  1.2 3.9 %collective-permute-start = (bf16[256,256]{1,0:T(8,128)(2,1)}, bf16[256,256]{1,0:T(8,128)(2,1)S(1)}, u32[]{:S(2)}, u32[]{:S(2)}) collective-permute-start(bf16[256,256]{1,0:T(8,128)(2,1)} %q_ref.1), channel_id=1, source_target_pairs={{0,4},{4,0},{8,12},{12,8},{16,20},{20,16},{24,28},{28,24},{1,5},{5... | collective-permute-start | bytes 393224 | tf_op jit(solution)/shard_map/ppermute | solution.py:329
  1.3 3.9 %collective-permute-start.1 = (bf16[256,256]{1,0:T(8,128)(2,1)}, bf16[256,256]{1,0:T(8,128)(2,1)S(1)}, u32[]{:S(2)}, u32[]{:S(2)}) collective-permute-start(bf16[256,256]{1,0:T(8,128)(2,1)} %k_ref.3), channel_id=1, source_target_pairs={{0,4},{4,0},{8,12},{12,8},{16,20},{20,16},{24,28},{28,24},{1,5},{5... | collective-permute-start | bytes 393224 | tf_op jit(solution)/shard_map/ppermute | solution.py:329
  1.7 3.4 %collective-permute-start.2 = (bf16[256,256]{1,0:T(8,128)(2,1)}, bf16[256,256]{1,0:T(8,128)(2,1)S(1)}, u32[]{:S(2)}, u32[]{:S(2)}) collective-permute-start(bf16[256,256]{1,0:T(8,128)(2,1)} %v_ref.3), channel_id=1, source_target_pairs={{0,4},{4,0},{8,12},{12,8},{16,20},{20,16},{24,28},{28,24},{1,5},{5... | collective-permute-start | bytes 393224 | tf_op jit(solution)/shard_map/ppermute | solution.py:329
  5.2 5.9 %collective-permute-start.4 = (bf16[256,1536]{1,0:T(8,128)(2,1)S(1)}, bf16[256,1536]{1,0:T(8,128)(2,1)S(1)}, u32[]{:S(2)}, u32[]{:S(2)}) collective-permute-start(bf16[256,1536]{1,0:T(8,128)(2,1)S(1)} %copy-done), channel_id=1, source_target_pairs={{0,4},{4,0},{8,12},{12,8},{16,20},{20,16},{24,28},{28,24},{1,5},{5... | collective-permute-start | bytes 2359304 | tf_op jit(solution)/shard_map/ppermute | solution.py:329
  5.7 9.3 %collective-permute-start.5 = (bf16[64,1536]{1,0:T(8,128)(2,1)S(1)}, bf16[64,1536]{1,0:T(8,128)(2,1)S(1)}, u32[]{:S(2)}, u32[]{:S(2)}) collective-permute-start(bf16[64,1536]{1,0:T(8,128)(2,1)S(1)} %dynamic_slice.12), channel_id=1, source_target_pairs={{0,3},{1,2},{2,1},{3,0},{4,7},{5,6},{6,5},{7,4},{8,11},{9,10},{10,... | collective-permute-start | bytes 589832 | tf_op jit(solution)/shard_map/ppermute | solution.py:326
  9.2 17.6 %collective-permute-start.10 = (bf16[128,1536]{1,0:T(8,128)(2,1)S(1)}, bf16[128,1536]{1,0:T(8,128)(2,1)S(1)}, u32[]{:S(2)}, u32[]{:S(2)}) collective-permute-start(bf16[128,1536]{1,0:T(8,128)(2,1)S(1)} %get-tuple-element.94), channel_id=1, source_target_pairs={{0,2},{1,3},{2,0},{3,1},{4,6},{5,7},{6,4},{7,5},{8,10},{9,11},{10,... | collective-permute-start | bytes 1179656 | tf_op jit(solution)/shard_map/ppermute | solution.py:326
  9.7 17.1 %collective-permute-start.9 = (bf16[128,1536]{1,0:T(8,128)(2,1)S(1)}, bf16[128,1536]{1,0:T(8,128)(2,1)S(1)}, u32[]{:S(2)}, u32[]{:S(2)}) collective-permute-start(bf16[128,1536]{1,0:T(8,128)(2,1)S(1)} %get-tuple-element.95), channel_id=1, source_target_pairs={{0,1},{1,0},{2,3},{3,2},{4,5},{5,4},{6,7},{7,6},{8,9},{9,8},{10,11... | collective-permute-start | bytes 1179656 | tf_op jit(solution)/shard_map/ppermute | solution.py:326
  11.1 5.5 %collective-permute-start.6 = (bf16[144,128]{1,0:T(8,128)(2,1)S(1)}, bf16[144,128]{1,0:T(8,128)(2,1)S(1)}, u32[]{:S(2)}, u32[]{:S(2)}) collective-permute-start(bf16[144,128]{1,0:T(8,128)(2,1)S(1)} %get-tuple-element.56.refs_0_), channel_id=1, source_target_pairs={{0,8},{4,12},{8,16},{12,20},{16,24},{20,28},{1,9},{5,13},{9,17},{1... | collective-permute-start | bytes 110600 | tf_op jit(solution)/shard_map/ppermute | solution.py:335
  16.6 9.0 %collective-permute-start.7 = (bf16[64,1536]{1,0:T(8,128)(2,1)S(1)}, bf16[64,1536]{1,0:T(8,128)(2,1)S(1)}, u32[]{:S(2)}, u32[]{:S(2)}) collective-permute-start(bf16[64,1536]{1,0:T(8,128)(2,1)S(1)} %collective-permute-done.5.refs_1_), channel_id=1, source_target_pairs={{0,8},{4,12},{8,0},{12,4},{16,24},{20,28},{24,16},{28,20},{1,9},{5... | collective-permute-start | bytes 589832 | tf_op jit(solution)/shard_map/ppermute | solution.py:332
  19.5 6.1 %collective-permute-start.8 = (bf16[144,128]{1,0:T(8,128)(2,1)S(1)}, bf16[144,128]{1,0:T(8,128)(2,1)S(1)}, u32[]{:S(2)}, u32[]{:S(2)}) collective-permute-start(bf16[144,128]{1,0:T(8,128)(2,1)S(1)} %join.1), channel_id=1, source_target_pairs={{0,16},{4,20},{8,24},{12,28},{1,17},{5,21},{9,25},{13,29},{2,18},{... | collective-permute-start | bytes 110600 | tf_op jit(solution)/shard_map/ppermute | solution.py:335
  27.9 7.6 %collective-permute-start.13 = (bf16[2,256,128]{2,1,0:T(8,128)(2,1)S(1)}, bf16[2,256,128]{2,1,0:T(8,128)(2,1)S(1)}, u32[]{:S(2)}, u32[]{:S(2)}) collective-permute-start(bf16[2,256,128]{2,1,0:T(8,128)(2,1)S(1)} %get-tuple-element.73), channel_id=1, source_target_pairs={{0,1},{1,0},{2,3},{3,2},{4,5},{5,4},{6,7},{7,6},{8,9},{9,8},{10,11... | collective-permute-start | bytes 393224 | tf_op jit(solution)/shard_map/ppermute | solution.py:326
  29.5 9.6 %collective-permute-start.12 = (bf16[2,256,128]{2,1,0:T(8,128)(2,1)S(1)}, bf16[2,256,128]{2,1,0:T(8,128)(2,1)S(1)}, u32[]{:S(2)}, u32[]{:S(2)}) collective-permute-start(bf16[2,256,128]{2,1,0:T(8,128)(2,1)S(1)} %get-tuple-element.69), channel_id=1, source_target_pairs={{0,3},{1,2},{2,1},{3,0},{4,7},{5,6},{6,5},{7,4},{8,11},{9,10},{10,... | collective-permute-start | bytes 393224 | tf_op jit(solution)/shard_map/ppermute | solution.py:326
  31.0 8.1 %collective-permute-start.14 = (bf16[2,256,128]{2,1,0:T(8,128)(2,1)S(1)}, bf16[2,256,128]{2,1,0:T(8,128)(2,1)S(1)}, u32[]{:S(2)}, u32[]{:S(2)}) collective-permute-start(bf16[2,256,128]{2,1,0:T(8,128)(2,1)S(1)} %get-tuple-element.74), channel_id=1, source_target_pairs={{0,2},{1,3},{2,0},{3,1},{4,6},{5,7},{6,4},{7,5},{8,10},{9,11},{10,... | collective-permute-start | bytes 393224 | tf_op jit(solution)/shard_map/ppermute | solution.py:326
  32.4 9.5 %collective-permute-start.17 = (bf16[2,256,128]{2,1,0:T(8,128)(2,1)S(1)}, bf16[2,256,128]{2,1,0:T(8,128)(2,1)S(1)}, u32[]{:S(2)}, u32[]{:S(2)}) collective-permute-start(bf16[2,256,128]{2,1,0:T(8,128)(2,1)S(1)} %get-tuple-element.79.refs_0_.refs_4_), channel_id=1, source_target_pairs={{0,2},{1,3},{2,0},{3,1},{4,6},{5,7},{6,4},{7,5},{8,10},{9,11},{10,... | collective-permute-start | bytes 393224 | tf_op jit(solution)/shard_map/ppermute | solution.py:326
  34.0 7.9 %collective-permute-start.16 = (bf16[2,256,128]{2,1,0:T(8,128)(2,1)S(1)}, bf16[2,256,128]{2,1,0:T(8,128)(2,1)S(1)}, u32[]{:S(2)}, u32[]{:S(2)}) collective-permute-start(bf16[2,256,128]{2,1,0:T(8,128)(2,1)S(1)} %get-tuple-element.79.refs_0_.refs_4_), channel_id=1, source_target_pairs={{0,1},{1,0},{2,3},{3,2},{4,5},{5,4},{6,7},{7,6},{8,9},{9,8},{10,11... | collective-permute-start | bytes 393224 | tf_op jit(solution)/shard_map/ppermute | solution.py:326
  35.5 6.4 %collective-permute-start.15 = (bf16[2,256,128]{2,1,0:T(8,128)(2,1)S(1)}, bf16[2,256,128]{2,1,0:T(8,128)(2,1)S(1)}, u32[]{:S(2)}, u32[]{:S(2)}) collective-permute-start(bf16[2,256,128]{2,1,0:T(8,128)(2,1)S(1)} %get-tuple-element.79.refs_0_.refs_4_), channel_id=1, source_target_pairs={{0,3},{1,2},{2,1},{3,0},{4,7},{5,6},{6,5},{7,4},{8,11},{9,10},{10,... | collective-permute-start | bytes 393224 | tf_op jit(solution)/shard_map/ppermute | solution.py:326
  41.9 6.5 %collective-permute-start.18 = (bf16[256,1536]{1,0:T(8,128)(2,1)S(1)}, bf16[256,1536]{1,0:T(8,128)(2,1)S(1)}, u32[]{:S(2)}, u32[]{:S(2)}) collective-permute-start(bf16[256,1536]{1,0:T(8,128)(2,1)S(1)} %get-tuple-element.81.refs_1_), channel_id=1, source_target_pairs={{0,4},{4,0},{8,12},{12,8},{16,20},{20,16},{24,28},{28,24},{1,5},{5... | collective-permute-start | bytes 2359304 | tf_op jit(solution)/shard_map/ppermute | solution.py:329
  41.9 6.5 %collective-permute-start.11 = (bf16[128,1536]{1,0:T(8,128)(2,1)S(1)}, bf16[128,1536]{1,0:T(8,128)(2,1)S(1)}, u32[]{:S(2)}, u32[]{:S(2)}) collective-permute-start(bf16[128,1536]{1,0:T(8,128)(2,1)S(1)} %get-tuple-element.67.refs_0_), channel_id=1, source_target_pairs={{0,4},{4,0},{8,12},{12,8},{16,20},{20,16},{24,28},{28,24},{1,5},{5... | collective-permute-start | bytes 1179656 | tf_op jit(solution)/shard_map/ppermute | solution.py:329
  43.0 2.7 %collective-permute-start.19 = (bf16[4,256,128]{2,1,0:T(8,128)(2,1)S(1)}, bf16[4,256,128]{2,1,0:T(8,128)(2,1)S(1)}, u32[]{:S(2)}, u32[]{:S(2)}) collective-permute-start(bf16[4,256,128]{2,1,0:T(8,128)(2,1)S(1)} %cross.1), channel_id=1, source_target_pairs={{0,4},{4,0},{8,12},{12,8},{16,20},{20,16},{24,28},{28,24},{1,5},{5... | collective-permute-start | bytes 786440 | tf_op jit(solution)/shard_map/ppermute | solution.py:329
  43.1 7.7 %collective-permute-start.22 = (bf16[144,128]{1,0:T(8,128)(2,1)S(1)}, bf16[144,128]{1,0:T(8,128)(2,1)S(1)}, u32[]{:S(2)}, u32[]{:S(2)}) collective-permute-start(bf16[144,128]{1,0:T(8,128)(2,1)S(1)} %get-tuple-element.80), channel_id=1, source_target_pairs={{8,0},{12,4},{16,8},{20,12},{24,16},{28,20},{9,1},{13,5},{17,9},{2... | collective-permute-start | bytes 110600 | tf_op jit(solution)/shard_map/ppermute | solution.py:335
  44.4 6.9 %collective-permute-start.21 = (bf16[144,128]{1,0:T(8,128)(2,1)S(1)}, bf16[144,128]{1,0:T(8,128)(2,1)S(1)}, u32[]{:S(2)}, u32[]{:S(2)}) collective-permute-start(bf16[144,128]{1,0:T(8,128)(2,1)S(1)} %get-tuple-element.80), channel_id=1, source_target_pairs={{16,0},{20,4},{24,8},{28,12},{17,1},{21,5},{25,9},{29,13},{18,2},{... | collective-permute-start | bytes 110600 | tf_op jit(solution)/shard_map/ppermute | solution.py:335
  45.7 8.8 %collective-permute-start.20 = (bf16[144,128]{1,0:T(8,128)(2,1)S(1)}, bf16[144,128]{1,0:T(8,128)(2,1)S(1)}, u32[]{:S(2)}, u32[]{:S(2)}) collective-permute-start(bf16[144,128]{1,0:T(8,128)(2,1)S(1)} %get-tuple-element.80), channel_id=1, source_target_pairs={{24,0},{28,4},{25,1},{29,5},{26,2},{30,6},{27,3},{31,7}} | collective-permute-start | bytes 110600 | tf_op jit(solution)/shard_map/ppermute | solution.py:335
  54.5 1.9 %collective-permute-start.23 = (bf16[256,512]{1,0:T(8,128)(2,1)S(1)}, bf16[256,512]{1,0:T(8,128)(2,1)S(1)}, u32[]{:S(2)}, u32[]{:S(2)}) collective-permute-start(bf16[256,512]{1,0:T(8,128)(2,1)S(1)} %get-tuple-element.90), channel_id=1, source_target_pairs={{0,4},{4,0},{8,12},{12,8},{16,20},{20,16},{24,28},{28,24},{1,5},{5... | collective-permute-start | bytes 786440 | tf_op jit(solution)/shard_map/ppermute | solution.py:329
  (9 other events, 66.1 us)

commit v16 on v13

--- a/solution.py
+++ b/solution.py
@@ -275,7 +275,7 @@
         normed += mine[begin : begin + 2] + theirs[begin : begin + 2]
     normed = jnp.concatenate(normed, axis=1)
     width = own_ref.shape[1]
-    step = 512 if width % 512 == 0 else 128
+    step = 768 if width % 768 == 0 else 128
     for begin in range(0, width, step):
         lanes = slice(begin, begin + step)
         weight = [own_ref[rows_of(core, HD), lanes], own_ref[rows_of(1 - core, HD), lanes]]

time: 56.2 us -> 56.2 us (level)
  no operation moved by 1% of the time
where the time goes in v16:
time: 56.2 us; the launch traced here: 55.9 us
  starting transfers between devices  29 us (52%)
  Pallas kernels  13 us (23%)
  waiting for transfers between devices  9.51 us (17%)
  local copies, waits for them, and re-layouts  3.34 us (6%)
  between operations  0.93 us (2%)
    pallas_call x11, Pallas kernels, call(): pl.pallas_call(kernel, name=name, out_shape=outs, in_specs=[SMEM] + [VMEM...  13 us
    ppermute x5, starting transfers between devices, to_chip(): lax.ppermute(value, 'seq', [(i, i + 2 * step) for i in range(seq) if 0 <=...  12.3 us
    ppermute x9, starting transfers between devices, swap_tensor(): return lax.ppermute(value, 'tensor', [(i, i ^ k) for i in range(tensor)])  11.3 us
    ppermute x9, waiting for transfers between devices, swap_tensor(): return lax.ppermute(value, 'tensor', [(i, i ^ k) for i in range(tensor)])  4.86 us
    ppermute x5, waiting for transfers between devices, to_chip(): lax.ppermute(value, 'seq', [(i, i + 2 * step) for i in range(seq) if 0 <=...  3.57 us
    ppermute x12, starting transfers between devices, swap_core(): return lax.ppermute(value, 'seq', [(i, i ^ 1) for i in range(seq)])  3.21 us
    ppermute x1, starting transfers between devices, swap_side(): return lax.ppermute(value, 'seq', [(i, i ^ 2) for i in range(seq)])  2.32 us
    dynamic_slice x2, local copies, waits for them, and re-layouts, slice_for(): lax.dynamic_slice(out_weight, (begin, (place ^ step) * width), (rows, wid...  2.12 us
  transfers between devices with their start and end apart: 27, of which 8 were waited for; matrix products, arithmetic and copies ran while one was open for 6% of the time, Pallas kernels for 18%

profile of v16, /device:TPU:0, one launch (start us, length us, event | category | flops | bytes accessed | tf_op | source)
XLA Modules:
  0.0 55.9 jit_solution(14153613781739791404)
XLA Ops:
  2.7 1.2 %fusion = (bf16[128,1536]{1,0:T(8,128)(2,1)S(1)}, bf16[128,1536]{1,0:T(8,128)(2,1)S(1)}) fusion(bf16[256,6144]{1,0:T(8,128)(2,1)} %param.12, s32[]{:T(128)S(6)} %select_n.27, s32[]{:T(128)S(6)} %select_n.29, s32[]{:T(128)S(6)} %select_n.28), kind=kLoop, calls=%fused_computation.2 | loop fusion | bytes 1572876 | tf_op jit(solution)/shard_map/dynamic_slice | solution.py:357
  3.9 1.2 %constant_dynamic-slice_fusion.refs_0_.own_ref = bf16[256,1536]{1,0:T(8,128)(2,1)S(1)} fusion(bf16[256,6144]{1,0:T(8,128)(2,1)} %param.12, s32[]{:T(128)S(6)} %select_n.30), kind=kLoop, calls=%fused_computation.1 | loop fusion | bytes 1572868 | tf_op jit(solution)/shard_map/dynamic_slice | solution.py:364
  5.7 3.5 %collective-permute-start.5 = (bf16[64,1536]{1,0:T(8,128)(2,1)S(1)}, bf16[64,1536]{1,0:T(8,128)(2,1)S(1)}, u32[]{:S(2)}, u32[]{:S(2)}) collective-permute-start(bf16[64,1536]{1,0:T(8,128)(2,1)S(1)} %dynamic_slice.12), channel_id=1, source_target_pairs={{0,3},{1,2},{2,1},{3,0},{4,7},{5,6},{6,5},{7,4},{8,11},{9,10},{10,... | collective-permute-start | bytes 589832 | tf_op jit(solution)/shard_map/ppermute | solution.py:326
  9.9 1.2 %fresh.1 = (bf16[2,256,128]{2,1,0:T(8,128)(2,1)S(1)}, bf16[2,256,128]{2,1,0:T(8,128)(2,1)S(1)}, bf16[2,256,128]{2,1,0:T(8,128)(2,1)S(1)}, f32[256,2]{1,0:T(8,128...) custom-call(s32[2]{0:T(128)S(1)} %pad_add_fusion.where_ref, ...), custom_call_target="tpu_custom_call" | custom-call | flops 1 | bytes 1 | tf_op jit(solution)/shard_map/fresh/pallas_call | solution.py:292
  11.1 3.9 %collective-permute-start.6 = (bf16[144,128]{1,0:T(8,128)(2,1)S(1)}, bf16[144,128]{1,0:T(8,128)(2,1)S(1)}, u32[]{:S(2)}, u32[]{:S(2)}) collective-permute-start(bf16[144,128]{1,0:T(8,128)(2,1)S(1)} %get-tuple-element.56.refs_0_), channel_id=1, source_target_pairs={{0,8},{4,12},{8,16},{12,20},{16,24},{20,28},{1,9},{5,13},{9,17},{1... | collective-permute-start | bytes 110600 | tf_op jit(solution)/shard_map/ppermute | solution.py:335
  15.0 1.6 %collective-permute-done.6.refs_1_.refs_0_ = bf16[144,128]{1,0:T(8,128)(2,1)S(1)} collective-permute-done((bf16[144,128]{1,0:T(8,128)(2,1)S(1)}, bf16[144,128]{1,0:T(8,128)(2,1)S(1)}, u32[]{:S(2)}, u32[]{:S(2)}) %collective-permute-start.6) | collective-permute-done | bytes 36896 | tf_op jit(solution)/shard_map/ppermute | solution.py:335
  16.6 2.3 %collective-permute-start.7 = (bf16[64,1536]{1,0:T(8,128)(2,1)S(1)}, bf16[64,1536]{1,0:T(8,128)(2,1)S(1)}, u32[]{:S(2)}, u32[]{:S(2)}) collective-permute-start(bf16[64,1536]{1,0:T(8,128)(2,1)S(1)} %collective-permute-done.5.refs_1_), channel_id=1, source_target_pairs={{0,8},{4,12},{8,0},{12,4},{16,24},{20,28},{24,16},{28,20},{1,9},{5... | collective-permute-start | bytes 589832 | tf_op jit(solution)/shard_map/ppermute | solution.py:332
  19.5 4.5 %collective-permute-start.8 = (bf16[144,128]{1,0:T(8,128)(2,1)S(1)}, bf16[144,128]{1,0:T(8,128)(2,1)S(1)}, u32[]{:S(2)}, u32[]{:S(2)}) collective-permute-start(bf16[144,128]{1,0:T(8,128)(2,1)S(1)} %join.1), channel_id=1, source_target_pairs={{0,16},{4,20},{8,24},{12,28},{1,17},{5,21},{9,25},{13,29},{2,18},{... | collective-permute-start | bytes 110600 | tf_op jit(solution)/shard_map/ppermute | solution.py:335
  24.0 1.1 %inner.1.inner_ref = f32[2,256,128]{2,1,0:T(8,128)S(1)} custom-call(s32[2]{0:T(128)S(1)} %pad_add_fusion.where_ref, bf16[2,256,128]{2,1,0:T(8,128)(2,1)S(1)} %get-tuple-element.58.refs_0_.q_ref, bf16[2,256,128]{2,1,0:T(8,128)(2,1)S(1)} %get-tuple-element.59.refs_1_.k_ref, bf16[2,256,128]{2,1,0:T(8,128)(2,1)S(1)} %get-tuple-element.60.refs_2_.v_ref, ...), custom_call_target="tpu_custom_call" | custom-call | flops 1 | bytes 1 | tf_op jit(solution)/shard_map/inner/pallas_call | solution.py:292
  25.6 1.1 %partial.2 = (f32[2,256,128]{2,1,0:T(8,128)S(1)}, bf16[2,256,128]{2,1,0:T(8,128)(2,1)S(1)}, bf16[128,1536]{1,0:T(8,128)(2,1)S(1)}) custom-call(s32[2]{0:T(128)S(1)} %pad_add_fusion.where_ref, bf16[256,1536]{1,0:T(8,128)(2,1)S(1)} %copy-done, bf16[256,1536]{1,0:T(8,128)(2,1)S(1)} %collective-permute-done.4.got_ref, ...), custom_call_target="tpu_custom_call" | custom-call | flops 1 | bytes 1 | tf_op jit(solution)/shard_map/partial/pallas_call | solution.py:292
  26.8 1.1 %partial.3 = (bf16[2,256,128]{2,1,0:T(8,128)(2,1)S(1)}, bf16[2,256,128]{2,1,0:T(8,128)(2,1)S(1)}, bf16[256,1536]{1,0:T(8,128)(2,1)S(1)}) custom-call(s32[2]{0:T(128)S(1)} %pad_add_fusion.where_ref, bf16[256,1536]{1,0:T(8,128)(2,1)S(1)} %copy-done, bf16[256,1536]{1,0:T(8,128)(2,1)S(1)} %collective-permute-done.4.got_ref, ...), custom_call_target="tpu_custom_call" | custom-call | flops 1 | bytes 1 | tf_op jit(solution)/shard_map/partial/pallas_call | solution.py:292
  27.9 1.6 %collective-permute-start.13 = (bf16[2,256,128]{2,1,0:T(8,128)(2,1)S(1)}, bf16[2,256,128]{2,1,0:T(8,128)(2,1)S(1)}, u32[]{:S(2)}, u32[]{:S(2)}) collective-permute-start(bf16[2,256,128]{2,1,0:T(8,128)(2,1)S(1)} %get-tuple-element.73), channel_id=1, source_target_pairs={{0,1},{1,0},{2,3},{3,2},{4,5},{5,4},{6,7},{7,6},{8,9},{9,8},{10,11... | collective-permute-start | bytes 393224 | tf_op jit(solution)/shard_map/ppermute | solution.py:326
  29.5 1.5 %collective-permute-start.12 = (bf16[2,256,128]{2,1,0:T(8,128)(2,1)S(1)}, bf16[2,256,128]{2,1,0:T(8,128)(2,1)S(1)}, u32[]{:S(2)}, u32[]{:S(2)}) collective-permute-start(bf16[2,256,128]{2,1,0:T(8,128)(2,1)S(1)} %get-tuple-element.69), channel_id=1, source_target_pairs={{0,3},{1,2},{2,1},{3,0},{4,7},{5,6},{6,5},{7,4},{8,11},{9,10},{10,... | collective-permute-start | bytes 393224 | tf_op jit(solution)/shard_map/ppermute | solution.py:326
  32.4 2.5 %collective-permute-start.15 = (bf16[2,256,128]{2,1,0:T(8,128)(2,1)S(1)}, bf16[2,256,128]{2,1,0:T(8,128)(2,1)S(1)}, u32[]{:S(2)}, u32[]{:S(2)}) collective-permute-start(bf16[2,256,128]{2,1,0:T(8,128)(2,1)S(1)} %get-tuple-element.79.refs_0_.refs_4_), channel_id=1, source_target_pairs={{0,3},{1,2},{2,1},{3,0},{4,7},{5,6},{6,5},{7,4},{8,11},{9,10},{10,... | collective-permute-start | bytes 393224 | tf_op jit(solution)/shard_map/ppermute | solution.py:326
  36.0 4.6 %collective-permute-done.14.refs_2_ = bf16[2,256,128]{2,1,0:T(8,128)(2,1)S(1)} collective-permute-done((bf16[2,256,128]{2,1,0:T(8,128)(2,1)S(1)}, bf16[2,256,128]{2,1,0:T(8,128)(2,1)S(1)}, u32[]{:S(2)}, u32[]{:S(2)}) %collective-permute-start.14) | collective-permute-done | bytes 131104 | tf_op jit(solution)/shard_map/ppermute | solution.py:326
  40.6 1.2 %grad_mixed.1 = (f32[2,256,128]{2,1,0:T(8,128)S(1)}, f32[128,128]{1,0:T(8,128)S(1)}, bf16[144,128]{1,0:T(8,128)(2,1)S(1)}) custom-call(s32[2]{0:T(128)S(1)} %pad_add_fusion.where_ref, bf16[2,256,128]{2,1,0:T(8,128)(2,1)S(1)} %get-tuple-element.58.refs_0_.q_ref, f32[256,2]{1,0:T(8,128)S(1)} %get-tuple-element.61.refs_3_.col_ref, f32[1,256]{1,0:T(1,128)S(1)} %bitcast.4, ...), custom_call_target="tpu_custom_call" | custom-call | flops 1 | bytes 1 | tf_op jit(solution)/shard_map/grad_mixed/pallas_call | solution.py:292
  43.2 1.3 %collective-permute-start.20 = (bf16[144,128]{1,0:T(8,128)(2,1)S(1)}, bf16[144,128]{1,0:T(8,128)(2,1)S(1)}, u32[]{:S(2)}, u32[]{:S(2)}) collective-permute-start(bf16[144,128]{1,0:T(8,128)(2,1)S(1)} %get-tuple-element.80), channel_id=1, source_target_pairs={{24,0},{28,4},{25,1},{29,5},{26,2},{30,6},{27,3},{31,7}} | collective-permute-start | bytes 110600 | tf_op jit(solution)/shard_map/ppermute | solution.py:335
  44.5 1.3 %collective-permute-start.21 = (bf16[144,128]{1,0:T(8,128)(2,1)S(1)}, bf16[144,128]{1,0:T(8,128)(2,1)S(1)}, u32[]{:S(2)}, u32[]{:S(2)}) collective-permute-start(bf16[144,128]{1,0:T(8,128)(2,1)S(1)} %get-tuple-element.80), channel_id=1, source_target_pairs={{16,0},{20,4},{24,8},{28,12},{17,1},{21,5},{25,9},{29,13},{18,2},{... | collective-permute-start | bytes 110600 | tf_op jit(solution)/shard_map/ppermute | solution.py:335
  45.8 1.3 %collective-permute-start.22 = (bf16[144,128]{1,0:T(8,128)(2,1)S(1)}, bf16[144,128]{1,0:T(8,128)(2,1)S(1)}, u32[]{:S(2)}, u32[]{:S(2)}) collective-permute-start(bf16[144,128]{1,0:T(8,128)(2,1)S(1)} %get-tuple-element.80), channel_id=1, source_target_pairs={{8,0},{12,4},{16,8},{20,12},{24,16},{28,20},{9,1},{13,5},{17,9},{2... | collective-permute-start | bytes 110600 | tf_op jit(solution)/shard_map/ppermute | solution.py:335
  47.1 1.4 %inner_grad.1 = (f32[256,512]{1,0:T(8,128)S(1)}, f32[256,512]{1,0:T(8,128)S(1)}) custom-call(s32[2]{0:T(128)S(1)} %pad_add_fusion.where_ref, bf16[2,256,128]{2,1,0:T(8,128)(2,1)S(1)} %get-tuple-element.58.refs_0_.q_ref, bf16[2,256,128]{2,1,0:T(8,128)(2,1)S(1)} %get-tuple-element.59.refs_1_.k_ref, bf16[2,256,128]{2,1,0:T(8,128)(2,1)S(1)} %get-tuple-element.60.refs_2_.v_ref, ...), custom_call_target="tpu_custom_call" | custom-call | flops 1 | bytes 1 | tf_op jit(solution)/shard_map/inner_grad/pallas_call | solution.py:292
  48.5 2.4 %layer.1 = bf16[256,1536]{1,0:T(8,128)(2,1)} custom-call(s32[2]{0:T(128)S(1)} %pad_add_fusion.where_ref, bf16[256,1536]{1,0:T(8,128)(2,1)S(1)} %constant_dynamic-slice_fusion.refs_0_.own_ref, bf16[128,1536]{1,0:T(8,128)(2,1)S(1)} %get-tuple-element.67.refs_0_, bf16[256,1536]{1,0:T(8,128)(2,1)S(1)} %get-tuple-element.81.refs_1_, ...), custom_call_target="tpu_custom_call" | custom-call | flops 1 | bytes 1 | tf_op jit(solution)/shard_map/layer/pallas_call | solution.py:292
  50.9 1.4 %collective-permute-done.21.refs_1_ = bf16[144,128]{1,0:T(8,128)(2,1)S(1)} collective-permute-done((bf16[144,128]{1,0:T(8,128)(2,1)S(1)}, bf16[144,128]{1,0:T(8,128)(2,1)S(1)}, u32[]{:S(2)}, u32[]{:S(2)}) %collective-permute-start.21) | collective-permute-done | bytes 36896 | tf_op jit(solution)/shard_map/ppermute | solution.py:335
  53.3 0.9 %collective-permute-done.24.refs_3_ = bf16[144,128]{1,0:T(8,128)(2,1)S(1)} collective-permute-done((bf16[144,128]{1,0:T(8,128)(2,1)S(1)}, bf16[144,128]{1,0:T(8,128)(2,1)S(1)}, u32[]{:S(2)}, u32[]{:S(2)}) %collective-permute-start.24) | collective-permute-done | bytes 36896 | tf_op jit(solution)/shard_map/ppermute | solution.py:329
  54.4 1.5 %outer_grad.1 = (bf16[256,256]{1,0:T(8,128)(2,1)}, bf16[256,256]{1,0:T(8,128)(2,1)}, bf16[256,256]{1,0:T(8,128)(2,1)}) custom-call(s32[2]{0:T(128)S(1)} %pad_add_fusion.where_ref, bf16[256,256]{1,0:T(8,128)(2,1)S(1)} %copy-done.1, bf16[256,256]{1,0:T(8,128)(2,1)S(1)} %copy-done.2, f32[256,512]{1,0:T(8,128)S(1)} %get-tuple-element.85.inner_ref, ...), custom_call_target="tpu_custom_call" | custom-call | flops 1 | bytes 1 | tf_op jit(solution)/shard_map/outer_grad/pallas_call | solution.py:292
  (57 shorter events, 9.4 us)
Async XLA Ops:
  0.7 4.4 %collective-permute-start = (bf16[256,256]{1,0:T(8,128)(2,1)}, bf16[256,256]{1,0:T(8,128)(2,1)S(1)}, u32[]{:S(2)}, u32[]{:S(2)}) collective-permute-start(bf16[256,256]{1,0:T(8,128)(2,1)} %q_ref.1), channel_id=1, source_target_pairs={{0,4},{4,0},{8,12},{12,8},{16,20},{20,16},{24,28},{28,24},{1,5},{5... | collective-permute-start | bytes 393224 | tf_op jit(solution)/shard_map/ppermute | solution.py:329
  1.2 3.9 %collective-permute-start.1 = (bf16[256,256]{1,0:T(8,128)(2,1)}, bf16[256,256]{1,0:T(8,128)(2,1)S(1)}, u32[]{:S(2)}, u32[]{:S(2)}) collective-permute-start(bf16[256,256]{1,0:T(8,128)(2,1)} %k_ref.3), channel_id=1, source_target_pairs={{0,4},{4,0},{8,12},{12,8},{16,20},{20,16},{24,28},{28,24},{1,5},{5... | collective-permute-start | bytes 393224 | tf_op jit(solution)/shard_map/ppermute | solution.py:329
  1.3 3.9 %collective-permute-start.2 = (bf16[256,256]{1,0:T(8,128)(2,1)}, bf16[256,256]{1,0:T(8,128)(2,1)S(1)}, u32[]{:S(2)}, u32[]{:S(2)}) collective-permute-start(bf16[256,256]{1,0:T(8,128)(2,1)} %v_ref.3), channel_id=1, source_target_pairs={{0,4},{4,0},{8,12},{12,8},{16,20},{20,16},{24,28},{28,24},{1,5},{5... | collective-permute-start | bytes 393224 | tf_op jit(solution)/shard_map/ppermute | solution.py:329
  1.7 3.4 %collective-permute-start.3 = (f32[2,256]{1,0:T(2,128)}, f32[2,256]{1,0:T(2,128)S(1)}, u32[]{:S(2)}, u32[]{:S(2)}) collective-permute-start(f32[2,256]{1,0:T(2,128)} %decay_ref.1), channel_id=1, source_target_pairs={{0,4},{4,0},{8,12},{12,8},{16,20},{20,16},{24,28},{28,24},{1,5},{5... | collective-permute-start | bytes 6152 | tf_op jit(solution)/shard_map/ppermute | solution.py:329
  5.2 5.9 %collective-permute-start.4 = (bf16[256,1536]{1,0:T(8,128)(2,1)S(1)}, bf16[256,1536]{1,0:T(8,128)(2,1)S(1)}, u32[]{:S(2)}, u32[]{:S(2)}) collective-permute-start(bf16[256,1536]{1,0:T(8,128)(2,1)S(1)} %copy-done), channel_id=1, source_target_pairs={{0,4},{4,0},{8,12},{12,8},{16,20},{20,16},{24,28},{28,24},{1,5},{5... | collective-permute-start | bytes 2359304 | tf_op jit(solution)/shard_map/ppermute | solution.py:329
  5.7 9.3 %collective-permute-start.5 = (bf16[64,1536]{1,0:T(8,128)(2,1)S(1)}, bf16[64,1536]{1,0:T(8,128)(2,1)S(1)}, u32[]{:S(2)}, u32[]{:S(2)}) collective-permute-start(bf16[64,1536]{1,0:T(8,128)(2,1)S(1)} %dynamic_slice.12), channel_id=1, source_target_pairs={{0,3},{1,2},{2,1},{3,0},{4,7},{5,6},{6,5},{7,4},{8,11},{9,10},{10,... | collective-permute-start | bytes 589832 | tf_op jit(solution)/shard_map/ppermute | solution.py:326
  9.2 17.6 %collective-permute-start.10 = (bf16[128,1536]{1,0:T(8,128)(2,1)S(1)}, bf16[128,1536]{1,0:T(8,128)(2,1)S(1)}, u32[]{:S(2)}, u32[]{:S(2)}) collective-permute-start(bf16[128,1536]{1,0:T(8,128)(2,1)S(1)} %get-tuple-element.94), channel_id=1, source_target_pairs={{0,2},{1,3},{2,0},{3,1},{4,6},{5,7},{6,4},{7,5},{8,10},{9,11},{10,... | collective-permute-start | bytes 1179656 | tf_op jit(solution)/shard_map/ppermute | solution.py:326
  9.7 17.1 %collective-permute-start.9 = (bf16[128,1536]{1,0:T(8,128)(2,1)S(1)}, bf16[128,1536]{1,0:T(8,128)(2,1)S(1)}, u32[]{:S(2)}, u32[]{:S(2)}) collective-permute-start(bf16[128,1536]{1,0:T(8,128)(2,1)S(1)} %get-tuple-element.95), channel_id=1, source_target_pairs={{0,1},{1,0},{2,3},{3,2},{4,5},{5,4},{6,7},{7,6},{8,9},{9,8},{10,11... | collective-permute-start | bytes 1179656 | tf_op jit(solution)/shard_map/ppermute | solution.py:326
  11.1 5.5 %collective-permute-start.6 = (bf16[144,128]{1,0:T(8,128)(2,1)S(1)}, bf16[144,128]{1,0:T(8,128)(2,1)S(1)}, u32[]{:S(2)}, u32[]{:S(2)}) collective-permute-start(bf16[144,128]{1,0:T(8,128)(2,1)S(1)} %get-tuple-element.56.refs_0_), channel_id=1, source_target_pairs={{0,8},{4,12},{8,16},{12,20},{16,24},{20,28},{1,9},{5,13},{9,17},{1... | collective-permute-start | bytes 110600 | tf_op jit(solution)/shard_map/ppermute | solution.py:335
  16.6 9.0 %collective-permute-start.7 = (bf16[64,1536]{1,0:T(8,128)(2,1)S(1)}, bf16[64,1536]{1,0:T(8,128)(2,1)S(1)}, u32[]{:S(2)}, u32[]{:S(2)}) collective-permute-start(bf16[64,1536]{1,0:T(8,128)(2,1)S(1)} %collective-permute-done.5.refs_1_), channel_id=1, source_target_pairs={{0,8},{4,12},{8,0},{12,4},{16,24},{20,28},{24,16},{28,20},{1,9},{5... | collective-permute-start | bytes 589832 | tf_op jit(solution)/shard_map/ppermute | solution.py:332
  19.5 6.1 %collective-permute-start.8 = (bf16[144,128]{1,0:T(8,128)(2,1)S(1)}, bf16[144,128]{1,0:T(8,128)(2,1)S(1)}, u32[]{:S(2)}, u32[]{:S(2)}) collective-permute-start(bf16[144,128]{1,0:T(8,128)(2,1)S(1)} %join.1), channel_id=1, source_target_pairs={{0,16},{4,20},{8,24},{12,28},{1,17},{5,21},{9,25},{13,29},{2,18},{... | collective-permute-start | bytes 110600 | tf_op jit(solution)/shard_map/ppermute | solution.py:335
  27.9 7.5 %collective-permute-start.13 = (bf16[2,256,128]{2,1,0:T(8,128)(2,1)S(1)}, bf16[2,256,128]{2,1,0:T(8,128)(2,1)S(1)}, u32[]{:S(2)}, u32[]{:S(2)}) collective-permute-start(bf16[2,256,128]{2,1,0:T(8,128)(2,1)S(1)} %get-tuple-element.73), channel_id=1, source_target_pairs={{0,1},{1,0},{2,3},{3,2},{4,5},{5,4},{6,7},{7,6},{8,9},{9,8},{10,11... | collective-permute-start | bytes 393224 | tf_op jit(solution)/shard_map/ppermute | solution.py:326
  29.5 11.1 %collective-permute-start.12 = (bf16[2,256,128]{2,1,0:T(8,128)(2,1)S(1)}, bf16[2,256,128]{2,1,0:T(8,128)(2,1)S(1)}, u32[]{:S(2)}, u32[]{:S(2)}) collective-permute-start(bf16[2,256,128]{2,1,0:T(8,128)(2,1)S(1)} %get-tuple-element.69), channel_id=1, source_target_pairs={{0,3},{1,2},{2,1},{3,0},{4,7},{5,6},{6,5},{7,4},{8,11},{9,10},{10,... | collective-permute-start | bytes 393224 | tf_op jit(solution)/shard_map/ppermute | solution.py:326
  31.0 9.6 %collective-permute-start.14 = (bf16[2,256,128]{2,1,0:T(8,128)(2,1)S(1)}, bf16[2,256,128]{2,1,0:T(8,128)(2,1)S(1)}, u32[]{:S(2)}, u32[]{:S(2)}) collective-permute-start(bf16[2,256,128]{2,1,0:T(8,128)(2,1)S(1)} %get-tuple-element.74), channel_id=1, source_target_pairs={{0,2},{1,3},{2,0},{3,1},{4,6},{5,7},{6,4},{7,5},{8,10},{9,11},{10,... | collective-permute-start | bytes 393224 | tf_op jit(solution)/shard_map/ppermute | solution.py:326
  32.4 9.3 %collective-permute-start.15 = (bf16[2,256,128]{2,1,0:T(8,128)(2,1)S(1)}, bf16[2,256,128]{2,1,0:T(8,128)(2,1)S(1)}, u32[]{:S(2)}, u32[]{:S(2)}) collective-permute-start(bf16[2,256,128]{2,1,0:T(8,128)(2,1)S(1)} %get-tuple-element.79.refs_0_.refs_4_), channel_id=1, source_target_pairs={{0,3},{1,2},{2,1},{3,0},{4,7},{5,6},{6,5},{7,4},{8,11},{9,10},{10,... | collective-permute-start | bytes 393224 | tf_op jit(solution)/shard_map/ppermute | solution.py:326
  34.9 6.8 %collective-permute-start.16 = (bf16[2,256,128]{2,1,0:T(8,128)(2,1)S(1)}, bf16[2,256,128]{2,1,0:T(8,128)(2,1)S(1)}, u32[]{:S(2)}, u32[]{:S(2)}) collective-permute-start(bf16[2,256,128]{2,1,0:T(8,128)(2,1)S(1)} %get-tuple-element.79.refs_0_.refs_4_), channel_id=1, source_target_pairs={{0,1},{1,0},{2,3},{3,2},{4,5},{5,4},{6,7},{7,6},{8,9},{9,8},{10,11... | collective-permute-start | bytes 393224 | tf_op jit(solution)/shard_map/ppermute | solution.py:326
  35.5 6.5 %collective-permute-start.17 = (bf16[2,256,128]{2,1,0:T(8,128)(2,1)S(1)}, bf16[2,256,128]{2,1,0:T(8,128)(2,1)S(1)}, u32[]{:S(2)}, u32[]{:S(2)}) collective-permute-start(bf16[2,256,128]{2,1,0:T(8,128)(2,1)S(1)} %get-tuple-element.79.refs_0_.refs_4_), channel_id=1, source_target_pairs={{0,2},{1,3},{2,0},{3,1},{4,6},{5,7},{6,4},{7,5},{8,10},{9,11},{10,... | collective-permute-start | bytes 393224 | tf_op jit(solution)/shard_map/ppermute | solution.py:326
  42.0 6.5 %collective-permute-start.18 = (bf16[256,1536]{1,0:T(8,128)(2,1)S(1)}, bf16[256,1536]{1,0:T(8,128)(2,1)S(1)}, u32[]{:S(2)}, u32[]{:S(2)}) collective-permute-start(bf16[256,1536]{1,0:T(8,128)(2,1)S(1)} %get-tuple-element.81.refs_1_), channel_id=1, source_target_pairs={{0,4},{4,0},{8,12},{12,8},{16,20},{20,16},{24,28},{28,24},{1,5},{5... | collective-permute-start | bytes 2359304 | tf_op jit(solution)/shard_map/ppermute | solution.py:329
  42.0 6.4 %collective-permute-start.11 = (bf16[128,1536]{1,0:T(8,128)(2,1)S(1)}, bf16[128,1536]{1,0:T(8,128)(2,1)S(1)}, u32[]{:S(2)}, u32[]{:S(2)}) collective-permute-start(bf16[128,1536]{1,0:T(8,128)(2,1)S(1)} %get-tuple-element.67.refs_0_), channel_id=1, source_target_pairs={{0,4},{4,0},{8,12},{12,8},{16,20},{20,16},{24,28},{28,24},{1,5},{5... | collective-permute-start | bytes 1179656 | tf_op jit(solution)/shard_map/ppermute | solution.py:329
  43.1 2.7 %collective-permute-start.19 = (bf16[4,256,128]{2,1,0:T(8,128)(2,1)S(1)}, bf16[4,256,128]{2,1,0:T(8,128)(2,1)S(1)}, u32[]{:S(2)}, u32[]{:S(2)}) collective-permute-start(bf16[4,256,128]{2,1,0:T(8,128)(2,1)S(1)} %cross.1), channel_id=1, source_target_pairs={{0,4},{4,0},{8,12},{12,8},{16,20},{20,16},{24,28},{28,24},{1,5},{5... | collective-permute-start | bytes 786440 | tf_op jit(solution)/shard_map/ppermute | solution.py:329
  43.2 7.8 %collective-permute-start.20 = (bf16[144,128]{1,0:T(8,128)(2,1)S(1)}, bf16[144,128]{1,0:T(8,128)(2,1)S(1)}, u32[]{:S(2)}, u32[]{:S(2)}) collective-permute-start(bf16[144,128]{1,0:T(8,128)(2,1)S(1)} %get-tuple-element.80), channel_id=1, source_target_pairs={{24,0},{28,4},{25,1},{29,5},{26,2},{30,6},{27,3},{31,7}} | collective-permute-start | bytes 110600 | tf_op jit(solution)/shard_map/ppermute | solution.py:335
  44.5 7.8 %collective-permute-start.21 = (bf16[144,128]{1,0:T(8,128)(2,1)S(1)}, bf16[144,128]{1,0:T(8,128)(2,1)S(1)}, u32[]{:S(2)}, u32[]{:S(2)}) collective-permute-start(bf16[144,128]{1,0:T(8,128)(2,1)S(1)} %get-tuple-element.80), channel_id=1, source_target_pairs={{16,0},{20,4},{24,8},{28,12},{17,1},{21,5},{25,9},{29,13},{18,2},{... | collective-permute-start | bytes 110600 | tf_op jit(solution)/shard_map/ppermute | solution.py:335
  45.8 6.5 %collective-permute-start.22 = (bf16[144,128]{1,0:T(8,128)(2,1)S(1)}, bf16[144,128]{1,0:T(8,128)(2,1)S(1)}, u32[]{:S(2)}, u32[]{:S(2)}) collective-permute-start(bf16[144,128]{1,0:T(8,128)(2,1)S(1)} %get-tuple-element.80), channel_id=1, source_target_pairs={{8,0},{12,4},{16,8},{20,12},{24,16},{28,20},{9,1},{13,5},{17,9},{2... | collective-permute-start | bytes 110600 | tf_op jit(solution)/shard_map/ppermute | solution.py:335
  52.3 2.1 %collective-permute-start.23 = (f32[256,512]{1,0:T(8,128)S(1)}, f32[256,512]{1,0:T(8,128)S(1)}, u32[]{:S(2)}, u32[]{:S(2)}) collective-permute-start(f32[256,512]{1,0:T(8,128)S(1)} %get-tuple-element.90), channel_id=1, source_target_pairs={{0,4},{4,0},{8,12},{12,8},{16,20},{20,16},{24,28},{28,24},{1,5},{5... | collective-permute-start | bytes 1572872 | tf_op jit(solution)/shard_map/ppermute | solution.py:329
  (9 other events, 67.0 us)
